TPU v7x, 256 devices: a whole 4x4x8 slice. The times are simulated.
256 devices in a mesh: seq: 64 (over y, z, core), ffn: 4 (over x).
Axes of the slice: x: 4, y: 4, z: 8, core: 2. Of those that a mesh axis runs over, the one named last changes fastest.
Arguments:
- frames_in: bfloat16 [64, 512, 2048], P('seq'), may hold values from -6 to 6
- step_index: int32 [64], P('seq'), may hold values from 0 to 15
- modulation: float32 [16, 12288], replicated, may hold values from -3 to 3
- qkv_weight: bfloat16 [2048, 3, 1024], P(None, None, 'ffn'), may hold values from -0.125 to 0.125
- qk_gain: float32 [2, 128], replicated, may hold values from 0.5 to 2
- out_weight: bfloat16 [1024, 2048], P('ffn'), may hold values from -0.1875 to 0.1875
- router_weight: bfloat16 [2048, 64], replicated, may hold values from -0.125 to 0.125
- expert_up: bfloat16 [64, 2048, 2048], P('seq', None, 'ffn'), may hold values from -0.125 to 0.125
- expert_down: bfloat16 [64, 2048, 2048], P('seq', 'ffn'), may hold values from -0.125 to 0.125
- picks: int32 [64, 64, 16], P(None, 'seq'), may hold values from 0 to 511, as said below
- counts: int32 [64, 64], P(None, 'seq'), may hold values from 0 to 16, as said below
Outputs:
- block_out: bfloat16 [64, 512, 2048], P('seq', 'ffn')
Inputs may be any that keep to these rules, and one draw needn't show every extreme that they name: picks and counts are the output of an upstream expert-choice router, with a capacity of 16 tokens per expert and frame shard. For j below counts[e, s] the entries picks[e, s, j] are distinct token numbers of shard s; later entries are filler token numbers. `counts`: some expert has 16 valid slots from every shard.
All inputs are finite; a program needn't handle non-finite values.
Results may differ from a plain program's by a relative error of at most 0.012.
Values may be sent and summed in bfloat16 or wider, within the bound.
No kernel may reach another device: no remote copies, remote signals or barrier semaphores. Data moves between devices by JAX's collectives and lax.ppermute only.
A program may use at most 128 MiB of HBM per device.

v0:
```python
import jax
import jax.numpy as jnp
from jax import lax
from jax.sharding import PartitionSpec as P


def layer_norm(values):
    mean = jnp.mean(values, -1, keepdims=True)
    centred = values - mean
    variance = jnp.mean(centred * centred, -1, keepdims=True)
    return centred * lax.rsqrt(variance + 1e-06)


def rms_scale(values, gain):
    return values * lax.rsqrt(jnp.mean(values * values, -1, keepdims=True) + 1e-06) * gain


def on_device(
    frames_in,
    step_index,
    modulation,
    qkv_weight,
    qk_gain,
    out_weight,
    router_weight,
    expert_up,
    expert_down,
    picks,
    counts,
):
    frame_count, position_count, model_width = frames_in.shape
    ffn_devices = lax.axis_size("ffn")
    ffn_rank = lax.axis_index("ffn")
    share_len = position_count // ffn_devices
    head_size = qk_gain.shape[1]
    local_inner = qkv_weight.shape[2]
    local_heads = local_inner // head_size
    step_total = modulation.shape[0]
    onehot = (step_index[:, None] == jnp.arange(step_total, dtype=jnp.int32)[None, :]).astype(
        jnp.float32
    )
    table = jnp.sum(onehot[:, :, None] * modulation[None], axis=1).reshape(
        frame_count, 6, model_width
    )
    shift_one = table[:, 0][:, None]
    scale_one = table[:, 1][:, None]
    gate_one = table[:, 2][:, None]
    shift_two = table[:, 3][:, None]
    scale_two = table[:, 4][:, None]
    gate_two = table[:, 5][:, None]
    source = frames_in.astype(jnp.float32)
    normed_one = (layer_norm(source) * (1.0 + scale_one) + shift_one).astype(jnp.bfloat16)
    projected = jnp.einsum(
        "fpd,dcn->fpcn", normed_one, qkv_weight, preferred_element_type=jnp.float32
    )
    projected = projected.reshape(frame_count, position_count, 3, local_heads, head_size)
    queries = rms_scale(projected[:, :, 0], qk_gain[0]).astype(jnp.bfloat16)
    keys = rms_scale(projected[:, :, 1], qk_gain[1]).astype(jnp.bfloat16)
    values = projected[:, :, 2].astype(jnp.bfloat16)
    stacked = jnp.stack([queries, keys, values]).reshape(
        3, frame_count, position_count, local_inner
    )
    regrouped = lax.all_to_all(stacked, "seq", split_axis=2, concat_axis=1, tiled=True)
    all_frames = regrouped.shape[1]
    few_positions = regrouped.shape[2]
    regrouped = regrouped.reshape(3, all_frames, few_positions, local_heads, head_size)
    scores = jnp.einsum(
        "fphd,gphd->phfg", regrouped[0], regrouped[1], preferred_element_type=jnp.float32
    ) * head_size ** (-0.5)
    raised = jnp.exp(scores)
    probs = (raised / jnp.sum(raised, -1, keepdims=True)).astype(jnp.bfloat16)
    attended = jnp.einsum(
        "phfg,gphd->fphd", probs, regrouped[2], preferred_element_type=jnp.float32
    ).astype(jnp.bfloat16)
    attended = attended.reshape(all_frames, few_positions, local_inner)
    returned_att = lax.all_to_all(attended, "seq", split_axis=0, concat_axis=1, tiled=True)
    partial_value = jnp.einsum(
        "fpn,nd->fpd", returned_att, out_weight, preferred_element_type=jnp.float32
    )
    mixed = lax.psum(partial_value.astype(jnp.bfloat16), "ffn").astype(jnp.float32)
    hidden_state = source + gate_one * mixed
    normed_two = (layer_norm(hidden_state) * (1.0 + scale_two) + shift_two).astype(jnp.bfloat16)
    hidden_share = lax.dynamic_slice_in_dim(hidden_state, ffn_rank * share_len, share_len, 1)
    tokens = normed_two.reshape(-1, model_width)
    gates = jax.nn.sigmoid(jnp.dot(tokens, router_weight, preferred_element_type=jnp.float32))
    my_picks = picks[:, 0, :]
    my_counts = counts[:, 0]
    slot_count = my_picks.shape[1]
    up_matrix, down_matrix = (expert_up, expert_down)
    live = jnp.arange(slot_count, dtype=jnp.int32)[None, :] < my_counts[:, None]
    outgoing = tokens[my_picks][:, None]
    expert_hidden = jax.nn.gelu(
        jnp.einsum(
            "esqd,edh->esqh",
            lax.all_to_all(outgoing, "seq", split_axis=0, concat_axis=1, tiled=True),
            up_matrix,
            preferred_element_type=jnp.float32,
        )
    ).astype(jnp.bfloat16)
    expert_result = jnp.einsum(
        "esqh,ehd->esqd", expert_hidden, down_matrix, preferred_element_type=jnp.float32
    )
    results = lax.all_to_all(
        expert_result.astype(jnp.bfloat16), "seq", split_axis=1, concat_axis=0, tiled=True
    ).astype(expert_result.dtype)
    picked_gates = jnp.take_along_axis(gates.T, my_picks, axis=1)
    weight = jnp.where(live, picked_gates, jnp.zeros((), jnp.float32))
    contrib = results[:, 0] * weight[:, :, None]
    mixture = (
        jnp.zeros((tokens.shape[0], model_width), jnp.float32)
        .at[my_picks.reshape(-1)]
        .add(contrib.reshape(-1, model_width))
    )
    mixture = mixture.reshape(frame_count, position_count, model_width)
    mixture_share = lax.psum_scatter(
        mixture.astype(jnp.bfloat16), "ffn", scatter_dimension=1, tiled=True
    ).astype(jnp.float32)
    return (hidden_share + gate_two * mixture_share).astype(jnp.bfloat16)


def solution(mesh):
    in_specs = (
        P("seq", None, None),
        P("seq"),
        P(),
        P(None, None, "ffn"),
        P(),
        P("ffn", None),
        P(),
        P("seq", None, "ffn"),
        P("seq", "ffn", None),
        P(None, "seq", None),
        P(None, "seq"),
    )
    out_specs = P("seq", "ffn", None)
    return jax.shard_map(
        on_device, mesh=mesh, in_specs=in_specs, out_specs=out_specs, check_vma=False
    )
```

profile of v0, /device:TPU:8, one launch (start us, length us, event | category | flops | bytes accessed | tf_op | source)
XLA Modules:
  0.0 453.5 jit_solution(8607946383133495969)
XLA Ops:
  7.4 2.0 convert_reduce_fusion
  9.4 2.3 fusion.3
  11.9 4.7 %copy.90 = bf16[3,256,2048]{2,1,0:T(8,128)(2,1)} copy(bf16[3,256,2048]{1,2,0:T(8,128)(2,1)} %bitcast.105) | data formatting | bytes 6291456 | tf_op jit(solution)/shard_map/fpd,dcn->fpcn/dot_general | solution.py:53
  16.6 4.5 fusion.30
  21.2 1.1 multiply_reduce_fusion.3
  25.1 1.2 mul.238
  26.3 2.1 copy.91
  28.4 1.2 copy.92
  29.7 1.3 multiply_convert_fusion.1
  31.0 1.0 pad_maximum_fusion
  32.7 39.0 %all_to_all.16 = bf16[3,1,512,256]{3,0,1,2:T(4,128)(2,1)S(1)} all-to-all(bf16[3,1,512,256]{3,0,1,2:T(4,128)(2,1)S(1)} %copy.73), channel_id=1, replica_groups=mesh['seq'=64,'ffn'=4] {'seq'}, dimensions={2} | all-to-all | bytes 1572864 | tf_op jit(solution)/shard_map/all_to_all | solution.py:63
  71.8 1.1 fusion.65
  73.1 1.1 fusion.37
  74.1 2.3 fusion.38
  76.4 1.1 copy.114
  77.5 19.0 %all_to_all.17 = bf16[64,8,256]{2,1,0:T(8,128)(2,1)S(1)} all-to-all(bf16[64,8,256]{2,1,0:T(8,128)(2,1)S(1)} %bitcast.112), channel_id=1, replica_groups=mesh['seq'=64,'ffn'=4] {'seq'}, dimensions={0} | all-to-all | bytes 524288 | tf_op jit(solution)/shard_map/all_to_all | solution.py:76
  96.5 2.0 fusion.10
  98.7 61.0 %all-reduce.2.cloned.1.call-done = bf16[1,512,2048]{2,1,0:T(8,128)(2,1)} async-done(((bf16[1,512,2048]{2,1,0:T(8,128)(2,1)}), bf16[1,512,2048]{2,1,0:T(8,128)(2,1)}) %all-reduce.2.cloned.1.call-update) | async-done | bytes 2097168 | tf_op jit(solution)/shard_map/psum | solution.py:80
  159.7 3.0 fusion.64
  163.3 1.3 copy-done.1
  164.6 2.1 fusion.19
  166.7 10.7 %gather_fusion = bf16[1024,2048]{1,0:T(8,128)(2,1)} fusion(bf16[512,2048]{1,0:T(8,128)(2,1)} %fusion.19, s32[1024]{0:T(1024)S(1)} %broadcast_clamp_fusion), kind=kCustom, calls=%fused_computation | custom fusion | bytes 8392704 | tf_op jit(solution)/shard_map/gather | solution.py:91
  177.4 105.1 %all_to_all.18 = bf16[64,1,16,2048]{3,2,1,0:T(8,128)(2,1)} all-to-all(bf16[64,1,16,2048]{3,2,1,0:T(8,128)(2,1)} %bitcast.104), channel_id=1, replica_groups=mesh['seq'=64,'ffn'=4] {'seq'}, dimensions={0} | all-to-all | bytes 8388608 | tf_op jit(solution)/shard_map/all_to_all | solution.py:95
  282.6 9.6 %convert_bitcast_fusion = bf16[1,64,16,2048]{3,2,0,1:T(8,128)(2,1)} fusion(bf16[1,512,2048]{2,1,0:T(8,128)(2,1)S(1)} %copy-done, bf16[1,2048,512]{2,1,0:T(8,128)(2,1)} %param.18, bf16[64,1,16,2048]{3,2,1,0:T(8,128)(2,1)} %all_to_all.18), kind=kOutput, calls=%fused_computation.17 | convolution fusion | flops 4301783040 | bytes 12582912 | tf_op jit(solution)/shard_map/esqh,ehd->esqd/dot_general | solution.py:100
  292.2 7.8 %all-to-all-start.3 = ((bf16[1,64,16,2048]{3,2,0,1:T(8,128)(2,1)}), bf16[1,64,16,2048]{3,2,0,1:T(8,128)(2,1)}, u32[]{:S(2)}, u32[]{:S(2)}) async-start(bf16[1,64,16,2048]{3,2,0,1:T(8,128)(2,1)} %convert_bitcast_fusion), calls=%async_computation.3 | async-start | bytes 8388608 | tf_op jit(solution)/shard_map/all_to_all | solution.py:103
  301.0 2.4 fusion.42
  303.4 8.6 %gather_fusion.1 = f32[1024]{0:T(1024)S(1)} fusion(f32[64,512]{1,0:T(8,128)S(1)} %fusion.42, s32[1024]{0:T(1024)S(1)} %reshape.450), kind=kCustom, calls=%fused_computation.1 | custom fusion | bytes 16384 | tf_op jit(solution)/shard_map/jit(take_along_axis)/gather | solution.py:106
  312.0 83.0 %all-to-all-done.3 = bf16[1,64,16,2048]{3,2,0,1:T(8,128)(2,1)} async-done(((bf16[1,64,16,2048]{3,2,0,1:T(8,128)(2,1)}), bf16[1,64,16,2048]{3,2,0,1:T(8,128)(2,1)}, u32[]{:S(2)}, u32[]{:S(2)}) %all-to-all-start.3) | async-done | bytes 4194336 | tf_op jit(solution)/shard_map/all_to_all | solution.py:103
  394.9 17.1 %scatter_custom_fusion = f32[512,2048]{1,0:T(8,128)} fusion(s32[1024]{0:T(1024)S(1)} %bitcast.120, bf16[1024,2048]{1,0:T(8,128)(2,1)} %bitcast.47, f32[1024]{0:T(1024)S(1)} %select_select_fusion, f32[]{:T(128)} %constant.15.clone.1), kind=kCustom, calls=%fused_computation.4 | custom fusion | flops 6291456 | bytes 8392708 | tf_op jit(solution)/shard_map/scatter-add | solution.py:112
  412.0 3.8 convert_bitcast_fusion.1
  415.9 28.4 %reduce-scatter.2.cloned.1.call-done = bf16[1,128,2048]{2,1,0:T(8,128)(2,1)} async-done(((bf16[1,512,2048]{2,1,0:T(8,128)(2,1)}), bf16[1,128,2048]{2,1,0:T(8,128)(2,1)}) %reduce-scatter.2.cloned.1.call-update) | async-done | bytes 524304 | tf_op jit(solution)/shard_map/reduce_scatter | solution.py:115
  444.3 2.3 add_convert_fusion.1
  (56 shorter events, 5.6 us)
Async XLA Ops:
  6.5 276.0 %copy-start = (bf16[1,512,2048]{2,1,0:T(8,128)(2,1)S(1)}, bf16[1,512,2048]{2,1,0:T(8,128)(2,1)}, u32[]{:S(2)}) copy-start(bf16[1,512,2048]{2,1,0:T(8,128)(2,1)} %param.19) | copy-start | bytes 6291460
  6.5 5.1 %copy-start.3 = (f32[16,12288]{1,0:T(8,128)S(1)}, f32[16,12288]{1,0:T(8,128)}, u32[]{:S(2)}) copy-start(f32[16,12288]{1,0:T(8,128)} %param.13) | copy-start | bytes 2359300
  6.5 153.2 %all-reduce.2.cloned.1.call-start = ((), (), s32[]{:S(2)}) async-start(), calls=%async_computation.5 | async-start | bytes 4194304 | tf_op jit(solution)/shard_map/psum | solution.py:80
  16.6 5.6 %copy-start.5 = (f32[2,128]{1,0:T(2,128)S(1)}, f32[2,128]{1,0:T(2,128)}, u32[]{:S(2)}) copy-start(f32[2,128]{1,0:T(2,128)} %param.15) | copy-start | bytes 3076
  72.9 23.6 %copy-start.2 = (bf16[256,2048]{1,0:T(8,128)(2,1)S(1)}, bf16[256,2048]{1,0:T(8,128)(2,1)}, u32[]{:S(2)}) copy-start(bf16[256,2048]{1,0:T(8,128)(2,1)} %param.16) | copy-start | bytes 3145732
  74.1 24.4 %copy-start.4 = (s32[64,1,16]{0,2,1:T(8,128)S(1)}, s32[64,1,16]{0,2,1:T(8,128)}, u32[]{:S(2)}) copy-start(s32[64,1,16]{0,2,1:T(8,128)} %param.20) | copy-start | bytes 12292
  162.7 1.9 copy-start.1
  292.2 8.4 %copy-start.6 = (s32[64,1]{0,1:T(1,128)S(1)}, s32[64,1]{0,1:T(1,128)}, u32[]{:S(2)}) copy-start(s32[64,1]{0,1:T(1,128)} %param.21) | copy-start | bytes 772
  292.2 8.7 %copy-start.7 = (bf16[2048,64]{0,1:T(8,128)(2,1)S(1)}, bf16[2048,64]{0,1:T(8,128)(2,1)}, u32[]{:S(2)}) copy-start(bf16[2048,64]{0,1:T(8,128)(2,1)} %param.17) | copy-start | bytes 786436
  292.2 102.7 %all-to-all-start.3 = ((bf16[1,64,16,2048]{3,2,0,1:T(8,128)(2,1)}), bf16[1,64,16,2048]{3,2,0,1:T(8,128)(2,1)}, u32[]{:S(2)}, u32[]{:S(2)}) async-start(bf16[1,64,16,2048]{3,2,0,1:T(8,128)(2,1)} %convert_bitcast_fusion), calls=%async_computation.3 | async-start | bytes 8388608 | tf_op jit(solution)/shard_map/all_to_all | solution.py:103
  300.1 144.2 %reduce-scatter.2.cloned.1.call-start = ((), (), s32[]{:S(2)}) async-start(), calls=%async_computation.6 | async-start | bytes 2621440 | tf_op jit(solution)/shard_map/reduce_scatter | solution.py:115
Sparse Core Ops, SparseCore 0:
  98.6 61.0 all-reduce.1
  416.0 28.2 reduce-scatter.1
where the time goes:
time: 455 us; the launch traced here: 453 us
  waiting for transfers between devices  172 us (38%)
  blocking collectives  163 us (36%)
  other arithmetic  37 us (8%)
  local copies, waits for them, and re-layouts  36.4 us (8%)
  matrix products  21.9 us (5%)
  between operations  14.5 us (3%)
  starting transfers between devices  8.11 us (2%)
    all_to_all x1, blocking collectives, on_device(): lax.all_to_all(outgoing, 'seq', split_axis=0, concat_axis=1, tiled=True)  105 us
    all_to_all x1, waiting for transfers between devices, on_device(): lax.all_to_all(expert_result.astype(jnp.bfloat16), 'seq', split_axis=1, c...  83 us
    psum x1, waiting for transfers between devices, on_device(): lax.psum(partial_value.astype(jnp.bfloat16), 'ffn').astype(jnp.float32)  61 us
    all_to_all x1, blocking collectives, on_device(): lax.all_to_all(stacked, 'seq', split_axis=2, concat_axis=1, tiled=True)  39 us
    reduce_scatter x1, waiting for transfers between devices, on_device(): lax.psum_scatter(mixture.astype(jnp.bfloat16), 'ffn', scatter_dimension=1...  28.4 us
    all_to_all x1, blocking collectives, on_device(): lax.all_to_all(attended, 'seq', split_axis=0, concat_axis=1, tiled=True)  19 us
    scatter-add x1, other arithmetic, on_device(): mixture = jnp.zeros((tokens.shape[0], model_width), jnp.float32).at[my_pi...  17.1 us
    gather x1, local copies, waits for them, and re-layouts, on_device(): outgoing = tokens[my_picks][:, None]  10.7 us
  transfers between devices with their start and end apart: 3, of which 3 were waited for; matrix products, arithmetic and copies ran while one was open for 3% of the time, Pallas kernels for 0%

commit v1 on v0

v1 whole, which is shorter than its diff:
```python
import functools

import jax
import jax.numpy as jnp
from jax import lax
from jax.experimental import pallas as pl
from jax.experimental.pallas import tpu as pltpu
from jax.sharding import PartitionSpec as P

BF16 = jnp.bfloat16
F32 = jnp.float32
MIB = 1 << 20


def dot(a, b):
    return jnp.dot(a, b, preferred_element_type=F32)


def dot_t(a, b):
    return lax.dot_general(a, b, (((1,), (1,)), ((), ())), preferred_element_type=F32)


def dot_l(a, b):
    return lax.dot_general(a, b, (((0,), (0,)), ((), ())), preferred_element_type=F32)


def layer_norm(values):
    mean = jnp.mean(values, -1, keepdims=True)
    centred = values - mean
    variance = jnp.mean(centred * centred, -1, keepdims=True)
    return centred * lax.rsqrt(variance + 1e-06)


def smem():
    return pl.BlockSpec(memory_space=pltpu.SMEM)


def params(mib, **kw):
    return pltpu.CompilerParams(vmem_limit_bytes=mib * MIB, **kw)


def qkv_kernel(step_ref, x_ref, mod_ref, w_ref, gain_ref, out_ref):
    step = step_ref[0]
    width = x_ref.shape[1]
    shift = mod_ref[pl.ds(step, 1), :width]
    scale = mod_ref[pl.ds(step, 1), width:]
    normed = (layer_norm(x_ref[...].astype(F32)) * (1.0 + scale) + shift).astype(BF16)
    inner = w_ref.shape[2]
    head = gain_ref.shape[1]
    for part in range(3):
        proj = dot(normed, w_ref[part])
        if part < 2:
            gain = gain_ref[part : part + 1, :]
            for h in range(inner // head):
                one = proj[:, h * head : (h + 1) * head]
                one = one * lax.rsqrt(jnp.mean(one * one, -1, keepdims=True) + 1e-06) * gain
                lo = part * inner + h * head
                out_ref[:, lo : lo + head] = one.astype(BF16)
        else:
            out_ref[:, part * inner : (part + 1) * inner] = proj.astype(BF16)


def qkv_call(step, x, modulation, w, gain):
    tokens, width = x.shape
    inner = w.shape[2]
    rows = 256
    return pl.pallas_call(
        qkv_kernel,
        grid=(tokens // rows,),
        in_specs=[
            smem(),
            pl.BlockSpec((rows, width), lambda i: (i, 0)),
            pl.BlockSpec((modulation.shape[0], 2 * width), lambda i: (0, 0)),
            pl.BlockSpec(w.shape, lambda i: (0, 0, 0)),
            pl.BlockSpec(gain.shape, lambda i: (0, 0)),
        ],
        out_specs=pl.BlockSpec((rows, 3 * inner), lambda i: (i, 0)),
        out_shape=jax.ShapeDtypeStruct((tokens, 3 * inner), BF16),
        compiler_params=params(40),
        name="qkv",
    )(step, x, modulation, w, gain)


def attention_kernel(few, head, in_ref, out_ref):
    rows = in_ref.shape[0]
    inner = out_ref.shape[1]
    row_pos = lax.broadcasted_iota(jnp.int32, (rows, rows), 0) % few
    col_pos = lax.broadcasted_iota(jnp.int32, (rows, rows), 1) % few
    same = row_pos == col_pos
    for h in range(inner // head):
        lo = h * head
        q = in_ref[:, lo : lo + head]
        k = in_ref[:, inner + lo : inner + lo + head]
        v = in_ref[:, 2 * inner + lo : 2 * inner + lo + head]
        raised = jnp.where(same, jnp.exp(dot_t(q, k) * head ** (-0.5)), 0.0)
        probs = (raised / jnp.sum(raised, -1, keepdims=True)).astype(BF16)
        out_ref[:, lo : lo + head] = dot(probs, v).astype(BF16)


def attention_call(stacked, few, head):
    rows, wide = stacked.shape
    return pl.pallas_call(
        functools.partial(attention_kernel, few, head),
        out_shape=jax.ShapeDtypeStruct((rows, wide // 3), BF16),
        compiler_params=params(40),
        name="attention",
    )(stacked)


def spread(values, per):
    experts = values.shape[1]
    shape = (experts, experts * per)
    expand = (
        lax.broadcasted_iota(jnp.int32, shape, 1) // per
        == lax.broadcasted_iota(jnp.int32, shape, 0)
    ).astype(F32)
    return jnp.dot(values, expand, precision=lax.Precision.HIGHEST, preferred_element_type=F32)


def slot_row(picks_f32, counts_f32, first, per):
    wide = spread(picks_f32, per)
    slot = lax.broadcasted_iota(jnp.int32, wide.shape, 0)
    wanted = first + lax.broadcasted_iota(jnp.int32, wide.shape, 1) % per
    mine = slot == wanted
    if counts_f32 is not None:
        limit = spread(counts_f32, per)
        wide = jnp.where(slot.astype(F32) < limit, wide, -1.0)
    return jnp.sum(jnp.where(mine, wide, 0.0), axis=0, keepdims=True).astype(jnp.int32)


def mix_kernel(
    per, rank_ref, step_ref, att_ref, w_ref, x_ref, gate_ref, shift_ref, scale_ref,
    router_ref, picks_ref, disp_ref, gates_ref, share_ref, hidden_ref, normed_ref,
):
    step = step_ref[0]
    rank = rank_ref[0]
    tile = pl.program_id(0)
    rows = x_ref.shape[0]
    gate = gate_ref[pl.ds(step, 1), :]
    shift = shift_ref[pl.ds(step, 1), :]
    scale = scale_ref[pl.ds(step, 1), :]
    parts = att_ref.shape[0]
    inner = att_ref.shape[2]
    mixed = dot(att_ref[0], w_ref[:inner])
    for part in range(1, parts):
        mixed += dot(att_ref[part], w_ref[part * inner : (part + 1) * inner])
    hidden = x_ref[...].astype(F32) + gate * mixed
    hidden_ref[...] = hidden
    normed = (layer_norm(hidden) * (1.0 + scale) + shift).astype(BF16)
    normed_ref[pl.ds(pl.multiple_of(tile * rows, rows), rows), :] = normed
    gates_ref[...] = jax.nn.sigmoid(dot_t(normed, router_ref[...]))
    share = share_ref.shape[0]
    each = rows // share

    @pl.when(tile == rank // each)
    def _():
        start = pl.multiple_of((rank % each) * share, share)
        share_ref[...] = hidden_ref[pl.ds(start, share), :]

    @pl.when(tile == pl.num_programs(0) - 1)
    def _():
        row = slot_row(picks_ref[...].astype(F32), None, rank * per, per)
        tokens = normed_ref.shape[0]
        shape = (tokens, row.shape[1])
        onehot = (lax.broadcasted_iota(jnp.int32, shape, 0) == row).astype(F32).astype(BF16)
        disp_ref[...] = dot_l(onehot, normed_ref[...]).astype(BF16)


def mix_call(rank, step, att, w, x, modulation, router_t, picks_t, per, share):
    tokens, width = x.shape
    parts, _, inner = att.shape
    experts = router_t.shape[0]
    steps = modulation.shape[0]
    rows = 256
    return pl.pallas_call(
        functools.partial(mix_kernel, per),
        grid=(tokens // rows,),
        in_specs=[
            smem(),
            smem(),
            pl.BlockSpec((parts, rows, inner), lambda i: (0, i, 0)),
            pl.BlockSpec(w.shape, lambda i: (0, 0)),
            pl.BlockSpec((rows, width), lambda i: (i, 0)),
            pl.BlockSpec((steps, width), lambda i: (0, 2)),
            pl.BlockSpec((steps, width), lambda i: (0, 3)),
            pl.BlockSpec((steps, width), lambda i: (0, 4)),
            pl.BlockSpec(router_t.shape, lambda i: (0, 0)),
            pl.BlockSpec(picks_t.shape, lambda i: (0, 0)),
        ],
        out_specs=[
            pl.BlockSpec((experts * per, width), lambda i: (0, 0)),
            pl.BlockSpec((rows, experts), lambda i: (i, 0)),
            pl.BlockSpec((share, width), lambda i: (0, 0)),
        ],
        out_shape=[
            jax.ShapeDtypeStruct((experts * per, width), BF16),
            jax.ShapeDtypeStruct((tokens, experts), F32),
            jax.ShapeDtypeStruct((share, width), F32),
        ],
        scratch_shapes=[pltpu.VMEM((rows, width), F32), pltpu.VMEM((tokens, width), BF16)],
        compiler_params=params(44),
        name="mix",
    )(rank, step, att, w, x, modulation, modulation, modulation, router_t, picks_t)


def up_kernel(tok_ref, w_ref, out_ref):
    out_ref[...] = jax.nn.gelu(dot(tok_ref[...], w_ref[0])).astype(BF16)


def up_call(tokens, w):
    rows, width = tokens.shape
    parts, _, units = w.shape
    return pl.pallas_call(
        up_kernel,
        grid=(parts,),
        in_specs=[
            pl.BlockSpec((rows, width), lambda i: (0, 0)),
            pl.BlockSpec((1, width, units), lambda i: (i, 0, 0)),
        ],
        out_specs=pl.BlockSpec((rows, units), lambda i: (0, i)),
        out_shape=jax.ShapeDtypeStruct((rows, parts * units), BF16),
        compiler_params=params(40),
        name="up",
    )(tokens, w)


def down_kernel(rank_ref, hid_ref, *refs):
    out_ref = refs[-1]
    blocks = refs[:-1]
    units = blocks[0].shape[0]
    total = None
    for turn, block in enumerate(blocks):
        at = lax.rem(rank_ref[0] + turn, len(blocks))
        some = hid_ref[:, pl.ds(pl.multiple_of(at * units, units), units)]
        term = dot(some, block[...])
        total = term if total is None else total + term
    out_ref[...] = total.astype(BF16)


def down_call(rank, hidden, blocks):
    rows, units = hidden.shape
    few, half = blocks[0].shape
    cols = 512
    return pl.pallas_call(
        down_kernel,
        grid=(half // cols,),
        in_specs=[smem(), pl.BlockSpec((rows, units), lambda i: (0, 0))]
        + [pl.BlockSpec((few, cols), lambda i: (0, i))] * len(blocks),
        out_specs=pl.BlockSpec((rows, cols), lambda i: (0, i)),
        out_shape=jax.ShapeDtypeStruct((rows, half), BF16),
        compiler_params=params(40),
        name="down",
    )(rank, hidden, *blocks)


def combine_kernel(per, rank_ref, gates_ref, picks_ref, counts_ref, own_ref, other_ref, out_ref):
    rank = rank_ref[0]
    tokens = gates_ref.shape[0]
    experts = gates_ref.shape[1]
    picks = picks_ref[...].astype(F32)
    counts = counts_ref[...].astype(F32)
    shape = (experts, experts * per)
    expand = (
        lax.broadcasted_iota(jnp.int32, shape, 1) // per
        == lax.broadcasted_iota(jnp.int32, shape, 0)
    ).astype(F32).astype(BF16)
    wide = dot(gates_ref[...].astype(BF16), expand)
    token = lax.broadcasted_iota(jnp.int32, (tokens, experts * per), 0)
    partner = rank + 1 - 2 * lax.rem(rank, 2)
    weights = []
    for who in (rank, partner):
        row = slot_row(picks, counts, who * per, per)
        weights.append(jnp.where(token == row, wide, 0.0).astype(BF16))
    out_ref[...] = (dot(weights[0], own_ref[...]) + dot(weights[1], other_ref[...])).astype(BF16)


def combine_call(rank, gates, picks_t, counts_t, own, other, per):
    half = own.shape[1]
    vmem = pl.BlockSpec(memory_space=pltpu.VMEM)
    return pl.pallas_call(
        functools.partial(combine_kernel, per),
        in_specs=[smem()] + [vmem] * 5,
        out_specs=vmem,
        out_shape=jax.ShapeDtypeStruct((gates.shape[0], half), BF16),
        compiler_params=params(40),
        name="combine",
    )(rank, gates, picks_t, counts_t, own, other)


def final_kernel(step_ref, share_ref, gate_ref, parts_ref, out_ref):
    gate = gate_ref[pl.ds(step_ref[0], 1), :]
    half = parts_ref.shape[2]
    for b in range(2):
        cols = slice(b * half, (b + 1) * half)
        mixture = parts_ref[b].astype(F32) + parts_ref[b + 2].astype(F32)
        out_ref[:, cols] = (share_ref[:, cols] + gate[:, cols] * mixture).astype(BF16)


def final_call(step, share, modulation, parts):
    rows, width = share.shape
    return pl.pallas_call(
        final_kernel,
        grid=(1,),
        in_specs=[
            smem(),
            pl.BlockSpec((rows, width), lambda i: (0, 0)),
            pl.BlockSpec((modulation.shape[0], width), lambda i: (0, 5)),
            pl.BlockSpec(parts.shape, lambda i: (0, 0, 0)),
        ],
        out_specs=pl.BlockSpec((rows, width), lambda i: (0, 0)),
        out_shape=jax.ShapeDtypeStruct((rows, width), BF16),
        compiler_params=params(40),
        name="final",
    )(step, share, modulation, parts)


def on_device(
    frames_in,
    step_index,
    modulation,
    qkv_weight,
    qk_gain,
    out_weight,
    router_weight,
    expert_up,
    expert_down,
    picks,
    counts,
):
    _, position_count, model_width = frames_in.shape
    ffn = lax.axis_size("ffn")
    seq = lax.axis_size("seq")
    rank = lax.axis_index("ffn").astype(jnp.int32)
    rank_arr = rank.reshape(1)
    head_size = qk_gain.shape[1]
    share_len = position_count // ffn
    slot_count = picks.shape[2]
    per = slot_count // ffn
    half = model_width // 2
    x = frames_in[0]
    picks_t = jnp.transpose(picks, (1, 2, 0))[0]
    counts_t = jnp.transpose(counts, (1, 0))

    def over_seq(values):
        return lax.all_to_all(values, "seq", split_axis=0, concat_axis=0, tiled=True)

    def over_ffn(values):
        return lax.all_to_all(values, "ffn", split_axis=0, concat_axis=0, tiled=True)

    out_full = lax.all_gather(out_weight, "ffn", axis=0, tiled=True)
    up_full = lax.all_gather(expert_up, "ffn", axis=0, tiled=True)
    down = expert_down[0]
    side = lax.rem(rank, 2)
    same_half = lax.dynamic_slice_in_dim(down, side * half, half, 1)
    other_half = lax.dynamic_slice_in_dim(down, (1 - side) * half, half, 1)

    def from_turn(values, turn):
        return lax.ppermute(values, "ffn", [((i + turn) % ffn, i) for i in range(ffn)])

    blocks = [
        same_half,
        from_turn(other_half, 1),
        from_turn(same_half, 2),
        from_turn(other_half, 3),
    ]

    stacked = qkv_call(step_index, x, modulation, jnp.transpose(qkv_weight, (1, 0, 2)), qk_gain)
    stacked = over_seq(stacked)
    attended = attention_call(stacked, position_count // seq, head_size)
    attended = over_seq(attended)
    every = over_ffn(jnp.broadcast_to(attended[None], (ffn,) + attended.shape))
    outgoing, gates, share = mix_call(
        rank_arr, step_index, every, out_full, x, modulation,
        jnp.transpose(router_weight, (1, 0)), picks_t, per, share_len,
    )
    expert_tokens = over_seq(outgoing)
    hidden = up_call(expert_tokens, up_full)
    hidden_other = lax.ppermute(hidden, "ffn", [(i, i ^ 1) for i in range(ffn)])
    own = over_seq(down_call(rank_arr, hidden, blocks))
    other = over_seq(down_call(rank_arr, hidden_other, blocks))
    mixture = combine_call(rank_arr, gates, picks_t, counts_t, own, other, per)
    parts = over_ffn(mixture).reshape(ffn, share_len, half)
    return final_call(step_index, share, modulation, parts)[None]


def solution(mesh):
    in_specs = (
        P("seq", None, None),
        P("seq"),
        P(),
        P(None, None, "ffn"),
        P(),
        P("ffn", None),
        P(),
        P("seq", None, "ffn"),
        P("seq", "ffn", None),
        P(None, "seq", None),
        P(None, "seq"),
    )
    out_specs = P("seq", "ffn", None)
    return jax.shard_map(
        on_device, mesh=mesh, in_specs=in_specs, out_specs=out_specs, check_vma=False
    )
```

time: 455 us -> 290 us (0.64)
  blocking collectives: 163 us -> 71.1 us
  waiting for transfers between devices: 172 us -> 133 us
  other arithmetic: 37 us -> 0 us
  Pallas kernels: 0 us -> 25.4 us
  matrix products: 21.9 us -> 0 us
  starting transfers between devices: 8.11 us -> 25.9 us
  local copies, waits for them, and re-layouts: 36.4 us -> 18.7 us
    all_to_all x3, blocking collectives: 163 us -> 71.1 us  [the longest x2 52.6 us: over_seq(): lax.all_to_all(values, 'seq', split_axis=0, concat_axis=0, tiled=True)]
    psum x1 -> x0, waiting for transfers between devices: 61 us -> none  [on_device(): lax.psum(partial_value.astype(jnp.bfloat16), 'ffn').astype(jnp.float32)]
    all_gather x0 -> x2, waiting for transfers between devices: none -> 57.9 us  [the longest x1 57.9 us: on_device(): up_full = lax.all_gather(expert_up, 'ffn', axis=0, tiled=True)]
    reduce_scatter x1 -> x0, waiting for transfers between devices: 28.4 us -> none  [on_device(): lax.psum_scatter(mixture.astype(jnp.bfloat16), 'ffn', scatter_dimension=1...]
    pallas_call x0 -> x8, Pallas kernels: none -> 25.4 us  [the longest x1 8.74 us: mix_call(): pl.pallas_call(functools.partial(mix_kernel, per), grid=(tokens // rows,)...]
    all_to_all x1 -> x4, waiting for transfers between devices: 83 us -> 59.6 us  [the longest x3 37.8 us: over_seq(): lax.all_to_all(values, 'seq', split_axis=0, concat_axis=0, tiled=True)]
    dot_general x6 -> x0, matrix products: 21.9 us -> none  [the longest x1 9.63 us: on_device(): jnp.einsum('esqh,ehd->esqd', expert_hidden, down_matrix, preferred_elemen...]
    gather x4 -> x0, local copies, waits for them, and re-layouts: 19.4 us -> none  [the longest x1 10.7 us: on_device(): outgoing = tokens[my_picks][:, None]]
  transfers between devices with their start and end apart: 3 -> 10, of which waited for: 3 -> 5; matrix products, arithmetic and copies ran while one was open for 3% -> 1% of each run, Pallas kernels for 0% -> 8%
where the time goes in v1:
time: 290 us; the launch traced here: 289 us
  waiting for transfers between devices  133 us (46%)
  blocking collectives  71.1 us (25%)
  starting transfers between devices  25.9 us (9%)
  Pallas kernels  25.4 us (9%)
  local copies, waits for them, and re-layouts  18.7 us (6%)
  between operations  14.3 us (5%)
    all_gather x1, waiting for transfers between devices, on_device(): up_full = lax.all_gather(expert_up, 'ffn', axis=0, tiled=True)  57.9 us
    all_to_all x2, blocking collectives, over_seq(): lax.all_to_all(values, 'seq', split_axis=0, concat_axis=0, tiled=True)  52.6 us
    all_to_all x3, waiting for transfers between devices, over_seq(): lax.all_to_all(values, 'seq', split_axis=0, concat_axis=0, tiled=True)  37.8 us
    all_to_all x1, waiting for transfers between devices, over_ffn(): lax.all_to_all(values, 'ffn', split_axis=0, concat_axis=0, tiled=True)  21.8 us
    all_to_all x3, starting transfers between devices, over_seq(): lax.all_to_all(values, 'seq', split_axis=0, concat_axis=0, tiled=True)  19.5 us
    all_to_all x1, blocking collectives, over_ffn(): lax.all_to_all(values, 'ffn', split_axis=0, concat_axis=0, tiled=True)  18.6 us
    ppermute x1, waiting for transfers between devices, on_device(): hidden_other = lax.ppermute(hidden, 'ffn', [(i, i ^ 1) for i in range(ffn)])  14.3 us
    pallas_call x1, Pallas kernels, mix_call(): pl.pallas_call(functools.partial(mix_kernel, per), grid=(tokens // rows,)...  8.74 us
  transfers between devices with their start and end apart: 10, of which 5 were waited for; matrix products, arithmetic and copies ran while one was open for 1% of the time, Pallas kernels for 8%

profile of v1, /device:TPU:8, one launch (start us, length us, event | category | flops | bytes accessed | tf_op | source)
XLA Modules:
  0.0 288.6 jit_solution(17591971237569275052)
XLA Ops:
  8.7 1.9 copy-done.3
  10.6 3.3 %qkv.1 = bf16[512,768]{1,0:T(8,128)(2,1)S(1)} custom-call(s32[1]{0:T(128)S(6)} %copy.12.step_ref, bf16[512,2048]{1,0:T(8,128)(2,1)S(1)} %bitcast.18, f32[16,12288]{1,0:T(8,128)S(1)} %copy-done, bf16[3,2048,256]{2,1,0:T(8,128)(2,1)S(1)} %bitcast.22, f32[2,128]{1,0:T(2,128)S(1)} %copy-done.11), custom_call_target="tpu_custom_call" | custom-call | tf_op jit(solution)/shard_map/qkv/pallas_call | solution.py:67
  13.9 33.8 %all_to_all.67 = bf16[64,8,768]{2,1,0:T(8,128)(2,1)S(1)} all-to-all(bf16[64,8,768]{2,1,0:T(8,128)(2,1)S(1)} %bitcast.21), channel_id=1, replica_groups=mesh['seq'=64,'ffn'=4] {'seq'}, dimensions={0} | all-to-all | bytes 1572864 | tf_op jit(solution)/shard_map/all_to_all | solution.py:345
  47.7 1.1 attention.1
  48.8 18.8 %all_to_all.68 = bf16[64,8,256]{2,1,0:T(8,128)(2,1)S(1)} all-to-all(bf16[64,8,256]{2,1,0:T(8,128)(2,1)S(1)} %bitcast.24), channel_id=1, replica_groups=mesh['seq'=64,'ffn'=4] {'seq'}, dimensions={0} | all-to-all | bytes 524288 | tf_op jit(solution)/shard_map/all_to_all | solution.py:345
  67.6 1.1 broadcast_in_dim.12
  68.6 4.3 %all-to-all-start.2 = ((bf16[4,512,256]{2,1,0:T(8,128)(2,1)}), bf16[4,512,256]{2,1,0:T(8,128)(2,1)}, u32[]{:S(2)}, u32[]{:S(2)}) async-start(bf16[4,512,256]{2,1,0:T(8,128)(2,1)} %broadcast_in_dim.12), calls=%async_computation.2 | async-start | bytes 2097152 | tf_op jit(solution)/shard_map/all_to_all | solution.py:348
  72.9 21.8 %all-to-all-done.2.att_ref = bf16[4,512,256]{2,1,0:T(8,128)(2,1)} async-done(((bf16[4,512,256]{2,1,0:T(8,128)(2,1)}), bf16[4,512,256]{2,1,0:T(8,128)(2,1)}, u32[]{:S(2)}, u32[]{:S(2)}) %all-to-all-start.2) | async-done | bytes 1048608 | tf_op jit(solution)/shard_map/all_to_all | solution.py:348
  94.7 8.7 %mix.1 = (bf16[256,2048]{1,0:T(8,128)(2,1)S(1)}, f32[512,64]{1,0:T(8,128)S(1)}, f32[128,2048]{1,0:T(8,128)S(1)}) custom-call(s32[1]{0:T(128)} %bitcast.rank_ref, s32[1]{0:T(128)S(6)} %copy.12.step_ref, bf16[4,512,256]{2,1,0:T(8,128)(2,1)} %all-to-all-done.2.att_ref, bf16[1024,2048]{1,0:T(8,128)(2,1)} %all-gather.3.cloned.1.call-done.w_ref, ...), custom_call_target="tpu_custom_call" | custom-call | tf_op jit(solution)/shard_map/mix/pallas_call | solution.py:175
  103.5 1.0 copy-done.4
  104.5 1.0 copy-done.6
  106.2 2.3 all_to_all.49
  108.5 6.2 %all-to-all-start.3 = ((bf16[64,4,2048]{2,1,0:T(4,128)(2,1)}), bf16[64,4,2048]{2,1,0:T(4,128)(2,1)}, u32[]{:S(2)}, u32[]{:S(2)}) async-start(bf16[64,4,2048]{2,1,0:T(4,128)(2,1)} %all_to_all.49), calls=%async_computation.3 | async-start | bytes 2097152 | tf_op jit(solution)/shard_map/all_to_all | solution.py:345
  114.6 2.7 dynamic-slice_bitcast_fusion
  117.4 1.4 collective-permute-start.1
  119.4 22.3 %all-to-all-done.3 = bf16[64,4,2048]{2,1,0:T(4,128)(2,1)} async-done(((bf16[64,4,2048]{2,1,0:T(4,128)(2,1)}), bf16[64,4,2048]{2,1,0:T(4,128)(2,1)}, u32[]{:S(2)}, u32[]{:S(2)}) %all-to-all-start.3) | async-done | bytes 1048608 | tf_op jit(solution)/shard_map/all_to_all | solution.py:345
  141.7 1.3 all_to_all.51.tok_ref
  143.0 57.9 %all-gather.5.cloned.1.call-done.w_ref = bf16[4,2048,512]{2,1,0:T(8,128)(2,1)} async-done(((bf16[1,2048,512]{2,1,0:T(8,128)(2,1)}), bf16[4,2048,512]{2,1,0:T(8,128)(2,1)}) %all-gather.5.cloned.1.call-update) | async-done | bytes 8388624 | tf_op jit(solution)/shard_map/all_gather | solution.py:351
  201.0 3.4 %copy-done.1 = bf16[4,2048,512]{2,1,0:T(8,128)(2,1)S(1)} copy-done((bf16[4,2048,512]{2,1,0:T(8,128)(2,1)S(1)}, bf16[4,2048,512]{2,1,0:T(8,128)(2,1)}, u32[]{:S(2)}) %copy-start.1) | copy-done | bytes 8388632
  204.3 4.0 %up.1.hid_ref = bf16[256,2048]{1,0:T(8,128)(2,1)} custom-call(bf16[256,2048]{1,0:T(8,128)(2,1)S(1)} %all_to_all.51.tok_ref, bf16[4,2048,512]{2,1,0:T(8,128)(2,1)S(1)} %copy-done.1), custom_call_target="tpu_custom_call" | custom-call | tf_op jit(solution)/shard_map/up/pallas_call | solution.py:213
  208.4 3.2 %down.2 = bf16[256,1024]{1,0:T(8,128)(2,1)S(1)} custom-call(s32[1]{0:T(128)} %bitcast.rank_ref, bf16[256,2048]{1,0:T(8,128)(2,1)} %up.1.hid_ref, bf16[512,1024]{1,0:T(8,128)(2,1)S(1)} %get-tuple-element.12.refs_0_, bf16[512,1024]{1,0:T(8,128)(2,1)} %collective-permute-done.refs_1_, bf16[512,1024]{1,0:T(8,128)(2,1)} %collective-permute-done.1.refs_2_, ...), custom_call_target="tpu_custom_call" | custom-call | tf_op jit(solution)/shard_map/down/pallas_call | solution.py:244
  211.6 1.0 all_to_all.52
  212.6 6.8 %all-to-all-start.4 = ((bf16[64,4,1024]{2,1,0:T(4,128)(2,1)}), bf16[64,4,1024]{2,1,0:T(4,128)(2,1)}, u32[]{:S(2)}, u32[]{:S(2)}) async-start(bf16[64,4,1024]{2,1,0:T(4,128)(2,1)} %all_to_all.52), calls=%async_computation.4 | async-start | bytes 1048576 | tf_op jit(solution)/shard_map/all_to_all | solution.py:345
  219.4 14.3 %collective-permute-done.3.hid_ref = bf16[256,2048]{1,0:T(8,128)(2,1)S(1)} collective-permute-done((bf16[256,2048]{1,0:T(8,128)(2,1)}, bf16[256,2048]{1,0:T(8,128)(2,1)S(1)}, u32[]{:S(2)}, u32[]{:S(2)}) %collective-permute-start.3) | collective-permute-done | bytes 1048608 | tf_op jit(solution)/shard_map/ppermute | solution.py:378
  233.7 2.9 down.3
  236.6 1.0 all_to_all.55
  237.6 6.6 %all-to-all-start.5 = ((bf16[64,4,1024]{2,1,0:T(4,128)(2,1)}), bf16[64,4,1024]{2,1,0:T(4,128)(2,1)S(1)}, u32[]{:S(2)}, u32[]{:S(2)}) async-start(bf16[64,4,1024]{2,1,0:T(4,128)(2,1)} %all_to_all.55), calls=%async_computation.5 | async-start | bytes 1048576 | tf_op jit(solution)/shard_map/all_to_all | solution.py:345
  244.2 1.2 all_to_all.54.own_ref
  245.3 15.5 %all-to-all-done.5 = bf16[64,4,1024]{2,1,0:T(4,128)(2,1)S(1)} async-done(((bf16[64,4,1024]{2,1,0:T(4,128)(2,1)}), bf16[64,4,1024]{2,1,0:T(4,128)(2,1)S(1)}, u32[]{:S(2)}, u32[]{:S(2)}) %all-to-all-start.5) | async-done | bytes 524320 | tf_op jit(solution)/shard_map/all_to_all | solution.py:345
  261.0 1.0 combine.1
  262.0 18.6 %all_to_all.69.parts_ref = bf16[4,128,1024]{2,1,0:T(8,128)(2,1)S(1)} all-to-all(bf16[4,128,1024]{2,1,0:T(8,128)(2,1)S(1)} %bitcast.20), channel_id=1, replica_groups=mesh['seq'=64,'ffn'=4] {'ffn'}, dimensions={0} | all-to-all | bytes 2097152 | tf_op jit(solution)/shard_map/all_to_all | solution.py:348
  280.6 1.2 final.1
  (35 shorter events, 3.0 us)
Async XLA Ops:
  6.5 2.1 copy-start.2
  6.5 2.1 copy-start
  6.5 2.1 copy-start.11
  6.5 88.2 %all-gather.3.cloned.1.call-start = ((), (), s32[]{:S(2)}) async-start(), calls=%async_computation.7 | async-start | bytes 5242880 | tf_op jit(solution)/shard_map/all_gather | solution.py:350
  7.3 193.7 %all-gather.5.cloned.1.call-start = ((), (), s32[]{:S(2)}) async-start(), calls=%async_computation.8 | async-start | bytes 10485760 | tf_op jit(solution)/shard_map/all_gather | solution.py:351
  8.7 1.9 copy-start.3
  48.8 45.9 %copy-start.7 = (bf16[2048,64]{0,1:T(8,128)(2,1)S(1)}, bf16[2048,64]{0,1:T(8,128)(2,1)}, u32[]{:S(2)}) copy-start(bf16[2048,64]{0,1:T(8,128)(2,1)} %param.17) | copy-start | bytes 786436
  48.8 45.9 %copy-start.10 = (s32[64,1,16]{0,2,1:T(8,128)S(1)}, s32[64,1,16]{0,2,1:T(8,128)}, u32[]{:S(2)}) copy-start(s32[64,1,16]{0,2,1:T(8,128)} %param.20) | copy-start | bytes 12292
  68.6 26.1 %all-to-all-start.2 = ((bf16[4,512,256]{2,1,0:T(8,128)(2,1)}), bf16[4,512,256]{2,1,0:T(8,128)(2,1)}, u32[]{:S(2)}, u32[]{:S(2)}) async-start(bf16[4,512,256]{2,1,0:T(8,128)(2,1)} %broadcast_in_dim.12), calls=%async_computation.2 | async-start | bytes 2097152 | tf_op jit(solution)/shard_map/all_to_all | solution.py:348
  103.5 1.0 copy-start.4
  104.5 1.0 copy-start.6
  105.5 0.7 copy-start.8
  108.5 33.2 %all-to-all-start.3 = ((bf16[64,4,2048]{2,1,0:T(4,128)(2,1)}), bf16[64,4,2048]{2,1,0:T(4,128)(2,1)}, u32[]{:S(2)}, u32[]{:S(2)}) async-start(bf16[64,4,2048]{2,1,0:T(4,128)(2,1)} %all_to_all.49), calls=%async_computation.3 | async-start | bytes 2097152 | tf_op jit(solution)/shard_map/all_to_all | solution.py:345
  117.4 91.0 %collective-permute-start = (bf16[512,1024]{1,0:T(8,128)(2,1)}, bf16[512,1024]{1,0:T(8,128)(2,1)}, u32[]{:S(2)}, u32[]{:S(2)}) collective-permute-start(bf16[512,1024]{1,0:T(8,128)(2,1)} %get-tuple-element.11), channel_id=1, source_target_pairs={{1,0},{2,1},{3,2},{0,3},{5,4},{6,5},{7,6},{4,7},{9,8},{10,9},{11,1... | collective-permute-start | bytes 3145736 | tf_op jit(solution)/shard_map/ppermute | solution.py:358
  117.4 91.0 %collective-permute-start.1 = (bf16[512,1024]{1,0:T(8,128)(2,1)S(1)}, bf16[512,1024]{1,0:T(8,128)(2,1)}, u32[]{:S(2)}, u32[]{:S(2)}) collective-permute-start(bf16[512,1024]{1,0:T(8,128)(2,1)S(1)} %get-tuple-element.12.refs_0_), channel_id=1, source_target_pairs={{2,0},{3,1},{0,2},{1,3},{6,4},{7,5},{4,6},{5,7},{10,8},{11,9},{8,1... | collective-permute-start | bytes 3145736 | tf_op jit(solution)/shard_map/ppermute | solution.py:358
  118.7 89.6 %collective-permute-start.2 = (bf16[512,1024]{1,0:T(8,128)(2,1)}, bf16[512,1024]{1,0:T(8,128)(2,1)}, u32[]{:S(2)}, u32[]{:S(2)}) collective-permute-start(bf16[512,1024]{1,0:T(8,128)(2,1)} %get-tuple-element.11), channel_id=1, source_target_pairs={{3,0},{0,1},{1,2},{2,3},{7,4},{4,5},{5,6},{6,7},{11,8},{8,9},{9,10... | collective-permute-start | bytes 3145736 | tf_op jit(solution)/shard_map/ppermute | solution.py:358
  201.0 3.4 %copy-start.1 = (bf16[4,2048,512]{2,1,0:T(8,128)(2,1)S(1)}, bf16[4,2048,512]{2,1,0:T(8,128)(2,1)}, u32[]{:S(2)}) copy-start(bf16[4,2048,512]{2,1,0:T(8,128)(2,1)} %all-gather.5.cloned.1.call-done.w_ref) | copy-start | bytes 25165828
  208.3 25.3 %collective-permute-start.3 = (bf16[256,2048]{1,0:T(8,128)(2,1)}, bf16[256,2048]{1,0:T(8,128)(2,1)S(1)}, u32[]{:S(2)}, u32[]{:S(2)}) collective-permute-start(bf16[256,2048]{1,0:T(8,128)(2,1)} %up.1.hid_ref), channel_id=1, source_target_pairs={{0,1},{1,0},{2,3},{3,2},{4,5},{5,4},{6,7},{7,6},{8,9},{9,8},{10,11... | collective-permute-start | bytes 3145736 | tf_op jit(solution)/shard_map/ppermute | solution.py:378
  212.6 25.0 %all-to-all-start.4 = ((bf16[64,4,1024]{2,1,0:T(4,128)(2,1)}), bf16[64,4,1024]{2,1,0:T(4,128)(2,1)}, u32[]{:S(2)}, u32[]{:S(2)}) async-start(bf16[64,4,1024]{2,1,0:T(4,128)(2,1)} %all_to_all.52), calls=%async_computation.4 | async-start | bytes 1048576 | tf_op jit(solution)/shard_map/all_to_all | solution.py:345
  236.5 24.5 %copy-start.9 = (f32[512,64]{1,0:T(8,128)S(1)}, f32[512,64]{1,0:T(8,128)}, u32[]{:S(2)}) copy-start(f32[512,64]{1,0:T(8,128)} %copy-done.8) | copy-start | bytes 393220
  236.5 24.5 %copy-start.12 = (s32[64,1]{0,1:T(1,128)S(1)}, s32[64,1]{0,1:T(1,128)}, u32[]{:S(2)}) copy-start(s32[64,1]{0,1:T(1,128)} %param.21) | copy-start | bytes 772
  237.6 23.3 %all-to-all-start.5 = ((bf16[64,4,1024]{2,1,0:T(4,128)(2,1)}), bf16[64,4,1024]{2,1,0:T(4,128)(2,1)S(1)}, u32[]{:S(2)}, u32[]{:S(2)}) async-start(bf16[64,4,1024]{2,1,0:T(4,128)(2,1)} %all_to_all.55), calls=%async_computation.5 | async-start | bytes 1048576 | tf_op jit(solution)/shard_map/all_to_all | solution.py:345
  261.0 19.6 %copy-start.5 = (f32[128,2048]{1,0:T(8,128)S(1)}, f32[128,2048]{1,0:T(8,128)}, u32[]{:S(2)}) copy-start(f32[128,2048]{1,0:T(8,128)} %copy-done.4) | copy-start | bytes 3145732
Sparse Core Ops, SparseCore 0:
  9.2 53.6 all-gather.2
  64.7 136.2 all-gather.4

commit v2 on v1

--- a/solution.py
+++ b/solution.py
@@ -76,7 +76,7 @@
         ],
         out_specs=pl.BlockSpec((rows, 3 * inner), lambda i: (i, 0)),
         out_shape=jax.ShapeDtypeStruct((tokens, 3 * inner), BF16),
-        compiler_params=params(40),
+        compiler_params=params(56),
         name="qkv",
     )(step, x, modulation, w, gain)
 
@@ -102,7 +102,7 @@
     return pl.pallas_call(
         functools.partial(attention_kernel, few, head),
         out_shape=jax.ShapeDtypeStruct((rows, wide // 3), BF16),
-        compiler_params=params(40),
+        compiler_params=params(16),
         name="attention",
     )(stacked)
 
@@ -118,20 +118,37 @@
 
 
 def slot_row(picks_f32, counts_f32, first, per):
-    wide = spread(picks_f32, per)
+    wide = spread(picks_f32, 2 * per)
     slot = lax.broadcasted_iota(jnp.int32, wide.shape, 0)
     wanted = first + lax.broadcasted_iota(jnp.int32, wide.shape, 1) % per
     mine = slot == wanted
     if counts_f32 is not None:
-        limit = spread(counts_f32, per)
+        limit = spread(counts_f32, 2 * per)
         wide = jnp.where(slot.astype(F32) < limit, wide, -1.0)
     return jnp.sum(jnp.where(mine, wide, 0.0), axis=0, keepdims=True).astype(jnp.int32)
 
 
+def row_half(shape, per, dim):
+    return (lax.broadcasted_iota(jnp.int32, shape, dim) // per) % 2
+
+
+def ones_where(mask):
+    return mask.astype(F32).astype(BF16)
+
+
+def halves_to_rows(count, per, half):
+    shape = (2 * count, count)
+    row = lax.broadcasted_iota(jnp.int32, shape, 0)
+    col = lax.broadcasted_iota(jnp.int32, shape, 1)
+    return ones_where(row == (col // per * 2 + half) * per + col % per)
+
+
 def mix_kernel(
-    per, rank_ref, step_ref, att_ref, w_ref, x_ref, gate_ref, shift_ref, scale_ref,
-    router_ref, picks_ref, disp_ref, gates_ref, share_ref, hidden_ref, normed_ref,
+    per, rank_ref, core_ref, step_ref, att_ref, *refs
 ):
+    weights = refs[:8]
+    (x_ref, gate_ref, shift_ref, scale_ref, router_ref, picks_ref,
+     disp_ref, gates_ref, share_ref, hidden_ref, normed_ref) = refs[8:]
     step = step_ref[0]
     rank = rank_ref[0]
     tile = pl.program_id(0)
@@ -140,10 +157,16 @@
     shift = shift_ref[pl.ds(step, 1), :]
     scale = scale_ref[pl.ds(step, 1), :]
     parts = att_ref.shape[0]
-    inner = att_ref.shape[2]
-    mixed = dot(att_ref[0], w_ref[:inner])
-    for part in range(1, parts):
-        mixed += dot(att_ref[part], w_ref[part * inner : (part + 1) * inner])
+    some = att_ref.shape[2] // 2
+    core = core_ref[0]
+    mixed = None
+    for turn in range(parts):
+        part = lax.rem(rank + turn, parts)
+        for which in range(2):
+            at = lax.rem(core + which, 2) * some
+            rows_of = att_ref[part, :, pl.ds(pl.multiple_of(at, some), some)]
+            term = dot(rows_of, weights[which * parts + turn][...])
+            mixed = term if mixed is None else mixed + term
     hidden = x_ref[...].astype(F32) + gate * mixed
     hidden_ref[...] = hidden
     normed = (layer_norm(hidden) * (1.0 + scale) + shift).astype(BF16)
@@ -162,11 +185,16 @@
         row = slot_row(picks_ref[...].astype(F32), None, rank * per, per)
         tokens = normed_ref.shape[0]
         shape = (tokens, row.shape[1])
-        onehot = (lax.broadcasted_iota(jnp.int32, shape, 0) == row).astype(F32).astype(BF16)
-        disp_ref[...] = dot_l(onehot, normed_ref[...]).astype(BF16)
-
-
-def mix_call(rank, step, att, w, x, modulation, router_t, picks_t, per, share):
+        picked = lax.broadcasted_iota(jnp.int32, shape, 0) == row
+        half = row_half(shape, per, 1)
+        cols = disp_ref.shape[1]
+        disp_ref[...] = (
+            dot_l(ones_where(picked & (half == 0)), normed_ref[:, :cols])
+            + dot_l(ones_where(picked & (half == 1)), normed_ref[:, cols:])
+        ).astype(BF16)
+
+
+def mix_call(rank, core, step, att, weights, x, modulation, router_t, picks_t, per, share):
     tokens, width = x.shape
     parts, _, inner = att.shape
     experts = router_t.shape[0]
@@ -178,8 +206,11 @@
         in_specs=[
             smem(),
             smem(),
+            smem(),
             pl.BlockSpec((parts, rows, inner), lambda i: (0, i, 0)),
-            pl.BlockSpec(w.shape, lambda i: (0, 0)),
+        ]
+        + [pl.BlockSpec(w.shape, lambda i: (0, 0)) for w in weights]
+        + [
             pl.BlockSpec((rows, width), lambda i: (i, 0)),
             pl.BlockSpec((steps, width), lambda i: (0, 2)),
             pl.BlockSpec((steps, width), lambda i: (0, 3)),
@@ -188,43 +219,52 @@
             pl.BlockSpec(picks_t.shape, lambda i: (0, 0)),
         ],
         out_specs=[
-            pl.BlockSpec((experts * per, width), lambda i: (0, 0)),
+            pl.BlockSpec((2 * experts * per, width // 2), lambda i: (0, 0)),
             pl.BlockSpec((rows, experts), lambda i: (i, 0)),
             pl.BlockSpec((share, width), lambda i: (0, 0)),
         ],
         out_shape=[
-            jax.ShapeDtypeStruct((experts * per, width), BF16),
+            jax.ShapeDtypeStruct((2 * experts * per, width // 2), BF16),
             jax.ShapeDtypeStruct((tokens, experts), F32),
             jax.ShapeDtypeStruct((share, width), F32),
         ],
         scratch_shapes=[pltpu.VMEM((rows, width), F32), pltpu.VMEM((tokens, width), BF16)],
-        compiler_params=params(44),
+        compiler_params=params(56),
         name="mix",
-    )(rank, step, att, w, x, modulation, modulation, modulation, router_t, picks_t)
-
-
-def up_kernel(tok_ref, w_ref, out_ref):
+    )(rank, core, step, att, *weights, x, modulation, modulation, modulation, router_t, picks_t)
+
+
+def up_kernel(per, rows_ref, w_ref, out_ref, tok_ref):
+    @pl.when(pl.program_id(0) == 0)
+    def _():
+        count = tok_ref.shape[0]
+        cols = rows_ref.shape[1]
+        for half in range(2):
+            pick = halves_to_rows(count, per, half)
+            tok_ref[:, half * cols : (half + 1) * cols] = dot_l(pick, rows_ref[...]).astype(BF16)
+
     out_ref[...] = jax.nn.gelu(dot(tok_ref[...], w_ref[0])).astype(BF16)
 
 
-def up_call(tokens, w):
-    rows, width = tokens.shape
-    parts, _, units = w.shape
-    return pl.pallas_call(
-        up_kernel,
+def up_call(rows, w, per):
+    parts, width, units = w.shape
+    count = rows.shape[0] // 2
+    return pl.pallas_call(
+        functools.partial(up_kernel, per),
         grid=(parts,),
         in_specs=[
-            pl.BlockSpec((rows, width), lambda i: (0, 0)),
+            pl.BlockSpec(rows.shape, lambda i: (0, 0)),
             pl.BlockSpec((1, width, units), lambda i: (i, 0, 0)),
         ],
-        out_specs=pl.BlockSpec((rows, units), lambda i: (0, i)),
-        out_shape=jax.ShapeDtypeStruct((rows, parts * units), BF16),
-        compiler_params=params(40),
+        out_specs=pl.BlockSpec((count, units), lambda i: (0, i)),
+        out_shape=jax.ShapeDtypeStruct((count, parts * units), BF16),
+        scratch_shapes=[pltpu.VMEM((count, width), BF16)],
+        compiler_params=params(56),
         name="up",
-    )(tokens, w)
-
-
-def down_kernel(rank_ref, hid_ref, *refs):
+    )(rows, w)
+
+
+def down_kernel(per, rank_ref, hid_ref, *refs):
     out_ref = refs[-1]
     blocks = refs[:-1]
     units = blocks[0].shape[0]
@@ -234,21 +274,30 @@
         some = hid_ref[:, pl.ds(pl.multiple_of(at * units, units), units)]
         term = dot(some, block[...])
         total = term if total is None else total + term
-    out_ref[...] = total.astype(BF16)
-
-
-def down_call(rank, hidden, blocks):
+    total = total.astype(BF16)
+    count = total.shape[0]
+
+    @pl.when(pl.program_id(0) == 0)
+    def _():
+        out_ref[...] = dot(halves_to_rows(count, per, 0), total).astype(BF16)
+
+    @pl.when(pl.program_id(0) == 1)
+    def _():
+        out_ref[...] += dot(halves_to_rows(count, per, 1), total).astype(BF16)
+
+
+def down_call(rank, hidden, blocks, per):
     rows, units = hidden.shape
     few, half = blocks[0].shape
-    cols = 512
-    return pl.pallas_call(
-        down_kernel,
-        grid=(half // cols,),
+    cols = half // 2
+    return pl.pallas_call(
+        functools.partial(down_kernel, per),
+        grid=(2,),
         in_specs=[smem(), pl.BlockSpec((rows, units), lambda i: (0, 0))]
         + [pl.BlockSpec((few, cols), lambda i: (0, i))] * len(blocks),
-        out_specs=pl.BlockSpec((rows, cols), lambda i: (0, i)),
-        out_shape=jax.ShapeDtypeStruct((rows, half), BF16),
-        compiler_params=params(40),
+        out_specs=pl.BlockSpec((2 * rows, cols), lambda i: (0, 0)),
+        out_shape=jax.ShapeDtypeStruct((2 * rows, cols), BF16),
+        compiler_params=params(56),
         name="down",
     )(rank, hidden, *blocks)
 
@@ -259,30 +308,36 @@
     experts = gates_ref.shape[1]
     picks = picks_ref[...].astype(F32)
     counts = counts_ref[...].astype(F32)
-    shape = (experts, experts * per)
-    expand = (
-        lax.broadcasted_iota(jnp.int32, shape, 1) // per
+    shape = (experts, 2 * experts * per)
+    expand = ones_where(
+        lax.broadcasted_iota(jnp.int32, shape, 1) // (2 * per)
         == lax.broadcasted_iota(jnp.int32, shape, 0)
-    ).astype(F32).astype(BF16)
+    )
     wide = dot(gates_ref[...].astype(BF16), expand)
-    token = lax.broadcasted_iota(jnp.int32, (tokens, experts * per), 0)
+    token = lax.broadcasted_iota(jnp.int32, wide.shape, 0)
+    which = row_half(wide.shape, per, 1)
     partner = rank + 1 - 2 * lax.rem(rank, 2)
-    weights = []
-    for who in (rank, partner):
+    cols = own_ref.shape[1]
+    sums = [None, None]
+    for who, rows_ref in ((rank, own_ref), (partner, other_ref)):
         row = slot_row(picks, counts, who * per, per)
-        weights.append(jnp.where(token == row, wide, 0.0).astype(BF16))
-    out_ref[...] = (dot(weights[0], own_ref[...]) + dot(weights[1], other_ref[...])).astype(BF16)
+        weight = jnp.where(token == row, wide, 0.0)
+        for half in range(2):
+            term = dot(jnp.where(which == half, weight, 0.0).astype(BF16), rows_ref[...])
+            sums[half] = term if sums[half] is None else sums[half] + term
+    for half in range(2):
+        out_ref[:, half * cols : (half + 1) * cols] = sums[half].astype(BF16)
 
 
 def combine_call(rank, gates, picks_t, counts_t, own, other, per):
-    half = own.shape[1]
+    half = 2 * own.shape[1]
     vmem = pl.BlockSpec(memory_space=pltpu.VMEM)
     return pl.pallas_call(
         functools.partial(combine_kernel, per),
         in_specs=[smem()] + [vmem] * 5,
         out_specs=vmem,
         out_shape=jax.ShapeDtypeStruct((gates.shape[0], half), BF16),
-        compiler_params=params(40),
+        compiler_params=params(16),
         name="combine",
     )(rank, gates, picks_t, counts_t, own, other)
 
@@ -309,7 +364,7 @@
         ],
         out_specs=pl.BlockSpec((rows, width), lambda i: (0, 0)),
         out_shape=jax.ShapeDtypeStruct((rows, width), BF16),
-        compiler_params=params(40),
+        compiler_params=params(16),
         name="final",
     )(step, share, modulation, parts)
 
@@ -347,7 +402,10 @@
     def over_ffn(values):
         return lax.all_to_all(values, "ffn", split_axis=0, concat_axis=0, tiled=True)
 
-    out_full = lax.all_gather(out_weight, "ffn", axis=0, tiled=True)
+    core = lax.rem(lax.axis_index("seq").astype(jnp.int32), 2)
+    core_arr = core.reshape(1)
+    out_rows = out_weight.shape[0] // 2
+    out_own = lax.dynamic_slice_in_dim(out_weight, core * out_rows, out_rows, 0)
     up_full = lax.all_gather(expert_up, "ffn", axis=0, tiled=True)
     down = expert_down[0]
     side = lax.rem(rank, 2)
@@ -357,6 +415,7 @@
     def from_turn(values, turn):
         return lax.ppermute(values, "ffn", [((i + turn) % ffn, i) for i in range(ffn)])
 
+    out_blocks = [out_own] + [from_turn(out_own, turn) for turn in range(1, ffn)]
     blocks = [
         same_half,
         from_turn(other_half, 1),
@@ -366,18 +425,21 @@
 
     stacked = qkv_call(step_index, x, modulation, jnp.transpose(qkv_weight, (1, 0, 2)), qk_gain)
     stacked = over_seq(stacked)
+    stacked, out_blocks = lax.optimization_barrier((stacked, out_blocks))
+    swap = [(i, i ^ 1) for i in range(seq)]
+    out_blocks = out_blocks + [lax.ppermute(b, "seq", swap) for b in out_blocks]
     attended = attention_call(stacked, position_count // seq, head_size)
     attended = over_seq(attended)
     every = over_ffn(jnp.broadcast_to(attended[None], (ffn,) + attended.shape))
     outgoing, gates, share = mix_call(
-        rank_arr, step_index, every, out_full, x, modulation,
+        rank_arr, core_arr, step_index, every, out_blocks, x, modulation,
         jnp.transpose(router_weight, (1, 0)), picks_t, per, share_len,
     )
     expert_tokens = over_seq(outgoing)
-    hidden = up_call(expert_tokens, up_full)
+    hidden = up_call(expert_tokens, up_full, per)
     hidden_other = lax.ppermute(hidden, "ffn", [(i, i ^ 1) for i in range(ffn)])
-    own = over_seq(down_call(rank_arr, hidden, blocks))
-    other = over_seq(down_call(rank_arr, hidden_other, blocks))
+    own = over_seq(down_call(rank_arr, hidden, blocks, per))
+    other = over_seq(down_call(rank_arr, hidden_other, blocks, per))
     mixture = combine_call(rank_arr, gates, picks_t, counts_t, own, other, per)
     parts = over_ffn(mixture).reshape(ffn, share_len, half)
     return final_call(step_index, share, modulation, parts)[None]

time: 290 us -> 290 us (level)
  starting transfers between devices: 25.9 us -> 43.6 us
  Pallas kernels: 25.4 us -> 40.9 us
  local copies, waits for them, and re-layouts: 18.7 us -> 5.66 us
  waiting for transfers between devices: 133 us -> 121 us
  blocking collectives: 71.1 us -> 64.1 us
    ppermute x3 -> x6, waiting for transfers between devices: 0.01 us -> 61.5 us  [from_turn(): lax.ppermute(values, 'ffn', [((i + turn) % ffn, i) for i in range(ffn)])]
    all_gather x1, waiting for transfers between devices: 57.9 us -> 0.01 us  [on_device(): up_full = lax.all_gather(expert_up, 'ffn', axis=0, tiled=True)]
    all_to_all x3, starting transfers between devices: 19.5 us -> 29.7 us  [over_seq(): lax.all_to_all(values, 'seq', split_axis=0, concat_axis=0, tiled=True)]
    all_to_all x3, waiting for transfers between devices: 37.8 us -> 28.4 us  [over_seq(): lax.all_to_all(values, 'seq', split_axis=0, concat_axis=0, tiled=True)]
    ppermute x1, waiting for transfers between devices: 14.3 us -> 5.07 us  [on_device(): hidden_other = lax.ppermute(hidden, 'ffn', [(i, i ^ 1) for i in range(ffn)])]
    pallas_call x3, Pallas kernels: 10.1 us -> 17.4 us  [the longest x2 9.7 us: down_call(): pl.pallas_call(functools.partial(down_kernel, per), grid=(2,), in_specs=[...]
    all_to_all x2, blocking collectives: 52.6 us -> 45.5 us  [over_seq(): lax.all_to_all(values, 'seq', split_axis=0, concat_axis=0, tiled=True)]
    all_to_all x6 -> x0, local copies, waits for them, and re-layouts: 6.89 us -> none  [over_seq(): lax.all_to_all(values, 'seq', split_axis=0, concat_axis=0, tiled=True)]
  transfers between devices with their start and end apart: 10 -> 16, of which waited for: 5 -> 12; matrix products, arithmetic and copies ran while one was open for 1% -> 1% of each run, Pallas kernels for 8% -> 13%
where the time goes in v2:
time: 290 us
  waiting for transfers between devices  121 us (42%)
  blocking collectives  64.1 us (22%)
  starting transfers between devices  43.6 us (15%)
  Pallas kernels  40.9 us (14%)
  between operations  14.2 us (5%)
  local copies, waits for them, and re-layouts  5.66 us (2%)
    ppermute x6, waiting for transfers between devices, from_turn(): lax.ppermute(values, 'ffn', [((i + turn) % ffn, i) for i in range(ffn)])  61.5 us
    all_to_all x2, blocking collectives, over_seq(): lax.all_to_all(values, 'seq', split_axis=0, concat_axis=0, tiled=True)  45.5 us
    all_to_all x3, starting transfers between devices, over_seq(): lax.all_to_all(values, 'seq', split_axis=0, concat_axis=0, tiled=True)  29.7 us
    all_to_all x3, waiting for transfers between devices, over_seq(): lax.all_to_all(values, 'seq', split_axis=0, concat_axis=0, tiled=True)  28.4 us
    all_to_all x1, waiting for transfers between devices, over_ffn(): lax.all_to_all(values, 'ffn', split_axis=0, concat_axis=0, tiled=True)  22.1 us
    all_to_all x1, blocking collectives, over_ffn(): lax.all_to_all(values, 'ffn', split_axis=0, concat_axis=0, tiled=True)  18.7 us
    pallas_call x1, Pallas kernels, mix_call(): pl.pallas_call(functools.partial(mix_kernel, per), grid=(tokens // rows,)...  13.1 us
    pallas_call x2, Pallas kernels, down_call(): pl.pallas_call(functools.partial(down_kernel, per), grid=(2,), in_specs=[...  9.7 us
  transfers between devices with their start and end apart: 16, of which 12 were waited for; matrix products, arithmetic and copies ran while one was open for 1% of the time, Pallas kernels for 13%

profile of v2, /device:TPU:8, one launch (start us, length us, event | category | flops | bytes accessed | tf_op | source)
XLA Modules:
  0.0 289.7 jit_solution(8668665939539061739)
XLA Ops:
  7.9 6.3 %qkv.1 = bf16[512,768]{1,0:T(8,128)(2,1)} custom-call(s32[1]{0:T(128)S(6)} %copy.12.step_ref, bf16[512,2048]{1,0:T(8,128)(2,1)} %bitcast.33, f32[16,12288]{1,0:T(8,128)} %gate_ref.1, bf16[3,2048,256]{2,1,0:T(8,128)(2,1)} %bitcast.36, f32[2,128]{1,0:T(2,128)} %gain_ref.1), custom_call_target="tpu_custom_call" | custom-call | tf_op jit(solution)/shard_map/qkv/pallas_call | solution.py:67
  14.2 12.1 %all-to-all-start = ((bf16[64,8,768]{2,1,0:T(8,128)(2,1)}), bf16[64,8,768]{2,1,0:T(8,128)(2,1)S(1)}, u32[]{:S(2)}, u32[]{:S(2)}) async-start(bf16[64,8,768]{2,1,0:T(8,128)(2,1)} %bitcast.35), calls=%async_computation | async-start | bytes 1572864 | tf_op jit(solution)/shard_map/all_to_all | solution.py:400
  26.4 2.8 collective-permute-start
  30.1 0.9 collective-permute-start.2
  31.0 23.1 %collective-permute-done.refs_1_ = bf16[128,2048]{1,0:T(8,128)(2,1)S(1)} collective-permute-done((bf16[128,2048]{1,0:T(8,128)(2,1)S(1)}, bf16[128,2048]{1,0:T(8,128)(2,1)S(1)}, u32[]{:S(2)}, u32[]{:S(2)}) %collective-permute-start) | collective-permute-done | bytes 524320 | tf_op jit(solution)/shard_map/ppermute | solution.py:416
  54.0 2.7 collective-permute-done.1.refs_2_
  57.6 18.1 %collective-permute-done.2.refs_3_ = bf16[128,2048]{1,0:T(8,128)(2,1)} collective-permute-done((bf16[128,2048]{1,0:T(8,128)(2,1)S(1)}, bf16[128,2048]{1,0:T(8,128)(2,1)}, u32[]{:S(2)}, u32[]{:S(2)}) %collective-permute-start.2) | collective-permute-done | bytes 524320 | tf_op jit(solution)/shard_map/ppermute | solution.py:416
  75.7 1.1 attention.1
  76.8 21.7 %all_to_all.68 = bf16[64,8,256]{2,1,0:T(8,128)(2,1)S(1)} all-to-all(bf16[64,8,256]{2,1,0:T(8,128)(2,1)S(1)} %bitcast.29), channel_id=1, replica_groups=mesh['seq'=64,'ffn'=4] {'seq'}, dimensions={0} | all-to-all | bytes 524288 | tf_op jit(solution)/shard_map/all_to_all | solution.py:400
  98.5 1.1 broadcast_in_dim.12
  99.5 5.1 %all-to-all-start.2 = ((bf16[4,512,256]{2,1,0:T(8,128)(2,1)}), bf16[4,512,256]{2,1,0:T(8,128)(2,1)S(1)}, u32[]{:S(2)}, u32[]{:S(2)}) async-start(bf16[4,512,256]{2,1,0:T(8,128)(2,1)} %broadcast_in_dim.12), calls=%async_computation.2 | async-start | bytes 2097152 | tf_op jit(solution)/shard_map/all_to_all | solution.py:403
  105.7 1.0 collective-permute-done.3.refs_4_
  106.7 1.5 collective-permute-done.4.refs_5_
  109.2 22.1 %all-to-all-done.2.att_ref = bf16[4,512,256]{2,1,0:T(8,128)(2,1)S(1)} async-done(((bf16[4,512,256]{2,1,0:T(8,128)(2,1)}), bf16[4,512,256]{2,1,0:T(8,128)(2,1)S(1)}, u32[]{:S(2)}, u32[]{:S(2)}) %all-to-all-start.2) | async-done | bytes 1048608 | tf_op jit(solution)/shard_map/all_to_all | solution.py:403
  131.3 1.0 copy-done.7
  132.3 13.1 %mix.1 = (bf16[512,1024]{1,0:T(8,128)(2,1)}, f32[512,64]{1,0:T(8,128)}, f32[128,2048]{1,0:T(8,128)}) custom-call(s32[1]{0:T(128)} %bitcast.rank_ref, s32[1]{0:T(128)} %bitcast.1.core_ref, s32[1]{0:T(128)S(6)} %copy.12.step_ref, bf16[4,512,256]{2,1,0:T(8,128)(2,1)} %copy-done.7, bf16[128,2048]{1,0:T(8,128)(2,1)} %copy-done.9, bf16[128,2048]{1,0:T(8,128)(2,1)} %copy-done.10, ...), custom_call_target="tpu_custom_call" | custom-call | tf_op jit(solution)/shard_map/mix/pallas_call | solution.py:203
  145.5 7.2 %all-to-all-start.3 = ((bf16[64,8,1024]{2,1,0:T(8,128)(2,1)}), bf16[64,8,1024]{2,1,0:T(8,128)(2,1)}, u32[]{:S(2)}, u32[]{:S(2)}) async-start(bf16[64,8,1024]{2,1,0:T(8,128)(2,1)} %bitcast.40), calls=%async_computation.3 | async-start | bytes 2097152 | tf_op jit(solution)/shard_map/all_to_all | solution.py:400
  152.7 2.7 dynamic-slice_bitcast_fusion
  155.4 1.2 collective-permute-start.7
  156.6 1.5 collective-permute-start.8
  158.1 21.7 %all-to-all-done.3 = bf16[64,8,1024]{2,1,0:T(8,128)(2,1)} async-done(((bf16[64,8,1024]{2,1,0:T(8,128)(2,1)}), bf16[64,8,1024]{2,1,0:T(8,128)(2,1)}, u32[]{:S(2)}, u32[]{:S(2)}) %all-to-all-start.3) | async-done | bytes 1048608 | tf_op jit(solution)/shard_map/all_to_all | solution.py:400
  179.8 7.7 %up.1.hid_ref = bf16[256,2048]{1,0:T(8,128)(2,1)} custom-call(bf16[512,1024]{1,0:T(8,128)(2,1)} %bitcast.14.rows_ref, bf16[4,2048,512]{2,1,0:T(8,128)(2,1)} %all-gather.2.cloned.1.call-done.w_ref), custom_call_target="tpu_custom_call" | custom-call | tf_op jit(solution)/shard_map/up/pallas_call | solution.py:252
  188.0 17.6 %collective-permute-done.9.refs_3_ = bf16[512,1024]{1,0:T(8,128)(2,1)} collective-permute-done((bf16[512,1024]{1,0:T(8,128)(2,1)}, bf16[512,1024]{1,0:T(8,128)(2,1)}, u32[]{:S(2)}, u32[]{:S(2)}) %collective-permute-start.9) | collective-permute-done | bytes 1048608 | tf_op jit(solution)/shard_map/ppermute | solution.py:416
  205.6 4.9 %down.2 = bf16[512,512]{1,0:T(8,128)(2,1)} custom-call(s32[1]{0:T(128)} %bitcast.rank_ref, bf16[256,2048]{1,0:T(8,128)(2,1)} %up.1.hid_ref, bf16[512,1024]{1,0:T(8,128)(2,1)} %copy-done.6, bf16[512,1024]{1,0:T(8,128)(2,1)} %copy-done.8, bf16[512,1024]{1,0:T(8,128)(2,1)} %collective-permute-done.8.refs_2_, bf16[512,1024]{1,0:T(8,128)(2,1)} %collective-permute-done.9.refs_3_), custom_call_target="tpu_custom_call" | custom-call | tf_op jit(solution)/shard_map/down/pallas_call | solution.py:293
  210.4 10.3 %all-to-all-start.4 = ((bf16[64,8,512]{2,1,0:T(8,128)(2,1)}), bf16[64,8,512]{2,1,0:T(8,128)(2,1)S(1)}, u32[]{:S(2)}, u32[]{:S(2)}) async-start(bf16[64,8,512]{2,1,0:T(8,128)(2,1)} %bitcast.37), calls=%async_computation.4 | async-start | bytes 1048576 | tf_op jit(solution)/shard_map/all_to_all | solution.py:400
  220.8 5.1 %collective-permute-done.10.hid_ref = bf16[256,2048]{1,0:T(8,128)(2,1)} collective-permute-done((bf16[256,2048]{1,0:T(8,128)(2,1)}, bf16[256,2048]{1,0:T(8,128)(2,1)}, u32[]{:S(2)}, u32[]{:S(2)}) %collective-permute-start.10) | collective-permute-done | bytes 1048608 | tf_op jit(solution)/shard_map/ppermute | solution.py:440
  225.9 4.8 %down.3 = bf16[512,512]{1,0:T(8,128)(2,1)} custom-call(s32[1]{0:T(128)} %bitcast.rank_ref, bf16[256,2048]{1,0:T(8,128)(2,1)} %collective-permute-done.10.hid_ref, bf16[512,1024]{1,0:T(8,128)(2,1)} %copy-done.6, bf16[512,1024]{1,0:T(8,128)(2,1)} %copy-done.8, bf16[512,1024]{1,0:T(8,128)(2,1)} %collective-permute-done.8.refs_2_, ...), custom_call_target="tpu_custom_call" | custom-call | tf_op jit(solution)/shard_map/down/pallas_call | solution.py:293
  230.7 6.7 %all-to-all-done.4 = bf16[64,8,512]{2,1,0:T(8,128)(2,1)S(1)} async-done(((bf16[64,8,512]{2,1,0:T(8,128)(2,1)}), bf16[64,8,512]{2,1,0:T(8,128)(2,1)S(1)}, u32[]{:S(2)}, u32[]{:S(2)}) %all-to-all-start.4) | async-done | bytes 524320 | tf_op jit(solution)/shard_map/all_to_all | solution.py:400
  237.5 23.8 %all_to_all.69 = bf16[64,8,512]{2,1,0:T(8,128)(2,1)S(1)} all-to-all(bf16[64,8,512]{2,1,0:T(8,128)(2,1)} %bitcast.38), channel_id=1, replica_groups=mesh['seq'=64,'ffn'=4] {'seq'}, dimensions={0} | all-to-all | bytes 1048576 | tf_op jit(solution)/shard_map/all_to_all | solution.py:400
  261.3 1.7 combine.1
  263.1 18.7 %all_to_all.70.parts_ref = bf16[4,128,1024]{2,1,0:T(8,128)(2,1)S(1)} all-to-all(bf16[4,128,1024]{2,1,0:T(8,128)(2,1)S(1)} %bitcast.25), channel_id=1, replica_groups=mesh['seq'=64,'ffn'=4] {'ffn'}, dimensions={0} | all-to-all | bytes 2097152 | tf_op jit(solution)/shard_map/all_to_all | solution.py:403
  281.7 1.2 final.1
  (39 shorter events, 4.9 us)
Async XLA Ops:
  6.5 19.8 %copy-start = (bf16[256,2048]{1,0:T(8,128)(2,1)S(1)}, bf16[256,2048]{1,0:T(8,128)(2,1)}, u32[]{:S(2)}) copy-start(bf16[256,2048]{1,0:T(8,128)(2,1)} %param.16) | copy-start | bytes 3145732
  6.5 173.2 %all-gather.2.cloned.1.call-start = ((), (), s32[]{:S(2)}) async-start(), calls=%async_computation.7 | async-start | bytes 10485760 | tf_op jit(solution)/shard_map/all_gather | solution.py:409
  14.2 61.4 %all-to-all-start = ((bf16[64,8,768]{2,1,0:T(8,128)(2,1)}), bf16[64,8,768]{2,1,0:T(8,128)(2,1)S(1)}, u32[]{:S(2)}, u32[]{:S(2)}) async-start(bf16[64,8,768]{2,1,0:T(8,128)(2,1)} %bitcast.35), calls=%async_computation | async-start | bytes 1572864 | tf_op jit(solution)/shard_map/all_to_all | solution.py:400
  26.4 78.3 %copy-start.9 = (bf16[128,2048]{1,0:T(8,128)(2,1)}, bf16[128,2048]{1,0:T(8,128)(2,1)S(1)}, u32[]{:S(2)}) copy-start(bf16[128,2048]{1,0:T(8,128)(2,1)S(1)} %constant_dynamic-slice_fusion.refs_0_) | copy-start | bytes 1572868
  26.4 27.6 %collective-permute-start = (bf16[128,2048]{1,0:T(8,128)(2,1)S(1)}, bf16[128,2048]{1,0:T(8,128)(2,1)S(1)}, u32[]{:S(2)}, u32[]{:S(2)}) collective-permute-start(bf16[128,2048]{1,0:T(8,128)(2,1)S(1)} %constant_dynamic-slice_fusion.refs_0_), channel_id=1, source_target_pairs={{1,0},{2,1},{3,2},{0,3},{5,4},{6,5},{7,6},{4,7},{9,8},{10,9},{11,1... | collective-permute-start | bytes 1572872 | tf_op jit(solution)/shard_map/ppermute | solution.py:416
  29.3 27.5 %collective-permute-start.1 = (bf16[128,2048]{1,0:T(8,128)(2,1)S(1)}, bf16[128,2048]{1,0:T(8,128)(2,1)S(1)}, u32[]{:S(2)}, u32[]{:S(2)}) collective-permute-start(bf16[128,2048]{1,0:T(8,128)(2,1)S(1)} %constant_dynamic-slice_fusion.refs_0_), channel_id=1, source_target_pairs={{2,0},{3,1},{0,2},{1,3},{6,4},{7,5},{4,6},{5,7},{10,8},{11,9},{8,1... | collective-permute-start | bytes 1572872 | tf_op jit(solution)/shard_map/ppermute | solution.py:416
  30.1 45.6 %collective-permute-start.2 = (bf16[128,2048]{1,0:T(8,128)(2,1)S(1)}, bf16[128,2048]{1,0:T(8,128)(2,1)}, u32[]{:S(2)}, u32[]{:S(2)}) collective-permute-start(bf16[128,2048]{1,0:T(8,128)(2,1)S(1)} %constant_dynamic-slice_fusion.refs_0_), channel_id=1, source_target_pairs={{3,0},{0,1},{1,2},{2,3},{7,4},{4,5},{5,6},{6,7},{11,8},{8,9},{9,10... | collective-permute-start | bytes 1572872 | tf_op jit(solution)/shard_map/ppermute | solution.py:416
  54.0 50.7 %copy-start.10 = (bf16[128,2048]{1,0:T(8,128)(2,1)}, bf16[128,2048]{1,0:T(8,128)(2,1)S(1)}, u32[]{:S(2)}) copy-start(bf16[128,2048]{1,0:T(8,128)(2,1)S(1)} %collective-permute-done.refs_1_) | copy-start | bytes 1572868
  56.8 0.8 copy-start.11
  99.5 31.8 %all-to-all-start.2 = ((bf16[4,512,256]{2,1,0:T(8,128)(2,1)}), bf16[4,512,256]{2,1,0:T(8,128)(2,1)S(1)}, u32[]{:S(2)}, u32[]{:S(2)}) async-start(bf16[4,512,256]{2,1,0:T(8,128)(2,1)} %broadcast_in_dim.12), calls=%async_computation.2 | async-start | bytes 2097152 | tf_op jit(solution)/shard_map/all_to_all | solution.py:403
  104.7 2.0 collective-permute-start.3
  104.7 3.5 %collective-permute-start.4 = (bf16[128,2048]{1,0:T(8,128)(2,1)S(1)}, bf16[128,2048]{1,0:T(8,128)(2,1)}, u32[]{:S(2)}, u32[]{:S(2)}) collective-permute-start(bf16[128,2048]{1,0:T(8,128)(2,1)S(1)} %collective-permute-done.refs_1_), channel_id=1, source_target_pairs={{0,4},{4,0},{8,12},{12,8},{16,20},{20,16},{24,28},{28,24},{32,36},... | collective-permute-start | bytes 1572872 | tf_op jit(solution)/shard_map/ppermute | solution.py:430
  105.2 3.2 %collective-permute-start.5 = (bf16[128,2048]{1,0:T(8,128)(2,1)}, bf16[128,2048]{1,0:T(8,128)(2,1)}, u32[]{:S(2)}, u32[]{:S(2)}) collective-permute-start(bf16[128,2048]{1,0:T(8,128)(2,1)} %copy-done.11), channel_id=1, source_target_pairs={{0,4},{4,0},{8,12},{12,8},{16,20},{20,16},{24,28},{28,24},{32,36},... | collective-permute-start | bytes 1572872 | tf_op jit(solution)/shard_map/ppermute | solution.py:430
  105.3 3.9 %collective-permute-start.6 = (bf16[128,2048]{1,0:T(8,128)(2,1)}, bf16[128,2048]{1,0:T(8,128)(2,1)}, u32[]{:S(2)}, u32[]{:S(2)}) collective-permute-start(bf16[128,2048]{1,0:T(8,128)(2,1)} %collective-permute-done.2.refs_3_), channel_id=1, source_target_pairs={{0,4},{4,0},{8,12},{12,8},{16,20},{20,16},{24,28},{28,24},{32,36},... | collective-permute-start | bytes 1572872 | tf_op jit(solution)/shard_map/ppermute | solution.py:430
  131.3 1.0 copy-start.7
  145.5 34.3 %all-to-all-start.3 = ((bf16[64,8,1024]{2,1,0:T(8,128)(2,1)}), bf16[64,8,1024]{2,1,0:T(8,128)(2,1)}, u32[]{:S(2)}, u32[]{:S(2)}) async-start(bf16[64,8,1024]{2,1,0:T(8,128)(2,1)} %bitcast.40), calls=%async_computation.3 | async-start | bytes 2097152 | tf_op jit(solution)/shard_map/all_to_all | solution.py:400
  155.4 32.0 %copy-start.6 = (bf16[512,1024]{1,0:T(8,128)(2,1)}, bf16[512,1024]{1,0:T(8,128)(2,1)S(1)}, u32[]{:S(2)}) copy-start(bf16[512,1024]{1,0:T(8,128)(2,1)S(1)} %get-tuple-element.22.refs_0_) | copy-start | bytes 3145732
  155.4 32.6 %collective-permute-start.7 = (bf16[512,1024]{1,0:T(8,128)(2,1)}, bf16[512,1024]{1,0:T(8,128)(2,1)S(1)}, u32[]{:S(2)}, u32[]{:S(2)}) collective-permute-start(bf16[512,1024]{1,0:T(8,128)(2,1)} %get-tuple-element.21), channel_id=1, source_target_pairs={{1,0},{2,1},{3,2},{0,3},{5,4},{6,5},{7,6},{4,7},{9,8},{10,9},{11,1... | collective-permute-start | bytes 3145736 | tf_op jit(solution)/shard_map/ppermute | solution.py:416
  156.6 31.4 %collective-permute-start.8 = (bf16[512,1024]{1,0:T(8,128)(2,1)S(1)}, bf16[512,1024]{1,0:T(8,128)(2,1)}, u32[]{:S(2)}, u32[]{:S(2)}) collective-permute-start(bf16[512,1024]{1,0:T(8,128)(2,1)S(1)} %get-tuple-element.22.refs_0_), channel_id=1, source_target_pairs={{2,0},{3,1},{0,2},{1,3},{6,4},{7,5},{4,6},{5,7},{10,8},{11,9},{8,1... | collective-permute-start | bytes 3145736 | tf_op jit(solution)/shard_map/ppermute | solution.py:416
  158.0 47.5 %collective-permute-start.9 = (bf16[512,1024]{1,0:T(8,128)(2,1)}, bf16[512,1024]{1,0:T(8,128)(2,1)}, u32[]{:S(2)}, u32[]{:S(2)}) collective-permute-start(bf16[512,1024]{1,0:T(8,128)(2,1)} %get-tuple-element.21), channel_id=1, source_target_pairs={{3,0},{0,1},{1,2},{2,3},{7,4},{4,5},{5,6},{6,7},{11,8},{8,9},{9,10... | collective-permute-start | bytes 3145736 | tf_op jit(solution)/shard_map/ppermute | solution.py:416
  187.4 38.4 %collective-permute-start.10 = (bf16[256,2048]{1,0:T(8,128)(2,1)}, bf16[256,2048]{1,0:T(8,128)(2,1)}, u32[]{:S(2)}, u32[]{:S(2)}) collective-permute-start(bf16[256,2048]{1,0:T(8,128)(2,1)} %up.1.hid_ref), channel_id=1, source_target_pairs={{0,1},{1,0},{2,3},{3,2},{4,5},{5,4},{6,7},{7,6},{8,9},{9,8},{10,11... | collective-permute-start | bytes 3145736 | tf_op jit(solution)/shard_map/ppermute | solution.py:440
  188.0 17.6 %copy-start.8 = (bf16[512,1024]{1,0:T(8,128)(2,1)}, bf16[512,1024]{1,0:T(8,128)(2,1)S(1)}, u32[]{:S(2)}) copy-start(bf16[512,1024]{1,0:T(8,128)(2,1)S(1)} %collective-permute-done.7.refs_1_) | copy-start | bytes 3145732
  210.4 27.0 %all-to-all-start.4 = ((bf16[64,8,512]{2,1,0:T(8,128)(2,1)}), bf16[64,8,512]{2,1,0:T(8,128)(2,1)S(1)}, u32[]{:S(2)}, u32[]{:S(2)}) async-start(bf16[64,8,512]{2,1,0:T(8,128)(2,1)} %bitcast.37), calls=%async_computation.4 | async-start | bytes 1048576 | tf_op jit(solution)/shard_map/all_to_all | solution.py:400
  220.8 40.5 %copy-start.3 = (f32[512,64]{1,0:T(8,128)S(1)}, f32[512,64]{1,0:T(8,128)}, u32[]{:S(2)}) copy-start(f32[512,64]{1,0:T(8,128)} %get-tuple-element.19.gates_ref) | copy-start | bytes 393220
  220.8 40.5 %copy-start.4 = (s32[64,1,16]{0,2,1:T(8,128)S(1)}, s32[64,1,16]{0,2,1:T(8,128)}, u32[]{:S(2)}) copy-start(s32[64,1,16]{0,2,1:T(8,128)} %param.20) | copy-start | bytes 12292
  220.8 40.5 %copy-start.5 = (s32[64,1]{0,1:T(1,128)S(1)}, s32[64,1]{0,1:T(1,128)}, u32[]{:S(2)}) copy-start(s32[64,1]{0,1:T(1,128)} %param.21) | copy-start | bytes 772
  261.3 20.4 %copy-start.1 = (f32[16,12288]{1,0:T(8,128)S(1)}, f32[16,12288]{1,0:T(8,128)}, u32[]{:S(2)}) copy-start(f32[16,12288]{1,0:T(8,128)} %gate_ref.1) | copy-start | bytes 2359300
  261.3 20.4 %copy-start.2 = (f32[128,2048]{1,0:T(8,128)S(1)}, f32[128,2048]{1,0:T(8,128)}, u32[]{:S(2)}) copy-start(f32[128,2048]{1,0:T(8,128)} %get-tuple-element.18.share_ref) | copy-start | bytes 3145732
Sparse Core Ops, SparseCore 0:
  9.2 121.6 all-gather.1

commit v3 on v2

--- a/solution.py
+++ b/solution.py
@@ -144,29 +144,47 @@
 
 
 def mix_kernel(
-    per, rank_ref, core_ref, step_ref, att_ref, *refs
+    per, pieces, rank_ref, core_ref, lane_ref, step_ref, att_ref, x_ref, gate_ref, shift_ref,
+    scale_ref, router_ref, picks_ref, *refs
 ):
-    weights = refs[:8]
-    (x_ref, gate_ref, shift_ref, scale_ref, router_ref, picks_ref,
-     disp_ref, gates_ref, share_ref, hidden_ref, normed_ref) = refs[8:]
+    blocks = refs[: 2 * pieces]
+    disp_ref, gates_ref, share_ref, hidden_ref, normed_ref, w_ref, sems = refs[2 * pieces :]
     step = step_ref[0]
     rank = rank_ref[0]
     tile = pl.program_id(0)
     rows = x_ref.shape[0]
+    parts = att_ref.shape[0]
+    inner = att_ref.shape[2]
+
+    @pl.when(tile == 0)
+    def _():
+        some = blocks[0].shape[0] // parts
+        copies = []
+        for number, block in enumerate(blocks):
+            which, turn = divmod(number, pieces)
+            half = lax.rem(core_ref[0] + which, 2)
+            place = lax.rem(lane_ref[0] + turn, pieces)
+            for part_turn in range(parts):
+                part = lax.rem(rank + part_turn, parts)
+                to = pl.multiple_of(part * inner + half * (inner // 2) + place * some, some)
+                copies.append(
+                    pltpu.make_async_copy(
+                        block.at[pl.ds(part_turn * some, some), :],
+                        w_ref.at[pl.ds(to, some), :],
+                        sems.at[number * parts + part_turn],
+                    )
+                )
+        for copy in copies:
+            copy.start()
+        for copy in copies:
+            copy.wait()
+
     gate = gate_ref[pl.ds(step, 1), :]
     shift = shift_ref[pl.ds(step, 1), :]
     scale = scale_ref[pl.ds(step, 1), :]
-    parts = att_ref.shape[0]
-    some = att_ref.shape[2] // 2
-    core = core_ref[0]
-    mixed = None
-    for turn in range(parts):
-        part = lax.rem(rank + turn, parts)
-        for which in range(2):
-            at = lax.rem(core + which, 2) * some
-            rows_of = att_ref[part, :, pl.ds(pl.multiple_of(at, some), some)]
-            term = dot(rows_of, weights[which * parts + turn][...])
-            mixed = term if mixed is None else mixed + term
+    mixed = dot(att_ref[0], w_ref[:inner, :])
+    for part in range(1, parts):
+        mixed += dot(att_ref[part], w_ref[part * inner : (part + 1) * inner, :])
     hidden = x_ref[...].astype(F32) + gate * mixed
     hidden_ref[...] = hidden
     normed = (layer_norm(hidden) * (1.0 + scale) + shift).astype(BF16)
@@ -194,30 +212,28 @@
         ).astype(BF16)
 
 
-def mix_call(rank, core, step, att, weights, x, modulation, router_t, picks_t, per, share):
+def mix_call(
+    rank, core, lane, step, att, blocks, x, modulation, router_t, picks_t, per, share
+):
     tokens, width = x.shape
     parts, _, inner = att.shape
     experts = router_t.shape[0]
     steps = modulation.shape[0]
     rows = 256
     return pl.pallas_call(
-        functools.partial(mix_kernel, per),
+        functools.partial(mix_kernel, per, len(blocks) // 2),
         grid=(tokens // rows,),
-        in_specs=[
-            smem(),
-            smem(),
-            smem(),
+        in_specs=[smem()] * 4
+        + [
             pl.BlockSpec((parts, rows, inner), lambda i: (0, i, 0)),
-        ]
-        + [pl.BlockSpec(w.shape, lambda i: (0, 0)) for w in weights]
-        + [
             pl.BlockSpec((rows, width), lambda i: (i, 0)),
             pl.BlockSpec((steps, width), lambda i: (0, 2)),
             pl.BlockSpec((steps, width), lambda i: (0, 3)),
             pl.BlockSpec((steps, width), lambda i: (0, 4)),
             pl.BlockSpec(router_t.shape, lambda i: (0, 0)),
             pl.BlockSpec(picks_t.shape, lambda i: (0, 0)),
-        ],
+        ]
+        + [pl.BlockSpec(memory_space=pl.ANY)] * len(blocks),
         out_specs=[
             pl.BlockSpec((2 * experts * per, width // 2), lambda i: (0, 0)),
             pl.BlockSpec((rows, experts), lambda i: (i, 0)),
@@ -228,10 +244,18 @@
             jax.ShapeDtypeStruct((tokens, experts), F32),
             jax.ShapeDtypeStruct((share, width), F32),
         ],
-        scratch_shapes=[pltpu.VMEM((rows, width), F32), pltpu.VMEM((tokens, width), BF16)],
-        compiler_params=params(56),
+        scratch_shapes=[
+            pltpu.VMEM((rows, width), F32),
+            pltpu.VMEM((tokens, width), BF16),
+            pltpu.VMEM((parts * inner, width), BF16),
+            pltpu.SemaphoreType.DMA((len(blocks) * parts,)),
+        ],
+        compiler_params=params(48),
         name="mix",
-    )(rank, core, step, att, *weights, x, modulation, modulation, modulation, router_t, picks_t)
+    )(
+        rank, core, lane, step, att, x, modulation, modulation, modulation, router_t, picks_t,
+        *blocks,
+    )
 
 
 def up_kernel(per, rows_ref, w_ref, out_ref, tok_ref):
@@ -402,10 +426,13 @@
     def over_ffn(values):
         return lax.all_to_all(values, "ffn", split_axis=0, concat_axis=0, tiled=True)
 
-    core = lax.rem(lax.axis_index("seq").astype(jnp.int32), 2)
-    core_arr = core.reshape(1)
-    out_rows = out_weight.shape[0] // 2
-    out_own = lax.dynamic_slice_in_dim(out_weight, core * out_rows, out_rows, 0)
+    place = lax.axis_index("seq").astype(jnp.int32)
+    core = lax.rem(place, 2)
+    lanes = 4
+    stride = seq // lanes
+    lane = place // stride
+    some = out_weight.shape[0] // (2 * lanes)
+    out_own = lax.dynamic_slice_in_dim(out_weight, (core * lanes + lane) * some, some, 0)
     up_full = lax.all_gather(expert_up, "ffn", axis=0, tiled=True)
     down = expert_down[0]
     side = lax.rem(rank, 2)
@@ -415,7 +442,7 @@
     def from_turn(values, turn):
         return lax.ppermute(values, "ffn", [((i + turn) % ffn, i) for i in range(ffn)])
 
-    out_blocks = [out_own] + [from_turn(out_own, turn) for turn in range(1, ffn)]
+    out_rows = [out_own] + [from_turn(out_own, turn) for turn in range(1, ffn)]
     blocks = [
         same_half,
         from_turn(other_half, 1),
@@ -425,14 +452,22 @@
 
     stacked = qkv_call(step_index, x, modulation, jnp.transpose(qkv_weight, (1, 0, 2)), qk_gain)
     stacked = over_seq(stacked)
-    stacked, out_blocks = lax.optimization_barrier((stacked, out_blocks))
+    stacked, out_rows = lax.optimization_barrier((stacked, out_rows))
+    out_rows = jnp.concatenate(out_rows, axis=0)
+
+    def from_lane(values, turn):
+        pairs = [((i + turn * stride) % seq, i) for i in range(seq)]
+        return lax.ppermute(values, "seq", pairs)
+
+    out_blocks = [out_rows] + [from_lane(out_rows, turn) for turn in range(1, lanes)]
+    attended = attention_call(stacked, position_count // seq, head_size)
+    attended = over_seq(attended)
+    attended, out_blocks = lax.optimization_barrier((attended, out_blocks))
     swap = [(i, i ^ 1) for i in range(seq)]
     out_blocks = out_blocks + [lax.ppermute(b, "seq", swap) for b in out_blocks]
-    attended = attention_call(stacked, position_count // seq, head_size)
-    attended = over_seq(attended)
     every = over_ffn(jnp.broadcast_to(attended[None], (ffn,) + attended.shape))
     outgoing, gates, share = mix_call(
-        rank_arr, core_arr, step_index, every, out_blocks, x, modulation,
+        rank_arr, core.reshape(1), lane.reshape(1), step_index, every, out_blocks, x, modulation,
         jnp.transpose(router_weight, (1, 0)), picks_t, per, share_len,
     )
     expert_tokens = over_seq(outgoing)

time: 290 us -> 275 us (0.948)
  waiting for transfers between devices: 121 us -> 94.9 us
  starting transfers between devices: 43.6 us -> 49 us
    ppermute x6, waiting for transfers between devices: 61.5 us -> 28.8 us  [from_turn(): lax.ppermute(values, 'ffn', [((i + turn) % ffn, i) for i in range(ffn)])]
    all_to_all x3, waiting for transfers between devices: 28.4 us -> 34 us  [over_seq(): lax.all_to_all(values, 'seq', split_axis=0, concat_axis=0, tiled=True)]
    ppermute x0 -> x3, starting transfers between devices: none -> 5.02 us  [from_lane(): return lax.ppermute(values, 'seq', pairs)]
  transfers between devices with their start and end apart: 16 -> 19, of which waited for: 12 -> 13; matrix products, arithmetic and copies ran while one was open for 1% -> 1% of each run, Pallas kernels for 13% -> 14%
where the time goes in v3:
time: 275 us
  waiting for transfers between devices  94.9 us (35%)
  blocking collectives  66.8 us (24%)
  starting transfers between devices  49 us (18%)
  Pallas kernels  42.3 us (15%)
  between operations  14.2 us (5%)
  local copies, waits for them, and re-layouts  7.33 us (3%)
    all_to_all x2, blocking collectives, over_seq(): lax.all_to_all(values, 'seq', split_axis=0, concat_axis=0, tiled=True)  48.2 us
    all_to_all x3, waiting for transfers between devices, over_seq(): lax.all_to_all(values, 'seq', split_axis=0, concat_axis=0, tiled=True)  34 us
    all_to_all x3, starting transfers between devices, over_seq(): lax.all_to_all(values, 'seq', split_axis=0, concat_axis=0, tiled=True)  29.8 us
    ppermute x6, waiting for transfers between devices, from_turn(): lax.ppermute(values, 'ffn', [((i + turn) % ffn, i) for i in range(ffn)])  28.8 us
    all_to_all x1, waiting for transfers between devices, over_ffn(): lax.all_to_all(values, 'ffn', split_axis=0, concat_axis=0, tiled=True)  23 us
    all_to_all x1, blocking collectives, over_ffn(): lax.all_to_all(values, 'ffn', split_axis=0, concat_axis=0, tiled=True)  18.7 us
    pallas_call x1, Pallas kernels, mix_call(): pl.pallas_call(functools.partial(mix_kernel, per, len(blocks) // 2), grid...  14.6 us
    pallas_call x2, Pallas kernels, down_call(): pl.pallas_call(functools.partial(down_kernel, per), grid=(2,), in_specs=[...  9.78 us
  transfers between devices with their start and end apart: 19, of which 13 were waited for; matrix products, arithmetic and copies ran while one was open for 1% of the time, Pallas kernels for 14%

profile of v3, /device:TPU:8, one launch (start us, length us, event | category | flops | bytes accessed | tf_op | source)
XLA Modules:
  0.0 274.6 jit_solution(7052830494847866478)
XLA Ops:
  7.9 6.3 %qkv.1 = bf16[512,768]{1,0:T(8,128)(2,1)} custom-call(s32[1]{0:T(128)S(6)} %copy.15.step_ref, bf16[512,2048]{1,0:T(8,128)(2,1)} %bitcast.35, f32[16,12288]{1,0:T(8,128)} %gate_ref.3, bf16[3,2048,256]{2,1,0:T(8,128)(2,1)} %bitcast.38, f32[2,128]{1,0:T(2,128)} %gain_ref.1), custom_call_target="tpu_custom_call" | custom-call | tf_op jit(solution)/shard_map/qkv/pallas_call | solution.py:67
  14.2 12.1 %all-to-all-start = ((bf16[64,8,768]{2,1,0:T(8,128)(2,1)}), bf16[64,8,768]{2,1,0:T(8,128)(2,1)S(1)}, u32[]{:S(2)}, u32[]{:S(2)}) async-start(bf16[64,8,768]{2,1,0:T(8,128)(2,1)} %bitcast.37), calls=%async_computation | async-start | bytes 1572864 | tf_op jit(solution)/shard_map/all_to_all | solution.py:424
  26.4 2.8 %collective-permute-start = (bf16[32,2048]{1,0:T(8,128)(2,1)S(1)}, bf16[32,2048]{1,0:T(8,128)(2,1)S(1)}, u32[]{:S(2)}, u32[]{:S(2)}) collective-permute-start(bf16[32,2048]{1,0:T(8,128)(2,1)S(1)} %constant_dynamic-slice_fusion), channel_id=1, source_target_pairs={{1,0},{2,1},{3,2},{0,3},{5,4},{6,5},{7,6},{4,7},{9,8},{10,9},{11,1... | collective-permute-start | bytes 393224 | tf_op jit(solution)/shard_map/ppermute | solution.py:443
  30.9 6.2 %collective-permute-done = bf16[32,2048]{1,0:T(8,128)(2,1)S(1)} collective-permute-done((bf16[32,2048]{1,0:T(8,128)(2,1)S(1)}, bf16[32,2048]{1,0:T(8,128)(2,1)S(1)}, u32[]{:S(2)}, u32[]{:S(2)}) %collective-permute-start) | collective-permute-done | bytes 131104 | tf_op jit(solution)/shard_map/ppermute | solution.py:443
  37.2 2.7 collective-permute-done.1
  39.9 2.4 collective-permute-done.2
  42.3 5.9 %all-to-all-done = bf16[64,8,768]{2,1,0:T(8,128)(2,1)S(1)} async-done(((bf16[64,8,768]{2,1,0:T(8,128)(2,1)}), bf16[64,8,768]{2,1,0:T(8,128)(2,1)S(1)}, u32[]{:S(2)}, u32[]{:S(2)}) %all-to-all-start) | async-done | bytes 786464 | tf_op jit(solution)/shard_map/all_to_all | solution.py:424
  48.3 1.6 collective-permute-start.3
  49.9 1.6 collective-permute-start.4
  51.4 1.9 collective-permute-start.5
  54.5 24.6 %all_to_all.71 = bf16[64,8,256]{2,1,0:T(8,128)(2,1)S(1)} all-to-all(bf16[64,8,256]{2,1,0:T(8,128)(2,1)S(1)} %bitcast.30), channel_id=1, replica_groups=mesh['seq'=64,'ffn'=4] {'seq'}, dimensions={0} | all-to-all | bytes 524288 | tf_op jit(solution)/shard_map/all_to_all | solution.py:424
  80.9 4.3 %all-to-all-start.2 = ((bf16[4,512,256]{2,1,0:T(8,128)(2,1)}), bf16[4,512,256]{2,1,0:T(8,128)(2,1)}, u32[]{:S(2)}, u32[]{:S(2)}) async-start(bf16[4,512,256]{2,1,0:T(8,128)(2,1)} %broadcast_in_dim.4), calls=%async_computation.2 | async-start | bytes 2097152 | tf_op jit(solution)/shard_map/all_to_all | solution.py:427
  88.1 1.5 collective-permute-done.8.refs_6_
  89.8 23.0 %all-to-all-done.2.att_ref = bf16[4,512,256]{2,1,0:T(8,128)(2,1)} async-done(((bf16[4,512,256]{2,1,0:T(8,128)(2,1)}), bf16[4,512,256]{2,1,0:T(8,128)(2,1)}, u32[]{:S(2)}, u32[]{:S(2)}) %all-to-all-start.2) | async-done | bytes 1048608 | tf_op jit(solution)/shard_map/all_to_all | solution.py:427
  114.8 14.6 %mix.1 = (bf16[512,1024]{1,0:T(8,128)(2,1)}, f32[512,64]{1,0:T(8,128)S(1)}, f32[128,2048]{1,0:T(8,128)}) custom-call(s32[1]{0:T(128)} %bitcast.rank_ref, s32[1]{0:T(128)} %bitcast.1.core_ref, s32[1]{0:T(128)} %bitcast.2.lane_ref, s32[1]{0:T(128)S(6)} %copy.15.step_ref, bf16[4,512,256]{2,1,0:T(8,128)(2,1)} %all-to-all-done.2.att_ref, ...), custom_call_target="tpu_custom_call" | custom-call | tf_op jit(solution)/shard_map/mix/pallas_call | solution.py:223
  130.0 7.3 %all-to-all-start.3 = ((bf16[64,8,1024]{2,1,0:T(8,128)(2,1)}), bf16[64,8,1024]{2,1,0:T(8,128)(2,1)}, u32[]{:S(2)}, u32[]{:S(2)}) async-start(bf16[64,8,1024]{2,1,0:T(8,128)(2,1)} %bitcast.42), calls=%async_computation.3 | async-start | bytes 2097152 | tf_op jit(solution)/shard_map/all_to_all | solution.py:424
  137.4 2.7 dynamic-slice_bitcast_fusion
  140.1 1.5 collective-permute-start.10
  141.6 1.7 collective-permute-start.11
  143.3 21.1 %all-to-all-done.3 = bf16[64,8,1024]{2,1,0:T(8,128)(2,1)} async-done(((bf16[64,8,1024]{2,1,0:T(8,128)(2,1)}), bf16[64,8,1024]{2,1,0:T(8,128)(2,1)}, u32[]{:S(2)}, u32[]{:S(2)}) %all-to-all-start.3) | async-done | bytes 1048608 | tf_op jit(solution)/shard_map/all_to_all | solution.py:424
  164.4 7.6 %up.1.hid_ref = bf16[256,2048]{1,0:T(8,128)(2,1)} custom-call(bf16[512,1024]{1,0:T(8,128)(2,1)} %bitcast.15.rows_ref, bf16[4,2048,512]{2,1,0:T(8,128)(2,1)} %all-gather.2.cloned.1.call-done.w_ref), custom_call_target="tpu_custom_call" | custom-call | tf_op jit(solution)/shard_map/up/pallas_call | solution.py:276
  172.0 1.1 collective-permute-start.13
  173.2 17.4 %collective-permute-done.12.refs_3_ = bf16[512,1024]{1,0:T(8,128)(2,1)} collective-permute-done((bf16[512,1024]{1,0:T(8,128)(2,1)}, bf16[512,1024]{1,0:T(8,128)(2,1)}, u32[]{:S(2)}, u32[]{:S(2)}) %collective-permute-start.12) | collective-permute-done | bytes 1048608 | tf_op jit(solution)/shard_map/ppermute | solution.py:443
  190.6 4.9 %down.2 = bf16[512,512]{1,0:T(8,128)(2,1)} custom-call(s32[1]{0:T(128)} %bitcast.rank_ref, bf16[256,2048]{1,0:T(8,128)(2,1)} %up.1.hid_ref, bf16[512,1024]{1,0:T(8,128)(2,1)} %copy-done.10, bf16[512,1024]{1,0:T(8,128)(2,1)} %collective-permute-done.10.refs_1_, bf16[512,1024]{1,0:T(8,128)(2,1)} %collective-permute-done.11.refs_2_, ...), custom_call_target="tpu_custom_call" | custom-call | tf_op jit(solution)/shard_map/down/pallas_call | solution.py:317
  195.5 10.3 %all-to-all-start.4 = ((bf16[64,8,512]{2,1,0:T(8,128)(2,1)}), bf16[64,8,512]{2,1,0:T(8,128)(2,1)S(1)}, u32[]{:S(2)}, u32[]{:S(2)}) async-start(bf16[64,8,512]{2,1,0:T(8,128)(2,1)} %bitcast.39), calls=%async_computation.4 | async-start | bytes 1048576 | tf_op jit(solution)/shard_map/all_to_all | solution.py:424
  205.9 4.9 %collective-permute-done.13.hid_ref = bf16[256,2048]{1,0:T(8,128)(2,1)} collective-permute-done((bf16[256,2048]{1,0:T(8,128)(2,1)}, bf16[256,2048]{1,0:T(8,128)(2,1)}, u32[]{:S(2)}, u32[]{:S(2)}) %collective-permute-start.13) | collective-permute-done | bytes 1048608 | tf_op jit(solution)/shard_map/ppermute | solution.py:475
  210.8 4.9 %down.3 = bf16[512,512]{1,0:T(8,128)(2,1)} custom-call(s32[1]{0:T(128)} %bitcast.rank_ref, bf16[256,2048]{1,0:T(8,128)(2,1)} %collective-permute-done.13.hid_ref, bf16[512,1024]{1,0:T(8,128)(2,1)} %copy-done.10, bf16[512,1024]{1,0:T(8,128)(2,1)} %collective-permute-done.10.refs_1_, bf16[512,1024]{1,0:T(8,128)(2,1)} %collective-permute-done.11.refs_2_, ...), custom_call_target="tpu_custom_call" | custom-call | tf_op jit(solution)/shard_map/down/pallas_call | solution.py:317
  215.7 6.9 %all-to-all-done.4 = bf16[64,8,512]{2,1,0:T(8,128)(2,1)S(1)} async-done(((bf16[64,8,512]{2,1,0:T(8,128)(2,1)}), bf16[64,8,512]{2,1,0:T(8,128)(2,1)S(1)}, u32[]{:S(2)}, u32[]{:S(2)}) %all-to-all-start.4) | async-done | bytes 524320 | tf_op jit(solution)/shard_map/all_to_all | solution.py:424
  222.6 23.6 %all_to_all.72 = bf16[64,8,512]{2,1,0:T(8,128)(2,1)S(1)} all-to-all(bf16[64,8,512]{2,1,0:T(8,128)(2,1)} %bitcast.40), channel_id=1, replica_groups=mesh['seq'=64,'ffn'=4] {'seq'}, dimensions={0} | all-to-all | bytes 1048576 | tf_op jit(solution)/shard_map/all_to_all | solution.py:424
  246.2 1.7 combine.1
  247.9 18.7 %all_to_all.73.parts_ref = bf16[4,128,1024]{2,1,0:T(8,128)(2,1)S(1)} all-to-all(bf16[4,128,1024]{2,1,0:T(8,128)(2,1)S(1)} %bitcast.26), channel_id=1, replica_groups=mesh['seq'=64,'ffn'=4] {'ffn'}, dimensions={0} | all-to-all | bytes 2097152 | tf_op jit(solution)/shard_map/all_to_all | solution.py:427
  266.6 1.2 final.1
  (47 shorter events, 11.2 us)
Async XLA Ops:
  6.5 19.9 %copy-start = (bf16[256,2048]{1,0:T(8,128)(2,1)S(1)}, bf16[256,2048]{1,0:T(8,128)(2,1)}, u32[]{:S(2)}) copy-start(bf16[256,2048]{1,0:T(8,128)(2,1)} %param.16) | copy-start | bytes 3145732
  6.5 157.9 %all-gather.2.cloned.1.call-start = ((), (), s32[]{:S(2)}) async-start(), calls=%async_computation.7 | async-start | bytes 10485760 | tf_op jit(solution)/shard_map/all_gather | solution.py:436
  14.2 34.0 %all-to-all-start = ((bf16[64,8,768]{2,1,0:T(8,128)(2,1)}), bf16[64,8,768]{2,1,0:T(8,128)(2,1)S(1)}, u32[]{:S(2)}, u32[]{:S(2)}) async-start(bf16[64,8,768]{2,1,0:T(8,128)(2,1)} %bitcast.37), calls=%async_computation | async-start | bytes 1572864 | tf_op jit(solution)/shard_map/all_to_all | solution.py:424
  26.4 10.7 %collective-permute-start = (bf16[32,2048]{1,0:T(8,128)(2,1)S(1)}, bf16[32,2048]{1,0:T(8,128)(2,1)S(1)}, u32[]{:S(2)}, u32[]{:S(2)}) collective-permute-start(bf16[32,2048]{1,0:T(8,128)(2,1)S(1)} %constant_dynamic-slice_fusion), channel_id=1, source_target_pairs={{1,0},{2,1},{3,2},{0,3},{5,4},{6,5},{7,6},{4,7},{9,8},{10,9},{11,1... | collective-permute-start | bytes 393224 | tf_op jit(solution)/shard_map/ppermute | solution.py:443
  29.3 10.6 %collective-permute-start.1 = (bf16[32,2048]{1,0:T(8,128)(2,1)S(1)}, bf16[32,2048]{1,0:T(8,128)(2,1)S(1)}, u32[]{:S(2)}, u32[]{:S(2)}) collective-permute-start(bf16[32,2048]{1,0:T(8,128)(2,1)S(1)} %constant_dynamic-slice_fusion), channel_id=1, source_target_pairs={{2,0},{3,1},{0,2},{1,3},{6,4},{7,5},{4,6},{5,7},{10,8},{11,9},{8,1... | collective-permute-start | bytes 393224 | tf_op jit(solution)/shard_map/ppermute | solution.py:443
  30.0 12.3 %collective-permute-start.2 = (bf16[32,2048]{1,0:T(8,128)(2,1)S(1)}, bf16[32,2048]{1,0:T(8,128)(2,1)S(1)}, u32[]{:S(2)}, u32[]{:S(2)}) collective-permute-start(bf16[32,2048]{1,0:T(8,128)(2,1)S(1)} %constant_dynamic-slice_fusion), channel_id=1, source_target_pairs={{3,0},{0,1},{1,2},{2,3},{7,4},{4,5},{5,6},{6,7},{11,8},{8,9},{9,10... | collective-permute-start | bytes 393224 | tf_op jit(solution)/shard_map/ppermute | solution.py:443
  48.3 30.7 %collective-permute-start.3 = (bf16[128,2048]{1,0:T(8,128)(2,1)S(1)}, bf16[128,2048]{1,0:T(8,128)(2,1)S(1)}, u32[]{:S(2)}, u32[]{:S(2)}) collective-permute-start(bf16[128,2048]{1,0:T(8,128)(2,1)S(1)} %constant_dynamic-update-slice_fusion.refs_0_), channel_id=1, source_target_pairs={{64,0},{68,4},{72,8},{76,12},{80,16},{84,20},{88,24},{92,28},{96,3... | collective-permute-start | bytes 1572872 | tf_op jit(solution)/shard_map/ppermute | solution.py:460
  49.9 29.2 %collective-permute-start.4 = (bf16[128,2048]{1,0:T(8,128)(2,1)S(1)}, bf16[128,2048]{1,0:T(8,128)(2,1)S(1)}, u32[]{:S(2)}, u32[]{:S(2)}) collective-permute-start(bf16[128,2048]{1,0:T(8,128)(2,1)S(1)} %constant_dynamic-update-slice_fusion.refs_0_), channel_id=1, source_target_pairs={{128,0},{132,4},{136,8},{140,12},{144,16},{148,20},{152,24},{156,2... | collective-permute-start | bytes 1572872 | tf_op jit(solution)/shard_map/ppermute | solution.py:460
  51.4 27.6 %collective-permute-start.5 = (bf16[128,2048]{1,0:T(8,128)(2,1)S(1)}, bf16[128,2048]{1,0:T(8,128)(2,1)S(1)}, u32[]{:S(2)}, u32[]{:S(2)}) collective-permute-start(bf16[128,2048]{1,0:T(8,128)(2,1)S(1)} %constant_dynamic-update-slice_fusion.refs_0_), channel_id=1, source_target_pairs={{192,0},{196,4},{200,8},{204,12},{208,16},{212,20},{216,24},{220,2... | collective-permute-start | bytes 1572872 | tf_op jit(solution)/shard_map/ppermute | solution.py:460
  54.4 58.3 %copy-start.1 = (f32[16,12288]{1,0:T(8,128)S(1)}, f32[16,12288]{1,0:T(8,128)}, u32[]{:S(2)}) copy-start(f32[16,12288]{1,0:T(8,128)} %gate_ref.3) | copy-start | bytes 2359300
  54.4 58.3 %copy-start.8 = (s32[64,1,16]{0,2,1:T(8,128)S(1)}, s32[64,1,16]{0,2,1:T(8,128)}, u32[]{:S(2)}) copy-start(s32[64,1,16]{0,2,1:T(8,128)} %param.20) | copy-start | bytes 12292
  79.1 0.8 copy-start.3
  80.9 31.8 %all-to-all-start.2 = ((bf16[4,512,256]{2,1,0:T(8,128)(2,1)}), bf16[4,512,256]{2,1,0:T(8,128)(2,1)}, u32[]{:S(2)}, u32[]{:S(2)}) async-start(bf16[4,512,256]{2,1,0:T(8,128)(2,1)} %broadcast_in_dim.4), calls=%async_computation.2 | async-start | bytes 2097152 | tf_op jit(solution)/shard_map/all_to_all | solution.py:427
  85.2 2.1 collective-permute-start.6
  85.6 2.5 collective-permute-start.7
  85.8 3.8 %collective-permute-start.8 = (bf16[128,2048]{1,0:T(8,128)(2,1)S(1)}, bf16[128,2048]{1,0:T(8,128)(2,1)}, u32[]{:S(2)}, u32[]{:S(2)}) collective-permute-start(bf16[128,2048]{1,0:T(8,128)(2,1)S(1)} %collective-permute-done.4.refs_2_), channel_id=1, source_target_pairs={{0,4},{4,0},{8,12},{12,8},{16,20},{20,16},{24,28},{28,24},{32,36},... | collective-permute-start | bytes 1572872 | tf_op jit(solution)/shard_map/ppermute | solution.py:467
  86.1 3.7 %collective-permute-start.9 = (bf16[128,2048]{1,0:T(8,128)(2,1)}, bf16[128,2048]{1,0:T(8,128)(2,1)}, u32[]{:S(2)}, u32[]{:S(2)}) collective-permute-start(bf16[128,2048]{1,0:T(8,128)(2,1)} %copy-done.3), channel_id=1, source_target_pairs={{0,4},{4,0},{8,12},{12,8},{16,20},{20,16},{24,28},{28,24},{32,36},... | collective-permute-start | bytes 1572872 | tf_op jit(solution)/shard_map/ppermute | solution.py:467
  112.8 1.0 copy-start.4
  113.8 0.9 copy-start.5
  129.3 0.7 copy-start.6
  130.0 34.4 %all-to-all-start.3 = ((bf16[64,8,1024]{2,1,0:T(8,128)(2,1)}), bf16[64,8,1024]{2,1,0:T(8,128)(2,1)}, u32[]{:S(2)}, u32[]{:S(2)}) async-start(bf16[64,8,1024]{2,1,0:T(8,128)(2,1)} %bitcast.42), calls=%async_computation.3 | async-start | bytes 2097152 | tf_op jit(solution)/shard_map/all_to_all | solution.py:424
  140.1 32.0 %copy-start.10 = (bf16[512,1024]{1,0:T(8,128)(2,1)}, bf16[512,1024]{1,0:T(8,128)(2,1)S(1)}, u32[]{:S(2)}) copy-start(bf16[512,1024]{1,0:T(8,128)(2,1)S(1)} %get-tuple-element.32.refs_0_) | copy-start | bytes 3145732
  140.1 33.1 %collective-permute-start.10 = (bf16[512,1024]{1,0:T(8,128)(2,1)}, bf16[512,1024]{1,0:T(8,128)(2,1)}, u32[]{:S(2)}, u32[]{:S(2)}) collective-permute-start(bf16[512,1024]{1,0:T(8,128)(2,1)} %get-tuple-element.31), channel_id=1, source_target_pairs={{1,0},{2,1},{3,2},{0,3},{5,4},{6,5},{7,6},{4,7},{9,8},{10,9},{11,1... | collective-permute-start | bytes 3145736 | tf_op jit(solution)/shard_map/ppermute | solution.py:443
  141.6 31.6 %collective-permute-start.11 = (bf16[512,1024]{1,0:T(8,128)(2,1)S(1)}, bf16[512,1024]{1,0:T(8,128)(2,1)}, u32[]{:S(2)}, u32[]{:S(2)}) collective-permute-start(bf16[512,1024]{1,0:T(8,128)(2,1)S(1)} %get-tuple-element.32.refs_0_), channel_id=1, source_target_pairs={{2,0},{3,1},{0,2},{1,3},{6,4},{7,5},{4,6},{5,7},{10,8},{11,9},{8,1... | collective-permute-start | bytes 3145736 | tf_op jit(solution)/shard_map/ppermute | solution.py:443
  143.3 47.3 %collective-permute-start.12 = (bf16[512,1024]{1,0:T(8,128)(2,1)}, bf16[512,1024]{1,0:T(8,128)(2,1)}, u32[]{:S(2)}, u32[]{:S(2)}) collective-permute-start(bf16[512,1024]{1,0:T(8,128)(2,1)} %get-tuple-element.31), channel_id=1, source_target_pairs={{3,0},{0,1},{1,2},{2,3},{7,4},{4,5},{5,6},{6,7},{11,8},{8,9},{9,10... | collective-permute-start | bytes 3145736 | tf_op jit(solution)/shard_map/ppermute | solution.py:443
  172.0 38.8 %collective-permute-start.13 = (bf16[256,2048]{1,0:T(8,128)(2,1)}, bf16[256,2048]{1,0:T(8,128)(2,1)}, u32[]{:S(2)}, u32[]{:S(2)}) collective-permute-start(bf16[256,2048]{1,0:T(8,128)(2,1)} %up.1.hid_ref), channel_id=1, source_target_pairs={{0,1},{1,0},{2,3},{3,2},{4,5},{5,4},{6,7},{7,6},{8,9},{9,8},{10,11... | collective-permute-start | bytes 3145736 | tf_op jit(solution)/shard_map/ppermute | solution.py:475
  195.5 27.0 %all-to-all-start.4 = ((bf16[64,8,512]{2,1,0:T(8,128)(2,1)}), bf16[64,8,512]{2,1,0:T(8,128)(2,1)S(1)}, u32[]{:S(2)}, u32[]{:S(2)}) async-start(bf16[64,8,512]{2,1,0:T(8,128)(2,1)} %bitcast.39), calls=%async_computation.4 | async-start | bytes 1048576 | tf_op jit(solution)/shard_map/all_to_all | solution.py:424
  205.9 40.3 %copy-start.7 = (f32[512,64]{1,0:T(8,128)S(1)}, f32[512,64]{1,0:T(8,128)}, u32[]{:S(2)}) copy-start(f32[512,64]{1,0:T(8,128)} %copy-done.6) | copy-start | bytes 393220
  205.9 40.3 %copy-start.9 = (s32[64,1]{0,1:T(1,128)S(1)}, s32[64,1]{0,1:T(1,128)}, u32[]{:S(2)}) copy-start(s32[64,1]{0,1:T(1,128)} %param.21) | copy-start | bytes 772
  246.2 20.4 %copy-start.2 = (f32[128,2048]{1,0:T(8,128)S(1)}, f32[128,2048]{1,0:T(8,128)}, u32[]{:S(2)}) copy-start(f32[128,2048]{1,0:T(8,128)} %get-tuple-element.28.share_ref) | copy-start | bytes 3145732
Sparse Core Ops, SparseCore 0:
  9.2 105.3 all-gather.1

commit v4 on v3

--- a/solution.py
+++ b/solution.py
@@ -29,6 +29,14 @@
     centred = values - mean
     variance = jnp.mean(centred * centred, -1, keepdims=True)
     return centred * lax.rsqrt(variance + 1e-06)
+
+
+def quotient(values, by):
+    return lax.shift_right_logical(values, by.bit_length() - 1)
+
+
+def remainder(values, by):
+    return values & (by - 1)
 
 
 def smem():
@@ -76,7 +84,7 @@
         ],
         out_specs=pl.BlockSpec((rows, 3 * inner), lambda i: (i, 0)),
         out_shape=jax.ShapeDtypeStruct((tokens, 3 * inner), BF16),
-        compiler_params=params(56),
+        compiler_params=params(60),
         name="qkv",
     )(step, x, modulation, w, gain)
 
@@ -84,8 +92,8 @@
 def attention_kernel(few, head, in_ref, out_ref):
     rows = in_ref.shape[0]
     inner = out_ref.shape[1]
-    row_pos = lax.broadcasted_iota(jnp.int32, (rows, rows), 0) % few
-    col_pos = lax.broadcasted_iota(jnp.int32, (rows, rows), 1) % few
+    row_pos = remainder(lax.broadcasted_iota(jnp.int32, (rows, rows), 0), few)
+    col_pos = remainder(lax.broadcasted_iota(jnp.int32, (rows, rows), 1), few)
     same = row_pos == col_pos
     for h in range(inner // head):
         lo = h * head
@@ -111,7 +119,7 @@
     experts = values.shape[1]
     shape = (experts, experts * per)
     expand = (
-        lax.broadcasted_iota(jnp.int32, shape, 1) // per
+        quotient(lax.broadcasted_iota(jnp.int32, shape, 1), per)
         == lax.broadcasted_iota(jnp.int32, shape, 0)
     ).astype(F32)
     return jnp.dot(values, expand, precision=lax.Precision.HIGHEST, preferred_element_type=F32)
@@ -120,7 +128,7 @@
 def slot_row(picks_f32, counts_f32, first, per):
     wide = spread(picks_f32, 2 * per)
     slot = lax.broadcasted_iota(jnp.int32, wide.shape, 0)
-    wanted = first + lax.broadcasted_iota(jnp.int32, wide.shape, 1) % per
+    wanted = first + remainder(lax.broadcasted_iota(jnp.int32, wide.shape, 1), per)
     mine = slot == wanted
     if counts_f32 is not None:
         limit = spread(counts_f32, 2 * per)
@@ -129,7 +137,7 @@
 
 
 def row_half(shape, per, dim):
-    return (lax.broadcasted_iota(jnp.int32, shape, dim) // per) % 2
+    return remainder(quotient(lax.broadcasted_iota(jnp.int32, shape, dim), per), 2)
 
 
 def ones_where(mask):
@@ -140,7 +148,8 @@
     shape = (2 * count, count)
     row = lax.broadcasted_iota(jnp.int32, shape, 0)
     col = lax.broadcasted_iota(jnp.int32, shape, 1)
-    return ones_where(row == (col // per * 2 + half) * per + col % per)
+    wanted = (quotient(col, per) * 2 + half) * per + remainder(col, per)
+    return ones_where(row == wanted)
 
 
 def mix_kernel(
@@ -182,9 +191,8 @@
     gate = gate_ref[pl.ds(step, 1), :]
     shift = shift_ref[pl.ds(step, 1), :]
     scale = scale_ref[pl.ds(step, 1), :]
-    mixed = dot(att_ref[0], w_ref[:inner, :])
-    for part in range(1, parts):
-        mixed += dot(att_ref[part], w_ref[part * inner : (part + 1) * inner, :])
+    every = jnp.concatenate([att_ref[part] for part in range(parts)], axis=1)
+    mixed = dot(every, w_ref[...])
     hidden = x_ref[...].astype(F32) + gate * mixed
     hidden_ref[...] = hidden
     normed = (layer_norm(hidden) * (1.0 + scale) + shift).astype(BF16)
@@ -250,7 +258,7 @@
             pltpu.VMEM((parts * inner, width), BF16),
             pltpu.SemaphoreType.DMA((len(blocks) * parts,)),
         ],
-        compiler_params=params(48),
+        compiler_params=params(60),
         name="mix",
     )(
         rank, core, lane, step, att, x, modulation, modulation, modulation, router_t, picks_t,
@@ -283,7 +291,7 @@
         out_specs=pl.BlockSpec((count, units), lambda i: (0, i)),
         out_shape=jax.ShapeDtypeStruct((count, parts * units), BF16),
         scratch_shapes=[pltpu.VMEM((count, width), BF16)],
-        compiler_params=params(56),
+        compiler_params=params(60),
         name="up",
     )(rows, w)
 
@@ -321,7 +329,7 @@
         + [pl.BlockSpec((few, cols), lambda i: (0, i))] * len(blocks),
         out_specs=pl.BlockSpec((2 * rows, cols), lambda i: (0, 0)),
         out_shape=jax.ShapeDtypeStruct((2 * rows, cols), BF16),
-        compiler_params=params(56),
+        compiler_params=params(60),
         name="down",
     )(rank, hidden, *blocks)
 
@@ -334,7 +342,7 @@
     counts = counts_ref[...].astype(F32)
     shape = (experts, 2 * experts * per)
     expand = ones_where(
-        lax.broadcasted_iota(jnp.int32, shape, 1) // (2 * per)
+        quotient(lax.broadcasted_iota(jnp.int32, shape, 1), 2 * per)
         == lax.broadcasted_iota(jnp.int32, shape, 0)
     )
     wide = dot(gates_ref[...].astype(BF16), expand)
@@ -462,7 +470,9 @@
     out_blocks = [out_rows] + [from_lane(out_rows, turn) for turn in range(1, lanes)]
     attended = attention_call(stacked, position_count // seq, head_size)
     attended = over_seq(attended)
-    attended, out_blocks = lax.optimization_barrier((attended, out_blocks))
+    near = (blocks[1], blocks[3])
+    attended, out_blocks, near = lax.optimization_barrier((attended, out_blocks, near))
+    blocks[1], blocks[3] = near
     swap = [(i, i ^ 1) for i in range(seq)]
     out_blocks = out_blocks + [lax.ppermute(b, "seq", swap) for b in out_blocks]
     every = over_ffn(jnp.broadcast_to(attended[None], (ffn,) + attended.shape))

time: 275 us -> 262 us (0.953)
  blocking collectives: 66.8 us -> 42.2 us
  starting transfers between devices: 49 us -> 55.7 us
  waiting for transfers between devices: 94.9 us -> 101 us
    all_to_all x2 -> x1, blocking collectives: 48.2 us -> 23.7 us  [over_seq(): lax.all_to_all(values, 'seq', split_axis=0, concat_axis=0, tiled=True)]
    ppermute x1, waiting for transfers between devices: 4.92 us -> 12.8 us  [on_device(): hidden_other = lax.ppermute(hidden, 'ffn', [(i, i ^ 1) for i in range(ffn)])]
    all_to_all x3 -> x4, starting transfers between devices: 29.8 us -> 37.3 us  [over_seq(): lax.all_to_all(values, 'seq', split_axis=0, concat_axis=0, tiled=True)]
    all_to_all x3 -> x4, waiting for transfers between devices: 34 us -> 32.5 us  [over_seq(): lax.all_to_all(values, 'seq', split_axis=0, concat_axis=0, tiled=True)]
  transfers between devices with their start and end apart: 19 -> 20, of which waited for: 13 -> 13; matrix products, arithmetic and copies ran while one was open for 1% -> 3% of each run, Pallas kernels for 14% -> 14%
where the time goes in v4:
time: 262 us; the launch traced here: 261 us
  waiting for transfers between devices  101 us (39%)
  starting transfers between devices  55.7 us (21%)
  blocking collectives  42.2 us (16%)
  Pallas kernels  40.6 us (15%)
  between operations  14.2 us (5%)
  local copies, waits for them, and re-layouts  6.65 us (3%)
    all_to_all x4, starting transfers between devices, over_seq(): lax.all_to_all(values, 'seq', split_axis=0, concat_axis=0, tiled=True)  37.3 us
    all_to_all x4, waiting for transfers between devices, over_seq(): lax.all_to_all(values, 'seq', split_axis=0, concat_axis=0, tiled=True)  32.5 us
    ppermute x6, waiting for transfers between devices, from_turn(): lax.ppermute(values, 'ffn', [((i + turn) % ffn, i) for i in range(ffn)])  29 us
    all_to_all x1, blocking collectives, over_seq(): lax.all_to_all(values, 'seq', split_axis=0, concat_axis=0, tiled=True)  23.7 us
    all_to_all x1, waiting for transfers between devices, over_ffn(): lax.all_to_all(values, 'ffn', split_axis=0, concat_axis=0, tiled=True)  22.6 us
    all_to_all x1, blocking collectives, over_ffn(): lax.all_to_all(values, 'ffn', split_axis=0, concat_axis=0, tiled=True)  18.6 us
    ppermute x1, waiting for transfers between devices, on_device(): hidden_other = lax.ppermute(hidden, 'ffn', [(i, i ^ 1) for i in range(ffn)])  12.8 us
    pallas_call x1, Pallas kernels, mix_call(): pl.pallas_call(functools.partial(mix_kernel, per, len(blocks) // 2), grid...  12.2 us
  transfers between devices with their start and end apart: 20, of which 13 were waited for; matrix products, arithmetic and copies ran while one was open for 3% of the time, Pallas kernels for 14%

profile of v4, /device:TPU:8, one launch (start us, length us, event | category | flops | bytes accessed | tf_op | source)
XLA Modules:
  0.0 260.5 jit_solution(15072518597740925961)
XLA Ops:
  7.9 6.3 %qkv.1 = bf16[512,768]{1,0:T(8,128)(2,1)} custom-call(s32[1]{0:T(128)S(6)} %copy.15.step_ref, bf16[512,2048]{1,0:T(8,128)(2,1)} %bitcast.33, f32[16,12288]{1,0:T(8,128)} %gate_ref.3, bf16[3,2048,256]{2,1,0:T(8,128)(2,1)} %bitcast.36, f32[2,128]{1,0:T(2,128)} %gain_ref.1), custom_call_target="tpu_custom_call" | custom-call | tf_op jit(solution)/shard_map/qkv/pallas_call | solution.py:75
  14.2 12.1 %all-to-all-start = ((bf16[64,8,768]{2,1,0:T(8,128)(2,1)}), bf16[64,8,768]{2,1,0:T(8,128)(2,1)S(1)}, u32[]{:S(2)}, u32[]{:S(2)}) async-start(bf16[64,8,768]{2,1,0:T(8,128)(2,1)} %bitcast.35), calls=%async_computation | async-start | bytes 1572864 | tf_op jit(solution)/shard_map/all_to_all | solution.py:432
  26.4 2.8 %collective-permute-start = (bf16[32,2048]{1,0:T(8,128)(2,1)S(1)}, bf16[32,2048]{1,0:T(8,128)(2,1)S(1)}, u32[]{:S(2)}, u32[]{:S(2)}) collective-permute-start(bf16[32,2048]{1,0:T(8,128)(2,1)S(1)} %constant_dynamic-slice_fusion), channel_id=1, source_target_pairs={{1,0},{2,1},{3,2},{0,3},{5,4},{6,5},{7,6},{4,7},{9,8},{10,9},{11,1... | collective-permute-start | bytes 393224 | tf_op jit(solution)/shard_map/ppermute | solution.py:451
  30.9 2.7 %dynamic-slice_bitcast_fusion = (bf16[512,1024]{1,0:T(8,128)(2,1)S(1)}, bf16[512,1024]{1,0:T(8,128)(2,1)}) fusion(bf16[1,512,2048]{2,1,0:T(8,128)(2,1)} %param.19, s32[]{:T(128)S(6)} %select_n.17, s32[]{:T(128)S(6)} %select_n.16), kind=kLoop, calls=%fused_computation | loop fusion | bytes 4194312 | tf_op jit(solution)/shard_map/dynamic_slice | solution.py:447
  33.7 2.3 collective-permute-start.6
  36.0 1.5 collective-permute-done
  37.4 2.4 collective-permute-done.1
  39.9 2.7 %collective-permute-done.2 = bf16[32,2048]{1,0:T(8,128)(2,1)S(1)} collective-permute-done((bf16[32,2048]{1,0:T(8,128)(2,1)S(1)}, bf16[32,2048]{1,0:T(8,128)(2,1)S(1)}, u32[]{:S(2)}, u32[]{:S(2)}) %collective-permute-start.2) | collective-permute-done | bytes 131104 | tf_op jit(solution)/shard_map/ppermute | solution.py:451
  42.6 5.7 %all-to-all-done = bf16[64,8,768]{2,1,0:T(8,128)(2,1)S(1)} async-done(((bf16[64,8,768]{2,1,0:T(8,128)(2,1)}), bf16[64,8,768]{2,1,0:T(8,128)(2,1)S(1)}, u32[]{:S(2)}, u32[]{:S(2)}) %all-to-all-start) | async-done | bytes 786464 | tf_op jit(solution)/shard_map/all_to_all | solution.py:432
  51.0 1.6 collective-permute-start.3
  52.6 1.6 collective-permute-start.4
  54.2 1.9 collective-permute-start.5
  56.0 1.8 attention.1
  57.9 7.1 %all-to-all-start.1 = ((bf16[64,8,256]{2,1,0:T(8,128)(2,1)}), bf16[64,8,256]{2,1,0:T(8,128)(2,1)S(1)}, u32[]{:S(2)}, u32[]{:S(2)}) async-start(bf16[64,8,256]{2,1,0:T(8,128)(2,1)} %bitcast.7), calls=%async_computation.1 | async-start | bytes 524288 | tf_op jit(solution)/shard_map/all_to_all | solution.py:432
  64.9 20.6 %collective-permute-done.6.refs_1_ = bf16[512,1024]{1,0:T(8,128)(2,1)} collective-permute-done((bf16[512,1024]{1,0:T(8,128)(2,1)}, bf16[512,1024]{1,0:T(8,128)(2,1)}, u32[]{:S(2)}, u32[]{:S(2)}) %collective-permute-start.6) | collective-permute-done | bytes 1048608 | tf_op jit(solution)/shard_map/ppermute | solution.py:451
  85.5 1.8 collective-permute-done.7.refs_3_
  87.4 1.1 broadcast_in_dim.4
  88.4 4.7 %all-to-all-start.2 = ((bf16[4,512,256]{2,1,0:T(8,128)(2,1)}), bf16[4,512,256]{2,1,0:T(8,128)(2,1)}, u32[]{:S(2)}, u32[]{:S(2)}) async-start(bf16[4,512,256]{2,1,0:T(8,128)(2,1)} %broadcast_in_dim.4), calls=%async_computation.2 | async-start | bytes 2097152 | tf_op jit(solution)/shard_map/all_to_all | solution.py:435
  95.1 1.1 collective-permute-done.9.refs_5_
  97.6 22.6 %all-to-all-done.2.att_ref = bf16[4,512,256]{2,1,0:T(8,128)(2,1)} async-done(((bf16[4,512,256]{2,1,0:T(8,128)(2,1)}), bf16[4,512,256]{2,1,0:T(8,128)(2,1)}, u32[]{:S(2)}, u32[]{:S(2)}) %all-to-all-start.2) | async-done | bytes 1048608 | tf_op jit(solution)/shard_map/all_to_all | solution.py:435
  120.2 12.2 %mix.1 = (bf16[512,1024]{1,0:T(8,128)(2,1)}, f32[512,64]{1,0:T(8,128)}, f32[128,2048]{1,0:T(8,128)}) custom-call(s32[1]{0:T(128)} %bitcast.rank_ref, s32[1]{0:T(128)} %bitcast.1.core_ref, s32[1]{0:T(128)} %bitcast.2.lane_ref, s32[1]{0:T(128)S(6)} %copy.15.step_ref, bf16[4,512,256]{2,1,0:T(8,128)(2,1)} %all-to-all-done.2.att_ref, bf16[512,2048]{1,0:T(8,128)(2,1)} %bitcast.34, ...), custom_call_target="tpu_custom_call" | custom-call | tf_op jit(solution)/shard_map/mix/pallas_call | solution.py:231
  132.5 10.5 %all-to-all-start.3 = ((bf16[64,8,1024]{2,1,0:T(8,128)(2,1)}), bf16[64,8,1024]{2,1,0:T(8,128)(2,1)}, u32[]{:S(2)}, u32[]{:S(2)}) async-start(bf16[64,8,1024]{2,1,0:T(8,128)(2,1)} %bitcast.40), calls=%async_computation.3 | async-start | bytes 2097152 | tf_op jit(solution)/shard_map/all_to_all | solution.py:432
  143.2 26.8 %all-to-all-done.3 = bf16[64,8,1024]{2,1,0:T(8,128)(2,1)} async-done(((bf16[64,8,1024]{2,1,0:T(8,128)(2,1)}), bf16[64,8,1024]{2,1,0:T(8,128)(2,1)}, u32[]{:S(2)}, u32[]{:S(2)}) %all-to-all-start.3) | async-done | bytes 1048608 | tf_op jit(solution)/shard_map/all_to_all | solution.py:432
  170.1 7.6 %up.1.hid_ref = bf16[256,2048]{1,0:T(8,128)(2,1)} custom-call(bf16[512,1024]{1,0:T(8,128)(2,1)} %bitcast.16.rows_ref, bf16[4,2048,512]{2,1,0:T(8,128)(2,1)} %all-gather.2.cloned.1.call-done.w_ref), custom_call_target="tpu_custom_call" | custom-call | tf_op jit(solution)/shard_map/up/pallas_call | solution.py:284
  178.4 4.8 %down.2 = bf16[512,512]{1,0:T(8,128)(2,1)} custom-call(s32[1]{0:T(128)} %bitcast.rank_ref, bf16[256,2048]{1,0:T(8,128)(2,1)} %up.1.hid_ref, bf16[512,1024]{1,0:T(8,128)(2,1)} %copy-done.6, bf16[512,1024]{1,0:T(8,128)(2,1)} %collective-permute-done.6.refs_1_, bf16[512,1024]{1,0:T(8,128)(2,1)} %collective-permute-done.12.refs_2_, ...), custom_call_target="tpu_custom_call" | custom-call | tf_op jit(solution)/shard_map/down/pallas_call | solution.py:325
  183.2 7.6 %all-to-all-start.4 = ((bf16[64,8,512]{2,1,0:T(8,128)(2,1)}), bf16[64,8,512]{2,1,0:T(8,128)(2,1)S(1)}, u32[]{:S(2)}, u32[]{:S(2)}) async-start(bf16[64,8,512]{2,1,0:T(8,128)(2,1)} %bitcast.37), calls=%async_computation.4 | async-start | bytes 1048576 | tf_op jit(solution)/shard_map/all_to_all | solution.py:432
  190.9 12.8 %collective-permute-done.13.hid_ref = bf16[256,2048]{1,0:T(8,128)(2,1)} collective-permute-done((bf16[256,2048]{1,0:T(8,128)(2,1)}, bf16[256,2048]{1,0:T(8,128)(2,1)}, u32[]{:S(2)}, u32[]{:S(2)}) %collective-permute-start.13) | collective-permute-done | bytes 1048608 | tf_op jit(solution)/shard_map/ppermute | solution.py:485
  203.7 4.8 %down.3 = bf16[512,512]{1,0:T(8,128)(2,1)} custom-call(s32[1]{0:T(128)} %bitcast.rank_ref, bf16[256,2048]{1,0:T(8,128)(2,1)} %collective-permute-done.13.hid_ref, bf16[512,1024]{1,0:T(8,128)(2,1)} %copy-done.6, bf16[512,1024]{1,0:T(8,128)(2,1)} %collective-permute-done.6.refs_1_, bf16[512,1024]{1,0:T(8,128)(2,1)} %collective-permute-done.12.refs_2_, ...), custom_call_target="tpu_custom_call" | custom-call | tf_op jit(solution)/shard_map/down/pallas_call | solution.py:325
  208.5 23.7 %all_to_all.71 = bf16[64,8,512]{2,1,0:T(8,128)(2,1)S(1)} all-to-all(bf16[64,8,512]{2,1,0:T(8,128)(2,1)} %bitcast.38), channel_id=1, replica_groups=mesh['seq'=64,'ffn'=4] {'seq'}, dimensions={0} | all-to-all | bytes 1048576 | tf_op jit(solution)/shard_map/all_to_all | solution.py:432
  232.2 1.7 combine.1
  233.9 18.6 %all_to_all.72.parts_ref = bf16[4,128,1024]{2,1,0:T(8,128)(2,1)S(1)} all-to-all(bf16[4,128,1024]{2,1,0:T(8,128)(2,1)S(1)} %bitcast.26), channel_id=1, replica_groups=mesh['seq'=64,'ffn'=4] {'ffn'}, dimensions={0} | all-to-all | bytes 2097152 | tf_op jit(solution)/shard_map/all_to_all | solution.py:435
  252.5 1.2 final.1
  (50 shorter events, 9.5 us)
Async XLA Ops:
  6.5 19.8 %copy-start = (bf16[256,2048]{1,0:T(8,128)(2,1)S(1)}, bf16[256,2048]{1,0:T(8,128)(2,1)}, u32[]{:S(2)}) copy-start(bf16[256,2048]{1,0:T(8,128)(2,1)} %param.16) | copy-start | bytes 3145732
  6.5 163.5 %all-gather.2.cloned.1.call-start = ((), (), s32[]{:S(2)}) async-start(), calls=%async_computation.7 | async-start | bytes 10485760 | tf_op jit(solution)/shard_map/all_gather | solution.py:444
  14.2 34.0 %all-to-all-start = ((bf16[64,8,768]{2,1,0:T(8,128)(2,1)}), bf16[64,8,768]{2,1,0:T(8,128)(2,1)S(1)}, u32[]{:S(2)}, u32[]{:S(2)}) async-start(bf16[64,8,768]{2,1,0:T(8,128)(2,1)} %bitcast.35), calls=%async_computation | async-start | bytes 1572864 | tf_op jit(solution)/shard_map/all_to_all | solution.py:432
  26.4 11.0 %collective-permute-start = (bf16[32,2048]{1,0:T(8,128)(2,1)S(1)}, bf16[32,2048]{1,0:T(8,128)(2,1)S(1)}, u32[]{:S(2)}, u32[]{:S(2)}) collective-permute-start(bf16[32,2048]{1,0:T(8,128)(2,1)S(1)} %constant_dynamic-slice_fusion), channel_id=1, source_target_pairs={{1,0},{2,1},{3,2},{0,3},{5,4},{6,5},{7,6},{4,7},{9,8},{10,9},{11,1... | collective-permute-start | bytes 393224 | tf_op jit(solution)/shard_map/ppermute | solution.py:451
  29.2 10.6 %collective-permute-start.1 = (bf16[32,2048]{1,0:T(8,128)(2,1)S(1)}, bf16[32,2048]{1,0:T(8,128)(2,1)S(1)}, u32[]{:S(2)}, u32[]{:S(2)}) collective-permute-start(bf16[32,2048]{1,0:T(8,128)(2,1)S(1)} %constant_dynamic-slice_fusion), channel_id=1, source_target_pairs={{2,0},{3,1},{0,2},{1,3},{6,4},{7,5},{4,6},{5,7},{10,8},{11,9},{8,1... | collective-permute-start | bytes 393224 | tf_op jit(solution)/shard_map/ppermute | solution.py:451
  30.0 12.5 %collective-permute-start.2 = (bf16[32,2048]{1,0:T(8,128)(2,1)S(1)}, bf16[32,2048]{1,0:T(8,128)(2,1)S(1)}, u32[]{:S(2)}, u32[]{:S(2)}) collective-permute-start(bf16[32,2048]{1,0:T(8,128)(2,1)S(1)} %constant_dynamic-slice_fusion), channel_id=1, source_target_pairs={{3,0},{0,1},{1,2},{2,3},{7,4},{4,5},{5,6},{6,7},{11,8},{8,9},{9,10... | collective-permute-start | bytes 393224 | tf_op jit(solution)/shard_map/ppermute | solution.py:451
  33.7 109.4 %copy-start.6 = (bf16[512,1024]{1,0:T(8,128)(2,1)}, bf16[512,1024]{1,0:T(8,128)(2,1)S(1)}, u32[]{:S(2)}) copy-start(bf16[512,1024]{1,0:T(8,128)(2,1)S(1)} %get-tuple-element.35.refs_0_) | copy-start | bytes 3145732
  33.7 51.9 %collective-permute-start.6 = (bf16[512,1024]{1,0:T(8,128)(2,1)}, bf16[512,1024]{1,0:T(8,128)(2,1)}, u32[]{:S(2)}, u32[]{:S(2)}) collective-permute-start(bf16[512,1024]{1,0:T(8,128)(2,1)} %get-tuple-element.36), channel_id=1, source_target_pairs={{1,0},{2,1},{3,2},{0,3},{5,4},{6,5},{7,6},{4,7},{9,8},{10,9},{11,1... | collective-permute-start | bytes 3145736 | tf_op jit(solution)/shard_map/ppermute | solution.py:451
  36.0 51.3 %collective-permute-start.7 = (bf16[512,1024]{1,0:T(8,128)(2,1)}, bf16[512,1024]{1,0:T(8,128)(2,1)}, u32[]{:S(2)}, u32[]{:S(2)}) collective-permute-start(bf16[512,1024]{1,0:T(8,128)(2,1)} %get-tuple-element.36), channel_id=1, source_target_pairs={{3,0},{0,1},{1,2},{2,3},{7,4},{4,5},{5,6},{6,7},{11,8},{8,9},{9,10... | collective-permute-start | bytes 3145736 | tf_op jit(solution)/shard_map/ppermute | solution.py:451
  37.4 10.8 %copy-start.9 = (bf16[32,2048]{1,0:T(8,128)(2,1)}, bf16[32,2048]{1,0:T(8,128)(2,1)S(1)}, u32[]{:S(2)}) copy-start(bf16[32,2048]{1,0:T(8,128)(2,1)S(1)} %collective-permute-done) | copy-start | bytes 393220
  39.9 8.3 %copy-start.10 = (bf16[32,2048]{1,0:T(8,128)(2,1)}, bf16[32,2048]{1,0:T(8,128)(2,1)S(1)}, u32[]{:S(2)}) copy-start(bf16[32,2048]{1,0:T(8,128)(2,1)S(1)} %collective-permute-done.1) | copy-start | bytes 393220
  42.6 5.7 %copy-start.11 = (bf16[32,2048]{1,0:T(8,128)(2,1)}, bf16[32,2048]{1,0:T(8,128)(2,1)S(1)}, u32[]{:S(2)}) copy-start(bf16[32,2048]{1,0:T(8,128)(2,1)S(1)} %collective-permute-done.2) | copy-start | bytes 393220
  51.0 42.1 %copy-start.7 = (bf16[128,2048]{1,0:T(8,128)(2,1)}, bf16[128,2048]{1,0:T(8,128)(2,1)S(1)}, u32[]{:S(2)}) copy-start(bf16[128,2048]{1,0:T(8,128)(2,1)S(1)} %constant_dynamic-update-slice_fusion.refs_0_) | copy-start | bytes 1572868
  51.0 36.3 %collective-permute-start.3 = (bf16[128,2048]{1,0:T(8,128)(2,1)S(1)}, bf16[128,2048]{1,0:T(8,128)(2,1)}, u32[]{:S(2)}, u32[]{:S(2)}) collective-permute-start(bf16[128,2048]{1,0:T(8,128)(2,1)S(1)} %constant_dynamic-update-slice_fusion.refs_0_), channel_id=1, source_target_pairs={{64,0},{68,4},{72,8},{76,12},{80,16},{84,20},{88,24},{92,28},{96,3... | collective-permute-start | bytes 1572872 | tf_op jit(solution)/shard_map/ppermute | solution.py:468
  52.6 34.7 %collective-permute-start.4 = (bf16[128,2048]{1,0:T(8,128)(2,1)S(1)}, bf16[128,2048]{1,0:T(8,128)(2,1)}, u32[]{:S(2)}, u32[]{:S(2)}) collective-permute-start(bf16[128,2048]{1,0:T(8,128)(2,1)S(1)} %constant_dynamic-update-slice_fusion.refs_0_), channel_id=1, source_target_pairs={{128,0},{132,4},{136,8},{140,12},{144,16},{148,20},{152,24},{156,2... | collective-permute-start | bytes 1572872 | tf_op jit(solution)/shard_map/ppermute | solution.py:468
  54.2 33.2 %collective-permute-start.5 = (bf16[128,2048]{1,0:T(8,128)(2,1)S(1)}, bf16[128,2048]{1,0:T(8,128)(2,1)}, u32[]{:S(2)}, u32[]{:S(2)}) collective-permute-start(bf16[128,2048]{1,0:T(8,128)(2,1)S(1)} %constant_dynamic-update-slice_fusion.refs_0_), channel_id=1, source_target_pairs={{192,0},{196,4},{200,8},{204,12},{208,16},{212,20},{216,24},{220,2... | collective-permute-start | bytes 1572872 | tf_op jit(solution)/shard_map/ppermute | solution.py:468
  57.9 29.5 %all-to-all-start.1 = ((bf16[64,8,256]{2,1,0:T(8,128)(2,1)}), bf16[64,8,256]{2,1,0:T(8,128)(2,1)S(1)}, u32[]{:S(2)}, u32[]{:S(2)}) async-start(bf16[64,8,256]{2,1,0:T(8,128)(2,1)} %bitcast.7), calls=%async_computation.1 | async-start | bytes 524288 | tf_op jit(solution)/shard_map/all_to_all | solution.py:432
  88.4 31.8 %all-to-all-start.2 = ((bf16[4,512,256]{2,1,0:T(8,128)(2,1)}), bf16[4,512,256]{2,1,0:T(8,128)(2,1)}, u32[]{:S(2)}, u32[]{:S(2)}) async-start(bf16[4,512,256]{2,1,0:T(8,128)(2,1)} %broadcast_in_dim.4), calls=%async_computation.2 | async-start | bytes 2097152 | tf_op jit(solution)/shard_map/all_to_all | solution.py:435
  93.1 1.9 collective-permute-start.8
  93.1 3.0 %collective-permute-start.9 = (bf16[128,2048]{1,0:T(8,128)(2,1)}, bf16[128,2048]{1,0:T(8,128)(2,1)}, u32[]{:S(2)}, u32[]{:S(2)}) collective-permute-start(bf16[128,2048]{1,0:T(8,128)(2,1)} %collective-permute-done.3.refs_1_), channel_id=1, source_target_pairs={{0,4},{4,0},{8,12},{12,8},{16,20},{20,16},{24,28},{28,24},{32,36},... | collective-permute-start | bytes 1572872 | tf_op jit(solution)/shard_map/ppermute | solution.py:477
  93.7 3.2 %collective-permute-start.10 = (bf16[128,2048]{1,0:T(8,128)(2,1)}, bf16[128,2048]{1,0:T(8,128)(2,1)}, u32[]{:S(2)}, u32[]{:S(2)}) collective-permute-start(bf16[128,2048]{1,0:T(8,128)(2,1)} %collective-permute-done.4.refs_2_), channel_id=1, source_target_pairs={{0,4},{4,0},{8,12},{12,8},{16,20},{20,16},{24,28},{28,24},{32,36},... | collective-permute-start | bytes 1572872 | tf_op jit(solution)/shard_map/ppermute | solution.py:477
  93.7 3.9 %collective-permute-start.11 = (bf16[128,2048]{1,0:T(8,128)(2,1)}, bf16[128,2048]{1,0:T(8,128)(2,1)}, u32[]{:S(2)}, u32[]{:S(2)}) collective-permute-start(bf16[128,2048]{1,0:T(8,128)(2,1)} %collective-permute-done.5.refs_3_), channel_id=1, source_target_pairs={{0,4},{4,0},{8,12},{12,8},{16,20},{20,16},{24,28},{28,24},{32,36},... | collective-permute-start | bytes 1572872 | tf_op jit(solution)/shard_map/ppermute | solution.py:477
  95.1 25.2 %copy-start.8 = (bf16[128,2048]{1,0:T(8,128)(2,1)}, bf16[128,2048]{1,0:T(8,128)(2,1)S(1)}, u32[]{:S(2)}) copy-start(bf16[128,2048]{1,0:T(8,128)(2,1)S(1)} %collective-permute-done.8.refs_4_) | copy-start | bytes 1572868
  132.5 37.6 %all-to-all-start.3 = ((bf16[64,8,1024]{2,1,0:T(8,128)(2,1)}), bf16[64,8,1024]{2,1,0:T(8,128)(2,1)}, u32[]{:S(2)}, u32[]{:S(2)}) async-start(bf16[64,8,1024]{2,1,0:T(8,128)(2,1)} %bitcast.40), calls=%async_computation.3 | async-start | bytes 2097152 | tf_op jit(solution)/shard_map/all_to_all | solution.py:432
  143.0 35.3 %collective-permute-start.12 = (bf16[512,1024]{1,0:T(8,128)(2,1)S(1)}, bf16[512,1024]{1,0:T(8,128)(2,1)}, u32[]{:S(2)}, u32[]{:S(2)}) collective-permute-start(bf16[512,1024]{1,0:T(8,128)(2,1)S(1)} %get-tuple-element.35.refs_0_), channel_id=1, source_target_pairs={{2,0},{3,1},{0,2},{1,3},{6,4},{7,5},{4,6},{5,7},{10,8},{11,9},{8,1... | collective-permute-start | bytes 3145736 | tf_op jit(solution)/shard_map/ppermute | solution.py:451
  177.7 26.0 %collective-permute-start.13 = (bf16[256,2048]{1,0:T(8,128)(2,1)}, bf16[256,2048]{1,0:T(8,128)(2,1)}, u32[]{:S(2)}, u32[]{:S(2)}) collective-permute-start(bf16[256,2048]{1,0:T(8,128)(2,1)} %up.1.hid_ref), channel_id=1, source_target_pairs={{0,1},{1,0},{2,3},{3,2},{4,5},{5,4},{6,7},{7,6},{8,9},{9,8},{10,11... | collective-permute-start | bytes 3145736 | tf_op jit(solution)/shard_map/ppermute | solution.py:485
  183.2 25.3 %all-to-all-start.4 = ((bf16[64,8,512]{2,1,0:T(8,128)(2,1)}), bf16[64,8,512]{2,1,0:T(8,128)(2,1)S(1)}, u32[]{:S(2)}, u32[]{:S(2)}) async-start(bf16[64,8,512]{2,1,0:T(8,128)(2,1)} %bitcast.37), calls=%async_computation.4 | async-start | bytes 1048576 | tf_op jit(solution)/shard_map/all_to_all | solution.py:432
  190.8 41.4 %copy-start.3 = (f32[512,64]{1,0:T(8,128)S(1)}, f32[512,64]{1,0:T(8,128)}, u32[]{:S(2)}) copy-start(f32[512,64]{1,0:T(8,128)} %get-tuple-element.31.gates_ref) | copy-start | bytes 393220
  190.8 41.3 %copy-start.4 = (s32[64,1,16]{0,2,1:T(8,128)S(1)}, s32[64,1,16]{0,2,1:T(8,128)}, u32[]{:S(2)}) copy-start(s32[64,1,16]{0,2,1:T(8,128)} %param.20) | copy-start | bytes 12292
  190.9 41.3 %copy-start.5 = (s32[64,1]{0,1:T(1,128)S(1)}, s32[64,1]{0,1:T(1,128)}, u32[]{:S(2)}) copy-start(s32[64,1]{0,1:T(1,128)} %param.21) | copy-start | bytes 772
  232.2 20.3 %copy-start.1 = (f32[16,12288]{1,0:T(8,128)S(1)}, f32[16,12288]{1,0:T(8,128)}, u32[]{:S(2)}) copy-start(f32[16,12288]{1,0:T(8,128)} %gate_ref.3) | copy-start | bytes 2359300
  232.2 20.3 %copy-start.2 = (f32[128,2048]{1,0:T(8,128)S(1)}, f32[128,2048]{1,0:T(8,128)}, u32[]{:S(2)}) copy-start(f32[128,2048]{1,0:T(8,128)} %get-tuple-element.30.share_ref) | copy-start | bytes 3145732
Sparse Core Ops, SparseCore 0:
  9.2 127.8 all-gather.1

commit v5 on v4

--- a/solution.py
+++ b/solution.py
@@ -89,7 +89,7 @@
     )(step, x, modulation, w, gain)
 
 
-def attention_kernel(few, head, in_ref, out_ref):
+def attention_kernel(few, head, copies, in_ref, out_ref):
     rows = in_ref.shape[0]
     inner = out_ref.shape[1]
     row_pos = remainder(lax.broadcasted_iota(jnp.int32, (rows, rows), 0), few)
@@ -102,14 +102,16 @@
         v = in_ref[:, 2 * inner + lo : 2 * inner + lo + head]
         raised = jnp.where(same, jnp.exp(dot_t(q, k) * head ** (-0.5)), 0.0)
         probs = (raised / jnp.sum(raised, -1, keepdims=True)).astype(BF16)
-        out_ref[:, lo : lo + head] = dot(probs, v).astype(BF16)
-
-
-def attention_call(stacked, few, head):
+        each = dot(probs, v).reshape(rows // few, 1, few, head)
+        each = jnp.broadcast_to(each, (rows // few, copies, few, head))
+        out_ref[:, lo : lo + head] = each.reshape(copies * rows, head).astype(BF16)
+
+
+def attention_call(stacked, few, head, copies):
     rows, wide = stacked.shape
     return pl.pallas_call(
-        functools.partial(attention_kernel, few, head),
-        out_shape=jax.ShapeDtypeStruct((rows, wide // 3), BF16),
+        functools.partial(attention_kernel, few, head, copies),
+        out_shape=jax.ShapeDtypeStruct((copies * rows, wide // 3), BF16),
         compiler_params=params(16),
         name="attention",
     )(stacked)
@@ -153,7 +155,7 @@
 
 
 def mix_kernel(
-    per, pieces, rank_ref, core_ref, lane_ref, step_ref, att_ref, x_ref, gate_ref, shift_ref,
+    per, pieces, parts, few, rank_ref, core_ref, lane_ref, step_ref, att_ref, x_ref, gate_ref, shift_ref,
     scale_ref, router_ref, picks_ref, *refs
 ):
     blocks = refs[: 2 * pieces]
@@ -162,8 +164,7 @@
     rank = rank_ref[0]
     tile = pl.program_id(0)
     rows = x_ref.shape[0]
-    parts = att_ref.shape[0]
-    inner = att_ref.shape[2]
+    inner = att_ref.shape[1]
 
     @pl.when(tile == 0)
     def _():
@@ -191,7 +192,10 @@
     gate = gate_ref[pl.ds(step, 1), :]
     shift = shift_ref[pl.ds(step, 1), :]
     scale = scale_ref[pl.ds(step, 1), :]
-    every = jnp.concatenate([att_ref[part] for part in range(parts)], axis=1)
+    split = att_ref[...].astype(F32).reshape(rows // few, parts, few, inner)
+    every = jnp.concatenate(
+        [split[:, part].reshape(rows, inner).astype(BF16) for part in range(parts)], axis=1
+    )
     mixed = dot(every, w_ref[...])
     hidden = x_ref[...].astype(F32) + gate * mixed
     hidden_ref[...] = hidden
@@ -221,19 +225,20 @@
 
 
 def mix_call(
-    rank, core, lane, step, att, blocks, x, modulation, router_t, picks_t, per, share
+    rank, core, lane, step, att, blocks, x, modulation, router_t, picks_t, per, share, few
 ):
     tokens, width = x.shape
-    parts, _, inner = att.shape
+    parts = att.shape[0] // tokens
+    inner = att.shape[1]
     experts = router_t.shape[0]
     steps = modulation.shape[0]
     rows = 256
     return pl.pallas_call(
-        functools.partial(mix_kernel, per, len(blocks) // 2),
+        functools.partial(mix_kernel, per, len(blocks) // 2, parts, few),
         grid=(tokens // rows,),
         in_specs=[smem()] * 4
         + [
-            pl.BlockSpec((parts, rows, inner), lambda i: (0, i, 0)),
+            pl.BlockSpec((parts * rows, inner), lambda i: (i, 0)),
             pl.BlockSpec((rows, width), lambda i: (i, 0)),
             pl.BlockSpec((steps, width), lambda i: (0, 2)),
             pl.BlockSpec((steps, width), lambda i: (0, 3)),
@@ -460,7 +465,9 @@
 
     stacked = qkv_call(step_index, x, modulation, jnp.transpose(qkv_weight, (1, 0, 2)), qk_gain)
     stacked = over_seq(stacked)
-    stacked, out_rows = lax.optimization_barrier((stacked, out_rows))
+    few = position_count // seq
+    attended = attention_call(stacked, few, head_size, ffn)
+    attended, out_rows = lax.optimization_barrier((attended, out_rows))
     out_rows = jnp.concatenate(out_rows, axis=0)
 
     def from_lane(values, turn):
@@ -468,18 +475,16 @@
         return lax.ppermute(values, "seq", pairs)
 
     out_blocks = [out_rows] + [from_lane(out_rows, turn) for turn in range(1, lanes)]
-    attended = attention_call(stacked, position_count // seq, head_size)
-    attended = over_seq(attended)
-    near = (blocks[1], blocks[3])
-    attended, out_blocks, near = lax.optimization_barrier((attended, out_blocks, near))
-    blocks[1], blocks[3] = near
     swap = [(i, i ^ 1) for i in range(seq)]
     out_blocks = out_blocks + [lax.ppermute(b, "seq", swap) for b in out_blocks]
-    every = over_ffn(jnp.broadcast_to(attended[None], (ffn,) + attended.shape))
+    every = lax.all_to_all(attended, ("seq", "ffn"), split_axis=0, concat_axis=0, tiled=True)
     outgoing, gates, share = mix_call(
         rank_arr, core.reshape(1), lane.reshape(1), step_index, every, out_blocks, x, modulation,
-        jnp.transpose(router_weight, (1, 0)), picks_t, per, share_len,
+        jnp.transpose(router_weight, (1, 0)), picks_t, per, share_len, few,
     )
+    near = (blocks[1], blocks[3])
+    outgoing, near = lax.optimization_barrier((outgoing, near))
+    blocks[1], blocks[3] = near
     expert_tokens = over_seq(outgoing)
     hidden = up_call(expert_tokens, up_full, per)
     hidden_other = lax.ppermute(hidden, "ffn", [(i, i ^ 1) for i in range(ffn)])

time: 262 us -> 266 us (1.015)
  waiting for transfers between devices: 101 us -> 104 us
    ppermute x3, waiting for transfers between devices: 0.01 us -> 23.8 us  [from_lane(): return lax.ppermute(values, 'seq', pairs)]
    all_to_all x1, waiting for transfers between devices: 22.6 us -> 0.01 us  [on_device(): lax.all_to_all(attended, ('seq', 'ffn'), split_axis=0, concat_axis=0, til...]
    all_to_all x4 -> x3, waiting for transfers between devices: 32.5 us -> 43.4 us  [over_seq(): lax.all_to_all(values, 'seq', split_axis=0, concat_axis=0, tiled=True)]
    ppermute x6, waiting for transfers between devices: 29 us -> 20.9 us  [from_turn(): lax.ppermute(values, 'ffn', [((i + turn) % ffn, i) for i in range(ffn)])]
    all_to_all x4 -> x3, starting transfers between devices: 37.3 us -> 31 us  [over_seq(): lax.all_to_all(values, 'seq', split_axis=0, concat_axis=0, tiled=True)]
    all_to_all x1, starting transfers between devices: 4.69 us -> 10.8 us  [on_device(): lax.all_to_all(attended, ('seq', 'ffn'), split_axis=0, concat_axis=0, til...]
  transfers between devices with their start and end apart: 20 -> 19, of which waited for: 13 -> 9; matrix products, arithmetic and copies ran while one was open for 3% -> 2% of each run, Pallas kernels for 14% -> 14%
where the time goes in v5:
time: 266 us; the launch traced here: 265 us
  waiting for transfers between devices  104 us (39%)
  starting transfers between devices  56.5 us (21%)
  blocking collectives  42.2 us (16%)
  Pallas kernels  41 us (15%)
  between operations  14.2 us (5%)
  local copies, waits for them, and re-layouts  7.24 us (3%)
    all_to_all x3, waiting for transfers between devices, over_seq(): lax.all_to_all(values, 'seq', split_axis=0, concat_axis=0, tiled=True)  43.4 us
    all_to_all x3, starting transfers between devices, over_seq(): lax.all_to_all(values, 'seq', split_axis=0, concat_axis=0, tiled=True)  31 us
    ppermute x3, waiting for transfers between devices, from_lane(): return lax.ppermute(values, 'seq', pairs)  23.8 us
    all_to_all x1, blocking collectives, over_seq(): lax.all_to_all(values, 'seq', split_axis=0, concat_axis=0, tiled=True)  23.7 us
    ppermute x6, waiting for transfers between devices, from_turn(): lax.ppermute(values, 'ffn', [((i + turn) % ffn, i) for i in range(ffn)])  20.9 us
    all_to_all x1, blocking collectives, over_ffn(): lax.all_to_all(values, 'ffn', split_axis=0, concat_axis=0, tiled=True)  18.6 us
    ppermute x1, waiting for transfers between devices, on_device(): hidden_other = lax.ppermute(hidden, 'ffn', [(i, i ^ 1) for i in range(ffn)])  13.4 us
    pallas_call x1, Pallas kernels, mix_call(): pl.pallas_call(functools.partial(mix_kernel, per, len(blocks) // 2, parts...  12.3 us
  transfers between devices with their start and end apart: 19, of which 9 were waited for; matrix products, arithmetic and copies ran while one was open for 2% of the time, Pallas kernels for 14%

profile of v5, /device:TPU:8, one launch (start us, length us, event | category | flops | bytes accessed | tf_op | source)
XLA Modules:
  0.0 264.8 jit_solution(6308017693307289037)
XLA Ops:
  7.9 6.3 %qkv.1 = bf16[512,768]{1,0:T(8,128)(2,1)} custom-call(s32[1]{0:T(128)S(6)} %copy.15.step_ref, bf16[512,2048]{1,0:T(8,128)(2,1)} %bitcast.33, f32[16,12288]{1,0:T(8,128)} %gate_ref.3, bf16[3,2048,256]{2,1,0:T(8,128)(2,1)} %bitcast.36, f32[2,128]{1,0:T(2,128)} %gain_ref.1), custom_call_target="tpu_custom_call" | custom-call | tf_op jit(solution)/shard_map/qkv/pallas_call | solution.py:75
  14.2 12.1 %all-to-all-start = ((bf16[64,8,768]{2,1,0:T(8,128)(2,1)}), bf16[64,8,768]{2,1,0:T(8,128)(2,1)S(1)}, u32[]{:S(2)}, u32[]{:S(2)}) async-start(bf16[64,8,768]{2,1,0:T(8,128)(2,1)} %bitcast.35), calls=%async_computation | async-start | bytes 1572864 | tf_op jit(solution)/shard_map/all_to_all | solution.py:437
  26.4 2.8 %collective-permute-start = (bf16[32,2048]{1,0:T(8,128)(2,1)S(1)}, bf16[32,2048]{1,0:T(8,128)(2,1)S(1)}, u32[]{:S(2)}, u32[]{:S(2)}) collective-permute-start(bf16[32,2048]{1,0:T(8,128)(2,1)S(1)} %constant_dynamic-slice_fusion), channel_id=1, source_target_pairs={{1,0},{2,1},{3,2},{0,3},{5,4},{6,5},{7,6},{4,7},{9,8},{10,9},{11,1... | collective-permute-start | bytes 393224 | tf_op jit(solution)/shard_map/ppermute | solution.py:456
  30.0 0.9 collective-permute-start.2
  30.9 17.3 %all-to-all-done = bf16[64,8,768]{2,1,0:T(8,128)(2,1)S(1)} async-done(((bf16[64,8,768]{2,1,0:T(8,128)(2,1)}), bf16[64,8,768]{2,1,0:T(8,128)(2,1)S(1)}, u32[]{:S(2)}, u32[]{:S(2)}) %all-to-all-start) | async-done | bytes 786464 | tf_op jit(solution)/shard_map/all_to_all | solution.py:437
  48.2 2.1 attention.1
  50.3 10.8 %all-to-all-start.1 = ((bf16[256,8,256]{2,1,0:T(8,128)(2,1)}), bf16[256,8,256]{2,1,0:T(8,128)(2,1)}, u32[]{:S(2)}, u32[]{:S(2)}) async-start(bf16[256,8,256]{2,1,0:T(8,128)(2,1)} %bitcast.7), calls=%async_computation.1 | async-start | bytes 2097152 | tf_op jit(solution)/shard_map/all_to_all | solution.py:480
  63.8 2.2 collective-permute-start.3
  66.7 1.8 collective-permute-start.5
  68.5 2.7 %dynamic-slice_bitcast_fusion = (bf16[512,1024]{1,0:T(8,128)(2,1)S(1)}, bf16[512,1024]{1,0:T(8,128)(2,1)}) fusion(bf16[1,512,2048]{2,1,0:T(8,128)(2,1)} %param.19, s32[]{:T(128)S(6)} %select_n.17, s32[]{:T(128)S(6)} %select_n.16), kind=kLoop, calls=%fused_computation | loop fusion | bytes 4194312 | tf_op jit(solution)/shard_map/dynamic_slice | solution.py:452
  71.3 2.7 %collective-permute-start.10 = (bf16[512,1024]{1,0:T(8,128)(2,1)}, bf16[512,1024]{1,0:T(8,128)(2,1)S(1)}, u32[]{:S(2)}, u32[]{:S(2)}) collective-permute-start(bf16[512,1024]{1,0:T(8,128)(2,1)} %get-tuple-element.28), channel_id=1, source_target_pairs={{1,0},{2,1},{3,2},{0,3},{5,4},{6,5},{7,6},{4,7},{9,8},{10,9},{11,1... | collective-permute-start | bytes 3145736 | tf_op jit(solution)/shard_map/ppermute | solution.py:456
  74.0 12.4 %collective-permute-done.3.refs_1_ = bf16[128,2048]{1,0:T(8,128)(2,1)} collective-permute-done((bf16[128,2048]{1,0:T(8,128)(2,1)}, bf16[128,2048]{1,0:T(8,128)(2,1)}, u32[]{:S(2)}, u32[]{:S(2)}) %collective-permute-start.3) | collective-permute-done | bytes 524320 | tf_op jit(solution)/shard_map/ppermute | solution.py:475
  86.4 1.3 collective-permute-start.11
  87.7 11.4 %collective-permute-done.4.refs_2_ = bf16[128,2048]{1,0:T(8,128)(2,1)S(1)} collective-permute-done((bf16[128,2048]{1,0:T(8,128)(2,1)}, bf16[128,2048]{1,0:T(8,128)(2,1)S(1)}, u32[]{:S(2)}, u32[]{:S(2)}) %collective-permute-start.4) | collective-permute-done | bytes 524320 | tf_op jit(solution)/shard_map/ppermute | solution.py:475
  99.1 0.8 copy-done.8
  100.4 0.8 collective-permute-done.7.refs_5_
  102.0 0.8 copy-done.12
  102.8 12.3 %mix.1 = (bf16[512,1024]{1,0:T(8,128)(2,1)}, f32[512,64]{1,0:T(8,128)}, f32[128,2048]{1,0:T(8,128)}) custom-call(s32[1]{0:T(128)} %bitcast.rank_ref, s32[1]{0:T(128)} %bitcast.1.core_ref, s32[1]{0:T(128)} %bitcast.2.lane_ref, s32[1]{0:T(128)S(6)} %copy.15.step_ref, bf16[2048,256]{1,0:T(8,128)(2,1)} %bitcast.8.att_ref, bf16[512,2048]{1,0:T(8,128)(2,1)} %bitcast.34, ...), custom_call_target="tpu_custom_call" | custom-call | tf_op jit(solution)/shard_map/mix/pallas_call | solution.py:236
  115.2 9.5 %collective-permute-done.10.refs_1_ = bf16[512,1024]{1,0:T(8,128)(2,1)S(1)} collective-permute-done((bf16[512,1024]{1,0:T(8,128)(2,1)}, bf16[512,1024]{1,0:T(8,128)(2,1)S(1)}, u32[]{:S(2)}, u32[]{:S(2)}) %collective-permute-start.10) | collective-permute-done | bytes 1048608 | tf_op jit(solution)/shard_map/ppermute | solution.py:456
  124.7 11.4 %collective-permute-done.11.refs_3_ = bf16[512,1024]{1,0:T(8,128)(2,1)} collective-permute-done((bf16[512,1024]{1,0:T(8,128)(2,1)}, bf16[512,1024]{1,0:T(8,128)(2,1)}, u32[]{:S(2)}, u32[]{:S(2)}) %collective-permute-start.11) | collective-permute-done | bytes 1048608 | tf_op jit(solution)/shard_map/ppermute | solution.py:456
  136.0 11.2 %all-to-all-start.2 = ((bf16[64,8,1024]{2,1,0:T(8,128)(2,1)}), bf16[64,8,1024]{2,1,0:T(8,128)(2,1)}, u32[]{:S(2)}, u32[]{:S(2)}) async-start(bf16[64,8,1024]{2,1,0:T(8,128)(2,1)} %bitcast.39), calls=%async_computation.2 | async-start | bytes 2097152 | tf_op jit(solution)/shard_map/all_to_all | solution.py:437
  147.3 0.9 collective-permute-start.12
  148.2 26.1 %all-to-all-done.2 = bf16[64,8,1024]{2,1,0:T(8,128)(2,1)} async-done(((bf16[64,8,1024]{2,1,0:T(8,128)(2,1)}), bf16[64,8,1024]{2,1,0:T(8,128)(2,1)}, u32[]{:S(2)}, u32[]{:S(2)}) %all-to-all-start.2) | async-done | bytes 1048608 | tf_op jit(solution)/shard_map/all_to_all | solution.py:437
  174.3 7.7 %up.1.hid_ref = bf16[256,2048]{1,0:T(8,128)(2,1)} custom-call(bf16[512,1024]{1,0:T(8,128)(2,1)} %bitcast.16.rows_ref, bf16[4,2048,512]{2,1,0:T(8,128)(2,1)} %all-gather.2.cloned.1.call-done.w_ref), custom_call_target="tpu_custom_call" | custom-call | tf_op jit(solution)/shard_map/up/pallas_call | solution.py:289
  182.0 4.9 %down.2 = bf16[512,512]{1,0:T(8,128)(2,1)} custom-call(s32[1]{0:T(128)} %bitcast.rank_ref, bf16[256,2048]{1,0:T(8,128)(2,1)} %up.1.hid_ref, bf16[512,1024]{1,0:T(8,128)(2,1)} %copy-done.6, bf16[512,1024]{1,0:T(8,128)(2,1)} %copy-done.7, bf16[512,1024]{1,0:T(8,128)(2,1)} %collective-permute-done.12.refs_2_, bf16[512,1024]{1,0:T(8,128)(2,1)} %collective-permute-done.11.refs_3_), custom_call_target="tpu_custom_call" | custom-call | tf_op jit(solution)/shard_map/down/pallas_call | solution.py:330
  186.9 7.6 %all-to-all-start.3 = ((bf16[64,8,512]{2,1,0:T(8,128)(2,1)}), bf16[64,8,512]{2,1,0:T(8,128)(2,1)S(1)}, u32[]{:S(2)}, u32[]{:S(2)}) async-start(bf16[64,8,512]{2,1,0:T(8,128)(2,1)} %bitcast.37), calls=%async_computation.3 | async-start | bytes 1048576 | tf_op jit(solution)/shard_map/all_to_all | solution.py:437
  194.5 13.4 %collective-permute-done.13.hid_ref = bf16[256,2048]{1,0:T(8,128)(2,1)} collective-permute-done((bf16[256,2048]{1,0:T(8,128)(2,1)}, bf16[256,2048]{1,0:T(8,128)(2,1)}, u32[]{:S(2)}, u32[]{:S(2)}) %collective-permute-start.13) | collective-permute-done | bytes 1048608 | tf_op jit(solution)/shard_map/ppermute | solution.py:490
  208.0 4.8 %down.3 = bf16[512,512]{1,0:T(8,128)(2,1)} custom-call(s32[1]{0:T(128)} %bitcast.rank_ref, bf16[256,2048]{1,0:T(8,128)(2,1)} %collective-permute-done.13.hid_ref, bf16[512,1024]{1,0:T(8,128)(2,1)} %copy-done.6, bf16[512,1024]{1,0:T(8,128)(2,1)} %copy-done.7, bf16[512,1024]{1,0:T(8,128)(2,1)} %collective-permute-done.12.refs_2_, ...), custom_call_target="tpu_custom_call" | custom-call | tf_op jit(solution)/shard_map/down/pallas_call | solution.py:330
  212.8 23.7 %all_to_all.64 = bf16[64,8,512]{2,1,0:T(8,128)(2,1)S(1)} all-to-all(bf16[64,8,512]{2,1,0:T(8,128)(2,1)} %bitcast.38), channel_id=1, replica_groups=mesh['seq'=64,'ffn'=4] {'seq'}, dimensions={0} | all-to-all | bytes 1048576 | tf_op jit(solution)/shard_map/all_to_all | solution.py:437
  236.5 1.7 combine.1
  238.2 18.6 %all_to_all.65.parts_ref = bf16[4,128,1024]{2,1,0:T(8,128)(2,1)S(1)} all-to-all(bf16[4,128,1024]{2,1,0:T(8,128)(2,1)S(1)} %bitcast.26), channel_id=1, replica_groups=mesh['seq'=64,'ffn'=4] {'ffn'}, dimensions={0} | all-to-all | bytes 2097152 | tf_op jit(solution)/shard_map/all_to_all | solution.py:440
  256.8 1.2 final.1
  (49 shorter events, 6.2 us)
Async XLA Ops:
  6.5 19.8 %copy-start = (bf16[256,2048]{1,0:T(8,128)(2,1)S(1)}, bf16[256,2048]{1,0:T(8,128)(2,1)}, u32[]{:S(2)}) copy-start(bf16[256,2048]{1,0:T(8,128)(2,1)} %param.16) | copy-start | bytes 3145732
  6.5 167.8 %all-gather.2.cloned.1.call-start = ((), (), s32[]{:S(2)}) async-start(), calls=%async_computation.6 | async-start | bytes 10485760 | tf_op jit(solution)/shard_map/all_gather | solution.py:449
  14.2 34.0 %all-to-all-start = ((bf16[64,8,768]{2,1,0:T(8,128)(2,1)}), bf16[64,8,768]{2,1,0:T(8,128)(2,1)S(1)}, u32[]{:S(2)}, u32[]{:S(2)}) async-start(bf16[64,8,768]{2,1,0:T(8,128)(2,1)} %bitcast.35), calls=%async_computation | async-start | bytes 1572864 | tf_op jit(solution)/shard_map/all_to_all | solution.py:437
  26.4 23.9 %collective-permute-start = (bf16[32,2048]{1,0:T(8,128)(2,1)S(1)}, bf16[32,2048]{1,0:T(8,128)(2,1)S(1)}, u32[]{:S(2)}, u32[]{:S(2)}) collective-permute-start(bf16[32,2048]{1,0:T(8,128)(2,1)S(1)} %constant_dynamic-slice_fusion), channel_id=1, source_target_pairs={{1,0},{2,1},{3,2},{0,3},{5,4},{6,5},{7,6},{4,7},{9,8},{10,9},{11,1... | collective-permute-start | bytes 393224 | tf_op jit(solution)/shard_map/ppermute | solution.py:456
  29.2 21.1 %collective-permute-start.1 = (bf16[32,2048]{1,0:T(8,128)(2,1)S(1)}, bf16[32,2048]{1,0:T(8,128)(2,1)S(1)}, u32[]{:S(2)}, u32[]{:S(2)}) collective-permute-start(bf16[32,2048]{1,0:T(8,128)(2,1)S(1)} %constant_dynamic-slice_fusion), channel_id=1, source_target_pairs={{2,0},{3,1},{0,2},{1,3},{6,4},{7,5},{4,6},{5,7},{10,8},{11,9},{8,1... | collective-permute-start | bytes 393224 | tf_op jit(solution)/shard_map/ppermute | solution.py:456
  30.0 20.3 %collective-permute-start.2 = (bf16[32,2048]{1,0:T(8,128)(2,1)S(1)}, bf16[32,2048]{1,0:T(8,128)(2,1)S(1)}, u32[]{:S(2)}, u32[]{:S(2)}) collective-permute-start(bf16[32,2048]{1,0:T(8,128)(2,1)S(1)} %constant_dynamic-slice_fusion), channel_id=1, source_target_pairs={{3,0},{0,1},{1,2},{2,3},{7,4},{4,5},{5,6},{6,7},{11,8},{8,9},{9,10... | collective-permute-start | bytes 393224 | tf_op jit(solution)/shard_map/ppermute | solution.py:456
  50.3 52.5 %all-to-all-start.1 = ((bf16[256,8,256]{2,1,0:T(8,128)(2,1)}), bf16[256,8,256]{2,1,0:T(8,128)(2,1)}, u32[]{:S(2)}, u32[]{:S(2)}) async-start(bf16[256,8,256]{2,1,0:T(8,128)(2,1)} %bitcast.7), calls=%async_computation.1 | async-start | bytes 2097152 | tf_op jit(solution)/shard_map/all_to_all | solution.py:480
  63.8 22.6 %collective-permute-start.3 = (bf16[128,2048]{1,0:T(8,128)(2,1)}, bf16[128,2048]{1,0:T(8,128)(2,1)}, u32[]{:S(2)}, u32[]{:S(2)}) collective-permute-start(bf16[128,2048]{1,0:T(8,128)(2,1)} %constant_dynamic-update-slice_fusion.refs_0_), channel_id=1, source_target_pairs={{64,0},{68,4},{72,8},{76,12},{80,16},{84,20},{88,24},{92,28},{96,3... | collective-permute-start | bytes 1572872 | tf_op jit(solution)/shard_map/ppermute | solution.py:475
  66.0 33.1 %collective-permute-start.4 = (bf16[128,2048]{1,0:T(8,128)(2,1)}, bf16[128,2048]{1,0:T(8,128)(2,1)S(1)}, u32[]{:S(2)}, u32[]{:S(2)}) collective-permute-start(bf16[128,2048]{1,0:T(8,128)(2,1)} %constant_dynamic-update-slice_fusion.refs_0_), channel_id=1, source_target_pairs={{128,0},{132,4},{136,8},{140,12},{144,16},{148,20},{152,24},{156,2... | collective-permute-start | bytes 1572872 | tf_op jit(solution)/shard_map/ppermute | solution.py:475
  66.7 32.4 %collective-permute-start.5 = (bf16[128,2048]{1,0:T(8,128)(2,1)}, bf16[128,2048]{1,0:T(8,128)(2,1)S(1)}, u32[]{:S(2)}, u32[]{:S(2)}) collective-permute-start(bf16[128,2048]{1,0:T(8,128)(2,1)} %constant_dynamic-update-slice_fusion.refs_0_), channel_id=1, source_target_pairs={{192,0},{196,4},{200,8},{204,12},{208,16},{212,20},{216,24},{220,2... | collective-permute-start | bytes 1572872 | tf_op jit(solution)/shard_map/ppermute | solution.py:475
  68.5 31.4 %collective-permute-start.6 = (bf16[128,2048]{1,0:T(8,128)(2,1)}, bf16[128,2048]{1,0:T(8,128)(2,1)S(1)}, u32[]{:S(2)}, u32[]{:S(2)}) collective-permute-start(bf16[128,2048]{1,0:T(8,128)(2,1)} %constant_dynamic-update-slice_fusion.refs_0_), channel_id=1, source_target_pairs={{0,4},{4,0},{8,12},{12,8},{16,20},{20,16},{24,28},{28,24},{32,36},... | collective-permute-start | bytes 1572872 | tf_op jit(solution)/shard_map/ppermute | solution.py:479
  71.3 76.0 %copy-start.6 = (bf16[512,1024]{1,0:T(8,128)(2,1)}, bf16[512,1024]{1,0:T(8,128)(2,1)S(1)}, u32[]{:S(2)}) copy-start(bf16[512,1024]{1,0:T(8,128)(2,1)S(1)} %get-tuple-element.27.refs_0_) | copy-start | bytes 3145732
  71.3 53.4 %collective-permute-start.10 = (bf16[512,1024]{1,0:T(8,128)(2,1)}, bf16[512,1024]{1,0:T(8,128)(2,1)S(1)}, u32[]{:S(2)}, u32[]{:S(2)}) collective-permute-start(bf16[512,1024]{1,0:T(8,128)(2,1)} %get-tuple-element.28), channel_id=1, source_target_pairs={{1,0},{2,1},{3,2},{0,3},{5,4},{6,5},{7,6},{4,7},{9,8},{10,9},{11,1... | collective-permute-start | bytes 3145736 | tf_op jit(solution)/shard_map/ppermute | solution.py:456
  86.4 49.6 %collective-permute-start.11 = (bf16[512,1024]{1,0:T(8,128)(2,1)}, bf16[512,1024]{1,0:T(8,128)(2,1)}, u32[]{:S(2)}, u32[]{:S(2)}) collective-permute-start(bf16[512,1024]{1,0:T(8,128)(2,1)} %get-tuple-element.28), channel_id=1, source_target_pairs={{3,0},{0,1},{1,2},{2,3},{7,4},{4,5},{5,6},{6,7},{11,8},{8,9},{9,10... | collective-permute-start | bytes 3145736 | tf_op jit(solution)/shard_map/ppermute | solution.py:456
  99.1 0.8 copy-start.8
  99.1 2.1 collective-permute-start.7
  99.9 1.9 copy-start.9
  99.9 1.9 collective-permute-start.8
  99.9 1.9 copy-start.10
  99.9 2.9 %collective-permute-start.9 = (bf16[128,2048]{1,0:T(8,128)(2,1)S(1)}, bf16[128,2048]{1,0:T(8,128)(2,1)}, u32[]{:S(2)}, u32[]{:S(2)}) collective-permute-start(bf16[128,2048]{1,0:T(8,128)(2,1)S(1)} %collective-permute-done.5.refs_3_), channel_id=1, source_target_pairs={{0,4},{4,0},{8,12},{12,8},{16,20},{20,16},{24,28},{28,24},{32,36},... | collective-permute-start | bytes 1572872 | tf_op jit(solution)/shard_map/ppermute | solution.py:479
  101.2 0.8 copy-start.11
  102.0 0.8 copy-start.12
  124.7 57.3 %copy-start.7 = (bf16[512,1024]{1,0:T(8,128)(2,1)}, bf16[512,1024]{1,0:T(8,128)(2,1)S(1)}, u32[]{:S(2)}) copy-start(bf16[512,1024]{1,0:T(8,128)(2,1)S(1)} %collective-permute-done.10.refs_1_) | copy-start | bytes 3145732
  136.0 38.3 %all-to-all-start.2 = ((bf16[64,8,1024]{2,1,0:T(8,128)(2,1)}), bf16[64,8,1024]{2,1,0:T(8,128)(2,1)}, u32[]{:S(2)}, u32[]{:S(2)}) async-start(bf16[64,8,1024]{2,1,0:T(8,128)(2,1)} %bitcast.39), calls=%async_computation.2 | async-start | bytes 2097152 | tf_op jit(solution)/shard_map/all_to_all | solution.py:437
  147.3 34.7 %collective-permute-start.12 = (bf16[512,1024]{1,0:T(8,128)(2,1)S(1)}, bf16[512,1024]{1,0:T(8,128)(2,1)}, u32[]{:S(2)}, u32[]{:S(2)}) collective-permute-start(bf16[512,1024]{1,0:T(8,128)(2,1)S(1)} %get-tuple-element.27.refs_0_), channel_id=1, source_target_pairs={{2,0},{3,1},{0,2},{1,3},{6,4},{7,5},{4,6},{5,7},{10,8},{11,9},{8,1... | collective-permute-start | bytes 3145736 | tf_op jit(solution)/shard_map/ppermute | solution.py:456
  182.0 26.0 %collective-permute-start.13 = (bf16[256,2048]{1,0:T(8,128)(2,1)}, bf16[256,2048]{1,0:T(8,128)(2,1)}, u32[]{:S(2)}, u32[]{:S(2)}) collective-permute-start(bf16[256,2048]{1,0:T(8,128)(2,1)} %up.1.hid_ref), channel_id=1, source_target_pairs={{0,1},{1,0},{2,3},{3,2},{4,5},{5,4},{6,7},{7,6},{8,9},{9,8},{10,11... | collective-permute-start | bytes 3145736 | tf_op jit(solution)/shard_map/ppermute | solution.py:490
  186.9 25.9 %all-to-all-start.3 = ((bf16[64,8,512]{2,1,0:T(8,128)(2,1)}), bf16[64,8,512]{2,1,0:T(8,128)(2,1)S(1)}, u32[]{:S(2)}, u32[]{:S(2)}) async-start(bf16[64,8,512]{2,1,0:T(8,128)(2,1)} %bitcast.37), calls=%async_computation.3 | async-start | bytes 1048576 | tf_op jit(solution)/shard_map/all_to_all | solution.py:437
  194.5 42.0 %copy-start.3 = (f32[512,64]{1,0:T(8,128)S(1)}, f32[512,64]{1,0:T(8,128)}, u32[]{:S(2)}) copy-start(f32[512,64]{1,0:T(8,128)} %get-tuple-element.22.gates_ref) | copy-start | bytes 393220
  194.5 42.0 %copy-start.4 = (s32[64,1,16]{0,2,1:T(8,128)S(1)}, s32[64,1,16]{0,2,1:T(8,128)}, u32[]{:S(2)}) copy-start(s32[64,1,16]{0,2,1:T(8,128)} %param.20) | copy-start | bytes 12292
  194.5 42.0 %copy-start.5 = (s32[64,1]{0,1:T(1,128)S(1)}, s32[64,1]{0,1:T(1,128)}, u32[]{:S(2)}) copy-start(s32[64,1]{0,1:T(1,128)} %param.21) | copy-start | bytes 772
  236.5 20.3 %copy-start.1 = (f32[16,12288]{1,0:T(8,128)S(1)}, f32[16,12288]{1,0:T(8,128)}, u32[]{:S(2)}) copy-start(f32[16,12288]{1,0:T(8,128)} %gate_ref.3) | copy-start | bytes 2359300
  236.5 20.3 %copy-start.2 = (f32[128,2048]{1,0:T(8,128)S(1)}, f32[128,2048]{1,0:T(8,128)}, u32[]{:S(2)}) copy-start(f32[128,2048]{1,0:T(8,128)} %get-tuple-element.21.share_ref) | copy-start | bytes 3145732
Sparse Core Ops, SparseCore 0:
  9.2 127.8 all-gather.1

commit v6 on v5

--- a/solution.py
+++ b/solution.py
@@ -464,10 +464,10 @@
     ]
 
     stacked = qkv_call(step_index, x, modulation, jnp.transpose(qkv_weight, (1, 0, 2)), qk_gain)
+    stacked, out_rows = lax.optimization_barrier((stacked, out_rows))
     stacked = over_seq(stacked)
     few = position_count // seq
     attended = attention_call(stacked, few, head_size, ffn)
-    attended, out_rows = lax.optimization_barrier((attended, out_rows))
     out_rows = jnp.concatenate(out_rows, axis=0)
 
     def from_lane(values, turn):
@@ -475,6 +475,7 @@
         return lax.ppermute(values, "seq", pairs)
 
     out_blocks = [out_rows] + [from_lane(out_rows, turn) for turn in range(1, lanes)]
+    attended, out_blocks = lax.optimization_barrier((attended, out_blocks))
     swap = [(i, i ^ 1) for i in range(seq)]
     out_blocks = out_blocks + [lax.ppermute(b, "seq", swap) for b in out_blocks]
     every = lax.all_to_all(attended, ("seq", "ffn"), split_axis=0, concat_axis=0, tiled=True)
@@ -482,9 +483,7 @@
         rank_arr, core.reshape(1), lane.reshape(1), step_index, every, out_blocks, x, modulation,
         jnp.transpose(router_weight, (1, 0)), picks_t, per, share_len, few,
     )
-    near = (blocks[1], blocks[3])
-    outgoing, near = lax.optimization_barrier((outgoing, near))
-    blocks[1], blocks[3] = near
+    outgoing, blocks[1] = lax.optimization_barrier((outgoing, blocks[1]))
     expert_tokens = over_seq(outgoing)
     hidden = up_call(expert_tokens, up_full, per)
     hidden_other = lax.ppermute(hidden, "ffn", [(i, i ^ 1) for i in range(ffn)])

time: 266 us -> 276 us (1.038)
  waiting for transfers between devices: 104 us -> 110 us
  starting transfers between devices: 56.5 us -> 62 us
    all_to_all x1, waiting for transfers between devices: 0.01 us -> 18.8 us  [on_device(): lax.all_to_all(attended, ('seq', 'ffn'), split_axis=0, concat_axis=0, til...]
    ppermute x3, waiting for transfers between devices: 23.8 us -> 10.7 us  [from_lane(): return lax.ppermute(values, 'seq', pairs)]
    ppermute x1, waiting for transfers between devices: 13.4 us -> 6.02 us  [on_device(): hidden_other = lax.ppermute(hidden, 'ffn', [(i, i ^ 1) for i in range(ffn)])]
    ppermute x6, waiting for transfers between devices: 20.9 us -> 25.2 us  [from_turn(): lax.ppermute(values, 'ffn', [((i + turn) % ffn, i) for i in range(ffn)])]
    all_to_all x3, waiting for transfers between devices: 43.4 us -> 46.9 us  [over_seq(): lax.all_to_all(values, 'seq', split_axis=0, concat_axis=0, tiled=True)]
  transfers between devices with their start and end apart: 19 -> 19, of which waited for: 9 -> 12; matrix products, arithmetic and copies ran while one was open for 2% -> 1% of each run, Pallas kernels for 14% -> 14%
where the time goes in v6:
time: 276 us; the launch traced here: 275 us
  waiting for transfers between devices  110 us (40%)
  starting transfers between devices  62 us (22%)
  blocking collectives  42.6 us (15%)
  Pallas kernels  40.8 us (15%)
  between operations  14.3 us (5%)
  local copies, waits for them, and re-layouts  5.76 us (2%)
    all_to_all x3, waiting for transfers between devices, over_seq(): lax.all_to_all(values, 'seq', split_axis=0, concat_axis=0, tiled=True)  46.9 us
    all_to_all x3, starting transfers between devices, over_seq(): lax.all_to_all(values, 'seq', split_axis=0, concat_axis=0, tiled=True)  33.2 us
    ppermute x6, waiting for transfers between devices, from_turn(): lax.ppermute(values, 'ffn', [((i + turn) % ffn, i) for i in range(ffn)])  25.2 us
    all_to_all x1, blocking collectives, over_seq(): lax.all_to_all(values, 'seq', split_axis=0, concat_axis=0, tiled=True)  23.6 us
    all_to_all x1, blocking collectives, over_ffn(): lax.all_to_all(values, 'ffn', split_axis=0, concat_axis=0, tiled=True)  19 us
    all_to_all x1, waiting for transfers between devices, on_device(): lax.all_to_all(attended, ('seq', 'ffn'), split_axis=0, concat_axis=0, til...  18.8 us
    pallas_call x1, Pallas kernels, mix_call(): pl.pallas_call(functools.partial(mix_kernel, per, len(blocks) // 2, parts...  12.2 us
    all_to_all x1, starting transfers between devices, on_device(): lax.all_to_all(attended, ('seq', 'ffn'), split_axis=0, concat_axis=0, til...  11.3 us
  transfers between devices with their start and end apart: 19, of which 12 were waited for; matrix products, arithmetic and copies ran while one was open for 1% of the time, Pallas kernels for 14%

profile of v6, /device:TPU:8, one launch (start us, length us, event | category | flops | bytes accessed | tf_op | source)
XLA Modules:
  0.0 275.4 jit_solution(14374564081206120809)
XLA Ops:
  7.8 2.8 %collective-permute-start = (bf16[32,2048]{1,0:T(8,128)(2,1)S(1)}, bf16[32,2048]{1,0:T(8,128)(2,1)S(1)}, u32[]{:S(2)}, u32[]{:S(2)}) collective-permute-start(bf16[32,2048]{1,0:T(8,128)(2,1)S(1)} %constant_dynamic-slice_fusion), channel_id=1, source_target_pairs={{1,0},{2,1},{3,2},{0,3},{5,4},{6,5},{7,6},{4,7},{9,8},{10,9},{11,1... | collective-permute-start | bytes 393224 | tf_op jit(solution)/shard_map/ppermute | solution.py:456
  11.4 0.9 collective-permute-start.2
  12.9 6.3 %qkv.1 = bf16[512,768]{1,0:T(8,128)(2,1)} custom-call(s32[1]{0:T(128)S(6)} %copy.15.step_ref, bf16[512,2048]{1,0:T(8,128)(2,1)} %bitcast.33, f32[16,12288]{1,0:T(8,128)} %gate_ref.3, bf16[3,2048,256]{2,1,0:T(8,128)(2,1)} %bitcast.36, f32[2,128]{1,0:T(2,128)} %gain_ref.1), custom_call_target="tpu_custom_call" | custom-call | tf_op jit(solution)/shard_map/qkv/pallas_call | solution.py:75
  19.9 12.1 %all-to-all-start = ((bf16[64,8,768]{2,1,0:T(8,128)(2,1)}), bf16[64,8,768]{2,1,0:T(8,128)(2,1)S(1)}, u32[]{:S(2)}, u32[]{:S(2)}) async-start(bf16[64,8,768]{2,1,0:T(8,128)(2,1)} %bitcast.35), calls=%async_computation | async-start | bytes 1572864 | tf_op jit(solution)/shard_map/all_to_all | solution.py:437
  32.6 2.6 collective-permute-start.4
  35.2 1.9 collective-permute-start.5
  37.1 16.8 %all-to-all-done = bf16[64,8,768]{2,1,0:T(8,128)(2,1)S(1)} async-done(((bf16[64,8,768]{2,1,0:T(8,128)(2,1)}), bf16[64,8,768]{2,1,0:T(8,128)(2,1)S(1)}, u32[]{:S(2)}, u32[]{:S(2)}) %all-to-all-start) | async-done | bytes 786464 | tf_op jit(solution)/shard_map/all_to_all | solution.py:437
  53.9 2.1 attention.1
  56.0 10.1 %collective-permute-done.4.refs_2_ = bf16[128,2048]{1,0:T(8,128)(2,1)S(1)} collective-permute-done((bf16[128,2048]{1,0:T(8,128)(2,1)S(1)}, bf16[128,2048]{1,0:T(8,128)(2,1)S(1)}, u32[]{:S(2)}, u32[]{:S(2)}) %collective-permute-start.4) | collective-permute-done | bytes 524320 | tf_op jit(solution)/shard_map/ppermute | solution.py:475
  66.7 11.3 %all-to-all-start.1 = ((bf16[256,8,256]{2,1,0:T(8,128)(2,1)}), bf16[256,8,256]{2,1,0:T(8,128)(2,1)}, u32[]{:S(2)}, u32[]{:S(2)}) async-start(bf16[256,8,256]{2,1,0:T(8,128)(2,1)} %bitcast.7), calls=%async_computation.1 | async-start | bytes 2097152 | tf_op jit(solution)/shard_map/all_to_all | solution.py:481
  78.0 2.8 dynamic-slice_bitcast_fusion
  80.8 2.7 collective-permute-start.10
  84.6 1.6 collective-permute-done.6.refs_4_
  87.0 0.8 copy-done.13
  88.7 18.8 %all-to-all-done.1 = bf16[256,8,256]{2,1,0:T(8,128)(2,1)} async-done(((bf16[256,8,256]{2,1,0:T(8,128)(2,1)}), bf16[256,8,256]{2,1,0:T(8,128)(2,1)}, u32[]{:S(2)}, u32[]{:S(2)}) %all-to-all-start.1) | async-done | bytes 1048608 | tf_op jit(solution)/shard_map/all_to_all | solution.py:481
  107.5 12.2 %mix.1 = (bf16[512,1024]{1,0:T(8,128)(2,1)}, f32[512,64]{1,0:T(8,128)}, f32[128,2048]{1,0:T(8,128)}) custom-call(s32[1]{0:T(128)} %bitcast.rank_ref, s32[1]{0:T(128)} %bitcast.1.core_ref, s32[1]{0:T(128)} %bitcast.2.lane_ref, s32[1]{0:T(128)S(6)} %copy.15.step_ref, bf16[2048,256]{1,0:T(8,128)(2,1)} %bitcast.8.att_ref, bf16[512,2048]{1,0:T(8,128)(2,1)} %bitcast.34, ...), custom_call_target="tpu_custom_call" | custom-call | tf_op jit(solution)/shard_map/mix/pallas_call | solution.py:236
  119.7 11.3 %collective-permute-done.10.refs_1_ = bf16[512,1024]{1,0:T(8,128)(2,1)S(1)} collective-permute-done((bf16[512,1024]{1,0:T(8,128)(2,1)}, bf16[512,1024]{1,0:T(8,128)(2,1)S(1)}, u32[]{:S(2)}, u32[]{:S(2)}) %collective-permute-start.10) | collective-permute-done | bytes 1048608 | tf_op jit(solution)/shard_map/ppermute | solution.py:456
  131.1 10.8 %all-to-all-start.2 = ((bf16[64,8,1024]{2,1,0:T(8,128)(2,1)}), bf16[64,8,1024]{2,1,0:T(8,128)(2,1)}, u32[]{:S(2)}, u32[]{:S(2)}) async-start(bf16[64,8,1024]{2,1,0:T(8,128)(2,1)} %bitcast.39), calls=%async_computation.2 | async-start | bytes 2097152 | tf_op jit(solution)/shard_map/all_to_all | solution.py:437
  141.8 2.8 %collective-permute-start.11 = (bf16[512,1024]{1,0:T(8,128)(2,1)S(1)}, bf16[512,1024]{1,0:T(8,128)(2,1)}, u32[]{:S(2)}, u32[]{:S(2)}) collective-permute-start(bf16[512,1024]{1,0:T(8,128)(2,1)S(1)} %get-tuple-element.35.refs_0_), channel_id=1, source_target_pairs={{2,0},{3,1},{0,2},{1,3},{6,4},{7,5},{4,6},{5,7},{10,8},{11,9},{8,1... | collective-permute-start | bytes 3145736 | tf_op jit(solution)/shard_map/ppermute | solution.py:456
  144.6 24.3 %all-to-all-done.2 = bf16[64,8,1024]{2,1,0:T(8,128)(2,1)} async-done(((bf16[64,8,1024]{2,1,0:T(8,128)(2,1)}), bf16[64,8,1024]{2,1,0:T(8,128)(2,1)}, u32[]{:S(2)}, u32[]{:S(2)}) %all-to-all-start.2) | async-done | bytes 1048608 | tf_op jit(solution)/shard_map/all_to_all | solution.py:437
  168.9 7.6 %up.1.hid_ref = bf16[256,2048]{1,0:T(8,128)(2,1)} custom-call(bf16[512,1024]{1,0:T(8,128)(2,1)} %bitcast.16.rows_ref, bf16[4,2048,512]{2,1,0:T(8,128)(2,1)} %all-gather.2.cloned.1.call-done.w_ref), custom_call_target="tpu_custom_call" | custom-call | tf_op jit(solution)/shard_map/up/pallas_call | solution.py:289
  176.5 1.5 collective-permute-start.13
  178.0 13.2 %collective-permute-done.12.refs_3_ = bf16[512,1024]{1,0:T(8,128)(2,1)} collective-permute-done((bf16[512,1024]{1,0:T(8,128)(2,1)}, bf16[512,1024]{1,0:T(8,128)(2,1)}, u32[]{:S(2)}, u32[]{:S(2)}) %collective-permute-start.12) | collective-permute-done | bytes 1048608 | tf_op jit(solution)/shard_map/ppermute | solution.py:456
  191.2 4.8 %down.2 = bf16[512,512]{1,0:T(8,128)(2,1)} custom-call(s32[1]{0:T(128)} %bitcast.rank_ref, bf16[256,2048]{1,0:T(8,128)(2,1)} %up.1.hid_ref, bf16[512,1024]{1,0:T(8,128)(2,1)} %copy-done.6, bf16[512,1024]{1,0:T(8,128)(2,1)} %copy-done.7, bf16[512,1024]{1,0:T(8,128)(2,1)} %collective-permute-done.11.refs_2_, bf16[512,1024]{1,0:T(8,128)(2,1)} %collective-permute-done.12.refs_3_), custom_call_target="tpu_custom_call" | custom-call | tf_op jit(solution)/shard_map/down/pallas_call | solution.py:330
  196.1 10.3 %all-to-all-start.3 = ((bf16[64,8,512]{2,1,0:T(8,128)(2,1)}), bf16[64,8,512]{2,1,0:T(8,128)(2,1)S(1)}, u32[]{:S(2)}, u32[]{:S(2)}) async-start(bf16[64,8,512]{2,1,0:T(8,128)(2,1)} %bitcast.37), calls=%async_computation.3 | async-start | bytes 1048576 | tf_op jit(solution)/shard_map/all_to_all | solution.py:437
  206.4 6.0 %collective-permute-done.13.hid_ref = bf16[256,2048]{1,0:T(8,128)(2,1)} collective-permute-done((bf16[256,2048]{1,0:T(8,128)(2,1)}, bf16[256,2048]{1,0:T(8,128)(2,1)}, u32[]{:S(2)}, u32[]{:S(2)}) %collective-permute-start.13) | collective-permute-done | bytes 1048608 | tf_op jit(solution)/shard_map/ppermute | solution.py:489
  212.4 4.8 %down.3 = bf16[512,512]{1,0:T(8,128)(2,1)} custom-call(s32[1]{0:T(128)} %bitcast.rank_ref, bf16[256,2048]{1,0:T(8,128)(2,1)} %collective-permute-done.13.hid_ref, bf16[512,1024]{1,0:T(8,128)(2,1)} %copy-done.6, bf16[512,1024]{1,0:T(8,128)(2,1)} %copy-done.7, bf16[512,1024]{1,0:T(8,128)(2,1)} %collective-permute-done.11.refs_2_, ...), custom_call_target="tpu_custom_call" | custom-call | tf_op jit(solution)/shard_map/down/pallas_call | solution.py:330
  217.3 5.8 %all-to-all-done.3 = bf16[64,8,512]{2,1,0:T(8,128)(2,1)S(1)} async-done(((bf16[64,8,512]{2,1,0:T(8,128)(2,1)}), bf16[64,8,512]{2,1,0:T(8,128)(2,1)S(1)}, u32[]{:S(2)}, u32[]{:S(2)}) %all-to-all-start.3) | async-done | bytes 524320 | tf_op jit(solution)/shard_map/all_to_all | solution.py:437
  223.1 23.6 %all_to_all.64 = bf16[64,8,512]{2,1,0:T(8,128)(2,1)S(1)} all-to-all(bf16[64,8,512]{2,1,0:T(8,128)(2,1)} %bitcast.38), channel_id=1, replica_groups=mesh['seq'=64,'ffn'=4] {'seq'}, dimensions={0} | all-to-all | bytes 1048576 | tf_op jit(solution)/shard_map/all_to_all | solution.py:437
  246.7 1.7 combine.1
  248.4 19.0 %all_to_all.65.parts_ref = bf16[4,128,1024]{2,1,0:T(8,128)(2,1)S(1)} all-to-all(bf16[4,128,1024]{2,1,0:T(8,128)(2,1)S(1)} %bitcast.26), channel_id=1, replica_groups=mesh['seq'=64,'ffn'=4] {'ffn'}, dimensions={0} | all-to-all | bytes 2097152 | tf_op jit(solution)/shard_map/all_to_all | solution.py:440
  267.4 1.2 final.1
  (53 shorter events, 6.6 us)
Async XLA Ops:
  6.5 1.2 copy-start
  6.5 162.3 %all-gather.2.cloned.1.call-start = ((), (), s32[]{:S(2)}) async-start(), calls=%async_computation.6 | async-start | bytes 10485760 | tf_op jit(solution)/shard_map/all_gather | solution.py:449
  7.8 11.5 %collective-permute-start = (bf16[32,2048]{1,0:T(8,128)(2,1)S(1)}, bf16[32,2048]{1,0:T(8,128)(2,1)S(1)}, u32[]{:S(2)}, u32[]{:S(2)}) collective-permute-start(bf16[32,2048]{1,0:T(8,128)(2,1)S(1)} %constant_dynamic-slice_fusion), channel_id=1, source_target_pairs={{1,0},{2,1},{3,2},{0,3},{5,4},{6,5},{7,6},{4,7},{9,8},{10,9},{11,1... | collective-permute-start | bytes 393224 | tf_op jit(solution)/shard_map/ppermute | solution.py:456
  10.6 8.7 %collective-permute-start.1 = (bf16[32,2048]{1,0:T(8,128)(2,1)S(1)}, bf16[32,2048]{1,0:T(8,128)(2,1)S(1)}, u32[]{:S(2)}, u32[]{:S(2)}) collective-permute-start(bf16[32,2048]{1,0:T(8,128)(2,1)S(1)} %constant_dynamic-slice_fusion), channel_id=1, source_target_pairs={{2,0},{3,1},{0,2},{1,3},{6,4},{7,5},{4,6},{5,7},{10,8},{11,9},{8,1... | collective-permute-start | bytes 393224 | tf_op jit(solution)/shard_map/ppermute | solution.py:456
  11.4 8.5 %collective-permute-start.2 = (bf16[32,2048]{1,0:T(8,128)(2,1)S(1)}, bf16[32,2048]{1,0:T(8,128)(2,1)S(1)}, u32[]{:S(2)}, u32[]{:S(2)}) collective-permute-start(bf16[32,2048]{1,0:T(8,128)(2,1)S(1)} %constant_dynamic-slice_fusion), channel_id=1, source_target_pairs={{3,0},{0,1},{1,2},{2,3},{7,4},{4,5},{5,6},{6,7},{11,8},{8,9},{9,10... | collective-permute-start | bytes 393224 | tf_op jit(solution)/shard_map/ppermute | solution.py:456
  19.9 34.0 %all-to-all-start = ((bf16[64,8,768]{2,1,0:T(8,128)(2,1)}), bf16[64,8,768]{2,1,0:T(8,128)(2,1)S(1)}, u32[]{:S(2)}, u32[]{:S(2)}) async-start(bf16[64,8,768]{2,1,0:T(8,128)(2,1)} %bitcast.35), calls=%async_computation | async-start | bytes 1572864 | tf_op jit(solution)/shard_map/all_to_all | solution.py:437
  32.1 45.9 %copy-start.8 = (bf16[128,2048]{1,0:T(8,128)(2,1)}, bf16[128,2048]{1,0:T(8,128)(2,1)S(1)}, u32[]{:S(2)}) copy-start(bf16[128,2048]{1,0:T(8,128)(2,1)S(1)} %constant_dynamic-update-slice_fusion.refs_0_) | copy-start | bytes 1572868
  32.1 23.9 %collective-permute-start.3 = (bf16[128,2048]{1,0:T(8,128)(2,1)S(1)}, bf16[128,2048]{1,0:T(8,128)(2,1)S(1)}, u32[]{:S(2)}, u32[]{:S(2)}) collective-permute-start(bf16[128,2048]{1,0:T(8,128)(2,1)S(1)} %constant_dynamic-update-slice_fusion.refs_0_), channel_id=1, source_target_pairs={{64,0},{68,4},{72,8},{76,12},{80,16},{84,20},{88,24},{92,28},{96,3... | collective-permute-start | bytes 1572872 | tf_op jit(solution)/shard_map/ppermute | solution.py:475
  32.6 33.5 %collective-permute-start.4 = (bf16[128,2048]{1,0:T(8,128)(2,1)S(1)}, bf16[128,2048]{1,0:T(8,128)(2,1)S(1)}, u32[]{:S(2)}, u32[]{:S(2)}) collective-permute-start(bf16[128,2048]{1,0:T(8,128)(2,1)S(1)} %constant_dynamic-update-slice_fusion.refs_0_), channel_id=1, source_target_pairs={{128,0},{132,4},{136,8},{140,12},{144,16},{148,20},{152,24},{156,2... | collective-permute-start | bytes 1572872 | tf_op jit(solution)/shard_map/ppermute | solution.py:475
  35.2 31.5 %collective-permute-start.5 = (bf16[128,2048]{1,0:T(8,128)(2,1)S(1)}, bf16[128,2048]{1,0:T(8,128)(2,1)}, u32[]{:S(2)}, u32[]{:S(2)}) collective-permute-start(bf16[128,2048]{1,0:T(8,128)(2,1)S(1)} %constant_dynamic-update-slice_fusion.refs_0_), channel_id=1, source_target_pairs={{192,0},{196,4},{200,8},{204,12},{208,16},{212,20},{216,24},{220,2... | collective-permute-start | bytes 1572872 | tf_op jit(solution)/shard_map/ppermute | solution.py:475
  56.0 24.8 %copy-start.10 = (bf16[128,2048]{1,0:T(8,128)(2,1)}, bf16[128,2048]{1,0:T(8,128)(2,1)S(1)}, u32[]{:S(2)}) copy-start(bf16[128,2048]{1,0:T(8,128)(2,1)S(1)} %collective-permute-done.3.refs_1_) | copy-start | bytes 1572868
  66.1 14.7 %copy-start.11 = (bf16[128,2048]{1,0:T(8,128)(2,1)}, bf16[128,2048]{1,0:T(8,128)(2,1)S(1)}, u32[]{:S(2)}) copy-start(bf16[128,2048]{1,0:T(8,128)(2,1)S(1)} %collective-permute-done.4.refs_2_) | copy-start | bytes 1572868
  66.7 40.9 %all-to-all-start.1 = ((bf16[256,8,256]{2,1,0:T(8,128)(2,1)}), bf16[256,8,256]{2,1,0:T(8,128)(2,1)}, u32[]{:S(2)}, u32[]{:S(2)}) async-start(bf16[256,8,256]{2,1,0:T(8,128)(2,1)} %bitcast.7), calls=%async_computation.1 | async-start | bytes 2097152 | tf_op jit(solution)/shard_map/all_to_all | solution.py:481
  78.0 5.5 %copy-start.9 = (bf16[128,2048]{1,0:T(8,128)(2,1)S(1)}, bf16[128,2048]{1,0:T(8,128)(2,1)}, u32[]{:S(2)}) copy-start(bf16[128,2048]{1,0:T(8,128)(2,1)} %copy-done.8) | copy-start | bytes 1572868
  80.8 61.0 %copy-start.6 = (bf16[512,1024]{1,0:T(8,128)(2,1)}, bf16[512,1024]{1,0:T(8,128)(2,1)S(1)}, u32[]{:S(2)}) copy-start(bf16[512,1024]{1,0:T(8,128)(2,1)S(1)} %get-tuple-element.35.refs_0_) | copy-start | bytes 3145732
  80.8 50.3 %collective-permute-start.10 = (bf16[512,1024]{1,0:T(8,128)(2,1)}, bf16[512,1024]{1,0:T(8,128)(2,1)S(1)}, u32[]{:S(2)}, u32[]{:S(2)}) collective-permute-start(bf16[512,1024]{1,0:T(8,128)(2,1)} %get-tuple-element.36), channel_id=1, source_target_pairs={{1,0},{2,1},{3,2},{0,3},{5,4},{6,5},{7,6},{4,7},{9,8},{10,9},{11,1... | collective-permute-start | bytes 3145736 | tf_op jit(solution)/shard_map/ppermute | solution.py:456
  83.5 2.6 collective-permute-start.6
  83.5 3.4 %collective-permute-start.7 = (bf16[128,2048]{1,0:T(8,128)(2,1)}, bf16[128,2048]{1,0:T(8,128)(2,1)S(1)}, u32[]{:S(2)}, u32[]{:S(2)}) collective-permute-start(bf16[128,2048]{1,0:T(8,128)(2,1)} %copy-done.10), channel_id=1, source_target_pairs={{0,4},{4,0},{8,12},{12,8},{16,20},{20,16},{24,28},{28,24},{32,36},... | collective-permute-start | bytes 1572872 | tf_op jit(solution)/shard_map/ppermute | solution.py:480
  84.1 3.9 %collective-permute-start.8 = (bf16[128,2048]{1,0:T(8,128)(2,1)}, bf16[128,2048]{1,0:T(8,128)(2,1)S(1)}, u32[]{:S(2)}, u32[]{:S(2)}) collective-permute-start(bf16[128,2048]{1,0:T(8,128)(2,1)} %copy-done.11), channel_id=1, source_target_pairs={{0,4},{4,0},{8,12},{12,8},{16,20},{20,16},{24,28},{28,24},{32,36},... | collective-permute-start | bytes 1572872 | tf_op jit(solution)/shard_map/ppermute | solution.py:480
  84.1 4.7 %collective-permute-start.9 = (bf16[128,2048]{1,0:T(8,128)(2,1)}, bf16[128,2048]{1,0:T(8,128)(2,1)}, u32[]{:S(2)}, u32[]{:S(2)}) collective-permute-start(bf16[128,2048]{1,0:T(8,128)(2,1)} %collective-permute-done.5.refs_3_), channel_id=1, source_target_pairs={{0,4},{4,0},{8,12},{12,8},{16,20},{20,16},{24,28},{28,24},{32,36},... | collective-permute-start | bytes 1572872 | tf_op jit(solution)/shard_map/ppermute | solution.py:480
  87.0 0.8 copy-start.13
  131.1 45.4 %copy-start.7 = (bf16[512,1024]{1,0:T(8,128)(2,1)}, bf16[512,1024]{1,0:T(8,128)(2,1)S(1)}, u32[]{:S(2)}) copy-start(bf16[512,1024]{1,0:T(8,128)(2,1)S(1)} %collective-permute-done.10.refs_1_) | copy-start | bytes 3145732
  131.1 37.8 %all-to-all-start.2 = ((bf16[64,8,1024]{2,1,0:T(8,128)(2,1)}), bf16[64,8,1024]{2,1,0:T(8,128)(2,1)}, u32[]{:S(2)}, u32[]{:S(2)}) async-start(bf16[64,8,1024]{2,1,0:T(8,128)(2,1)} %bitcast.39), calls=%async_computation.2 | async-start | bytes 2097152 | tf_op jit(solution)/shard_map/all_to_all | solution.py:437
  141.8 36.1 %collective-permute-start.11 = (bf16[512,1024]{1,0:T(8,128)(2,1)S(1)}, bf16[512,1024]{1,0:T(8,128)(2,1)}, u32[]{:S(2)}, u32[]{:S(2)}) collective-permute-start(bf16[512,1024]{1,0:T(8,128)(2,1)S(1)} %get-tuple-element.35.refs_0_), channel_id=1, source_target_pairs={{2,0},{3,1},{0,2},{1,3},{6,4},{7,5},{4,6},{5,7},{10,8},{11,9},{8,1... | collective-permute-start | bytes 3145736 | tf_op jit(solution)/shard_map/ppermute | solution.py:456
  144.6 46.6 %collective-permute-start.12 = (bf16[512,1024]{1,0:T(8,128)(2,1)}, bf16[512,1024]{1,0:T(8,128)(2,1)}, u32[]{:S(2)}, u32[]{:S(2)}) collective-permute-start(bf16[512,1024]{1,0:T(8,128)(2,1)} %get-tuple-element.36), channel_id=1, source_target_pairs={{3,0},{0,1},{1,2},{2,3},{7,4},{4,5},{5,6},{6,7},{11,8},{8,9},{9,10... | collective-permute-start | bytes 3145736 | tf_op jit(solution)/shard_map/ppermute | solution.py:456
  176.5 35.9 %collective-permute-start.13 = (bf16[256,2048]{1,0:T(8,128)(2,1)}, bf16[256,2048]{1,0:T(8,128)(2,1)}, u32[]{:S(2)}, u32[]{:S(2)}) collective-permute-start(bf16[256,2048]{1,0:T(8,128)(2,1)} %up.1.hid_ref), channel_id=1, source_target_pairs={{0,1},{1,0},{2,3},{3,2},{4,5},{5,4},{6,7},{7,6},{8,9},{9,8},{10,11... | collective-permute-start | bytes 3145736 | tf_op jit(solution)/shard_map/ppermute | solution.py:489
  196.1 27.0 %all-to-all-start.3 = ((bf16[64,8,512]{2,1,0:T(8,128)(2,1)}), bf16[64,8,512]{2,1,0:T(8,128)(2,1)S(1)}, u32[]{:S(2)}, u32[]{:S(2)}) async-start(bf16[64,8,512]{2,1,0:T(8,128)(2,1)} %bitcast.37), calls=%async_computation.3 | async-start | bytes 1048576 | tf_op jit(solution)/shard_map/all_to_all | solution.py:437
  206.4 40.3 %copy-start.3 = (f32[512,64]{1,0:T(8,128)S(1)}, f32[512,64]{1,0:T(8,128)}, u32[]{:S(2)}) copy-start(f32[512,64]{1,0:T(8,128)} %get-tuple-element.31.gates_ref) | copy-start | bytes 393220
  206.4 40.3 %copy-start.4 = (s32[64,1,16]{0,2,1:T(8,128)S(1)}, s32[64,1,16]{0,2,1:T(8,128)}, u32[]{:S(2)}) copy-start(s32[64,1,16]{0,2,1:T(8,128)} %param.20) | copy-start | bytes 12292
  206.4 40.3 %copy-start.5 = (s32[64,1]{0,1:T(1,128)S(1)}, s32[64,1]{0,1:T(1,128)}, u32[]{:S(2)}) copy-start(s32[64,1]{0,1:T(1,128)} %param.21) | copy-start | bytes 772
  246.7 20.7 %copy-start.1 = (f32[16,12288]{1,0:T(8,128)S(1)}, f32[16,12288]{1,0:T(8,128)}, u32[]{:S(2)}) copy-start(f32[16,12288]{1,0:T(8,128)} %gate_ref.3) | copy-start | bytes 2359300
  246.7 20.7 %copy-start.2 = (f32[128,2048]{1,0:T(8,128)S(1)}, f32[128,2048]{1,0:T(8,128)}, u32[]{:S(2)}) copy-start(f32[128,2048]{1,0:T(8,128)} %get-tuple-element.30.share_ref) | copy-start | bytes 3145732
  (2 other events, 1.6 us)
Sparse Core Ops, SparseCore 0:
  9.2 116.1 all-gather.1

commit v7 on v6

--- a/solution.py
+++ b/solution.py
@@ -18,10 +18,6 @@
 
 def dot_t(a, b):
     return lax.dot_general(a, b, (((1,), (1,)), ((), ())), preferred_element_type=F32)
-
-
-def dot_l(a, b):
-    return lax.dot_general(a, b, (((0,), (0,)), ((), ())), preferred_element_type=F32)
 
 
 def layer_norm(values):
@@ -131,11 +127,33 @@
     wide = spread(picks_f32, 2 * per)
     slot = lax.broadcasted_iota(jnp.int32, wide.shape, 0)
     wanted = first + remainder(lax.broadcasted_iota(jnp.int32, wide.shape, 1), per)
-    mine = slot == wanted
-    if counts_f32 is not None:
-        limit = spread(counts_f32, 2 * per)
-        wide = jnp.where(slot.astype(F32) < limit, wide, -1.0)
-    return jnp.sum(jnp.where(mine, wide, 0.0), axis=0, keepdims=True).astype(jnp.int32)
+    limit = spread(counts_f32, 2 * per)
+    wide = jnp.where(slot.astype(F32) < limit, wide, -1.0)
+    return jnp.sum(jnp.where(slot == wanted, wide, 0.0), axis=0, keepdims=True).astype(jnp.int32)
+
+
+def slot_column(picks_f32, first, per):
+    experts = picks_f32.shape[1]
+    shape = (experts * 2 * per, experts)
+    expand = (
+        quotient(lax.broadcasted_iota(jnp.int32, shape, 0), 2 * per)
+        == lax.broadcasted_iota(jnp.int32, shape, 1)
+    ).astype(F32)
+    wide = lax.dot_general(
+        expand, picks_f32, (((1,), (1,)), ((), ())),
+        precision=lax.Precision.HIGHEST, preferred_element_type=F32,
+    )
+    wanted = first + remainder(lax.broadcasted_iota(jnp.int32, wide.shape, 0), per)
+    mine = lax.broadcasted_iota(jnp.int32, wide.shape, 1) == wanted
+    return jnp.sum(jnp.where(mine, wide, 0.0), axis=1, keepdims=True).astype(jnp.int32)
+
+
+def rows_to_half(count, per, half):
+    shape = (count, 2 * count)
+    row = lax.broadcasted_iota(jnp.int32, shape, 0)
+    col = lax.broadcasted_iota(jnp.int32, shape, 1)
+    wanted = (quotient(row, per) * 2 + half) * per + remainder(row, per)
+    return ones_where(col == wanted)
 
 
 def row_half(shape, per, dim):
@@ -212,15 +230,15 @@
 
     @pl.when(tile == pl.num_programs(0) - 1)
     def _():
-        row = slot_row(picks_ref[...].astype(F32), None, rank * per, per)
+        column = slot_column(picks_ref[...].astype(F32), rank * per, per)
         tokens = normed_ref.shape[0]
-        shape = (tokens, row.shape[1])
-        picked = lax.broadcasted_iota(jnp.int32, shape, 0) == row
-        half = row_half(shape, per, 1)
+        shape = (column.shape[0], tokens)
+        picked = lax.broadcasted_iota(jnp.int32, shape, 1) == column
+        half = row_half(shape, per, 0)
         cols = disp_ref.shape[1]
         disp_ref[...] = (
-            dot_l(ones_where(picked & (half == 0)), normed_ref[:, :cols])
-            + dot_l(ones_where(picked & (half == 1)), normed_ref[:, cols:])
+            dot(ones_where(picked & (half == 0)), normed_ref[:, :cols])
+            + dot(ones_where(picked & (half == 1)), normed_ref[:, cols:])
         ).astype(BF16)
 
 
@@ -263,7 +281,7 @@
             pltpu.VMEM((parts * inner, width), BF16),
             pltpu.SemaphoreType.DMA((len(blocks) * parts,)),
         ],
-        compiler_params=params(60),
+        compiler_params=params(62),
         name="mix",
     )(
         rank, core, lane, step, att, x, modulation, modulation, modulation, router_t, picks_t,
@@ -277,8 +295,8 @@
         count = tok_ref.shape[0]
         cols = rows_ref.shape[1]
         for half in range(2):
-            pick = halves_to_rows(count, per, half)
-            tok_ref[:, half * cols : (half + 1) * cols] = dot_l(pick, rows_ref[...]).astype(BF16)
+            pick = rows_to_half(count, per, half)
+            tok_ref[:, half * cols : (half + 1) * cols] = dot(pick, rows_ref[...]).astype(BF16)
 
     out_ref[...] = jax.nn.gelu(dot(tok_ref[...], w_ref[0])).astype(BF16)
 
@@ -301,14 +319,14 @@
     )(rows, w)
 
 
-def down_kernel(per, rank_ref, hid_ref, *refs):
+def down_kernel(per, places, rank_ref, hid_ref, *refs):
     out_ref = refs[-1]
-    blocks = refs[:-1]
-    units = blocks[0].shape[0]
+    parts = 4
+    units = hid_ref.shape[1] // parts
     total = None
-    for turn, block in enumerate(blocks):
-        at = lax.rem(rank_ref[0] + turn, len(blocks))
-        some = hid_ref[:, pl.ds(pl.multiple_of(at * units, units), units)]
+    for (turn, row), block in zip(places, refs[:-1]):
+        at = lax.rem(rank_ref[0] + turn, parts) * units + row
+        some = hid_ref[:, pl.ds(pl.multiple_of(at, 128), block.shape[0])]
         term = dot(some, block[...])
         total = term if total is None else total + term
     total = total.astype(BF16)
@@ -323,15 +341,15 @@
         out_ref[...] += dot(halves_to_rows(count, per, 1), total).astype(BF16)
 
 
-def down_call(rank, hidden, blocks, per):
+def down_call(rank, hidden, blocks, places, per):
     rows, units = hidden.shape
-    few, half = blocks[0].shape
+    half = blocks[0].shape[1]
     cols = half // 2
     return pl.pallas_call(
-        functools.partial(down_kernel, per),
+        functools.partial(down_kernel, per, places),
         grid=(2,),
         in_specs=[smem(), pl.BlockSpec((rows, units), lambda i: (0, 0))]
-        + [pl.BlockSpec((few, cols), lambda i: (0, i))] * len(blocks),
+        + [pl.BlockSpec((block.shape[0], cols), lambda i: (0, i)) for block in blocks],
         out_specs=pl.BlockSpec((2 * rows, cols), lambda i: (0, 0)),
         out_shape=jax.ShapeDtypeStruct((2 * rows, cols), BF16),
         compiler_params=params(60),
@@ -450,45 +468,46 @@
     down = expert_down[0]
     side = lax.rem(rank, 2)
     same_half = lax.dynamic_slice_in_dim(down, side * half, half, 1)
-    other_half = lax.dynamic_slice_in_dim(down, (1 - side) * half, half, 1)
 
     def from_turn(values, turn):
         return lax.ppermute(values, "ffn", [((i + turn) % ffn, i) for i in range(ffn)])
 
     out_rows = [out_own] + [from_turn(out_own, turn) for turn in range(1, ffn)]
-    blocks = [
-        same_half,
-        from_turn(other_half, 1),
-        from_turn(same_half, 2),
-        from_turn(other_half, 3),
-    ]
+    few_units = down.shape[0] // 2
+    first, second = (
+        lax.dynamic_slice(down, (at, (1 - side) * half), (few_units, half))
+        for at in (0, few_units)
+    )
+    places = ((0, 0), (1, 0), (3, 0), (2, 0), (1, few_units), (3, few_units))
+    early = (from_turn(first, 1), from_turn(first, 3))
+    late = (from_turn(same_half, 2), from_turn(second, 1), from_turn(second, 3))
 
     stacked = qkv_call(step_index, x, modulation, jnp.transpose(qkv_weight, (1, 0, 2)), qk_gain)
-    stacked, out_rows = lax.optimization_barrier((stacked, out_rows))
     stacked = over_seq(stacked)
     few = position_count // seq
     attended = attention_call(stacked, few, head_size, ffn)
     out_rows = jnp.concatenate(out_rows, axis=0)
+    attended, out_rows = lax.optimization_barrier((attended, out_rows))
 
     def from_lane(values, turn):
         pairs = [((i + turn * stride) % seq, i) for i in range(seq)]
         return lax.ppermute(values, "seq", pairs)
 
     out_blocks = [out_rows] + [from_lane(out_rows, turn) for turn in range(1, lanes)]
-    attended, out_blocks = lax.optimization_barrier((attended, out_blocks))
     swap = [(i, i ^ 1) for i in range(seq)]
     out_blocks = out_blocks + [lax.ppermute(b, "seq", swap) for b in out_blocks]
     every = lax.all_to_all(attended, ("seq", "ffn"), split_axis=0, concat_axis=0, tiled=True)
+    every, early = lax.optimization_barrier((every, early))
     outgoing, gates, share = mix_call(
         rank_arr, core.reshape(1), lane.reshape(1), step_index, every, out_blocks, x, modulation,
         jnp.transpose(router_weight, (1, 0)), picks_t, per, share_len, few,
     )
-    outgoing, blocks[1] = lax.optimization_barrier((outgoing, blocks[1]))
     expert_tokens = over_seq(outgoing)
+    blocks = (same_half,) + tuple(early) + late
     hidden = up_call(expert_tokens, up_full, per)
     hidden_other = lax.ppermute(hidden, "ffn", [(i, i ^ 1) for i in range(ffn)])
-    own = over_seq(down_call(rank_arr, hidden, blocks, per))
-    other = over_seq(down_call(rank_arr, hidden_other, blocks, per))
+    own = over_seq(down_call(rank_arr, hidden, blocks, places, per))
+    other = over_seq(down_call(rank_arr, hidden_other, blocks, places, per))
     mixture = combine_call(rank_arr, gates, picks_t, counts_t, own, other, per)
     parts = over_ffn(mixture).reshape(ffn, share_len, half)
     return final_call(step_index, share, modulation, parts)[None]

time: 276 us -> 251 us (0.909)
  waiting for transfers between devices: 110 us -> 84.6 us
    ppermute x6 -> x8, waiting for transfers between devices: 25.2 us -> 44.6 us  [from_turn(): lax.ppermute(values, 'ffn', [((i + turn) % ffn, i) for i in range(ffn)])]
    all_to_all x1, waiting for transfers between devices: 18.8 us -> 0.01 us  [on_device(): lax.all_to_all(attended, ('seq', 'ffn'), split_axis=0, concat_axis=0, til...]
    all_to_all x3, waiting for transfers between devices: 46.9 us -> 31.8 us  [over_seq(): lax.all_to_all(values, 'seq', split_axis=0, concat_axis=0, tiled=True)]
    ppermute x3, waiting for transfers between devices: 10.7 us -> 2.11 us  [from_lane(): return lax.ppermute(values, 'seq', pairs)]
    ppermute x6 -> x8, starting transfers between devices: 10 us -> 13 us  [from_turn(): lax.ppermute(values, 'ffn', [((i + turn) % ffn, i) for i in range(ffn)])]
  transfers between devices with their start and end apart: 19 -> 21, of which waited for: 12 -> 11; matrix products, arithmetic and copies ran while one was open for 1% -> 1% of each run, Pallas kernels for 14% -> 15%
where the time goes in v7:
time: 251 us; the launch traced here: 250 us
  waiting for transfers between devices  84.6 us (34%)
  starting transfers between devices  63.1 us (25%)
  blocking collectives  42.6 us (17%)
  Pallas kernels  41.6 us (17%)
  between operations  14.3 us (6%)
  local copies, waits for them, and re-layouts  3.21 us (1%)
    ppermute x8, waiting for transfers between devices, from_turn(): lax.ppermute(values, 'ffn', [((i + turn) % ffn, i) for i in range(ffn)])  44.6 us
    all_to_all x3, starting transfers between devices, over_seq(): lax.all_to_all(values, 'seq', split_axis=0, concat_axis=0, tiled=True)  32.6 us
    all_to_all x3, waiting for transfers between devices, over_seq(): lax.all_to_all(values, 'seq', split_axis=0, concat_axis=0, tiled=True)  31.8 us
    all_to_all x1, blocking collectives, over_seq(): lax.all_to_all(values, 'seq', split_axis=0, concat_axis=0, tiled=True)  23.6 us
    all_to_all x1, blocking collectives, over_ffn(): lax.all_to_all(values, 'ffn', split_axis=0, concat_axis=0, tiled=True)  19 us
    ppermute x8, starting transfers between devices, from_turn(): lax.ppermute(values, 'ffn', [((i + turn) % ffn, i) for i in range(ffn)])  13 us
    pallas_call x1, Pallas kernels, mix_call(): pl.pallas_call(functools.partial(mix_kernel, per, len(blocks) // 2, parts...  12.8 us
    all_to_all x1, starting transfers between devices, on_device(): lax.all_to_all(attended, ('seq', 'ffn'), split_axis=0, concat_axis=0, til...  10.8 us
  transfers between devices with their start and end apart: 21, of which 11 were waited for; matrix products, arithmetic and copies ran while one was open for 1% of the time, Pallas kernels for 15%

profile of v7, /device:TPU:8, one launch (start us, length us, event | category | flops | bytes accessed | tf_op | source)
XLA Modules:
  0.0 250.2 jit_solution(5758408638778866398)
XLA Ops:
  7.9 6.3 %qkv.1 = bf16[512,768]{1,0:T(8,128)(2,1)} custom-call(s32[1]{0:T(128)S(6)} %copy.12.step_ref, bf16[512,2048]{1,0:T(8,128)(2,1)} %bitcast.35, f32[16,12288]{1,0:T(8,128)} %gate_ref.3, bf16[3,2048,256]{2,1,0:T(8,128)(2,1)} %bitcast.38, f32[2,128]{1,0:T(2,128)} %gain_ref.1), custom_call_target="tpu_custom_call" | custom-call | tf_op jit(solution)/shard_map/qkv/pallas_call | solution.py:71
  14.2 12.1 %all-to-all-start = ((bf16[64,8,768]{2,1,0:T(8,128)(2,1)}), bf16[64,8,768]{2,1,0:T(8,128)(2,1)S(1)}, u32[]{:S(2)}, u32[]{:S(2)}) async-start(bf16[64,8,768]{2,1,0:T(8,128)(2,1)} %bitcast.37), calls=%async_computation | async-start | bytes 1572864 | tf_op jit(solution)/shard_map/all_to_all | solution.py:455
  26.4 1.5 collective-permute-start.2
  28.0 2.8 %collective-permute-start.1 = (bf16[32,2048]{1,0:T(8,128)(2,1)S(1)}, bf16[32,2048]{1,0:T(8,128)(2,1)S(1)}, u32[]{:S(2)}, u32[]{:S(2)}) collective-permute-start(bf16[32,2048]{1,0:T(8,128)(2,1)S(1)} %constant_dynamic-slice_fusion), channel_id=1, source_target_pairs={{2,0},{3,1},{0,2},{1,3},{6,4},{7,5},{4,6},{5,7},{10,8},{11,9},{8,1... | collective-permute-start | bytes 393224 | tf_op jit(solution)/shard_map/ppermute | solution.py:473
  30.7 1.4 collective-permute-start
  32.1 4.2 %collective-permute-done.2 = bf16[32,2048]{1,0:T(8,128)(2,1)S(1)} collective-permute-done((bf16[32,2048]{1,0:T(8,128)(2,1)S(1)}, bf16[32,2048]{1,0:T(8,128)(2,1)S(1)}, u32[]{:S(2)}, u32[]{:S(2)}) %collective-permute-start.2) | collective-permute-done | bytes 131104 | tf_op jit(solution)/shard_map/ppermute | solution.py:473
  36.3 6.8 %collective-permute-done.1 = bf16[32,2048]{1,0:T(8,128)(2,1)S(1)} collective-permute-done((bf16[32,2048]{1,0:T(8,128)(2,1)S(1)}, bf16[32,2048]{1,0:T(8,128)(2,1)S(1)}, u32[]{:S(2)}, u32[]{:S(2)}) %collective-permute-start.1) | collective-permute-done | bytes 131104 | tf_op jit(solution)/shard_map/ppermute | solution.py:473
  43.9 4.3 %all-to-all-done = bf16[64,8,768]{2,1,0:T(8,128)(2,1)S(1)} async-done(((bf16[64,8,768]{2,1,0:T(8,128)(2,1)}), bf16[64,8,768]{2,1,0:T(8,128)(2,1)S(1)}, u32[]{:S(2)}, u32[]{:S(2)}) %all-to-all-start) | async-done | bytes 786464 | tf_op jit(solution)/shard_map/all_to_all | solution.py:455
  48.2 2.1 attention.1
  50.3 10.8 %all-to-all-start.1 = ((bf16[256,8,256]{2,1,0:T(8,128)(2,1)}), bf16[256,8,256]{2,1,0:T(8,128)(2,1)}, u32[]{:S(2)}, u32[]{:S(2)}) async-start(bf16[256,8,256]{2,1,0:T(8,128)(2,1)} %bitcast.7), calls=%async_computation.1 | async-start | bytes 2097152 | tf_op jit(solution)/shard_map/all_to_all | solution.py:499
  62.0 2.7 %collective-permute-start.3 = (bf16[256,1024]{1,0:T(8,128)(2,1)S(1)}, bf16[256,1024]{1,0:T(8,128)(2,1)}, u32[]{:S(2)}, u32[]{:S(2)}) collective-permute-start(bf16[256,1024]{1,0:T(8,128)(2,1)S(1)} %get-tuple-element.22), channel_id=1, source_target_pairs={{1,0},{2,1},{3,2},{0,3},{5,4},{6,5},{7,6},{4,7},{9,8},{10,9},{11,1... | collective-permute-start | bytes 1572872 | tf_op jit(solution)/shard_map/ppermute | solution.py:473
  65.3 2.4 collective-permute-start.6
  67.7 1.8 collective-permute-start.7
  69.5 27.4 %collective-permute-done.3.refs_1_ = bf16[256,1024]{1,0:T(8,128)(2,1)} collective-permute-done((bf16[256,1024]{1,0:T(8,128)(2,1)S(1)}, bf16[256,1024]{1,0:T(8,128)(2,1)}, u32[]{:S(2)}, u32[]{:S(2)}) %collective-permute-start.3) | collective-permute-done | bytes 524320 | tf_op jit(solution)/shard_map/ppermute | solution.py:473
  97.4 2.1 collective-permute-done.6.refs_2_
  100.0 2.3 collective-permute-done.4.refs_2_
  102.4 12.8 %mix.1 = (bf16[512,1024]{1,0:T(8,128)(2,1)}, f32[512,64]{1,0:T(8,128)}, f32[128,2048]{1,0:T(8,128)}) custom-call(s32[1]{0:T(128)} %bitcast.rank_ref, s32[1]{0:T(128)} %bitcast.1.core_ref, s32[1]{0:T(128)} %bitcast.2.lane_ref, s32[1]{0:T(128)S(6)} %copy.12.step_ref, bf16[2048,256]{1,0:T(8,128)(2,1)} %bitcast.8.att_ref, bf16[512,2048]{1,0:T(8,128)(2,1)} %bitcast.36, ...), custom_call_target="tpu_custom_call" | custom-call | tf_op jit(solution)/shard_map/mix/pallas_call | solution.py:254
  115.3 9.8 %all-to-all-start.2 = ((bf16[64,8,1024]{2,1,0:T(8,128)(2,1)}), bf16[64,8,1024]{2,1,0:T(8,128)(2,1)}, u32[]{:S(2)}, u32[]{:S(2)}) async-start(bf16[64,8,1024]{2,1,0:T(8,128)(2,1)} %bitcast.41), calls=%async_computation.2 | async-start | bytes 2097152 | tf_op jit(solution)/shard_map/all_to_all | solution.py:455
  125.1 1.3 dynamic-slice_bitcast_fusion.refs_0_
  126.4 2.5 %collective-permute-start.12 = (bf16[512,1024]{1,0:T(8,128)(2,1)S(1)}, bf16[512,1024]{1,0:T(8,128)(2,1)S(1)}, u32[]{:S(2)}, u32[]{:S(2)}) collective-permute-start(bf16[512,1024]{1,0:T(8,128)(2,1)S(1)} %dynamic-slice_bitcast_fusion.refs_0_), channel_id=1, source_target_pairs={{2,0},{3,1},{0,2},{1,3},{6,4},{7,5},{4,6},{5,7},{10,8},{11,9},{8,1... | collective-permute-start | bytes 3145736 | tf_op jit(solution)/shard_map/ppermute | solution.py:473
  130.9 21.2 %all-to-all-done.2 = bf16[64,8,1024]{2,1,0:T(8,128)(2,1)} async-done(((bf16[64,8,1024]{2,1,0:T(8,128)(2,1)}), bf16[64,8,1024]{2,1,0:T(8,128)(2,1)}, u32[]{:S(2)}, u32[]{:S(2)}) %all-to-all-start.2) | async-done | bytes 1048608 | tf_op jit(solution)/shard_map/all_to_all | solution.py:455
  152.1 7.6 %up.1.hid_ref = bf16[256,2048]{1,0:T(8,128)(2,1)} custom-call(bf16[512,1024]{1,0:T(8,128)(2,1)} %bitcast.16.rows_ref, bf16[4,2048,512]{2,1,0:T(8,128)(2,1)} %all-gather.2.cloned.1.call-done.w_ref), custom_call_target="tpu_custom_call" | custom-call | tf_op jit(solution)/shard_map/up/pallas_call | solution.py:307
  160.6 3.6 %collective-permute-done.13.refs_4_ = bf16[256,1024]{1,0:T(8,128)(2,1)} collective-permute-done((bf16[256,1024]{1,0:T(8,128)(2,1)}, bf16[256,1024]{1,0:T(8,128)(2,1)}, u32[]{:S(2)}, u32[]{:S(2)}) %collective-permute-start.13) | collective-permute-done | bytes 524320 | tf_op jit(solution)/shard_map/ppermute | solution.py:473
  165.5 4.9 %down.2 = bf16[512,512]{1,0:T(8,128)(2,1)} custom-call(s32[1]{0:T(128)} %bitcast.rank_ref, bf16[256,2048]{1,0:T(8,128)(2,1)} %up.1.hid_ref, bf16[512,1024]{1,0:T(8,128)(2,1)} %copy-done.6, bf16[256,1024]{1,0:T(8,128)(2,1)} %collective-permute-done.3.refs_1_, bf16[256,1024]{1,0:T(8,128)(2,1)} %collective-permute-done.4.refs_2_, bf16[512,1024]{1,0:T(8,128)(2,1)} %copy-done.7, ...), custom_call_target="tpu_custom_call" | custom-call | tf_op jit(solution)/shard_map/down/pallas_call | solution.py:348
  170.4 10.8 %all-to-all-start.3 = ((bf16[64,8,512]{2,1,0:T(8,128)(2,1)}), bf16[64,8,512]{2,1,0:T(8,128)(2,1)S(1)}, u32[]{:S(2)}, u32[]{:S(2)}) async-start(bf16[64,8,512]{2,1,0:T(8,128)(2,1)} %bitcast.39), calls=%async_computation.3 | async-start | bytes 1048576 | tf_op jit(solution)/shard_map/all_to_all | solution.py:455
  181.2 5.4 %collective-permute-done.15.hid_ref = bf16[256,2048]{1,0:T(8,128)(2,1)} collective-permute-done((bf16[256,2048]{1,0:T(8,128)(2,1)}, bf16[256,2048]{1,0:T(8,128)(2,1)}, u32[]{:S(2)}, u32[]{:S(2)}) %collective-permute-start.15) | collective-permute-done | bytes 1048608 | tf_op jit(solution)/shard_map/ppermute | solution.py:508
  186.6 4.9 %down.3 = bf16[512,512]{1,0:T(8,128)(2,1)} custom-call(s32[1]{0:T(128)} %bitcast.rank_ref, bf16[256,2048]{1,0:T(8,128)(2,1)} %collective-permute-done.15.hid_ref, bf16[512,1024]{1,0:T(8,128)(2,1)} %copy-done.6, bf16[256,1024]{1,0:T(8,128)(2,1)} %collective-permute-done.3.refs_1_, bf16[256,1024]{1,0:T(8,128)(2,1)} %collective-permute-done.4.refs_2_, ...), custom_call_target="tpu_custom_call" | custom-call | tf_op jit(solution)/shard_map/down/pallas_call | solution.py:348
  191.5 6.3 %all-to-all-done.3 = bf16[64,8,512]{2,1,0:T(8,128)(2,1)S(1)} async-done(((bf16[64,8,512]{2,1,0:T(8,128)(2,1)}), bf16[64,8,512]{2,1,0:T(8,128)(2,1)S(1)}, u32[]{:S(2)}, u32[]{:S(2)}) %all-to-all-start.3) | async-done | bytes 524320 | tf_op jit(solution)/shard_map/all_to_all | solution.py:455
  197.9 23.6 %all_to_all.65 = bf16[64,8,512]{2,1,0:T(8,128)(2,1)S(1)} all-to-all(bf16[64,8,512]{2,1,0:T(8,128)(2,1)} %bitcast.40), channel_id=1, replica_groups=mesh['seq'=64,'ffn'=4] {'seq'}, dimensions={0} | all-to-all | bytes 1048576 | tf_op jit(solution)/shard_map/all_to_all | solution.py:455
  221.5 1.7 combine.1
  223.2 19.0 %all_to_all.66.parts_ref = bf16[4,128,1024]{2,1,0:T(8,128)(2,1)S(1)} all-to-all(bf16[4,128,1024]{2,1,0:T(8,128)(2,1)S(1)} %bitcast.28), channel_id=1, replica_groups=mesh['seq'=64,'ffn'=4] {'ffn'}, dimensions={0} | all-to-all | bytes 2097152 | tf_op jit(solution)/shard_map/all_to_all | solution.py:458
  242.2 1.2 final.1
  (49 shorter events, 8.3 us)
Async XLA Ops:
  6.5 19.8 %copy-start = (bf16[256,2048]{1,0:T(8,128)(2,1)S(1)}, bf16[256,2048]{1,0:T(8,128)(2,1)}, u32[]{:S(2)}) copy-start(bf16[256,2048]{1,0:T(8,128)(2,1)} %param.16) | copy-start | bytes 3145732
  6.5 145.6 %all-gather.2.cloned.1.call-start = ((), (), s32[]{:S(2)}) async-start(), calls=%async_computation.6 | async-start | bytes 10485760 | tf_op jit(solution)/shard_map/all_gather | solution.py:467
  14.2 34.0 %all-to-all-start = ((bf16[64,8,768]{2,1,0:T(8,128)(2,1)}), bf16[64,8,768]{2,1,0:T(8,128)(2,1)S(1)}, u32[]{:S(2)}, u32[]{:S(2)}) async-start(bf16[64,8,768]{2,1,0:T(8,128)(2,1)} %bitcast.37), calls=%async_computation | async-start | bytes 1572864 | tf_op jit(solution)/shard_map/all_to_all | solution.py:455
  26.4 9.9 %collective-permute-start.2 = (bf16[32,2048]{1,0:T(8,128)(2,1)S(1)}, bf16[32,2048]{1,0:T(8,128)(2,1)S(1)}, u32[]{:S(2)}, u32[]{:S(2)}) collective-permute-start(bf16[32,2048]{1,0:T(8,128)(2,1)S(1)} %constant_dynamic-slice_fusion), channel_id=1, source_target_pairs={{3,0},{0,1},{1,2},{2,3},{7,4},{4,5},{5,6},{6,7},{11,8},{8,9},{9,10... | collective-permute-start | bytes 393224 | tf_op jit(solution)/shard_map/ppermute | solution.py:473
  28.0 15.1 %collective-permute-start.1 = (bf16[32,2048]{1,0:T(8,128)(2,1)S(1)}, bf16[32,2048]{1,0:T(8,128)(2,1)S(1)}, u32[]{:S(2)}, u32[]{:S(2)}) collective-permute-start(bf16[32,2048]{1,0:T(8,128)(2,1)S(1)} %constant_dynamic-slice_fusion), channel_id=1, source_target_pairs={{2,0},{3,1},{0,2},{1,3},{6,4},{7,5},{4,6},{5,7},{10,8},{11,9},{8,1... | collective-permute-start | bytes 393224 | tf_op jit(solution)/shard_map/ppermute | solution.py:473
  30.7 12.4 %collective-permute-start = (bf16[32,2048]{1,0:T(8,128)(2,1)S(1)}, bf16[32,2048]{1,0:T(8,128)(2,1)S(1)}, u32[]{:S(2)}, u32[]{:S(2)}) collective-permute-start(bf16[32,2048]{1,0:T(8,128)(2,1)S(1)} %constant_dynamic-slice_fusion), channel_id=1, source_target_pairs={{1,0},{2,1},{3,2},{0,3},{5,4},{6,5},{7,6},{4,7},{9,8},{10,9},{11,1... | collective-permute-start | bytes 393224 | tf_op jit(solution)/shard_map/ppermute | solution.py:473
  50.3 10.8 %copy-start.8 = (bf16[1,512,2048]{2,1,0:T(8,128)(2,1)S(1)}, bf16[1,512,2048]{2,1,0:T(8,128)(2,1)}, u32[]{:S(2)}) copy-start(bf16[1,512,2048]{2,1,0:T(8,128)(2,1)} %param.19) | copy-start | bytes 6291460
  50.3 52.0 %all-to-all-start.1 = ((bf16[256,8,256]{2,1,0:T(8,128)(2,1)}), bf16[256,8,256]{2,1,0:T(8,128)(2,1)}, u32[]{:S(2)}, u32[]{:S(2)}) async-start(bf16[256,8,256]{2,1,0:T(8,128)(2,1)} %bitcast.7), calls=%async_computation.1 | async-start | bytes 2097152 | tf_op jit(solution)/shard_map/all_to_all | solution.py:499
  62.0 34.9 %collective-permute-start.3 = (bf16[256,1024]{1,0:T(8,128)(2,1)S(1)}, bf16[256,1024]{1,0:T(8,128)(2,1)}, u32[]{:S(2)}, u32[]{:S(2)}) collective-permute-start(bf16[256,1024]{1,0:T(8,128)(2,1)S(1)} %get-tuple-element.22), channel_id=1, source_target_pairs={{1,0},{2,1},{3,2},{0,3},{5,4},{6,5},{7,6},{4,7},{9,8},{10,9},{11,1... | collective-permute-start | bytes 1572872 | tf_op jit(solution)/shard_map/ppermute | solution.py:473
  64.7 32.2 %collective-permute-start.5 = (bf16[128,2048]{1,0:T(8,128)(2,1)}, bf16[128,2048]{1,0:T(8,128)(2,1)S(1)}, u32[]{:S(2)}, u32[]{:S(2)}) collective-permute-start(bf16[128,2048]{1,0:T(8,128)(2,1)} %pad_maximum_fusion.refs_0_), channel_id=1, source_target_pairs={{64,0},{68,4},{72,8},{76,12},{80,16},{84,20},{88,24},{92,28},{96,3... | collective-permute-start | bytes 1572872 | tf_op jit(solution)/shard_map/ppermute | solution.py:494
  65.3 34.3 %collective-permute-start.6 = (bf16[128,2048]{1,0:T(8,128)(2,1)}, bf16[128,2048]{1,0:T(8,128)(2,1)S(1)}, u32[]{:S(2)}, u32[]{:S(2)}) collective-permute-start(bf16[128,2048]{1,0:T(8,128)(2,1)} %pad_maximum_fusion.refs_0_), channel_id=1, source_target_pairs={{128,0},{132,4},{136,8},{140,12},{144,16},{148,20},{152,24},{156,2... | collective-permute-start | bytes 1572872 | tf_op jit(solution)/shard_map/ppermute | solution.py:494
  67.7 31.9 %collective-permute-start.7 = (bf16[128,2048]{1,0:T(8,128)(2,1)}, bf16[128,2048]{1,0:T(8,128)(2,1)S(1)}, u32[]{:S(2)}, u32[]{:S(2)}) collective-permute-start(bf16[128,2048]{1,0:T(8,128)(2,1)} %pad_maximum_fusion.refs_0_), channel_id=1, source_target_pairs={{192,0},{196,4},{200,8},{204,12},{208,16},{212,20},{216,24},{220,2... | collective-permute-start | bytes 1572872 | tf_op jit(solution)/shard_map/ppermute | solution.py:494
  69.5 32.9 %collective-permute-start.4 = (bf16[256,1024]{1,0:T(8,128)(2,1)S(1)}, bf16[256,1024]{1,0:T(8,128)(2,1)}, u32[]{:S(2)}, u32[]{:S(2)}) collective-permute-start(bf16[256,1024]{1,0:T(8,128)(2,1)S(1)} %get-tuple-element.22), channel_id=1, source_target_pairs={{3,0},{0,1},{1,2},{2,3},{7,4},{4,5},{5,6},{6,7},{11,8},{8,9},{9,10... | collective-permute-start | bytes 1572872 | tf_op jit(solution)/shard_map/ppermute | solution.py:473
  96.9 5.5 %collective-permute-start.8 = (bf16[128,2048]{1,0:T(8,128)(2,1)}, bf16[128,2048]{1,0:T(8,128)(2,1)}, u32[]{:S(2)}, u32[]{:S(2)}) collective-permute-start(bf16[128,2048]{1,0:T(8,128)(2,1)} %pad_maximum_fusion.refs_0_), channel_id=1, source_target_pairs={{0,4},{4,0},{8,12},{12,8},{16,20},{20,16},{24,28},{28,24},{32,36},... | collective-permute-start | bytes 1572872 | tf_op jit(solution)/shard_map/ppermute | solution.py:498
  96.9 5.5 %copy-start.9 = (bf16[128,2048]{1,0:T(8,128)(2,1)}, bf16[128,2048]{1,0:T(8,128)(2,1)S(1)}, u32[]{:S(2)}) copy-start(bf16[128,2048]{1,0:T(8,128)(2,1)S(1)} %collective-permute-done.5.refs_1_) | copy-start | bytes 1572868
  96.9 5.5 %collective-permute-start.9 = (bf16[128,2048]{1,0:T(8,128)(2,1)S(1)}, bf16[128,2048]{1,0:T(8,128)(2,1)}, u32[]{:S(2)}, u32[]{:S(2)}) collective-permute-start(bf16[128,2048]{1,0:T(8,128)(2,1)S(1)} %collective-permute-done.5.refs_1_), channel_id=1, source_target_pairs={{0,4},{4,0},{8,12},{12,8},{16,20},{20,16},{24,28},{28,24},{32,36},... | collective-permute-start | bytes 1572872 | tf_op jit(solution)/shard_map/ppermute | solution.py:498
  99.5 2.9 %copy-start.10 = (bf16[128,2048]{1,0:T(8,128)(2,1)}, bf16[128,2048]{1,0:T(8,128)(2,1)S(1)}, u32[]{:S(2)}) copy-start(bf16[128,2048]{1,0:T(8,128)(2,1)S(1)} %collective-permute-done.6.refs_2_) | copy-start | bytes 1572868
  99.5 2.9 %collective-permute-start.10 = (bf16[128,2048]{1,0:T(8,128)(2,1)S(1)}, bf16[128,2048]{1,0:T(8,128)(2,1)}, u32[]{:S(2)}, u32[]{:S(2)}) collective-permute-start(bf16[128,2048]{1,0:T(8,128)(2,1)S(1)} %collective-permute-done.6.refs_2_), channel_id=1, source_target_pairs={{0,4},{4,0},{8,12},{12,8},{16,20},{20,16},{24,28},{28,24},{32,36},... | collective-permute-start | bytes 1572872 | tf_op jit(solution)/shard_map/ppermute | solution.py:498
  99.5 2.9 %copy-start.11 = (bf16[128,2048]{1,0:T(8,128)(2,1)}, bf16[128,2048]{1,0:T(8,128)(2,1)S(1)}, u32[]{:S(2)}) copy-start(bf16[128,2048]{1,0:T(8,128)(2,1)S(1)} %collective-permute-done.7.refs_3_) | copy-start | bytes 1572868
  99.5 2.9 %collective-permute-start.11 = (bf16[128,2048]{1,0:T(8,128)(2,1)S(1)}, bf16[128,2048]{1,0:T(8,128)(2,1)}, u32[]{:S(2)}, u32[]{:S(2)}) collective-permute-start(bf16[128,2048]{1,0:T(8,128)(2,1)S(1)} %collective-permute-done.7.refs_3_), channel_id=1, source_target_pairs={{0,4},{4,0},{8,12},{12,8},{16,20},{20,16},{24,28},{28,24},{32,36},... | collective-permute-start | bytes 1572872 | tf_op jit(solution)/shard_map/ppermute | solution.py:498
  115.3 36.8 %all-to-all-start.2 = ((bf16[64,8,1024]{2,1,0:T(8,128)(2,1)}), bf16[64,8,1024]{2,1,0:T(8,128)(2,1)}, u32[]{:S(2)}, u32[]{:S(2)}) async-start(bf16[64,8,1024]{2,1,0:T(8,128)(2,1)} %bitcast.41), calls=%async_computation.2 | async-start | bytes 2097152 | tf_op jit(solution)/shard_map/all_to_all | solution.py:455
  126.4 33.4 %copy-start.6 = (bf16[512,1024]{1,0:T(8,128)(2,1)}, bf16[512,1024]{1,0:T(8,128)(2,1)S(1)}, u32[]{:S(2)}) copy-start(bf16[512,1024]{1,0:T(8,128)(2,1)S(1)} %dynamic-slice_bitcast_fusion.refs_0_) | copy-start | bytes 3145732
  126.4 38.1 %collective-permute-start.12 = (bf16[512,1024]{1,0:T(8,128)(2,1)S(1)}, bf16[512,1024]{1,0:T(8,128)(2,1)S(1)}, u32[]{:S(2)}, u32[]{:S(2)}) collective-permute-start(bf16[512,1024]{1,0:T(8,128)(2,1)S(1)} %dynamic-slice_bitcast_fusion.refs_0_), channel_id=1, source_target_pairs={{2,0},{3,1},{0,2},{1,3},{6,4},{7,5},{4,6},{5,7},{10,8},{11,9},{8,1... | collective-permute-start | bytes 3145736 | tf_op jit(solution)/shard_map/ppermute | solution.py:473
  128.9 35.3 %collective-permute-start.13 = (bf16[256,1024]{1,0:T(8,128)(2,1)}, bf16[256,1024]{1,0:T(8,128)(2,1)}, u32[]{:S(2)}, u32[]{:S(2)}) collective-permute-start(bf16[256,1024]{1,0:T(8,128)(2,1)} %get-tuple-element.21), channel_id=1, source_target_pairs={{1,0},{2,1},{3,2},{0,3},{5,4},{6,5},{7,6},{4,7},{9,8},{10,9},{11,1... | collective-permute-start | bytes 1572872 | tf_op jit(solution)/shard_map/ppermute | solution.py:473
  130.0 34.5 %collective-permute-start.14 = (bf16[256,1024]{1,0:T(8,128)(2,1)}, bf16[256,1024]{1,0:T(8,128)(2,1)}, u32[]{:S(2)}, u32[]{:S(2)}) collective-permute-start(bf16[256,1024]{1,0:T(8,128)(2,1)} %get-tuple-element.21), channel_id=1, source_target_pairs={{3,0},{0,1},{1,2},{2,3},{7,4},{4,5},{5,6},{6,7},{11,8},{8,9},{9,10... | collective-permute-start | bytes 1572872 | tf_op jit(solution)/shard_map/ppermute | solution.py:473
  159.7 26.9 %collective-permute-start.15 = (bf16[256,2048]{1,0:T(8,128)(2,1)}, bf16[256,2048]{1,0:T(8,128)(2,1)}, u32[]{:S(2)}, u32[]{:S(2)}) collective-permute-start(bf16[256,2048]{1,0:T(8,128)(2,1)} %up.1.hid_ref), channel_id=1, source_target_pairs={{0,1},{1,0},{2,3},{3,2},{4,5},{5,4},{6,7},{7,6},{8,9},{9,8},{10,11... | collective-permute-start | bytes 3145736 | tf_op jit(solution)/shard_map/ppermute | solution.py:508
  170.4 27.5 %all-to-all-start.3 = ((bf16[64,8,512]{2,1,0:T(8,128)(2,1)}), bf16[64,8,512]{2,1,0:T(8,128)(2,1)S(1)}, u32[]{:S(2)}, u32[]{:S(2)}) async-start(bf16[64,8,512]{2,1,0:T(8,128)(2,1)} %bitcast.39), calls=%async_computation.3 | async-start | bytes 1048576 | tf_op jit(solution)/shard_map/all_to_all | solution.py:455
  181.2 40.3 %copy-start.3 = (f32[512,64]{1,0:T(8,128)S(1)}, f32[512,64]{1,0:T(8,128)}, u32[]{:S(2)}) copy-start(f32[512,64]{1,0:T(8,128)} %get-tuple-element.17.gates_ref) | copy-start | bytes 393220
  181.2 40.3 %copy-start.4 = (s32[64,1,16]{0,2,1:T(8,128)S(1)}, s32[64,1,16]{0,2,1:T(8,128)}, u32[]{:S(2)}) copy-start(s32[64,1,16]{0,2,1:T(8,128)} %param.20) | copy-start | bytes 12292
  181.2 40.3 %copy-start.5 = (s32[64,1]{0,1:T(1,128)S(1)}, s32[64,1]{0,1:T(1,128)}, u32[]{:S(2)}) copy-start(s32[64,1]{0,1:T(1,128)} %param.21) | copy-start | bytes 772
  221.5 20.7 %copy-start.1 = (f32[16,12288]{1,0:T(8,128)S(1)}, f32[16,12288]{1,0:T(8,128)}, u32[]{:S(2)}) copy-start(f32[16,12288]{1,0:T(8,128)} %gate_ref.3) | copy-start | bytes 2359300
  221.5 20.7 %copy-start.2 = (f32[128,2048]{1,0:T(8,128)S(1)}, f32[128,2048]{1,0:T(8,128)}, u32[]{:S(2)}) copy-start(f32[128,2048]{1,0:T(8,128)} %get-tuple-element.16.share_ref) | copy-start | bytes 3145732
  (1 other events, 1.0 us)
Sparse Core Ops, SparseCore 0:
  9.2 116.6 all-gather.1

commit v8 on v7

--- a/solution.py
+++ b/solution.py
@@ -177,17 +177,16 @@
     scale_ref, router_ref, picks_ref, *refs
 ):
     blocks = refs[: 2 * pieces]
-    disp_ref, gates_ref, share_ref, hidden_ref, normed_ref, w_ref, sems = refs[2 * pieces :]
+    (disp_ref, gates_ref, share_ref, hidden_ref, normed_ref, w_ref, every_ref, pick_ref,
+     sems) = refs[2 * pieces :]
     step = step_ref[0]
     rank = rank_ref[0]
     tile = pl.program_id(0)
     rows = x_ref.shape[0]
     inner = att_ref.shape[1]
 
-    @pl.when(tile == 0)
-    def _():
+    def weight_copies():
         some = blocks[0].shape[0] // parts
-        copies = []
         for number, block in enumerate(blocks):
             which, turn = divmod(number, pieces)
             half = lax.rem(core_ref[0] + which, 2)
@@ -195,26 +194,45 @@
             for part_turn in range(parts):
                 part = lax.rem(rank + part_turn, parts)
                 to = pl.multiple_of(part * inner + half * (inner // 2) + place * some, some)
-                copies.append(
-                    pltpu.make_async_copy(
-                        block.at[pl.ds(part_turn * some, some), :],
-                        w_ref.at[pl.ds(to, some), :],
-                        sems.at[number * parts + part_turn],
-                    )
+                yield pltpu.make_async_copy(
+                    block.at[pl.ds(part_turn * some, some), :],
+                    w_ref.at[pl.ds(to, some), :],
+                    sems.at[number * parts + part_turn],
                 )
+
+    def pick_matrices():
+        column = slot_column(picks_ref[...].astype(F32), rank * per, per)
+        shape = (column.shape[0], normed_ref.shape[0])
+        picked = lax.broadcasted_iota(jnp.int32, shape, 1) == column
+        half = row_half(shape, per, 0)
+        for which in range(2):
+            pick_ref[which] = ones_where(picked & (half == which))
+
+    def join():
+        split = att_ref[...].astype(F32).reshape(rows // few, parts, few, inner)
+        for part in range(parts):
+            every_ref[:, part * inner : (part + 1) * inner] = (
+                split[:, part].reshape(rows, inner).astype(BF16)
+            )
+
+    @pl.when(tile == 0)
+    def _():
+        copies = list(weight_copies())
         for copy in copies:
             copy.start()
+        join()
+        pick_matrices()
         for copy in copies:
             copy.wait()
+
+    @pl.when(tile > 0)
+    def _():
+        join()
 
     gate = gate_ref[pl.ds(step, 1), :]
     shift = shift_ref[pl.ds(step, 1), :]
     scale = scale_ref[pl.ds(step, 1), :]
-    split = att_ref[...].astype(F32).reshape(rows // few, parts, few, inner)
-    every = jnp.concatenate(
-        [split[:, part].reshape(rows, inner).astype(BF16) for part in range(parts)], axis=1
-    )
-    mixed = dot(every, w_ref[...])
+    mixed = dot(every_ref[...], w_ref[...])
     hidden = x_ref[...].astype(F32) + gate * mixed
     hidden_ref[...] = hidden
     normed = (layer_norm(hidden) * (1.0 + scale) + shift).astype(BF16)
@@ -230,15 +248,9 @@
 
     @pl.when(tile == pl.num_programs(0) - 1)
     def _():
-        column = slot_column(picks_ref[...].astype(F32), rank * per, per)
-        tokens = normed_ref.shape[0]
-        shape = (column.shape[0], tokens)
-        picked = lax.broadcasted_iota(jnp.int32, shape, 1) == column
-        half = row_half(shape, per, 0)
         cols = disp_ref.shape[1]
         disp_ref[...] = (
-            dot(ones_where(picked & (half == 0)), normed_ref[:, :cols])
-            + dot(ones_where(picked & (half == 1)), normed_ref[:, cols:])
+            dot(pick_ref[0], normed_ref[:, :cols]) + dot(pick_ref[1], normed_ref[:, cols:])
         ).astype(BF16)
 
 
@@ -279,6 +291,8 @@
             pltpu.VMEM((rows, width), F32),
             pltpu.VMEM((tokens, width), BF16),
             pltpu.VMEM((parts * inner, width), BF16),
+            pltpu.VMEM((rows, parts * inner), BF16),
+            pltpu.VMEM((2, 2 * experts * per, tokens), BF16),
             pltpu.SemaphoreType.DMA((len(blocks) * parts,)),
         ],
         compiler_params=params(62),
@@ -483,25 +497,26 @@
     late = (from_turn(same_half, 2), from_turn(second, 1), from_turn(second, 3))
 
     stacked = qkv_call(step_index, x, modulation, jnp.transpose(qkv_weight, (1, 0, 2)), qk_gain)
+    stacked, out_rows = lax.optimization_barrier((stacked, out_rows))
     stacked = over_seq(stacked)
     few = position_count // seq
     attended = attention_call(stacked, few, head_size, ffn)
     out_rows = jnp.concatenate(out_rows, axis=0)
-    attended, out_rows = lax.optimization_barrier((attended, out_rows))
 
     def from_lane(values, turn):
         pairs = [((i + turn * stride) % seq, i) for i in range(seq)]
         return lax.ppermute(values, "seq", pairs)
 
     out_blocks = [out_rows] + [from_lane(out_rows, turn) for turn in range(1, lanes)]
+    attended, out_blocks[2] = lax.optimization_barrier((attended, out_blocks[2]))
     swap = [(i, i ^ 1) for i in range(seq)]
     out_blocks = out_blocks + [lax.ppermute(b, "seq", swap) for b in out_blocks]
     every = lax.all_to_all(attended, ("seq", "ffn"), split_axis=0, concat_axis=0, tiled=True)
-    every, early = lax.optimization_barrier((every, early))
     outgoing, gates, share = mix_call(
         rank_arr, core.reshape(1), lane.reshape(1), step_index, every, out_blocks, x, modulation,
         jnp.transpose(router_weight, (1, 0)), picks_t, per, share_len, few,
     )
+    outgoing, early = lax.optimization_barrier((outgoing, early))
     expert_tokens = over_seq(outgoing)
     blocks = (same_half,) + tuple(early) + late
     hidden = up_call(expert_tokens, up_full, per)

time: 251 us -> 257 us (1.024)
  local copies, waits for them, and re-layouts: 3.21 us -> 6.54 us
  waiting for transfers between devices: 84.6 us -> 87.9 us
    ppermute x8, waiting for transfers between devices: 44.6 us -> 13.6 us  [from_turn(): lax.ppermute(values, 'ffn', [((i + turn) % ffn, i) for i in range(ffn)])]
    ppermute x3, waiting for transfers between devices: 2.11 us -> 22.8 us  [from_lane(): return lax.ppermute(values, 'seq', pairs)]
    all_to_all x3, waiting for transfers between devices: 31.8 us -> 44.8 us  [over_seq(): lax.all_to_all(values, 'seq', split_axis=0, concat_axis=0, tiled=True)]
  transfers between devices with their start and end apart: 21 -> 21, of which waited for: 11 -> 13; matrix products, arithmetic and copies ran while one was open for 1% -> 2% of each run, Pallas kernels for 15% -> 15%
where the time goes in v8:
time: 257 us; the launch traced here: 256 us
  waiting for transfers between devices  87.9 us (34%)
  starting transfers between devices  63.3 us (25%)
  blocking collectives  43.6 us (17%)
  Pallas kernels  40.9 us (16%)
  between operations  14.2 us (6%)
  local copies, waits for them, and re-layouts  6.54 us (3%)
    all_to_all x3, waiting for transfers between devices, over_seq(): lax.all_to_all(values, 'seq', split_axis=0, concat_axis=0, tiled=True)  44.8 us
    all_to_all x3, starting transfers between devices, over_seq(): lax.all_to_all(values, 'seq', split_axis=0, concat_axis=0, tiled=True)  33.2 us
    all_to_all x1, blocking collectives, over_seq(): lax.all_to_all(values, 'seq', split_axis=0, concat_axis=0, tiled=True)  23.8 us
    ppermute x3, waiting for transfers between devices, from_lane(): return lax.ppermute(values, 'seq', pairs)  22.8 us
    all_to_all x1, blocking collectives, over_ffn(): lax.all_to_all(values, 'ffn', split_axis=0, concat_axis=0, tiled=True)  19.8 us
    ppermute x8, waiting for transfers between devices, from_turn(): lax.ppermute(values, 'ffn', [((i + turn) % ffn, i) for i in range(ffn)])  13.6 us
    pallas_call x1, Pallas kernels, mix_call(): pl.pallas_call(functools.partial(mix_kernel, per, len(blocks) // 2, parts...  12.1 us
    all_to_all x1, starting transfers between devices, on_device(): lax.all_to_all(attended, ('seq', 'ffn'), split_axis=0, concat_axis=0, til...  12 us
  transfers between devices with their start and end apart: 21, of which 13 were waited for; matrix products, arithmetic and copies ran while one was open for 2% of the time, Pallas kernels for 15%

profile of v8, /device:TPU:8, one launch (start us, length us, event | category | flops | bytes accessed | tf_op | source)
XLA Modules:
  0.0 256.4 jit_solution(11873207052817754097)
XLA Ops:
  7.8 2.8 %collective-permute-start = (bf16[32,2048]{1,0:T(8,128)(2,1)S(1)}, bf16[32,2048]{1,0:T(8,128)(2,1)S(1)}, u32[]{:S(2)}, u32[]{:S(2)}) collective-permute-start(bf16[32,2048]{1,0:T(8,128)(2,1)S(1)} %constant_dynamic-slice_fusion), channel_id=1, source_target_pairs={{1,0},{2,1},{3,2},{0,3},{5,4},{6,5},{7,6},{4,7},{9,8},{10,9},{11,1... | collective-permute-start | bytes 393224 | tf_op jit(solution)/shard_map/ppermute | solution.py:487
  12.9 6.3 %qkv.1 = bf16[512,768]{1,0:T(8,128)(2,1)} custom-call(s32[1]{0:T(128)S(6)} %copy.15.step_ref, bf16[512,2048]{1,0:T(8,128)(2,1)} %bitcast.35, f32[16,12288]{1,0:T(8,128)} %gate_ref.3, bf16[3,2048,256]{2,1,0:T(8,128)(2,1)} %bitcast.38, f32[2,128]{1,0:T(2,128)} %gain_ref.1), custom_call_target="tpu_custom_call" | custom-call | tf_op jit(solution)/shard_map/qkv/pallas_call | solution.py:71
  19.9 12.1 %all-to-all-start = ((bf16[64,8,768]{2,1,0:T(8,128)(2,1)}), bf16[64,8,768]{2,1,0:T(8,128)(2,1)S(1)}, u32[]{:S(2)}, u32[]{:S(2)}) async-start(bf16[64,8,768]{2,1,0:T(8,128)(2,1)} %bitcast.37), calls=%async_computation | async-start | bytes 1572864 | tf_op jit(solution)/shard_map/all_to_all | solution.py:469
  34.7 2.3 collective-permute-start.3
  36.9 16.9 %all-to-all-done = bf16[64,8,768]{2,1,0:T(8,128)(2,1)S(1)} async-done(((bf16[64,8,768]{2,1,0:T(8,128)(2,1)}), bf16[64,8,768]{2,1,0:T(8,128)(2,1)S(1)}, u32[]{:S(2)}, u32[]{:S(2)}) %all-to-all-start) | async-done | bytes 786464 | tf_op jit(solution)/shard_map/all_to_all | solution.py:469
  53.9 2.1 attention.1
  56.8 12.0 %all-to-all-start.1 = ((bf16[256,8,256]{2,1,0:T(8,128)(2,1)}), bf16[256,8,256]{2,1,0:T(8,128)(2,1)}, u32[]{:S(2)}, u32[]{:S(2)}) async-start(bf16[256,8,256]{2,1,0:T(8,128)(2,1)} %bitcast.7), calls=%async_computation.1 | async-start | bytes 2097152 | tf_op jit(solution)/shard_map/all_to_all | solution.py:514
  68.8 2.3 collective-permute-start.4
  71.1 21.3 %collective-permute-done.4.refs_1_ = bf16[128,2048]{1,0:T(8,128)(2,1)} collective-permute-done((bf16[128,2048]{1,0:T(8,128)(2,1)}, bf16[128,2048]{1,0:T(8,128)(2,1)}, u32[]{:S(2)}, u32[]{:S(2)}) %collective-permute-start.4) | collective-permute-done | bytes 524320 | tf_op jit(solution)/shard_map/ppermute | solution.py:508
  93.6 1.1 dynamic-slice_bitcast_fusion.1
  94.7 2.5 collective-permute-start.10
  97.2 1.1 all-to-all-done.1
  98.3 12.1 %mix.1 = (bf16[512,1024]{1,0:T(8,128)(2,1)}, f32[512,64]{1,0:T(8,128)}, f32[128,2048]{1,0:T(8,128)}) custom-call(s32[1]{0:T(128)} %bitcast.rank_ref, s32[1]{0:T(128)} %bitcast.1.core_ref, s32[1]{0:T(128)} %bitcast.2.lane_ref, s32[1]{0:T(128)S(6)} %copy.15.step_ref, bf16[2048,256]{1,0:T(8,128)(2,1)} %bitcast.8.att_ref, bf16[512,2048]{1,0:T(8,128)(2,1)} %bitcast.36, ...), custom_call_target="tpu_custom_call" | custom-call | tf_op jit(solution)/shard_map/mix/pallas_call | solution.py:266
  110.4 9.5 %collective-permute-done.10.refs_1_ = bf16[256,1024]{1,0:T(8,128)(2,1)S(1)} collective-permute-done((bf16[256,1024]{1,0:T(8,128)(2,1)}, bf16[256,1024]{1,0:T(8,128)(2,1)S(1)}, u32[]{:S(2)}, u32[]{:S(2)}) %collective-permute-start.10) | collective-permute-done | bytes 524320 | tf_op jit(solution)/shard_map/ppermute | solution.py:487
  119.9 10.8 %all-to-all-start.2 = ((bf16[64,8,1024]{2,1,0:T(8,128)(2,1)}), bf16[64,8,1024]{2,1,0:T(8,128)(2,1)}, u32[]{:S(2)}, u32[]{:S(2)}) async-start(bf16[64,8,1024]{2,1,0:T(8,128)(2,1)} %bitcast.41), calls=%async_computation.2 | async-start | bytes 2097152 | tf_op jit(solution)/shard_map/all_to_all | solution.py:469
  130.7 1.3 dynamic-slice_bitcast_fusion.refs_0_
  132.0 2.7 %collective-permute-start.12 = (bf16[512,1024]{1,0:T(8,128)(2,1)S(1)}, bf16[512,1024]{1,0:T(8,128)(2,1)S(1)}, u32[]{:S(2)}, u32[]{:S(2)}) collective-permute-start(bf16[512,1024]{1,0:T(8,128)(2,1)S(1)} %dynamic-slice_bitcast_fusion.refs_0_), channel_id=1, source_target_pairs={{2,0},{3,1},{0,2},{1,3},{6,4},{7,5},{4,6},{5,7},{10,8},{11,9},{8,1... | collective-permute-start | bytes 3145736 | tf_op jit(solution)/shard_map/ppermute | solution.py:487
  134.7 1.4 collective-permute-start.13
  136.7 21.0 %all-to-all-done.2 = bf16[64,8,1024]{2,1,0:T(8,128)(2,1)} async-done(((bf16[64,8,1024]{2,1,0:T(8,128)(2,1)}), bf16[64,8,1024]{2,1,0:T(8,128)(2,1)}, u32[]{:S(2)}, u32[]{:S(2)}) %all-to-all-start.2) | async-done | bytes 1048608 | tf_op jit(solution)/shard_map/all_to_all | solution.py:469
  157.7 7.6 %up.1.hid_ref = bf16[256,2048]{1,0:T(8,128)(2,1)} custom-call(bf16[512,1024]{1,0:T(8,128)(2,1)} %bitcast.16.rows_ref, bf16[4,2048,512]{2,1,0:T(8,128)(2,1)} %all-gather.2.cloned.1.call-done.w_ref), custom_call_target="tpu_custom_call" | custom-call | tf_op jit(solution)/shard_map/up/pallas_call | solution.py:321
  165.3 1.4 collective-permute-start.15
  166.7 2.5 collective-permute-done.13.refs_4_
  170.2 1.0 copy-done.7
  171.1 4.9 %down.2 = bf16[512,512]{1,0:T(8,128)(2,1)} custom-call(s32[1]{0:T(128)} %bitcast.rank_ref, bf16[256,2048]{1,0:T(8,128)(2,1)} %up.1.hid_ref, bf16[512,1024]{1,0:T(8,128)(2,1)} %copy-done.6, bf16[256,1024]{1,0:T(8,128)(2,1)} %copy-done.8, bf16[256,1024]{1,0:T(8,128)(2,1)} %collective-permute-done.11.refs_2_, bf16[512,1024]{1,0:T(8,128)(2,1)} %copy-done.7, ...), custom_call_target="tpu_custom_call" | custom-call | tf_op jit(solution)/shard_map/down/pallas_call | solution.py:362
  176.1 10.3 %all-to-all-start.3 = ((bf16[64,8,512]{2,1,0:T(8,128)(2,1)}), bf16[64,8,512]{2,1,0:T(8,128)(2,1)S(1)}, u32[]{:S(2)}, u32[]{:S(2)}) async-start(bf16[64,8,512]{2,1,0:T(8,128)(2,1)} %bitcast.39), calls=%async_computation.3 | async-start | bytes 1048576 | tf_op jit(solution)/shard_map/all_to_all | solution.py:469
  186.4 4.9 %collective-permute-done.15.hid_ref = bf16[256,2048]{1,0:T(8,128)(2,1)} collective-permute-done((bf16[256,2048]{1,0:T(8,128)(2,1)}, bf16[256,2048]{1,0:T(8,128)(2,1)}, u32[]{:S(2)}, u32[]{:S(2)}) %collective-permute-start.15) | collective-permute-done | bytes 1048608 | tf_op jit(solution)/shard_map/ppermute | solution.py:523
  191.3 4.9 %down.3 = bf16[512,512]{1,0:T(8,128)(2,1)} custom-call(s32[1]{0:T(128)} %bitcast.rank_ref, bf16[256,2048]{1,0:T(8,128)(2,1)} %collective-permute-done.15.hid_ref, bf16[512,1024]{1,0:T(8,128)(2,1)} %copy-done.6, bf16[256,1024]{1,0:T(8,128)(2,1)} %copy-done.8, bf16[256,1024]{1,0:T(8,128)(2,1)} %collective-permute-done.11.refs_2_, bf16[512,1024]{1,0:T(8,128)(2,1)} %copy-done.7, ...), custom_call_target="tpu_custom_call" | custom-call | tf_op jit(solution)/shard_map/down/pallas_call | solution.py:362
  196.3 6.8 %all-to-all-done.3 = bf16[64,8,512]{2,1,0:T(8,128)(2,1)S(1)} async-done(((bf16[64,8,512]{2,1,0:T(8,128)(2,1)}), bf16[64,8,512]{2,1,0:T(8,128)(2,1)S(1)}, u32[]{:S(2)}, u32[]{:S(2)}) %all-to-all-start.3) | async-done | bytes 524320 | tf_op jit(solution)/shard_map/all_to_all | solution.py:469
  203.1 23.8 %all_to_all.64 = bf16[64,8,512]{2,1,0:T(8,128)(2,1)S(1)} all-to-all(bf16[64,8,512]{2,1,0:T(8,128)(2,1)} %bitcast.40), channel_id=1, replica_groups=mesh['seq'=64,'ffn'=4] {'seq'}, dimensions={0} | all-to-all | bytes 1048576 | tf_op jit(solution)/shard_map/all_to_all | solution.py:469
  227.0 1.7 combine.1
  228.6 19.8 %all_to_all.65.parts_ref = bf16[4,128,1024]{2,1,0:T(8,128)(2,1)S(1)} all-to-all(bf16[4,128,1024]{2,1,0:T(8,128)(2,1)S(1)} %bitcast.28), channel_id=1, replica_groups=mesh['seq'=64,'ffn'=4] {'ffn'}, dimensions={0} | all-to-all | bytes 2097152 | tf_op jit(solution)/shard_map/all_to_all | solution.py:472
  248.4 1.2 final.1
  (48 shorter events, 9.8 us)
Async XLA Ops:
  6.5 1.2 copy-start
  6.5 151.2 %all-gather.2.cloned.1.call-start = ((), (), s32[]{:S(2)}) async-start(), calls=%async_computation.6 | async-start | bytes 10485760 | tf_op jit(solution)/shard_map/all_gather | solution.py:481
  7.8 11.5 %collective-permute-start = (bf16[32,2048]{1,0:T(8,128)(2,1)S(1)}, bf16[32,2048]{1,0:T(8,128)(2,1)S(1)}, u32[]{:S(2)}, u32[]{:S(2)}) collective-permute-start(bf16[32,2048]{1,0:T(8,128)(2,1)S(1)} %constant_dynamic-slice_fusion), channel_id=1, source_target_pairs={{1,0},{2,1},{3,2},{0,3},{5,4},{6,5},{7,6},{4,7},{9,8},{10,9},{11,1... | collective-permute-start | bytes 393224 | tf_op jit(solution)/shard_map/ppermute | solution.py:487
  10.6 8.7 %collective-permute-start.1 = (bf16[32,2048]{1,0:T(8,128)(2,1)S(1)}, bf16[32,2048]{1,0:T(8,128)(2,1)S(1)}, u32[]{:S(2)}, u32[]{:S(2)}) collective-permute-start(bf16[32,2048]{1,0:T(8,128)(2,1)S(1)} %constant_dynamic-slice_fusion), channel_id=1, source_target_pairs={{2,0},{3,1},{0,2},{1,3},{6,4},{7,5},{4,6},{5,7},{10,8},{11,9},{8,1... | collective-permute-start | bytes 393224 | tf_op jit(solution)/shard_map/ppermute | solution.py:487
  11.4 8.5 %collective-permute-start.2 = (bf16[32,2048]{1,0:T(8,128)(2,1)S(1)}, bf16[32,2048]{1,0:T(8,128)(2,1)S(1)}, u32[]{:S(2)}, u32[]{:S(2)}) collective-permute-start(bf16[32,2048]{1,0:T(8,128)(2,1)S(1)} %constant_dynamic-slice_fusion), channel_id=1, source_target_pairs={{3,0},{0,1},{1,2},{2,3},{7,4},{4,5},{5,6},{6,7},{11,8},{8,9},{9,10... | collective-permute-start | bytes 393224 | tf_op jit(solution)/shard_map/ppermute | solution.py:487
  19.9 34.0 %all-to-all-start = ((bf16[64,8,768]{2,1,0:T(8,128)(2,1)}), bf16[64,8,768]{2,1,0:T(8,128)(2,1)S(1)}, u32[]{:S(2)}, u32[]{:S(2)}) async-start(bf16[64,8,768]{2,1,0:T(8,128)(2,1)} %bitcast.37), calls=%async_computation | async-start | bytes 1572864 | tf_op jit(solution)/shard_map/all_to_all | solution.py:469
  34.7 22.2 %collective-permute-start.3 = (bf16[128,2048]{1,0:T(8,128)(2,1)}, bf16[128,2048]{1,0:T(8,128)(2,1)}, u32[]{:S(2)}, u32[]{:S(2)}) collective-permute-start(bf16[128,2048]{1,0:T(8,128)(2,1)} %constant_dynamic-update-slice_fusion.refs_0_), channel_id=1, source_target_pairs={{128,0},{132,4},{136,8},{140,12},{144,16},{148,20},{152,24},{156,2... | collective-permute-start | bytes 1572872 | tf_op jit(solution)/shard_map/ppermute | solution.py:508
  56.0 37.6 %copy-start.9 = (bf16[1,512,2048]{2,1,0:T(8,128)(2,1)S(1)}, bf16[1,512,2048]{2,1,0:T(8,128)(2,1)}, u32[]{:S(2)}) copy-start(bf16[1,512,2048]{2,1,0:T(8,128)(2,1)} %param.19) | copy-start | bytes 6291460
  56.8 41.5 %all-to-all-start.1 = ((bf16[256,8,256]{2,1,0:T(8,128)(2,1)}), bf16[256,8,256]{2,1,0:T(8,128)(2,1)}, u32[]{:S(2)}, u32[]{:S(2)}) async-start(bf16[256,8,256]{2,1,0:T(8,128)(2,1)} %bitcast.7), calls=%async_computation.1 | async-start | bytes 2097152 | tf_op jit(solution)/shard_map/all_to_all | solution.py:514
  68.8 23.6 %collective-permute-start.4 = (bf16[128,2048]{1,0:T(8,128)(2,1)}, bf16[128,2048]{1,0:T(8,128)(2,1)}, u32[]{:S(2)}, u32[]{:S(2)}) collective-permute-start(bf16[128,2048]{1,0:T(8,128)(2,1)} %constant_dynamic-update-slice_fusion.refs_0_), channel_id=1, source_target_pairs={{64,0},{68,4},{72,8},{76,12},{80,16},{84,20},{88,24},{92,28},{96,3... | collective-permute-start | bytes 1572872 | tf_op jit(solution)/shard_map/ppermute | solution.py:508
  71.1 22.0 %collective-permute-start.5 = (bf16[128,2048]{1,0:T(8,128)(2,1)}, bf16[128,2048]{1,0:T(8,128)(2,1)}, u32[]{:S(2)}, u32[]{:S(2)}) collective-permute-start(bf16[128,2048]{1,0:T(8,128)(2,1)} %constant_dynamic-update-slice_fusion.refs_0_), channel_id=1, source_target_pairs={{192,0},{196,4},{200,8},{204,12},{208,16},{212,20},{216,24},{220,2... | collective-permute-start | bytes 1572872 | tf_op jit(solution)/shard_map/ppermute | solution.py:508
  71.1 26.1 %collective-permute-start.6 = (bf16[128,2048]{1,0:T(8,128)(2,1)}, bf16[128,2048]{1,0:T(8,128)(2,1)}, u32[]{:S(2)}, u32[]{:S(2)}) collective-permute-start(bf16[128,2048]{1,0:T(8,128)(2,1)} %constant_dynamic-update-slice_fusion.refs_0_), channel_id=1, source_target_pairs={{0,4},{4,0},{8,12},{12,8},{16,20},{20,16},{24,28},{28,24},{32,36},... | collective-permute-start | bytes 1572872 | tf_op jit(solution)/shard_map/ppermute | solution.py:513
  92.4 4.8 %collective-permute-start.7 = (bf16[128,2048]{1,0:T(8,128)(2,1)}, bf16[128,2048]{1,0:T(8,128)(2,1)}, u32[]{:S(2)}, u32[]{:S(2)}) collective-permute-start(bf16[128,2048]{1,0:T(8,128)(2,1)} %collective-permute-done.4.refs_1_), channel_id=1, source_target_pairs={{0,4},{4,0},{8,12},{12,8},{16,20},{20,16},{24,28},{28,24},{32,36},... | collective-permute-start | bytes 1572872 | tf_op jit(solution)/shard_map/ppermute | solution.py:513
  93.1 4.1 %collective-permute-start.9 = (bf16[128,2048]{1,0:T(8,128)(2,1)}, bf16[128,2048]{1,0:T(8,128)(2,1)}, u32[]{:S(2)}, u32[]{:S(2)}) collective-permute-start(bf16[128,2048]{1,0:T(8,128)(2,1)} %collective-permute-done.5.refs_3_), channel_id=1, source_target_pairs={{0,4},{4,0},{8,12},{12,8},{16,20},{20,16},{24,28},{28,24},{32,36},... | collective-permute-start | bytes 1572872 | tf_op jit(solution)/shard_map/ppermute | solution.py:513
  93.1 4.1 %collective-permute-start.8 = (bf16[128,2048]{1,0:T(8,128)(2,1)}, bf16[128,2048]{1,0:T(8,128)(2,1)}, u32[]{:S(2)}, u32[]{:S(2)}) collective-permute-start(bf16[128,2048]{1,0:T(8,128)(2,1)} %collective-permute-done.3.refs_2_), channel_id=1, source_target_pairs={{0,4},{4,0},{8,12},{12,8},{16,20},{20,16},{24,28},{28,24},{32,36},... | collective-permute-start | bytes 1572872 | tf_op jit(solution)/shard_map/ppermute | solution.py:513
  94.7 25.2 %collective-permute-start.10 = (bf16[256,1024]{1,0:T(8,128)(2,1)}, bf16[256,1024]{1,0:T(8,128)(2,1)S(1)}, u32[]{:S(2)}, u32[]{:S(2)}) collective-permute-start(bf16[256,1024]{1,0:T(8,128)(2,1)} %get-tuple-element.32), channel_id=1, source_target_pairs={{1,0},{2,1},{3,2},{0,3},{5,4},{6,5},{7,6},{4,7},{9,8},{10,9},{11,1... | collective-permute-start | bytes 1572872 | tf_op jit(solution)/shard_map/ppermute | solution.py:487
  97.1 22.8 %collective-permute-start.11 = (bf16[256,1024]{1,0:T(8,128)(2,1)}, bf16[256,1024]{1,0:T(8,128)(2,1)}, u32[]{:S(2)}, u32[]{:S(2)}) collective-permute-start(bf16[256,1024]{1,0:T(8,128)(2,1)} %get-tuple-element.32), channel_id=1, source_target_pairs={{3,0},{0,1},{1,2},{2,3},{7,4},{4,5},{5,6},{6,7},{11,8},{8,9},{9,10... | collective-permute-start | bytes 1572872 | tf_op jit(solution)/shard_map/ppermute | solution.py:487
  119.8 10.9 %copy-start.8 = (bf16[256,1024]{1,0:T(8,128)(2,1)}, bf16[256,1024]{1,0:T(8,128)(2,1)S(1)}, u32[]{:S(2)}) copy-start(bf16[256,1024]{1,0:T(8,128)(2,1)S(1)} %collective-permute-done.10.refs_1_) | copy-start | bytes 1572868
  119.9 37.8 %all-to-all-start.2 = ((bf16[64,8,1024]{2,1,0:T(8,128)(2,1)}), bf16[64,8,1024]{2,1,0:T(8,128)(2,1)}, u32[]{:S(2)}, u32[]{:S(2)}) async-start(bf16[64,8,1024]{2,1,0:T(8,128)(2,1)} %bitcast.41), calls=%async_computation.2 | async-start | bytes 2097152 | tf_op jit(solution)/shard_map/all_to_all | solution.py:469
  132.0 33.3 %copy-start.6 = (bf16[512,1024]{1,0:T(8,128)(2,1)}, bf16[512,1024]{1,0:T(8,128)(2,1)S(1)}, u32[]{:S(2)}) copy-start(bf16[512,1024]{1,0:T(8,128)(2,1)S(1)} %dynamic-slice_bitcast_fusion.refs_0_) | copy-start | bytes 3145732
  132.0 38.1 %collective-permute-start.12 = (bf16[512,1024]{1,0:T(8,128)(2,1)S(1)}, bf16[512,1024]{1,0:T(8,128)(2,1)S(1)}, u32[]{:S(2)}, u32[]{:S(2)}) collective-permute-start(bf16[512,1024]{1,0:T(8,128)(2,1)S(1)} %dynamic-slice_bitcast_fusion.refs_0_), channel_id=1, source_target_pairs={{2,0},{3,1},{0,2},{1,3},{6,4},{7,5},{4,6},{5,7},{10,8},{11,9},{8,1... | collective-permute-start | bytes 3145736 | tf_op jit(solution)/shard_map/ppermute | solution.py:487
  134.7 34.5 %collective-permute-start.13 = (bf16[256,1024]{1,0:T(8,128)(2,1)}, bf16[256,1024]{1,0:T(8,128)(2,1)}, u32[]{:S(2)}, u32[]{:S(2)}) collective-permute-start(bf16[256,1024]{1,0:T(8,128)(2,1)} %get-tuple-element.31), channel_id=1, source_target_pairs={{1,0},{2,1},{3,2},{0,3},{5,4},{6,5},{7,6},{4,7},{9,8},{10,9},{11,1... | collective-permute-start | bytes 1572872 | tf_op jit(solution)/shard_map/ppermute | solution.py:487
  136.2 34.0 %collective-permute-start.14 = (bf16[256,1024]{1,0:T(8,128)(2,1)}, bf16[256,1024]{1,0:T(8,128)(2,1)}, u32[]{:S(2)}, u32[]{:S(2)}) collective-permute-start(bf16[256,1024]{1,0:T(8,128)(2,1)} %get-tuple-element.31), channel_id=1, source_target_pairs={{3,0},{0,1},{1,2},{2,3},{7,4},{4,5},{5,6},{6,7},{11,8},{8,9},{9,10... | collective-permute-start | bytes 1572872 | tf_op jit(solution)/shard_map/ppermute | solution.py:487
  165.3 26.0 %collective-permute-start.15 = (bf16[256,2048]{1,0:T(8,128)(2,1)}, bf16[256,2048]{1,0:T(8,128)(2,1)}, u32[]{:S(2)}, u32[]{:S(2)}) collective-permute-start(bf16[256,2048]{1,0:T(8,128)(2,1)} %up.1.hid_ref), channel_id=1, source_target_pairs={{0,1},{1,0},{2,3},{3,2},{4,5},{5,4},{6,7},{7,6},{8,9},{9,8},{10,11... | collective-permute-start | bytes 3145736 | tf_op jit(solution)/shard_map/ppermute | solution.py:523
  170.2 1.0 copy-start.7
  176.1 27.0 %all-to-all-start.3 = ((bf16[64,8,512]{2,1,0:T(8,128)(2,1)}), bf16[64,8,512]{2,1,0:T(8,128)(2,1)S(1)}, u32[]{:S(2)}, u32[]{:S(2)}) async-start(bf16[64,8,512]{2,1,0:T(8,128)(2,1)} %bitcast.39), calls=%async_computation.3 | async-start | bytes 1048576 | tf_op jit(solution)/shard_map/all_to_all | solution.py:469
  186.4 40.5 %copy-start.3 = (f32[512,64]{1,0:T(8,128)S(1)}, f32[512,64]{1,0:T(8,128)}, u32[]{:S(2)}) copy-start(f32[512,64]{1,0:T(8,128)} %get-tuple-element.26.gates_ref) | copy-start | bytes 393220
  186.4 40.5 %copy-start.4 = (s32[64,1,16]{0,2,1:T(8,128)S(1)}, s32[64,1,16]{0,2,1:T(8,128)}, u32[]{:S(2)}) copy-start(s32[64,1,16]{0,2,1:T(8,128)} %param.20) | copy-start | bytes 12292
  186.4 40.5 %copy-start.5 = (s32[64,1]{0,1:T(1,128)S(1)}, s32[64,1]{0,1:T(1,128)}, u32[]{:S(2)}) copy-start(s32[64,1]{0,1:T(1,128)} %param.21) | copy-start | bytes 772
  226.9 21.5 %copy-start.1 = (f32[16,12288]{1,0:T(8,128)S(1)}, f32[16,12288]{1,0:T(8,128)}, u32[]{:S(2)}) copy-start(f32[16,12288]{1,0:T(8,128)} %gate_ref.3) | copy-start | bytes 2359300
  226.9 21.4 %copy-start.2 = (f32[128,2048]{1,0:T(8,128)S(1)}, f32[128,2048]{1,0:T(8,128)}, u32[]{:S(2)}) copy-start(f32[128,2048]{1,0:T(8,128)} %get-tuple-element.25.share_ref) | copy-start | bytes 3145732
Sparse Core Ops, SparseCore 0:
  9.2 110.7 all-gather.1

commit v9 on v8

--- a/solution.py
+++ b/solution.py
@@ -328,7 +328,7 @@
         out_specs=pl.BlockSpec((count, units), lambda i: (0, i)),
         out_shape=jax.ShapeDtypeStruct((count, parts * units), BF16),
         scratch_shapes=[pltpu.VMEM((count, width), BF16)],
-        compiler_params=params(60),
+        compiler_params=params(62),
         name="up",
     )(rows, w)
 
@@ -366,7 +366,7 @@
         + [pl.BlockSpec((block.shape[0], cols), lambda i: (0, i)) for block in blocks],
         out_specs=pl.BlockSpec((2 * rows, cols), lambda i: (0, 0)),
         out_shape=jax.ShapeDtypeStruct((2 * rows, cols), BF16),
-        compiler_params=params(60),
+        compiler_params=params(62),
         name="down",
     )(rank, hidden, *blocks)
 
@@ -512,11 +512,11 @@
     swap = [(i, i ^ 1) for i in range(seq)]
     out_blocks = out_blocks + [lax.ppermute(b, "seq", swap) for b in out_blocks]
     every = lax.all_to_all(attended, ("seq", "ffn"), split_axis=0, concat_axis=0, tiled=True)
+    every, early = lax.optimization_barrier((every, early))
     outgoing, gates, share = mix_call(
         rank_arr, core.reshape(1), lane.reshape(1), step_index, every, out_blocks, x, modulation,
         jnp.transpose(router_weight, (1, 0)), picks_t, per, share_len, few,
     )
-    outgoing, early = lax.optimization_barrier((outgoing, early))
     expert_tokens = over_seq(outgoing)
     blocks = (same_half,) + tuple(early) + late
     hidden = up_call(expert_tokens, up_full, per)

time: 257 us -> 257 us (level)
  waiting for transfers between devices: 87.9 us -> 92 us
  starting transfers between devices: 63.3 us -> 60.6 us
    ppermute x8, waiting for transfers between devices: 13.6 us -> 20.3 us  [from_turn(): lax.ppermute(values, 'ffn', [((i + turn) % ffn, i) for i in range(ffn)])]
    ppermute x3, waiting for transfers between devices: 22.8 us -> 19.8 us  [from_lane(): return lax.ppermute(values, 'seq', pairs)]
  transfers between devices with their start and end apart: 21 -> 21, of which waited for: 13 -> 12; matrix products, arithmetic and copies ran while one was open for 2% -> 2% of each run, Pallas kernels for 15% -> 15%
where the time goes in v9:
time: 257 us; the launch traced here: 256 us
  waiting for transfers between devices  92 us (36%)
  starting transfers between devices  60.6 us (24%)
  blocking collectives  42.6 us (17%)
  Pallas kernels  40.9 us (16%)
  between operations  14.3 us (6%)
  local copies, waits for them, and re-layouts  5.97 us (2%)
    all_to_all x3, waiting for transfers between devices, over_seq(): lax.all_to_all(values, 'seq', split_axis=0, concat_axis=0, tiled=True)  45.8 us
    all_to_all x3, starting transfers between devices, over_seq(): lax.all_to_all(values, 'seq', split_axis=0, concat_axis=0, tiled=True)  33.6 us
    all_to_all x1, blocking collectives, over_seq(): lax.all_to_all(values, 'seq', split_axis=0, concat_axis=0, tiled=True)  23.8 us
    ppermute x8, waiting for transfers between devices, from_turn(): lax.ppermute(values, 'ffn', [((i + turn) % ffn, i) for i in range(ffn)])  20.3 us
    ppermute x3, waiting for transfers between devices, from_lane(): return lax.ppermute(values, 'seq', pairs)  19.8 us
    all_to_all x1, blocking collectives, over_ffn(): lax.all_to_all(values, 'ffn', split_axis=0, concat_axis=0, tiled=True)  18.8 us
    pallas_call x1, Pallas kernels, mix_call(): pl.pallas_call(functools.partial(mix_kernel, per, len(blocks) // 2, parts...  12.1 us
    all_to_all x1, starting transfers between devices, on_device(): lax.all_to_all(attended, ('seq', 'ffn'), split_axis=0, concat_axis=0, til...  12 us
  transfers between devices with their start and end apart: 21, of which 12 were waited for; matrix products, arithmetic and copies ran while one was open for 2% of the time, Pallas kernels for 15%

profile of v9, /device:TPU:8, one launch (start us, length us, event | category | flops | bytes accessed | tf_op | source)
XLA Modules:
  0.0 256.4 jit_solution(5732905387762777863)
XLA Ops:
  7.8 2.8 %collective-permute-start = (bf16[32,2048]{1,0:T(8,128)(2,1)S(1)}, bf16[32,2048]{1,0:T(8,128)(2,1)S(1)}, u32[]{:S(2)}, u32[]{:S(2)}) collective-permute-start(bf16[32,2048]{1,0:T(8,128)(2,1)S(1)} %constant_dynamic-slice_fusion), channel_id=1, source_target_pairs={{1,0},{2,1},{3,2},{0,3},{5,4},{6,5},{7,6},{4,7},{9,8},{10,9},{11,1... | collective-permute-start | bytes 393224 | tf_op jit(solution)/shard_map/ppermute | solution.py:487
  12.9 6.3 %qkv.1 = bf16[512,768]{1,0:T(8,128)(2,1)} custom-call(s32[1]{0:T(128)S(6)} %copy.15.step_ref, bf16[512,2048]{1,0:T(8,128)(2,1)} %bitcast.35, f32[16,12288]{1,0:T(8,128)} %gate_ref.3, bf16[3,2048,256]{2,1,0:T(8,128)(2,1)} %bitcast.38, f32[2,128]{1,0:T(2,128)} %gain_ref.1), custom_call_target="tpu_custom_call" | custom-call | tf_op jit(solution)/shard_map/qkv/pallas_call | solution.py:71
  19.9 12.1 %all-to-all-start = ((bf16[64,8,768]{2,1,0:T(8,128)(2,1)}), bf16[64,8,768]{2,1,0:T(8,128)(2,1)S(1)}, u32[]{:S(2)}, u32[]{:S(2)}) async-start(bf16[64,8,768]{2,1,0:T(8,128)(2,1)} %bitcast.37), calls=%async_computation | async-start | bytes 1572864 | tf_op jit(solution)/shard_map/all_to_all | solution.py:469
  34.7 2.3 collective-permute-start.3
  36.9 16.9 %all-to-all-done = bf16[64,8,768]{2,1,0:T(8,128)(2,1)S(1)} async-done(((bf16[64,8,768]{2,1,0:T(8,128)(2,1)}), bf16[64,8,768]{2,1,0:T(8,128)(2,1)S(1)}, u32[]{:S(2)}, u32[]{:S(2)}) %all-to-all-start) | async-done | bytes 786464 | tf_op jit(solution)/shard_map/all_to_all | solution.py:469
  53.9 2.1 attention.1
  56.8 12.0 %all-to-all-start.1 = ((bf16[256,8,256]{2,1,0:T(8,128)(2,1)}), bf16[256,8,256]{2,1,0:T(8,128)(2,1)}, u32[]{:S(2)}, u32[]{:S(2)}) async-start(bf16[256,8,256]{2,1,0:T(8,128)(2,1)} %bitcast.7), calls=%async_computation.1 | async-start | bytes 2097152 | tf_op jit(solution)/shard_map/all_to_all | solution.py:514
  68.8 2.3 collective-permute-start.6
  71.1 0.9 dynamic-slice_bitcast_fusion.1
  72.0 2.5 collective-permute-start.4
  74.5 17.9 %collective-permute-done.6.refs_1_ = bf16[128,2048]{1,0:T(8,128)(2,1)} collective-permute-done((bf16[128,2048]{1,0:T(8,128)(2,1)}, bf16[128,2048]{1,0:T(8,128)(2,1)}, u32[]{:S(2)}, u32[]{:S(2)}) %collective-permute-start.6) | collective-permute-done | bytes 524320 | tf_op jit(solution)/shard_map/ppermute | solution.py:508
  92.4 1.1 collective-permute-done.7.refs_3_
  93.4 12.3 %collective-permute-done.4.refs_1_ = bf16[256,1024]{1,0:T(8,128)(2,1)S(1)} collective-permute-done((bf16[256,1024]{1,0:T(8,128)(2,1)S(1)}, bf16[256,1024]{1,0:T(8,128)(2,1)S(1)}, u32[]{:S(2)}, u32[]{:S(2)}) %collective-permute-start.4) | collective-permute-done | bytes 524320 | tf_op jit(solution)/shard_map/ppermute | solution.py:487
  105.7 2.8 %collective-permute-done.5.refs_2_ = bf16[256,1024]{1,0:T(8,128)(2,1)} collective-permute-done((bf16[256,1024]{1,0:T(8,128)(2,1)S(1)}, bf16[256,1024]{1,0:T(8,128)(2,1)}, u32[]{:S(2)}, u32[]{:S(2)}) %collective-permute-start.5) | collective-permute-done | bytes 524320 | tf_op jit(solution)/shard_map/ppermute | solution.py:487
  109.4 12.1 %mix.1 = (bf16[512,1024]{1,0:T(8,128)(2,1)}, f32[512,64]{1,0:T(8,128)}, f32[128,2048]{1,0:T(8,128)}) custom-call(s32[1]{0:T(128)} %bitcast.rank_ref, s32[1]{0:T(128)} %bitcast.1.core_ref, s32[1]{0:T(128)} %bitcast.2.lane_ref, s32[1]{0:T(128)S(6)} %copy.15.step_ref, bf16[2048,256]{1,0:T(8,128)(2,1)} %bitcast.8.att_ref, bf16[512,2048]{1,0:T(8,128)(2,1)} %bitcast.36, ...), custom_call_target="tpu_custom_call" | custom-call | tf_op jit(solution)/shard_map/mix/pallas_call | solution.py:266
  121.5 10.6 %all-to-all-start.2 = ((bf16[64,8,1024]{2,1,0:T(8,128)(2,1)}), bf16[64,8,1024]{2,1,0:T(8,128)(2,1)}, u32[]{:S(2)}, u32[]{:S(2)}) async-start(bf16[64,8,1024]{2,1,0:T(8,128)(2,1)} %bitcast.41), calls=%async_computation.2 | async-start | bytes 2097152 | tf_op jit(solution)/shard_map/all_to_all | solution.py:469
  132.1 1.1 dynamic-slice_bitcast_fusion.refs_0_
  133.2 1.4 collective-permute-start.12
  134.6 1.4 collective-permute-start.13
  136.6 22.5 %all-to-all-done.2 = bf16[64,8,1024]{2,1,0:T(8,128)(2,1)} async-done(((bf16[64,8,1024]{2,1,0:T(8,128)(2,1)}), bf16[64,8,1024]{2,1,0:T(8,128)(2,1)}, u32[]{:S(2)}, u32[]{:S(2)}) %all-to-all-start.2) | async-done | bytes 1048608 | tf_op jit(solution)/shard_map/all_to_all | solution.py:469
  159.1 7.6 %up.1.hid_ref = bf16[256,2048]{1,0:T(8,128)(2,1)} custom-call(bf16[512,1024]{1,0:T(8,128)(2,1)} %bitcast.16.rows_ref, bf16[4,2048,512]{2,1,0:T(8,128)(2,1)} %all-gather.2.cloned.1.call-done.w_ref), custom_call_target="tpu_custom_call" | custom-call | tf_op jit(solution)/shard_map/up/pallas_call | solution.py:321
  166.8 3.6 %collective-permute-done.13.refs_4_ = bf16[256,1024]{1,0:T(8,128)(2,1)S(1)} collective-permute-done((bf16[256,1024]{1,0:T(8,128)(2,1)}, bf16[256,1024]{1,0:T(8,128)(2,1)S(1)}, u32[]{:S(2)}, u32[]{:S(2)}) %collective-permute-start.13) | collective-permute-done | bytes 524320 | tf_op jit(solution)/shard_map/ppermute | solution.py:487
  170.5 1.0 collective-permute-done.14.refs_5_
  171.5 4.9 %down.2 = bf16[512,512]{1,0:T(8,128)(2,1)} custom-call(s32[1]{0:T(128)} %bitcast.rank_ref, bf16[256,2048]{1,0:T(8,128)(2,1)} %up.1.hid_ref, bf16[512,1024]{1,0:T(8,128)(2,1)} %dynamic-slice_bitcast_fusion.refs_0_, bf16[256,1024]{1,0:T(8,128)(2,1)} %copy-done.6, bf16[256,1024]{1,0:T(8,128)(2,1)} %collective-permute-done.5.refs_2_, ...), custom_call_target="tpu_custom_call" | custom-call | tf_op jit(solution)/shard_map/down/pallas_call | solution.py:362
  176.4 10.9 %all-to-all-start.3 = ((bf16[64,8,512]{2,1,0:T(8,128)(2,1)}), bf16[64,8,512]{2,1,0:T(8,128)(2,1)S(1)}, u32[]{:S(2)}, u32[]{:S(2)}) async-start(bf16[64,8,512]{2,1,0:T(8,128)(2,1)} %bitcast.39), calls=%async_computation.3 | async-start | bytes 1048576 | tf_op jit(solution)/shard_map/all_to_all | solution.py:469
  187.4 5.4 %collective-permute-done.15.hid_ref = bf16[256,2048]{1,0:T(8,128)(2,1)} collective-permute-done((bf16[256,2048]{1,0:T(8,128)(2,1)}, bf16[256,2048]{1,0:T(8,128)(2,1)}, u32[]{:S(2)}, u32[]{:S(2)}) %collective-permute-start.15) | collective-permute-done | bytes 1048608 | tf_op jit(solution)/shard_map/ppermute | solution.py:523
  192.7 5.0 %down.3 = bf16[512,512]{1,0:T(8,128)(2,1)} custom-call(s32[1]{0:T(128)} %bitcast.rank_ref, bf16[256,2048]{1,0:T(8,128)(2,1)} %collective-permute-done.15.hid_ref, bf16[512,1024]{1,0:T(8,128)(2,1)} %dynamic-slice_bitcast_fusion.refs_0_, bf16[256,1024]{1,0:T(8,128)(2,1)} %copy-done.6, bf16[256,1024]{1,0:T(8,128)(2,1)} %collective-permute-done.5.refs_2_, ...), custom_call_target="tpu_custom_call" | custom-call | tf_op jit(solution)/shard_map/down/pallas_call | solution.py:362
  197.7 6.3 %all-to-all-done.3 = bf16[64,8,512]{2,1,0:T(8,128)(2,1)S(1)} async-done(((bf16[64,8,512]{2,1,0:T(8,128)(2,1)}), bf16[64,8,512]{2,1,0:T(8,128)(2,1)S(1)}, u32[]{:S(2)}, u32[]{:S(2)}) %all-to-all-start.3) | async-done | bytes 524320 | tf_op jit(solution)/shard_map/all_to_all | solution.py:469
  204.0 23.8 %all_to_all.65 = bf16[64,8,512]{2,1,0:T(8,128)(2,1)S(1)} all-to-all(bf16[64,8,512]{2,1,0:T(8,128)(2,1)} %bitcast.40), channel_id=1, replica_groups=mesh['seq'=64,'ffn'=4] {'seq'}, dimensions={0} | all-to-all | bytes 1048576 | tf_op jit(solution)/shard_map/all_to_all | solution.py:469
  227.9 1.7 combine.1
  229.5 18.8 %all_to_all.66.parts_ref = bf16[4,128,1024]{2,1,0:T(8,128)(2,1)S(1)} all-to-all(bf16[4,128,1024]{2,1,0:T(8,128)(2,1)S(1)} %bitcast.28), channel_id=1, replica_groups=mesh['seq'=64,'ffn'=4] {'ffn'}, dimensions={0} | all-to-all | bytes 2097152 | tf_op jit(solution)/shard_map/all_to_all | solution.py:472
  248.3 1.2 final.1
  (52 shorter events, 8.6 us)
Async XLA Ops:
  6.5 1.2 copy-start
  6.5 152.6 %all-gather.2.cloned.1.call-start = ((), (), s32[]{:S(2)}) async-start(), calls=%async_computation.6 | async-start | bytes 10485760 | tf_op jit(solution)/shard_map/all_gather | solution.py:481
  7.8 11.5 %collective-permute-start = (bf16[32,2048]{1,0:T(8,128)(2,1)S(1)}, bf16[32,2048]{1,0:T(8,128)(2,1)S(1)}, u32[]{:S(2)}, u32[]{:S(2)}) collective-permute-start(bf16[32,2048]{1,0:T(8,128)(2,1)S(1)} %constant_dynamic-slice_fusion), channel_id=1, source_target_pairs={{1,0},{2,1},{3,2},{0,3},{5,4},{6,5},{7,6},{4,7},{9,8},{10,9},{11,1... | collective-permute-start | bytes 393224 | tf_op jit(solution)/shard_map/ppermute | solution.py:487
  10.6 8.7 %collective-permute-start.1 = (bf16[32,2048]{1,0:T(8,128)(2,1)S(1)}, bf16[32,2048]{1,0:T(8,128)(2,1)S(1)}, u32[]{:S(2)}, u32[]{:S(2)}) collective-permute-start(bf16[32,2048]{1,0:T(8,128)(2,1)S(1)} %constant_dynamic-slice_fusion), channel_id=1, source_target_pairs={{2,0},{3,1},{0,2},{1,3},{6,4},{7,5},{4,6},{5,7},{10,8},{11,9},{8,1... | collective-permute-start | bytes 393224 | tf_op jit(solution)/shard_map/ppermute | solution.py:487
  11.4 8.5 %collective-permute-start.2 = (bf16[32,2048]{1,0:T(8,128)(2,1)S(1)}, bf16[32,2048]{1,0:T(8,128)(2,1)S(1)}, u32[]{:S(2)}, u32[]{:S(2)}) collective-permute-start(bf16[32,2048]{1,0:T(8,128)(2,1)S(1)} %constant_dynamic-slice_fusion), channel_id=1, source_target_pairs={{3,0},{0,1},{1,2},{2,3},{7,4},{4,5},{5,6},{6,7},{11,8},{8,9},{9,10... | collective-permute-start | bytes 393224 | tf_op jit(solution)/shard_map/ppermute | solution.py:487
  19.9 34.0 %all-to-all-start = ((bf16[64,8,768]{2,1,0:T(8,128)(2,1)}), bf16[64,8,768]{2,1,0:T(8,128)(2,1)S(1)}, u32[]{:S(2)}, u32[]{:S(2)}) async-start(bf16[64,8,768]{2,1,0:T(8,128)(2,1)} %bitcast.37), calls=%async_computation | async-start | bytes 1572864 | tf_op jit(solution)/shard_map/all_to_all | solution.py:469
  34.7 22.2 %collective-permute-start.3 = (bf16[128,2048]{1,0:T(8,128)(2,1)}, bf16[128,2048]{1,0:T(8,128)(2,1)}, u32[]{:S(2)}, u32[]{:S(2)}) collective-permute-start(bf16[128,2048]{1,0:T(8,128)(2,1)} %constant_dynamic-update-slice_fusion.refs_0_), channel_id=1, source_target_pairs={{128,0},{132,4},{136,8},{140,12},{144,16},{148,20},{152,24},{156,2... | collective-permute-start | bytes 1572872 | tf_op jit(solution)/shard_map/ppermute | solution.py:508
  56.0 15.1 %copy-start.8 = (bf16[1,512,2048]{2,1,0:T(8,128)(2,1)S(1)}, bf16[1,512,2048]{2,1,0:T(8,128)(2,1)}, u32[]{:S(2)}) copy-start(bf16[1,512,2048]{2,1,0:T(8,128)(2,1)} %param.19) | copy-start | bytes 6291460
  56.8 51.7 %all-to-all-start.1 = ((bf16[256,8,256]{2,1,0:T(8,128)(2,1)}), bf16[256,8,256]{2,1,0:T(8,128)(2,1)}, u32[]{:S(2)}, u32[]{:S(2)}) async-start(bf16[256,8,256]{2,1,0:T(8,128)(2,1)} %bitcast.7), calls=%async_computation.1 | async-start | bytes 2097152 | tf_op jit(solution)/shard_map/all_to_all | solution.py:514
  68.8 23.6 %collective-permute-start.6 = (bf16[128,2048]{1,0:T(8,128)(2,1)}, bf16[128,2048]{1,0:T(8,128)(2,1)}, u32[]{:S(2)}, u32[]{:S(2)}) collective-permute-start(bf16[128,2048]{1,0:T(8,128)(2,1)} %constant_dynamic-update-slice_fusion.refs_0_), channel_id=1, source_target_pairs={{64,0},{68,4},{72,8},{76,12},{80,16},{84,20},{88,24},{92,28},{96,3... | collective-permute-start | bytes 1572872 | tf_op jit(solution)/shard_map/ppermute | solution.py:508
  72.0 21.4 %collective-permute-start.7 = (bf16[128,2048]{1,0:T(8,128)(2,1)}, bf16[128,2048]{1,0:T(8,128)(2,1)S(1)}, u32[]{:S(2)}, u32[]{:S(2)}) collective-permute-start(bf16[128,2048]{1,0:T(8,128)(2,1)} %constant_dynamic-update-slice_fusion.refs_0_), channel_id=1, source_target_pairs={{192,0},{196,4},{200,8},{204,12},{208,16},{212,20},{216,24},{220,2... | collective-permute-start | bytes 1572872 | tf_op jit(solution)/shard_map/ppermute | solution.py:508
  72.0 33.7 %collective-permute-start.4 = (bf16[256,1024]{1,0:T(8,128)(2,1)S(1)}, bf16[256,1024]{1,0:T(8,128)(2,1)S(1)}, u32[]{:S(2)}, u32[]{:S(2)}) collective-permute-start(bf16[256,1024]{1,0:T(8,128)(2,1)S(1)} %get-tuple-element.32), channel_id=1, source_target_pairs={{1,0},{2,1},{3,2},{0,3},{5,4},{6,5},{7,6},{4,7},{9,8},{10,9},{11,1... | collective-permute-start | bytes 1572872 | tf_op jit(solution)/shard_map/ppermute | solution.py:487
  74.5 34.1 %collective-permute-start.5 = (bf16[256,1024]{1,0:T(8,128)(2,1)S(1)}, bf16[256,1024]{1,0:T(8,128)(2,1)}, u32[]{:S(2)}, u32[]{:S(2)}) collective-permute-start(bf16[256,1024]{1,0:T(8,128)(2,1)S(1)} %get-tuple-element.32), channel_id=1, source_target_pairs={{3,0},{0,1},{1,2},{2,3},{7,4},{4,5},{5,6},{6,7},{11,8},{8,9},{9,10... | collective-permute-start | bytes 1572872 | tf_op jit(solution)/shard_map/ppermute | solution.py:487
  74.5 34.1 %collective-permute-start.8 = (bf16[128,2048]{1,0:T(8,128)(2,1)}, bf16[128,2048]{1,0:T(8,128)(2,1)S(1)}, u32[]{:S(2)}, u32[]{:S(2)}) collective-permute-start(bf16[128,2048]{1,0:T(8,128)(2,1)} %constant_dynamic-update-slice_fusion.refs_0_), channel_id=1, source_target_pairs={{0,4},{4,0},{8,12},{12,8},{16,20},{20,16},{24,28},{28,24},{32,36},... | collective-permute-start | bytes 1572872 | tf_op jit(solution)/shard_map/ppermute | solution.py:513
  92.4 16.2 %collective-permute-start.9 = (bf16[128,2048]{1,0:T(8,128)(2,1)}, bf16[128,2048]{1,0:T(8,128)(2,1)}, u32[]{:S(2)}, u32[]{:S(2)}) collective-permute-start(bf16[128,2048]{1,0:T(8,128)(2,1)} %collective-permute-done.6.refs_1_), channel_id=1, source_target_pairs={{0,4},{4,0},{8,12},{12,8},{16,20},{20,16},{24,28},{28,24},{32,36},... | collective-permute-start | bytes 1572872 | tf_op jit(solution)/shard_map/ppermute | solution.py:513
  93.4 12.3 %copy-start.10 = (bf16[128,2048]{1,0:T(8,128)(2,1)}, bf16[128,2048]{1,0:T(8,128)(2,1)S(1)}, u32[]{:S(2)}) copy-start(bf16[128,2048]{1,0:T(8,128)(2,1)S(1)} %collective-permute-done.7.refs_3_) | copy-start | bytes 1572868
  93.4 15.2 %collective-permute-start.11 = (bf16[128,2048]{1,0:T(8,128)(2,1)S(1)}, bf16[128,2048]{1,0:T(8,128)(2,1)}, u32[]{:S(2)}, u32[]{:S(2)}) collective-permute-start(bf16[128,2048]{1,0:T(8,128)(2,1)S(1)} %collective-permute-done.7.refs_3_), channel_id=1, source_target_pairs={{0,4},{4,0},{8,12},{12,8},{16,20},{20,16},{24,28},{28,24},{32,36},... | collective-permute-start | bytes 1572872 | tf_op jit(solution)/shard_map/ppermute | solution.py:513
  105.7 15.8 %copy-start.6 = (bf16[256,1024]{1,0:T(8,128)(2,1)}, bf16[256,1024]{1,0:T(8,128)(2,1)S(1)}, u32[]{:S(2)}) copy-start(bf16[256,1024]{1,0:T(8,128)(2,1)S(1)} %collective-permute-done.4.refs_1_) | copy-start | bytes 1572868
  105.7 3.7 %collective-permute-start.10 = (bf16[128,2048]{1,0:T(8,128)(2,1)}, bf16[128,2048]{1,0:T(8,128)(2,1)}, u32[]{:S(2)}, u32[]{:S(2)}) collective-permute-start(bf16[128,2048]{1,0:T(8,128)(2,1)} %collective-permute-done.3.refs_2_), channel_id=1, source_target_pairs={{0,4},{4,0},{8,12},{12,8},{16,20},{20,16},{24,28},{28,24},{32,36},... | collective-permute-start | bytes 1572872 | tf_op jit(solution)/shard_map/ppermute | solution.py:513
  121.5 10.6 %copy-start.9 = (bf16[1,512,2048]{2,1,0:T(8,128)(2,1)S(1)}, bf16[1,512,2048]{2,1,0:T(8,128)(2,1)}, u32[]{:S(2)}) copy-start(bf16[1,512,2048]{2,1,0:T(8,128)(2,1)} %param.19) | copy-start | bytes 6291460
  121.5 37.7 %all-to-all-start.2 = ((bf16[64,8,1024]{2,1,0:T(8,128)(2,1)}), bf16[64,8,1024]{2,1,0:T(8,128)(2,1)}, u32[]{:S(2)}, u32[]{:S(2)}) async-start(bf16[64,8,1024]{2,1,0:T(8,128)(2,1)} %bitcast.41), calls=%async_computation.2 | async-start | bytes 2097152 | tf_op jit(solution)/shard_map/all_to_all | solution.py:469
  133.2 38.3 %collective-permute-start.12 = (bf16[512,1024]{1,0:T(8,128)(2,1)}, bf16[512,1024]{1,0:T(8,128)(2,1)}, u32[]{:S(2)}, u32[]{:S(2)}) collective-permute-start(bf16[512,1024]{1,0:T(8,128)(2,1)} %dynamic-slice_bitcast_fusion.refs_0_), channel_id=1, source_target_pairs={{2,0},{3,1},{0,2},{1,3},{6,4},{7,5},{4,6},{5,7},{10,8},{11,9},{8,1... | collective-permute-start | bytes 3145736 | tf_op jit(solution)/shard_map/ppermute | solution.py:487
  134.6 35.9 %collective-permute-start.13 = (bf16[256,1024]{1,0:T(8,128)(2,1)}, bf16[256,1024]{1,0:T(8,128)(2,1)S(1)}, u32[]{:S(2)}, u32[]{:S(2)}) collective-permute-start(bf16[256,1024]{1,0:T(8,128)(2,1)} %get-tuple-element.31), channel_id=1, source_target_pairs={{1,0},{2,1},{3,2},{0,3},{5,4},{6,5},{7,6},{4,7},{9,8},{10,9},{11,1... | collective-permute-start | bytes 1572872 | tf_op jit(solution)/shard_map/ppermute | solution.py:487
  136.0 35.5 %collective-permute-start.14 = (bf16[256,1024]{1,0:T(8,128)(2,1)}, bf16[256,1024]{1,0:T(8,128)(2,1)}, u32[]{:S(2)}, u32[]{:S(2)}) collective-permute-start(bf16[256,1024]{1,0:T(8,128)(2,1)} %get-tuple-element.31), channel_id=1, source_target_pairs={{3,0},{0,1},{1,2},{2,3},{7,4},{4,5},{5,6},{6,7},{11,8},{8,9},{9,10... | collective-permute-start | bytes 1572872 | tf_op jit(solution)/shard_map/ppermute | solution.py:487
  166.7 26.0 %collective-permute-start.15 = (bf16[256,2048]{1,0:T(8,128)(2,1)}, bf16[256,2048]{1,0:T(8,128)(2,1)}, u32[]{:S(2)}, u32[]{:S(2)}) collective-permute-start(bf16[256,2048]{1,0:T(8,128)(2,1)} %up.1.hid_ref), channel_id=1, source_target_pairs={{0,1},{1,0},{2,3},{3,2},{4,5},{5,4},{6,7},{7,6},{8,9},{9,8},{10,11... | collective-permute-start | bytes 3145736 | tf_op jit(solution)/shard_map/ppermute | solution.py:523
  170.5 1.0 copy-start.7
  176.4 27.6 %all-to-all-start.3 = ((bf16[64,8,512]{2,1,0:T(8,128)(2,1)}), bf16[64,8,512]{2,1,0:T(8,128)(2,1)S(1)}, u32[]{:S(2)}, u32[]{:S(2)}) async-start(bf16[64,8,512]{2,1,0:T(8,128)(2,1)} %bitcast.39), calls=%async_computation.3 | async-start | bytes 1048576 | tf_op jit(solution)/shard_map/all_to_all | solution.py:469
  187.3 40.5 %copy-start.3 = (f32[512,64]{1,0:T(8,128)S(1)}, f32[512,64]{1,0:T(8,128)}, u32[]{:S(2)}) copy-start(f32[512,64]{1,0:T(8,128)} %get-tuple-element.27.gates_ref) | copy-start | bytes 393220
  187.3 40.5 %copy-start.4 = (s32[64,1,16]{0,2,1:T(8,128)S(1)}, s32[64,1,16]{0,2,1:T(8,128)}, u32[]{:S(2)}) copy-start(s32[64,1,16]{0,2,1:T(8,128)} %param.20) | copy-start | bytes 12292
  187.3 40.5 %copy-start.5 = (s32[64,1]{0,1:T(1,128)S(1)}, s32[64,1]{0,1:T(1,128)}, u32[]{:S(2)}) copy-start(s32[64,1]{0,1:T(1,128)} %param.21) | copy-start | bytes 772
  227.9 20.5 %copy-start.1 = (f32[16,12288]{1,0:T(8,128)S(1)}, f32[16,12288]{1,0:T(8,128)}, u32[]{:S(2)}) copy-start(f32[16,12288]{1,0:T(8,128)} %gate_ref.3) | copy-start | bytes 2359300
  227.9 20.5 %copy-start.2 = (f32[128,2048]{1,0:T(8,128)S(1)}, f32[128,2048]{1,0:T(8,128)}, u32[]{:S(2)}) copy-start(f32[128,2048]{1,0:T(8,128)} %get-tuple-element.26.share_ref) | copy-start | bytes 3145732
  (1 other events, 0.8 us)
Sparse Core Ops, SparseCore 0:
  9.2 110.9 all-gather.1

commit v10 on v9

--- a/solution.py
+++ b/solution.py
@@ -333,42 +333,67 @@
     )(rows, w)
 
 
-def down_kernel(per, places, rank_ref, hid_ref, *refs):
-    out_ref = refs[-1]
+def down_terms(places, rank_ref, hid_ref, blocks, total):
     parts = 4
     units = hid_ref.shape[1] // parts
-    total = None
-    for (turn, row), block in zip(places, refs[:-1]):
+    for (turn, row), block in zip(places, blocks):
         at = lax.rem(rank_ref[0] + turn, parts) * units + row
         some = hid_ref[:, pl.ds(pl.multiple_of(at, 128), block.shape[0])]
         term = dot(some, block[...])
         total = term if total is None else total + term
-    total = total.astype(BF16)
-    count = total.shape[0]
-
-    @pl.when(pl.program_id(0) == 0)
-    def _():
-        out_ref[...] = dot(halves_to_rows(count, per, 0), total).astype(BF16)
-
-    @pl.when(pl.program_id(0) == 1)
-    def _():
-        out_ref[...] += dot(halves_to_rows(count, per, 1), total).astype(BF16)
-
-
-def down_call(rank, hidden, blocks, places, per):
+    return total
+
+
+def begin_kernel(places, rank_ref, hid_ref, *refs):
+    refs[-1][...] = down_terms(places, rank_ref, hid_ref, refs[:-1], None)
+
+
+def begin_call(rank, hidden, blocks, places):
     rows, units = hidden.shape
     half = blocks[0].shape[1]
     cols = half // 2
     return pl.pallas_call(
-        functools.partial(down_kernel, per, places),
+        functools.partial(begin_kernel, places),
         grid=(2,),
         in_specs=[smem(), pl.BlockSpec((rows, units), lambda i: (0, 0))]
         + [pl.BlockSpec((block.shape[0], cols), lambda i: (0, i)) for block in blocks],
+        out_specs=pl.BlockSpec((rows, cols), lambda i: (0, i)),
+        out_shape=jax.ShapeDtypeStruct((rows, half), F32),
+        compiler_params=params(62),
+        name="begin",
+    )(rank, hidden, *blocks)
+
+
+def down_kernel(per, places, begun, rank_ref, hid_ref, *refs):
+    out_ref = refs[-1]
+    total = refs[0][...] if begun else None
+    total = down_terms(places, rank_ref, hid_ref, refs[1 if begun else 0 : -1], total)
+    total = total.astype(BF16)
+    count = total.shape[0]
+
+    @pl.when(pl.program_id(0) == 0)
+    def _():
+        out_ref[...] = dot(halves_to_rows(count, per, 0), total).astype(BF16)
+
+    @pl.when(pl.program_id(0) == 1)
+    def _():
+        out_ref[...] += dot(halves_to_rows(count, per, 1), total).astype(BF16)
+
+
+def down_call(rank, hidden, blocks, places, per, begun=()):
+    rows, units = hidden.shape
+    half = blocks[0].shape[1]
+    cols = half // 2
+    return pl.pallas_call(
+        functools.partial(down_kernel, per, places, len(begun) > 0),
+        grid=(2,),
+        in_specs=[smem(), pl.BlockSpec((rows, units), lambda i: (0, 0))]
+        + [pl.BlockSpec((part.shape[0], cols), lambda i: (0, i)) for part in (*begun, *blocks)],
         out_specs=pl.BlockSpec((2 * rows, cols), lambda i: (0, 0)),
         out_shape=jax.ShapeDtypeStruct((2 * rows, cols), BF16),
         compiler_params=params(62),
         name="down",
-    )(rank, hidden, *blocks)
+    )(rank, hidden, *begun, *blocks)
 
 
 def combine_kernel(per, rank_ref, gates_ref, picks_ref, counts_ref, own_ref, other_ref, out_ref):
@@ -497,18 +522,17 @@
     late = (from_turn(same_half, 2), from_turn(second, 1), from_turn(second, 3))
 
     stacked = qkv_call(step_index, x, modulation, jnp.transpose(qkv_weight, (1, 0, 2)), qk_gain)
-    stacked, out_rows = lax.optimization_barrier((stacked, out_rows))
     stacked = over_seq(stacked)
     few = position_count // seq
     attended = attention_call(stacked, few, head_size, ffn)
     out_rows = jnp.concatenate(out_rows, axis=0)
+    attended, out_rows = lax.optimization_barrier((attended, out_rows))
 
     def from_lane(values, turn):
         pairs = [((i + turn * stride) % seq, i) for i in range(seq)]
         return lax.ppermute(values, "seq", pairs)
 
     out_blocks = [out_rows] + [from_lane(out_rows, turn) for turn in range(1, lanes)]
-    attended, out_blocks[2] = lax.optimization_barrier((attended, out_blocks[2]))
     swap = [(i, i ^ 1) for i in range(seq)]
     out_blocks = out_blocks + [lax.ppermute(b, "seq", swap) for b in out_blocks]
     every = lax.all_to_all(attended, ("seq", "ffn"), split_axis=0, concat_axis=0, tiled=True)
@@ -521,7 +545,8 @@
     blocks = (same_half,) + tuple(early) + late
     hidden = up_call(expert_tokens, up_full, per)
     hidden_other = lax.ppermute(hidden, "ffn", [(i, i ^ 1) for i in range(ffn)])
-    own = over_seq(down_call(rank_arr, hidden, blocks, places, per))
+    begun = begin_call(rank_arr, hidden, blocks[:3], places[:3])
+    own = over_seq(down_call(rank_arr, hidden, blocks[3:], places[3:], per, (begun,)))
     other = over_seq(down_call(rank_arr, hidden_other, blocks, places, per))
     mixture = combine_call(rank_arr, gates, picks_t, counts_t, own, other, per)
     parts = over_ffn(mixture).reshape(ffn, share_len, half)

time: 257 us -> 250 us (0.973)
  waiting for transfers between devices: 92 us -> 82.1 us
  local copies, waits for them, and re-layouts: 5.97 us -> 2.91 us
  Pallas kernels: 40.9 us -> 43.7 us
    ppermute x8, waiting for transfers between devices: 20.3 us -> 41.7 us  [from_turn(): lax.ppermute(values, 'ffn', [((i + turn) % ffn, i) for i in range(ffn)])]
    ppermute x3, waiting for transfers between devices: 19.8 us -> 1.37 us  [from_lane(): return lax.ppermute(values, 'seq', pairs)]
    all_to_all x3, waiting for transfers between devices: 45.8 us -> 32 us  [over_seq(): lax.all_to_all(values, 'seq', split_axis=0, concat_axis=0, tiled=True)]
    pallas_call x2 -> x3, Pallas kernels: 9.91 us -> 12.7 us  [the longest x2 9.3 us: down_call(): pl.pallas_call(functools.partial(down_kernel, per, places, len(begun) > 0...]
  transfers between devices with their start and end apart: 21 -> 21, of which waited for: 12 -> 11; matrix products, arithmetic and copies ran while one was open for 2% -> 1% of each run, Pallas kernels for 15% -> 16%
where the time goes in v10:
time: 250 us; the launch traced here: 249 us
  waiting for transfers between devices  82.1 us (33%)
  starting transfers between devices  62.6 us (25%)
  Pallas kernels  43.7 us (17%)
  blocking collectives  42.5 us (17%)
  between operations  14.3 us (6%)
  local copies, waits for them, and re-layouts  2.91 us (1%)
    ppermute x8, waiting for transfers between devices, from_turn(): lax.ppermute(values, 'ffn', [((i + turn) % ffn, i) for i in range(ffn)])  41.7 us
    all_to_all x3, starting transfers between devices, over_seq(): lax.all_to_all(values, 'seq', split_axis=0, concat_axis=0, tiled=True)  33.7 us
    all_to_all x3, waiting for transfers between devices, over_seq(): lax.all_to_all(values, 'seq', split_axis=0, concat_axis=0, tiled=True)  32 us
    all_to_all x1, blocking collectives, over_seq(): lax.all_to_all(values, 'seq', split_axis=0, concat_axis=0, tiled=True)  23.6 us
    all_to_all x1, blocking collectives, over_ffn(): lax.all_to_all(values, 'ffn', split_axis=0, concat_axis=0, tiled=True)  18.9 us
    ppermute x8, starting transfers between devices, from_turn(): lax.ppermute(values, 'ffn', [((i + turn) % ffn, i) for i in range(ffn)])  12.2 us
    pallas_call x1, Pallas kernels, mix_call(): pl.pallas_call(functools.partial(mix_kernel, per, len(blocks) // 2, parts...  12.1 us
    all_to_all x1, starting transfers between devices, on_device(): lax.all_to_all(attended, ('seq', 'ffn'), split_axis=0, concat_axis=0, til...  10.8 us
  transfers between devices with their start and end apart: 21, of which 11 were waited for; matrix products, arithmetic and copies ran while one was open for 1% of the time, Pallas kernels for 16%

profile of v10, /device:TPU:8, one launch (start us, length us, event | category | flops | bytes accessed | tf_op | source)
XLA Modules:
  0.0 248.9 jit_solution(6561525044582869968)
XLA Ops:
  7.9 6.3 %qkv.1 = bf16[512,768]{1,0:T(8,128)(2,1)} custom-call(s32[1]{0:T(128)S(6)} %copy.12.step_ref, bf16[512,2048]{1,0:T(8,128)(2,1)} %bitcast.35, f32[16,12288]{1,0:T(8,128)} %gate_ref.3, bf16[3,2048,256]{2,1,0:T(8,128)(2,1)} %bitcast.38, f32[2,128]{1,0:T(2,128)} %gain_ref.1), custom_call_target="tpu_custom_call" | custom-call | tf_op jit(solution)/shard_map/qkv/pallas_call | solution.py:71
  14.2 12.1 %all-to-all-start = ((bf16[64,8,768]{2,1,0:T(8,128)(2,1)}), bf16[64,8,768]{2,1,0:T(8,128)(2,1)S(1)}, u32[]{:S(2)}, u32[]{:S(2)}) async-start(bf16[64,8,768]{2,1,0:T(8,128)(2,1)} %bitcast.37), calls=%async_computation | async-start | bytes 1572864 | tf_op jit(solution)/shard_map/all_to_all | solution.py:494
  26.4 1.5 collective-permute-start.2
  28.0 2.8 %collective-permute-start.1 = (bf16[32,2048]{1,0:T(8,128)(2,1)S(1)}, bf16[32,2048]{1,0:T(8,128)(2,1)S(1)}, u32[]{:S(2)}, u32[]{:S(2)}) collective-permute-start(bf16[32,2048]{1,0:T(8,128)(2,1)S(1)} %constant_dynamic-slice_fusion), channel_id=1, source_target_pairs={{2,0},{3,1},{0,2},{1,3},{6,4},{7,5},{4,6},{5,7},{10,8},{11,9},{8,1... | collective-permute-start | bytes 393224 | tf_op jit(solution)/shard_map/ppermute | solution.py:512
  30.7 1.4 collective-permute-start
  32.1 4.2 %collective-permute-done.2 = bf16[32,2048]{1,0:T(8,128)(2,1)S(1)} collective-permute-done((bf16[32,2048]{1,0:T(8,128)(2,1)S(1)}, bf16[32,2048]{1,0:T(8,128)(2,1)S(1)}, u32[]{:S(2)}, u32[]{:S(2)}) %collective-permute-start.2) | collective-permute-done | bytes 131104 | tf_op jit(solution)/shard_map/ppermute | solution.py:512
  36.3 6.8 %collective-permute-done.1 = bf16[32,2048]{1,0:T(8,128)(2,1)S(1)} collective-permute-done((bf16[32,2048]{1,0:T(8,128)(2,1)S(1)}, bf16[32,2048]{1,0:T(8,128)(2,1)S(1)}, u32[]{:S(2)}, u32[]{:S(2)}) %collective-permute-start.1) | collective-permute-done | bytes 131104 | tf_op jit(solution)/shard_map/ppermute | solution.py:512
  43.9 4.3 %all-to-all-done = bf16[64,8,768]{2,1,0:T(8,128)(2,1)S(1)} async-done(((bf16[64,8,768]{2,1,0:T(8,128)(2,1)}), bf16[64,8,768]{2,1,0:T(8,128)(2,1)S(1)}, u32[]{:S(2)}, u32[]{:S(2)}) %all-to-all-start) | async-done | bytes 786464 | tf_op jit(solution)/shard_map/all_to_all | solution.py:494
  48.2 2.1 attention.1
  50.3 10.8 %all-to-all-start.1 = ((bf16[256,8,256]{2,1,0:T(8,128)(2,1)}), bf16[256,8,256]{2,1,0:T(8,128)(2,1)}, u32[]{:S(2)}, u32[]{:S(2)}) async-start(bf16[256,8,256]{2,1,0:T(8,128)(2,1)} %bitcast.7), calls=%async_computation.1 | async-start | bytes 2097152 | tf_op jit(solution)/shard_map/all_to_all | solution.py:538
  62.1 2.7 %collective-permute-start.3 = (bf16[256,1024]{1,0:T(8,128)(2,1)S(1)}, bf16[256,1024]{1,0:T(8,128)(2,1)S(1)}, u32[]{:S(2)}, u32[]{:S(2)}) collective-permute-start(bf16[256,1024]{1,0:T(8,128)(2,1)S(1)} %get-tuple-element.22), channel_id=1, source_target_pairs={{1,0},{2,1},{3,2},{0,3},{5,4},{6,5},{7,6},{4,7},{9,8},{10,9},{11,1... | collective-permute-start | bytes 1572872 | tf_op jit(solution)/shard_map/ppermute | solution.py:512
  65.3 2.4 collective-permute-start.6
  67.7 1.8 collective-permute-start.7
  69.5 27.3 %collective-permute-done.3.refs_1_ = bf16[256,1024]{1,0:T(8,128)(2,1)S(1)} collective-permute-done((bf16[256,1024]{1,0:T(8,128)(2,1)S(1)}, bf16[256,1024]{1,0:T(8,128)(2,1)S(1)}, u32[]{:S(2)}, u32[]{:S(2)}) %collective-permute-start.3) | collective-permute-done | bytes 524320 | tf_op jit(solution)/shard_map/ppermute | solution.py:512
  98.2 1.4 collective-permute-done.6.refs_2_
  100.0 2.4 collective-permute-done.4.refs_2_
  102.5 12.1 %mix.1 = (bf16[512,1024]{1,0:T(8,128)(2,1)}, f32[512,64]{1,0:T(8,128)}, f32[128,2048]{1,0:T(8,128)}) custom-call(s32[1]{0:T(128)} %bitcast.rank_ref, s32[1]{0:T(128)} %bitcast.1.core_ref, s32[1]{0:T(128)} %bitcast.2.lane_ref, s32[1]{0:T(128)S(6)} %copy.12.step_ref, bf16[2048,256]{1,0:T(8,128)(2,1)} %bitcast.8.att_ref, bf16[512,2048]{1,0:T(8,128)(2,1)} %bitcast.36, ...), custom_call_target="tpu_custom_call" | custom-call | tf_op jit(solution)/shard_map/mix/pallas_call | solution.py:266
  114.7 10.9 %all-to-all-start.2 = ((bf16[64,8,1024]{2,1,0:T(8,128)(2,1)}), bf16[64,8,1024]{2,1,0:T(8,128)(2,1)}, u32[]{:S(2)}, u32[]{:S(2)}) async-start(bf16[64,8,1024]{2,1,0:T(8,128)(2,1)} %bitcast.41), calls=%async_computation.2 | async-start | bytes 2097152 | tf_op jit(solution)/shard_map/all_to_all | solution.py:494
  126.7 1.7 collective-permute-start.12
  130.5 22.2 %all-to-all-done.2 = bf16[64,8,1024]{2,1,0:T(8,128)(2,1)} async-done(((bf16[64,8,1024]{2,1,0:T(8,128)(2,1)}), bf16[64,8,1024]{2,1,0:T(8,128)(2,1)}, u32[]{:S(2)}, u32[]{:S(2)}) %all-to-all-start.2) | async-done | bytes 1048608 | tf_op jit(solution)/shard_map/all_to_all | solution.py:494
  152.6 7.6 %up.1.hid_ref = bf16[256,2048]{1,0:T(8,128)(2,1)} custom-call(bf16[512,1024]{1,0:T(8,128)(2,1)} %bitcast.16.rows_ref, bf16[4,2048,512]{2,1,0:T(8,128)(2,1)} %all-gather.2.cloned.1.call-done.w_ref), custom_call_target="tpu_custom_call" | custom-call | tf_op jit(solution)/shard_map/up/pallas_call | solution.py:321
  160.5 3.4 %begin.1.refs_0_ = f32[256,1024]{1,0:T(8,128)} custom-call(s32[1]{0:T(128)} %bitcast.rank_ref, bf16[256,2048]{1,0:T(8,128)(2,1)} %up.1.hid_ref, bf16[512,1024]{1,0:T(8,128)(2,1)} %dynamic-slice_bitcast_fusion.refs_0_, bf16[256,1024]{1,0:T(8,128)(2,1)} %copy-done.6, bf16[256,1024]{1,0:T(8,128)(2,1)} %collective-permute-done.4.refs_2_), custom_call_target="tpu_custom_call" | custom-call | tf_op jit(solution)/shard_map/begin/pallas_call | solution.py:355
  163.8 1.2 collective-permute-done.14.refs_3_.refs_5_
  165.0 4.3 %down.2 = bf16[512,512]{1,0:T(8,128)(2,1)} custom-call(s32[1]{0:T(128)} %bitcast.rank_ref, bf16[256,2048]{1,0:T(8,128)(2,1)} %up.1.hid_ref, f32[256,1024]{1,0:T(8,128)} %begin.1.refs_0_, bf16[512,1024]{1,0:T(8,128)(2,1)} %collective-permute-done.12.refs_1_.refs_3_, bf16[256,1024]{1,0:T(8,128)(2,1)} %copy-done.7, ...), custom_call_target="tpu_custom_call" | custom-call | tf_op jit(solution)/shard_map/down/pallas_call | solution.py:387
  169.3 10.7 %all-to-all-start.3 = ((bf16[64,8,512]{2,1,0:T(8,128)(2,1)}), bf16[64,8,512]{2,1,0:T(8,128)(2,1)S(1)}, u32[]{:S(2)}, u32[]{:S(2)}) async-start(bf16[64,8,512]{2,1,0:T(8,128)(2,1)} %bitcast.39), calls=%async_computation.3 | async-start | bytes 1048576 | tf_op jit(solution)/shard_map/all_to_all | solution.py:494
  180.1 6.2 %collective-permute-done.15.hid_ref = bf16[256,2048]{1,0:T(8,128)(2,1)} collective-permute-done((bf16[256,2048]{1,0:T(8,128)(2,1)}, bf16[256,2048]{1,0:T(8,128)(2,1)}, u32[]{:S(2)}, u32[]{:S(2)}) %collective-permute-start.15) | collective-permute-done | bytes 1048608 | tf_op jit(solution)/shard_map/ppermute | solution.py:547
  186.3 5.0 %down.3 = bf16[512,512]{1,0:T(8,128)(2,1)} custom-call(s32[1]{0:T(128)} %bitcast.rank_ref, bf16[256,2048]{1,0:T(8,128)(2,1)} %collective-permute-done.15.hid_ref, bf16[512,1024]{1,0:T(8,128)(2,1)} %dynamic-slice_bitcast_fusion.refs_0_, bf16[256,1024]{1,0:T(8,128)(2,1)} %copy-done.6, bf16[256,1024]{1,0:T(8,128)(2,1)} %collective-permute-done.4.refs_2_, ...), custom_call_target="tpu_custom_call" | custom-call | tf_op jit(solution)/shard_map/down/pallas_call | solution.py:387
  191.2 5.5 %all-to-all-done.3 = bf16[64,8,512]{2,1,0:T(8,128)(2,1)S(1)} async-done(((bf16[64,8,512]{2,1,0:T(8,128)(2,1)}), bf16[64,8,512]{2,1,0:T(8,128)(2,1)S(1)}, u32[]{:S(2)}, u32[]{:S(2)}) %all-to-all-start.3) | async-done | bytes 524320 | tf_op jit(solution)/shard_map/all_to_all | solution.py:494
  196.7 23.6 %all_to_all.65 = bf16[64,8,512]{2,1,0:T(8,128)(2,1)S(1)} all-to-all(bf16[64,8,512]{2,1,0:T(8,128)(2,1)} %bitcast.40), channel_id=1, replica_groups=mesh['seq'=64,'ffn'=4] {'seq'}, dimensions={0} | all-to-all | bytes 1048576 | tf_op jit(solution)/shard_map/all_to_all | solution.py:494
  220.4 1.7 combine.1
  222.0 18.9 %all_to_all.66.parts_ref = bf16[4,128,1024]{2,1,0:T(8,128)(2,1)S(1)} all-to-all(bf16[4,128,1024]{2,1,0:T(8,128)(2,1)S(1)} %bitcast.28), channel_id=1, replica_groups=mesh['seq'=64,'ffn'=4] {'ffn'}, dimensions={0} | all-to-all | bytes 2097152 | tf_op jit(solution)/shard_map/all_to_all | solution.py:497
  240.9 1.2 final.1
  (50 shorter events, 8.4 us)
Async XLA Ops:
  6.5 19.8 %copy-start = (bf16[256,2048]{1,0:T(8,128)(2,1)S(1)}, bf16[256,2048]{1,0:T(8,128)(2,1)}, u32[]{:S(2)}) copy-start(bf16[256,2048]{1,0:T(8,128)(2,1)} %param.16) | copy-start | bytes 3145732
  6.5 146.1 %all-gather.2.cloned.1.call-start = ((), (), s32[]{:S(2)}) async-start(), calls=%async_computation.6 | async-start | bytes 10485760 | tf_op jit(solution)/shard_map/all_gather | solution.py:506
  14.2 34.0 %all-to-all-start = ((bf16[64,8,768]{2,1,0:T(8,128)(2,1)}), bf16[64,8,768]{2,1,0:T(8,128)(2,1)S(1)}, u32[]{:S(2)}, u32[]{:S(2)}) async-start(bf16[64,8,768]{2,1,0:T(8,128)(2,1)} %bitcast.37), calls=%async_computation | async-start | bytes 1572864 | tf_op jit(solution)/shard_map/all_to_all | solution.py:494
  26.4 9.9 %collective-permute-start.2 = (bf16[32,2048]{1,0:T(8,128)(2,1)S(1)}, bf16[32,2048]{1,0:T(8,128)(2,1)S(1)}, u32[]{:S(2)}, u32[]{:S(2)}) collective-permute-start(bf16[32,2048]{1,0:T(8,128)(2,1)S(1)} %constant_dynamic-slice_fusion), channel_id=1, source_target_pairs={{3,0},{0,1},{1,2},{2,3},{7,4},{4,5},{5,6},{6,7},{11,8},{8,9},{9,10... | collective-permute-start | bytes 393224 | tf_op jit(solution)/shard_map/ppermute | solution.py:512
  28.0 15.1 %collective-permute-start.1 = (bf16[32,2048]{1,0:T(8,128)(2,1)S(1)}, bf16[32,2048]{1,0:T(8,128)(2,1)S(1)}, u32[]{:S(2)}, u32[]{:S(2)}) collective-permute-start(bf16[32,2048]{1,0:T(8,128)(2,1)S(1)} %constant_dynamic-slice_fusion), channel_id=1, source_target_pairs={{2,0},{3,1},{0,2},{1,3},{6,4},{7,5},{4,6},{5,7},{10,8},{11,9},{8,1... | collective-permute-start | bytes 393224 | tf_op jit(solution)/shard_map/ppermute | solution.py:512
  30.7 12.4 %collective-permute-start = (bf16[32,2048]{1,0:T(8,128)(2,1)S(1)}, bf16[32,2048]{1,0:T(8,128)(2,1)S(1)}, u32[]{:S(2)}, u32[]{:S(2)}) collective-permute-start(bf16[32,2048]{1,0:T(8,128)(2,1)S(1)} %constant_dynamic-slice_fusion), channel_id=1, source_target_pairs={{1,0},{2,1},{3,2},{0,3},{5,4},{6,5},{7,6},{4,7},{9,8},{10,9},{11,1... | collective-permute-start | bytes 393224 | tf_op jit(solution)/shard_map/ppermute | solution.py:512
  50.3 10.8 %copy-start.8 = (bf16[1,512,2048]{2,1,0:T(8,128)(2,1)S(1)}, bf16[1,512,2048]{2,1,0:T(8,128)(2,1)}, u32[]{:S(2)}) copy-start(bf16[1,512,2048]{2,1,0:T(8,128)(2,1)} %param.19) | copy-start | bytes 6291460
  50.3 52.1 %all-to-all-start.1 = ((bf16[256,8,256]{2,1,0:T(8,128)(2,1)}), bf16[256,8,256]{2,1,0:T(8,128)(2,1)}, u32[]{:S(2)}, u32[]{:S(2)}) async-start(bf16[256,8,256]{2,1,0:T(8,128)(2,1)} %bitcast.7), calls=%async_computation.1 | async-start | bytes 2097152 | tf_op jit(solution)/shard_map/all_to_all | solution.py:538
  62.1 34.8 %collective-permute-start.3 = (bf16[256,1024]{1,0:T(8,128)(2,1)S(1)}, bf16[256,1024]{1,0:T(8,128)(2,1)S(1)}, u32[]{:S(2)}, u32[]{:S(2)}) collective-permute-start(bf16[256,1024]{1,0:T(8,128)(2,1)S(1)} %get-tuple-element.22), channel_id=1, source_target_pairs={{1,0},{2,1},{3,2},{0,3},{5,4},{6,5},{7,6},{4,7},{9,8},{10,9},{11,1... | collective-permute-start | bytes 1572872 | tf_op jit(solution)/shard_map/ppermute | solution.py:512
  64.7 32.1 %collective-permute-start.5 = (bf16[128,2048]{1,0:T(8,128)(2,1)}, bf16[128,2048]{1,0:T(8,128)(2,1)S(1)}, u32[]{:S(2)}, u32[]{:S(2)}) collective-permute-start(bf16[128,2048]{1,0:T(8,128)(2,1)} %pad_maximum_fusion.refs_0_), channel_id=1, source_target_pairs={{64,0},{68,4},{72,8},{76,12},{80,16},{84,20},{88,24},{92,28},{96,3... | collective-permute-start | bytes 1572872 | tf_op jit(solution)/shard_map/ppermute | solution.py:533
  65.3 34.2 %collective-permute-start.6 = (bf16[128,2048]{1,0:T(8,128)(2,1)}, bf16[128,2048]{1,0:T(8,128)(2,1)S(1)}, u32[]{:S(2)}, u32[]{:S(2)}) collective-permute-start(bf16[128,2048]{1,0:T(8,128)(2,1)} %pad_maximum_fusion.refs_0_), channel_id=1, source_target_pairs={{128,0},{132,4},{136,8},{140,12},{144,16},{148,20},{152,24},{156,2... | collective-permute-start | bytes 1572872 | tf_op jit(solution)/shard_map/ppermute | solution.py:533
  67.7 31.8 %collective-permute-start.7 = (bf16[128,2048]{1,0:T(8,128)(2,1)}, bf16[128,2048]{1,0:T(8,128)(2,1)}, u32[]{:S(2)}, u32[]{:S(2)}) collective-permute-start(bf16[128,2048]{1,0:T(8,128)(2,1)} %pad_maximum_fusion.refs_0_), channel_id=1, source_target_pairs={{192,0},{196,4},{200,8},{204,12},{208,16},{212,20},{216,24},{220,2... | collective-permute-start | bytes 1572872 | tf_op jit(solution)/shard_map/ppermute | solution.py:533
  69.5 32.9 %collective-permute-start.4 = (bf16[256,1024]{1,0:T(8,128)(2,1)S(1)}, bf16[256,1024]{1,0:T(8,128)(2,1)}, u32[]{:S(2)}, u32[]{:S(2)}) collective-permute-start(bf16[256,1024]{1,0:T(8,128)(2,1)S(1)} %get-tuple-element.22), channel_id=1, source_target_pairs={{3,0},{0,1},{1,2},{2,3},{7,4},{4,5},{5,6},{6,7},{11,8},{8,9},{9,10... | collective-permute-start | bytes 1572872 | tf_op jit(solution)/shard_map/ppermute | solution.py:512
  96.8 17.8 %copy-start.6 = (bf16[256,1024]{1,0:T(8,128)(2,1)}, bf16[256,1024]{1,0:T(8,128)(2,1)S(1)}, u32[]{:S(2)}) copy-start(bf16[256,1024]{1,0:T(8,128)(2,1)S(1)} %collective-permute-done.3.refs_1_) | copy-start | bytes 1572868
  96.8 5.6 %collective-permute-start.8 = (bf16[128,2048]{1,0:T(8,128)(2,1)}, bf16[128,2048]{1,0:T(8,128)(2,1)}, u32[]{:S(2)}, u32[]{:S(2)}) collective-permute-start(bf16[128,2048]{1,0:T(8,128)(2,1)} %pad_maximum_fusion.refs_0_), channel_id=1, source_target_pairs={{0,4},{4,0},{8,12},{12,8},{16,20},{20,16},{24,28},{28,24},{32,36},... | collective-permute-start | bytes 1572872 | tf_op jit(solution)/shard_map/ppermute | solution.py:537
  97.7 4.7 %collective-permute-start.9 = (bf16[128,2048]{1,0:T(8,128)(2,1)S(1)}, bf16[128,2048]{1,0:T(8,128)(2,1)}, u32[]{:S(2)}, u32[]{:S(2)}) collective-permute-start(bf16[128,2048]{1,0:T(8,128)(2,1)S(1)} %collective-permute-done.5.refs_1_), channel_id=1, source_target_pairs={{0,4},{4,0},{8,12},{12,8},{16,20},{20,16},{24,28},{28,24},{32,36},... | collective-permute-start | bytes 1572872 | tf_op jit(solution)/shard_map/ppermute | solution.py:537
  99.5 2.9 %copy-start.11 = (bf16[128,2048]{1,0:T(8,128)(2,1)}, bf16[128,2048]{1,0:T(8,128)(2,1)S(1)}, u32[]{:S(2)}) copy-start(bf16[128,2048]{1,0:T(8,128)(2,1)S(1)} %collective-permute-done.6.refs_2_) | copy-start | bytes 1572868
  99.5 2.9 %collective-permute-start.10 = (bf16[128,2048]{1,0:T(8,128)(2,1)S(1)}, bf16[128,2048]{1,0:T(8,128)(2,1)}, u32[]{:S(2)}, u32[]{:S(2)}) collective-permute-start(bf16[128,2048]{1,0:T(8,128)(2,1)S(1)} %collective-permute-done.6.refs_2_), channel_id=1, source_target_pairs={{0,4},{4,0},{8,12},{12,8},{16,20},{20,16},{24,28},{28,24},{32,36},... | collective-permute-start | bytes 1572872 | tf_op jit(solution)/shard_map/ppermute | solution.py:537
  99.5 3.0 %collective-permute-start.11 = (bf16[128,2048]{1,0:T(8,128)(2,1)}, bf16[128,2048]{1,0:T(8,128)(2,1)}, u32[]{:S(2)}, u32[]{:S(2)}) collective-permute-start(bf16[128,2048]{1,0:T(8,128)(2,1)} %collective-permute-done.7.refs_3_), channel_id=1, source_target_pairs={{0,4},{4,0},{8,12},{12,8},{16,20},{20,16},{24,28},{28,24},{32,36},... | collective-permute-start | bytes 1572872 | tf_op jit(solution)/shard_map/ppermute | solution.py:537
  114.7 10.9 %copy-start.9 = (bf16[1,512,2048]{2,1,0:T(8,128)(2,1)S(1)}, bf16[1,512,2048]{2,1,0:T(8,128)(2,1)}, u32[]{:S(2)}) copy-start(bf16[1,512,2048]{2,1,0:T(8,128)(2,1)} %param.19) | copy-start | bytes 6291460
  114.7 38.0 %all-to-all-start.2 = ((bf16[64,8,1024]{2,1,0:T(8,128)(2,1)}), bf16[64,8,1024]{2,1,0:T(8,128)(2,1)}, u32[]{:S(2)}, u32[]{:S(2)}) async-start(bf16[64,8,1024]{2,1,0:T(8,128)(2,1)} %bitcast.41), calls=%async_computation.2 | async-start | bytes 2097152 | tf_op jit(solution)/shard_map/all_to_all | solution.py:494
  126.7 38.3 %collective-permute-start.12 = (bf16[512,1024]{1,0:T(8,128)(2,1)}, bf16[512,1024]{1,0:T(8,128)(2,1)}, u32[]{:S(2)}, u32[]{:S(2)}) collective-permute-start(bf16[512,1024]{1,0:T(8,128)(2,1)} %dynamic-slice_bitcast_fusion.refs_0_), channel_id=1, source_target_pairs={{2,0},{3,1},{0,2},{1,3},{6,4},{7,5},{4,6},{5,7},{10,8},{11,9},{8,1... | collective-permute-start | bytes 3145736 | tf_op jit(solution)/shard_map/ppermute | solution.py:512
  128.4 35.4 %collective-permute-start.13 = (bf16[256,1024]{1,0:T(8,128)(2,1)}, bf16[256,1024]{1,0:T(8,128)(2,1)S(1)}, u32[]{:S(2)}, u32[]{:S(2)}) collective-permute-start(bf16[256,1024]{1,0:T(8,128)(2,1)} %get-tuple-element.21), channel_id=1, source_target_pairs={{1,0},{2,1},{3,2},{0,3},{5,4},{6,5},{7,6},{4,7},{9,8},{10,9},{11,1... | collective-permute-start | bytes 1572872 | tf_op jit(solution)/shard_map/ppermute | solution.py:512
  129.6 35.4 %collective-permute-start.14 = (bf16[256,1024]{1,0:T(8,128)(2,1)}, bf16[256,1024]{1,0:T(8,128)(2,1)}, u32[]{:S(2)}, u32[]{:S(2)}) collective-permute-start(bf16[256,1024]{1,0:T(8,128)(2,1)} %get-tuple-element.21), channel_id=1, source_target_pairs={{3,0},{0,1},{1,2},{2,3},{7,4},{4,5},{5,6},{6,7},{11,8},{8,9},{9,10... | collective-permute-start | bytes 1572872 | tf_op jit(solution)/shard_map/ppermute | solution.py:512
  160.3 26.0 %collective-permute-start.15 = (bf16[256,2048]{1,0:T(8,128)(2,1)}, bf16[256,2048]{1,0:T(8,128)(2,1)}, u32[]{:S(2)}, u32[]{:S(2)}) collective-permute-start(bf16[256,2048]{1,0:T(8,128)(2,1)} %up.1.hid_ref), channel_id=1, source_target_pairs={{0,1},{1,0},{2,3},{3,2},{4,5},{5,4},{6,7},{7,6},{8,9},{9,8},{10,11... | collective-permute-start | bytes 3145736 | tf_op jit(solution)/shard_map/ppermute | solution.py:547
  163.8 1.2 copy-start.7
  169.3 27.4 %all-to-all-start.3 = ((bf16[64,8,512]{2,1,0:T(8,128)(2,1)}), bf16[64,8,512]{2,1,0:T(8,128)(2,1)S(1)}, u32[]{:S(2)}, u32[]{:S(2)}) async-start(bf16[64,8,512]{2,1,0:T(8,128)(2,1)} %bitcast.39), calls=%async_computation.3 | async-start | bytes 1048576 | tf_op jit(solution)/shard_map/all_to_all | solution.py:494
  180.0 40.3 %copy-start.3 = (f32[512,64]{1,0:T(8,128)S(1)}, f32[512,64]{1,0:T(8,128)}, u32[]{:S(2)}) copy-start(f32[512,64]{1,0:T(8,128)} %get-tuple-element.17.gates_ref) | copy-start | bytes 393220
  180.0 40.3 %copy-start.4 = (s32[64,1,16]{0,2,1:T(8,128)S(1)}, s32[64,1,16]{0,2,1:T(8,128)}, u32[]{:S(2)}) copy-start(s32[64,1,16]{0,2,1:T(8,128)} %param.20) | copy-start | bytes 12292
  180.1 40.3 %copy-start.5 = (s32[64,1]{0,1:T(1,128)S(1)}, s32[64,1]{0,1:T(1,128)}, u32[]{:S(2)}) copy-start(s32[64,1]{0,1:T(1,128)} %param.21) | copy-start | bytes 772
  220.3 20.6 %copy-start.1 = (f32[16,12288]{1,0:T(8,128)S(1)}, f32[16,12288]{1,0:T(8,128)}, u32[]{:S(2)}) copy-start(f32[16,12288]{1,0:T(8,128)} %gate_ref.3) | copy-start | bytes 2359300
  220.3 20.6 %copy-start.2 = (f32[128,2048]{1,0:T(8,128)S(1)}, f32[128,2048]{1,0:T(8,128)}, u32[]{:S(2)}) copy-start(f32[128,2048]{1,0:T(8,128)} %get-tuple-element.16.share_ref) | copy-start | bytes 3145732
  (1 other events, 0.8 us)
Sparse Core Ops, SparseCore 0:
  9.2 116.6 all-gather.1

commit v11 on v10

--- a/solution.py
+++ b/solution.py
@@ -262,7 +262,7 @@
     inner = att.shape[1]
     experts = router_t.shape[0]
     steps = modulation.shape[0]
-    rows = 256
+    rows = 512
     return pl.pallas_call(
         functools.partial(mix_kernel, per, len(blocks) // 2, parts, few),
         grid=(tokens // rows,),

time: 250 us -> 250 us (level)
  no operation moved by 1% of the time
where the time goes in v11:
time: 250 us; the launch traced here: 249 us
  waiting for transfers between devices  82.1 us (33%)
  starting transfers between devices  62.6 us (25%)
  Pallas kernels  43.9 us (18%)
  blocking collectives  42.5 us (17%)
  between operations  14.3 us (6%)
  local copies, waits for them, and re-layouts  2.91 us (1%)
    ppermute x8, waiting for transfers between devices, from_turn(): lax.ppermute(values, 'ffn', [((i + turn) % ffn, i) for i in range(ffn)])  41.7 us
    all_to_all x3, starting transfers between devices, over_seq(): lax.all_to_all(values, 'seq', split_axis=0, concat_axis=0, tiled=True)  33.7 us
    all_to_all x3, waiting for transfers between devices, over_seq(): lax.all_to_all(values, 'seq', split_axis=0, concat_axis=0, tiled=True)  32 us
    all_to_all x1, blocking collectives, over_seq(): lax.all_to_all(values, 'seq', split_axis=0, concat_axis=0, tiled=True)  23.6 us
    all_to_all x1, blocking collectives, over_ffn(): lax.all_to_all(values, 'ffn', split_axis=0, concat_axis=0, tiled=True)  18.9 us
    pallas_call x1, Pallas kernels, mix_call(): pl.pallas_call(functools.partial(mix_kernel, per, len(blocks) // 2, parts...  12.4 us
    ppermute x8, starting transfers between devices, from_turn(): lax.ppermute(values, 'ffn', [((i + turn) % ffn, i) for i in range(ffn)])  12.2 us
    all_to_all x1, starting transfers between devices, on_device(): lax.all_to_all(attended, ('seq', 'ffn'), split_axis=0, concat_axis=0, til...  10.8 us
  transfers between devices with their start and end apart: 21, of which 11 were waited for; matrix products, arithmetic and copies ran while one was open for 1% of the time, Pallas kernels for 16%

profile of v11, /device:TPU:8, one launch (start us, length us, event | category | flops | bytes accessed | tf_op | source)
XLA Modules:
  0.0 249.2 jit_solution(4505333154320875542)
XLA Ops:
  7.9 6.3 %qkv.1 = bf16[512,768]{1,0:T(8,128)(2,1)} custom-call(s32[1]{0:T(128)S(6)} %copy.12.step_ref, bf16[512,2048]{1,0:T(8,128)(2,1)} %bitcast.35, f32[16,12288]{1,0:T(8,128)} %gate_ref.3, bf16[3,2048,256]{2,1,0:T(8,128)(2,1)} %bitcast.38, f32[2,128]{1,0:T(2,128)} %gain_ref.1), custom_call_target="tpu_custom_call" | custom-call | tf_op jit(solution)/shard_map/qkv/pallas_call | solution.py:71
  14.2 12.1 %all-to-all-start = ((bf16[64,8,768]{2,1,0:T(8,128)(2,1)}), bf16[64,8,768]{2,1,0:T(8,128)(2,1)S(1)}, u32[]{:S(2)}, u32[]{:S(2)}) async-start(bf16[64,8,768]{2,1,0:T(8,128)(2,1)} %bitcast.37), calls=%async_computation | async-start | bytes 1572864 | tf_op jit(solution)/shard_map/all_to_all | solution.py:494
  26.4 1.5 collective-permute-start.2
  28.0 2.8 %collective-permute-start.1 = (bf16[32,2048]{1,0:T(8,128)(2,1)S(1)}, bf16[32,2048]{1,0:T(8,128)(2,1)S(1)}, u32[]{:S(2)}, u32[]{:S(2)}) collective-permute-start(bf16[32,2048]{1,0:T(8,128)(2,1)S(1)} %constant_dynamic-slice_fusion), channel_id=1, source_target_pairs={{2,0},{3,1},{0,2},{1,3},{6,4},{7,5},{4,6},{5,7},{10,8},{11,9},{8,1... | collective-permute-start | bytes 393224 | tf_op jit(solution)/shard_map/ppermute | solution.py:512
  30.7 1.4 collective-permute-start
  32.1 4.2 %collective-permute-done.2 = bf16[32,2048]{1,0:T(8,128)(2,1)S(1)} collective-permute-done((bf16[32,2048]{1,0:T(8,128)(2,1)S(1)}, bf16[32,2048]{1,0:T(8,128)(2,1)S(1)}, u32[]{:S(2)}, u32[]{:S(2)}) %collective-permute-start.2) | collective-permute-done | bytes 131104 | tf_op jit(solution)/shard_map/ppermute | solution.py:512
  36.3 6.8 %collective-permute-done.1 = bf16[32,2048]{1,0:T(8,128)(2,1)S(1)} collective-permute-done((bf16[32,2048]{1,0:T(8,128)(2,1)S(1)}, bf16[32,2048]{1,0:T(8,128)(2,1)S(1)}, u32[]{:S(2)}, u32[]{:S(2)}) %collective-permute-start.1) | collective-permute-done | bytes 131104 | tf_op jit(solution)/shard_map/ppermute | solution.py:512
  43.9 4.3 %all-to-all-done = bf16[64,8,768]{2,1,0:T(8,128)(2,1)S(1)} async-done(((bf16[64,8,768]{2,1,0:T(8,128)(2,1)}), bf16[64,8,768]{2,1,0:T(8,128)(2,1)S(1)}, u32[]{:S(2)}, u32[]{:S(2)}) %all-to-all-start) | async-done | bytes 786464 | tf_op jit(solution)/shard_map/all_to_all | solution.py:494
  48.2 2.1 attention.1
  50.3 10.8 %all-to-all-start.1 = ((bf16[256,8,256]{2,1,0:T(8,128)(2,1)}), bf16[256,8,256]{2,1,0:T(8,128)(2,1)}, u32[]{:S(2)}, u32[]{:S(2)}) async-start(bf16[256,8,256]{2,1,0:T(8,128)(2,1)} %bitcast.7), calls=%async_computation.1 | async-start | bytes 2097152 | tf_op jit(solution)/shard_map/all_to_all | solution.py:538
  62.1 2.7 %collective-permute-start.3 = (bf16[256,1024]{1,0:T(8,128)(2,1)S(1)}, bf16[256,1024]{1,0:T(8,128)(2,1)S(1)}, u32[]{:S(2)}, u32[]{:S(2)}) collective-permute-start(bf16[256,1024]{1,0:T(8,128)(2,1)S(1)} %get-tuple-element.22), channel_id=1, source_target_pairs={{1,0},{2,1},{3,2},{0,3},{5,4},{6,5},{7,6},{4,7},{9,8},{10,9},{11,1... | collective-permute-start | bytes 1572872 | tf_op jit(solution)/shard_map/ppermute | solution.py:512
  65.3 2.4 collective-permute-start.6
  67.7 1.8 collective-permute-start.7
  69.5 27.3 %collective-permute-done.3.refs_1_ = bf16[256,1024]{1,0:T(8,128)(2,1)S(1)} collective-permute-done((bf16[256,1024]{1,0:T(8,128)(2,1)S(1)}, bf16[256,1024]{1,0:T(8,128)(2,1)S(1)}, u32[]{:S(2)}, u32[]{:S(2)}) %collective-permute-start.3) | collective-permute-done | bytes 524320 | tf_op jit(solution)/shard_map/ppermute | solution.py:512
  98.2 1.4 collective-permute-done.6.refs_2_
  100.0 2.4 collective-permute-done.4.refs_2_
  102.5 12.4 %mix.1 = (bf16[512,1024]{1,0:T(8,128)(2,1)}, f32[512,64]{1,0:T(8,128)}, f32[128,2048]{1,0:T(8,128)}) custom-call(s32[1]{0:T(128)} %bitcast.rank_ref, s32[1]{0:T(128)} %bitcast.1.core_ref, s32[1]{0:T(128)} %bitcast.2.lane_ref, s32[1]{0:T(128)S(6)} %copy.12.step_ref, bf16[2048,256]{1,0:T(8,128)(2,1)} %bitcast.8.att_ref, bf16[512,2048]{1,0:T(8,128)(2,1)} %bitcast.36, ...), custom_call_target="tpu_custom_call" | custom-call | tf_op jit(solution)/shard_map/mix/pallas_call | solution.py:266
  114.9 10.9 %all-to-all-start.2 = ((bf16[64,8,1024]{2,1,0:T(8,128)(2,1)}), bf16[64,8,1024]{2,1,0:T(8,128)(2,1)}, u32[]{:S(2)}, u32[]{:S(2)}) async-start(bf16[64,8,1024]{2,1,0:T(8,128)(2,1)} %bitcast.41), calls=%async_computation.2 | async-start | bytes 2097152 | tf_op jit(solution)/shard_map/all_to_all | solution.py:494
  126.9 1.7 collective-permute-start.12
  130.7 22.2 %all-to-all-done.2 = bf16[64,8,1024]{2,1,0:T(8,128)(2,1)} async-done(((bf16[64,8,1024]{2,1,0:T(8,128)(2,1)}), bf16[64,8,1024]{2,1,0:T(8,128)(2,1)}, u32[]{:S(2)}, u32[]{:S(2)}) %all-to-all-start.2) | async-done | bytes 1048608 | tf_op jit(solution)/shard_map/all_to_all | solution.py:494
  152.9 7.6 %up.1.hid_ref = bf16[256,2048]{1,0:T(8,128)(2,1)} custom-call(bf16[512,1024]{1,0:T(8,128)(2,1)} %bitcast.16.rows_ref, bf16[4,2048,512]{2,1,0:T(8,128)(2,1)} %all-gather.2.cloned.1.call-done.w_ref), custom_call_target="tpu_custom_call" | custom-call | tf_op jit(solution)/shard_map/up/pallas_call | solution.py:321
  160.7 3.4 %begin.1.refs_0_ = f32[256,1024]{1,0:T(8,128)} custom-call(s32[1]{0:T(128)} %bitcast.rank_ref, bf16[256,2048]{1,0:T(8,128)(2,1)} %up.1.hid_ref, bf16[512,1024]{1,0:T(8,128)(2,1)} %dynamic-slice_bitcast_fusion.refs_0_, bf16[256,1024]{1,0:T(8,128)(2,1)} %copy-done.6, bf16[256,1024]{1,0:T(8,128)(2,1)} %collective-permute-done.4.refs_2_), custom_call_target="tpu_custom_call" | custom-call | tf_op jit(solution)/shard_map/begin/pallas_call | solution.py:355
  164.0 1.1 collective-permute-done.14.refs_3_.refs_5_
  165.2 4.4 %down.2 = bf16[512,512]{1,0:T(8,128)(2,1)} custom-call(s32[1]{0:T(128)} %bitcast.rank_ref, bf16[256,2048]{1,0:T(8,128)(2,1)} %up.1.hid_ref, f32[256,1024]{1,0:T(8,128)} %begin.1.refs_0_, bf16[512,1024]{1,0:T(8,128)(2,1)} %collective-permute-done.12.refs_1_.refs_3_, bf16[256,1024]{1,0:T(8,128)(2,1)} %copy-done.7, ...), custom_call_target="tpu_custom_call" | custom-call | tf_op jit(solution)/shard_map/down/pallas_call | solution.py:387
  169.6 10.7 %all-to-all-start.3 = ((bf16[64,8,512]{2,1,0:T(8,128)(2,1)}), bf16[64,8,512]{2,1,0:T(8,128)(2,1)S(1)}, u32[]{:S(2)}, u32[]{:S(2)}) async-start(bf16[64,8,512]{2,1,0:T(8,128)(2,1)} %bitcast.39), calls=%async_computation.3 | async-start | bytes 1048576 | tf_op jit(solution)/shard_map/all_to_all | solution.py:494
  180.3 6.2 %collective-permute-done.15.hid_ref = bf16[256,2048]{1,0:T(8,128)(2,1)} collective-permute-done((bf16[256,2048]{1,0:T(8,128)(2,1)}, bf16[256,2048]{1,0:T(8,128)(2,1)}, u32[]{:S(2)}, u32[]{:S(2)}) %collective-permute-start.15) | collective-permute-done | bytes 1048608 | tf_op jit(solution)/shard_map/ppermute | solution.py:547
  186.5 5.0 %down.3 = bf16[512,512]{1,0:T(8,128)(2,1)} custom-call(s32[1]{0:T(128)} %bitcast.rank_ref, bf16[256,2048]{1,0:T(8,128)(2,1)} %collective-permute-done.15.hid_ref, bf16[512,1024]{1,0:T(8,128)(2,1)} %dynamic-slice_bitcast_fusion.refs_0_, bf16[256,1024]{1,0:T(8,128)(2,1)} %copy-done.6, bf16[256,1024]{1,0:T(8,128)(2,1)} %collective-permute-done.4.refs_2_, ...), custom_call_target="tpu_custom_call" | custom-call | tf_op jit(solution)/shard_map/down/pallas_call | solution.py:387
  191.4 5.5 %all-to-all-done.3 = bf16[64,8,512]{2,1,0:T(8,128)(2,1)S(1)} async-done(((bf16[64,8,512]{2,1,0:T(8,128)(2,1)}), bf16[64,8,512]{2,1,0:T(8,128)(2,1)S(1)}, u32[]{:S(2)}, u32[]{:S(2)}) %all-to-all-start.3) | async-done | bytes 524320 | tf_op jit(solution)/shard_map/all_to_all | solution.py:494
  196.9 23.6 %all_to_all.65 = bf16[64,8,512]{2,1,0:T(8,128)(2,1)S(1)} all-to-all(bf16[64,8,512]{2,1,0:T(8,128)(2,1)} %bitcast.40), channel_id=1, replica_groups=mesh['seq'=64,'ffn'=4] {'seq'}, dimensions={0} | all-to-all | bytes 1048576 | tf_op jit(solution)/shard_map/all_to_all | solution.py:494
  220.6 1.7 combine.1
  222.3 18.9 %all_to_all.66.parts_ref = bf16[4,128,1024]{2,1,0:T(8,128)(2,1)S(1)} all-to-all(bf16[4,128,1024]{2,1,0:T(8,128)(2,1)S(1)} %bitcast.28), channel_id=1, replica_groups=mesh['seq'=64,'ffn'=4] {'ffn'}, dimensions={0} | all-to-all | bytes 2097152 | tf_op jit(solution)/shard_map/all_to_all | solution.py:497
  241.1 1.2 final.1
  (50 shorter events, 8.4 us)
Async XLA Ops:
  6.5 19.8 %copy-start = (bf16[256,2048]{1,0:T(8,128)(2,1)S(1)}, bf16[256,2048]{1,0:T(8,128)(2,1)}, u32[]{:S(2)}) copy-start(bf16[256,2048]{1,0:T(8,128)(2,1)} %param.16) | copy-start | bytes 3145732
  6.5 146.3 %all-gather.2.cloned.1.call-start = ((), (), s32[]{:S(2)}) async-start(), calls=%async_computation.6 | async-start | bytes 10485760 | tf_op jit(solution)/shard_map/all_gather | solution.py:506
  14.2 34.0 %all-to-all-start = ((bf16[64,8,768]{2,1,0:T(8,128)(2,1)}), bf16[64,8,768]{2,1,0:T(8,128)(2,1)S(1)}, u32[]{:S(2)}, u32[]{:S(2)}) async-start(bf16[64,8,768]{2,1,0:T(8,128)(2,1)} %bitcast.37), calls=%async_computation | async-start | bytes 1572864 | tf_op jit(solution)/shard_map/all_to_all | solution.py:494
  26.4 9.9 %collective-permute-start.2 = (bf16[32,2048]{1,0:T(8,128)(2,1)S(1)}, bf16[32,2048]{1,0:T(8,128)(2,1)S(1)}, u32[]{:S(2)}, u32[]{:S(2)}) collective-permute-start(bf16[32,2048]{1,0:T(8,128)(2,1)S(1)} %constant_dynamic-slice_fusion), channel_id=1, source_target_pairs={{3,0},{0,1},{1,2},{2,3},{7,4},{4,5},{5,6},{6,7},{11,8},{8,9},{9,10... | collective-permute-start | bytes 393224 | tf_op jit(solution)/shard_map/ppermute | solution.py:512
  28.0 15.1 %collective-permute-start.1 = (bf16[32,2048]{1,0:T(8,128)(2,1)S(1)}, bf16[32,2048]{1,0:T(8,128)(2,1)S(1)}, u32[]{:S(2)}, u32[]{:S(2)}) collective-permute-start(bf16[32,2048]{1,0:T(8,128)(2,1)S(1)} %constant_dynamic-slice_fusion), channel_id=1, source_target_pairs={{2,0},{3,1},{0,2},{1,3},{6,4},{7,5},{4,6},{5,7},{10,8},{11,9},{8,1... | collective-permute-start | bytes 393224 | tf_op jit(solution)/shard_map/ppermute | solution.py:512
  30.7 12.4 %collective-permute-start = (bf16[32,2048]{1,0:T(8,128)(2,1)S(1)}, bf16[32,2048]{1,0:T(8,128)(2,1)S(1)}, u32[]{:S(2)}, u32[]{:S(2)}) collective-permute-start(bf16[32,2048]{1,0:T(8,128)(2,1)S(1)} %constant_dynamic-slice_fusion), channel_id=1, source_target_pairs={{1,0},{2,1},{3,2},{0,3},{5,4},{6,5},{7,6},{4,7},{9,8},{10,9},{11,1... | collective-permute-start | bytes 393224 | tf_op jit(solution)/shard_map/ppermute | solution.py:512
  50.3 10.8 %copy-start.8 = (bf16[1,512,2048]{2,1,0:T(8,128)(2,1)S(1)}, bf16[1,512,2048]{2,1,0:T(8,128)(2,1)}, u32[]{:S(2)}) copy-start(bf16[1,512,2048]{2,1,0:T(8,128)(2,1)} %param.19) | copy-start | bytes 6291460
  50.3 52.1 %all-to-all-start.1 = ((bf16[256,8,256]{2,1,0:T(8,128)(2,1)}), bf16[256,8,256]{2,1,0:T(8,128)(2,1)}, u32[]{:S(2)}, u32[]{:S(2)}) async-start(bf16[256,8,256]{2,1,0:T(8,128)(2,1)} %bitcast.7), calls=%async_computation.1 | async-start | bytes 2097152 | tf_op jit(solution)/shard_map/all_to_all | solution.py:538
  62.1 34.8 %collective-permute-start.3 = (bf16[256,1024]{1,0:T(8,128)(2,1)S(1)}, bf16[256,1024]{1,0:T(8,128)(2,1)S(1)}, u32[]{:S(2)}, u32[]{:S(2)}) collective-permute-start(bf16[256,1024]{1,0:T(8,128)(2,1)S(1)} %get-tuple-element.22), channel_id=1, source_target_pairs={{1,0},{2,1},{3,2},{0,3},{5,4},{6,5},{7,6},{4,7},{9,8},{10,9},{11,1... | collective-permute-start | bytes 1572872 | tf_op jit(solution)/shard_map/ppermute | solution.py:512
  64.7 32.1 %collective-permute-start.5 = (bf16[128,2048]{1,0:T(8,128)(2,1)}, bf16[128,2048]{1,0:T(8,128)(2,1)S(1)}, u32[]{:S(2)}, u32[]{:S(2)}) collective-permute-start(bf16[128,2048]{1,0:T(8,128)(2,1)} %pad_maximum_fusion.refs_0_), channel_id=1, source_target_pairs={{64,0},{68,4},{72,8},{76,12},{80,16},{84,20},{88,24},{92,28},{96,3... | collective-permute-start | bytes 1572872 | tf_op jit(solution)/shard_map/ppermute | solution.py:533
  65.3 34.2 %collective-permute-start.6 = (bf16[128,2048]{1,0:T(8,128)(2,1)}, bf16[128,2048]{1,0:T(8,128)(2,1)S(1)}, u32[]{:S(2)}, u32[]{:S(2)}) collective-permute-start(bf16[128,2048]{1,0:T(8,128)(2,1)} %pad_maximum_fusion.refs_0_), channel_id=1, source_target_pairs={{128,0},{132,4},{136,8},{140,12},{144,16},{148,20},{152,24},{156,2... | collective-permute-start | bytes 1572872 | tf_op jit(solution)/shard_map/ppermute | solution.py:533
  67.7 31.8 %collective-permute-start.7 = (bf16[128,2048]{1,0:T(8,128)(2,1)}, bf16[128,2048]{1,0:T(8,128)(2,1)}, u32[]{:S(2)}, u32[]{:S(2)}) collective-permute-start(bf16[128,2048]{1,0:T(8,128)(2,1)} %pad_maximum_fusion.refs_0_), channel_id=1, source_target_pairs={{192,0},{196,4},{200,8},{204,12},{208,16},{212,20},{216,24},{220,2... | collective-permute-start | bytes 1572872 | tf_op jit(solution)/shard_map/ppermute | solution.py:533
  69.5 32.9 %collective-permute-start.4 = (bf16[256,1024]{1,0:T(8,128)(2,1)S(1)}, bf16[256,1024]{1,0:T(8,128)(2,1)}, u32[]{:S(2)}, u32[]{:S(2)}) collective-permute-start(bf16[256,1024]{1,0:T(8,128)(2,1)S(1)} %get-tuple-element.22), channel_id=1, source_target_pairs={{3,0},{0,1},{1,2},{2,3},{7,4},{4,5},{5,6},{6,7},{11,8},{8,9},{9,10... | collective-permute-start | bytes 1572872 | tf_op jit(solution)/shard_map/ppermute | solution.py:512
  96.8 18.1 %copy-start.6 = (bf16[256,1024]{1,0:T(8,128)(2,1)}, bf16[256,1024]{1,0:T(8,128)(2,1)S(1)}, u32[]{:S(2)}) copy-start(bf16[256,1024]{1,0:T(8,128)(2,1)S(1)} %collective-permute-done.3.refs_1_) | copy-start | bytes 1572868
  96.8 5.6 %collective-permute-start.8 = (bf16[128,2048]{1,0:T(8,128)(2,1)}, bf16[128,2048]{1,0:T(8,128)(2,1)}, u32[]{:S(2)}, u32[]{:S(2)}) collective-permute-start(bf16[128,2048]{1,0:T(8,128)(2,1)} %pad_maximum_fusion.refs_0_), channel_id=1, source_target_pairs={{0,4},{4,0},{8,12},{12,8},{16,20},{20,16},{24,28},{28,24},{32,36},... | collective-permute-start | bytes 1572872 | tf_op jit(solution)/shard_map/ppermute | solution.py:537
  97.7 4.7 %collective-permute-start.9 = (bf16[128,2048]{1,0:T(8,128)(2,1)S(1)}, bf16[128,2048]{1,0:T(8,128)(2,1)}, u32[]{:S(2)}, u32[]{:S(2)}) collective-permute-start(bf16[128,2048]{1,0:T(8,128)(2,1)S(1)} %collective-permute-done.5.refs_1_), channel_id=1, source_target_pairs={{0,4},{4,0},{8,12},{12,8},{16,20},{20,16},{24,28},{28,24},{32,36},... | collective-permute-start | bytes 1572872 | tf_op jit(solution)/shard_map/ppermute | solution.py:537
  99.5 2.9 %copy-start.11 = (bf16[128,2048]{1,0:T(8,128)(2,1)}, bf16[128,2048]{1,0:T(8,128)(2,1)S(1)}, u32[]{:S(2)}) copy-start(bf16[128,2048]{1,0:T(8,128)(2,1)S(1)} %collective-permute-done.6.refs_2_) | copy-start | bytes 1572868
  99.5 2.9 %collective-permute-start.10 = (bf16[128,2048]{1,0:T(8,128)(2,1)S(1)}, bf16[128,2048]{1,0:T(8,128)(2,1)}, u32[]{:S(2)}, u32[]{:S(2)}) collective-permute-start(bf16[128,2048]{1,0:T(8,128)(2,1)S(1)} %collective-permute-done.6.refs_2_), channel_id=1, source_target_pairs={{0,4},{4,0},{8,12},{12,8},{16,20},{20,16},{24,28},{28,24},{32,36},... | collective-permute-start | bytes 1572872 | tf_op jit(solution)/shard_map/ppermute | solution.py:537
  99.5 3.0 %collective-permute-start.11 = (bf16[128,2048]{1,0:T(8,128)(2,1)}, bf16[128,2048]{1,0:T(8,128)(2,1)}, u32[]{:S(2)}, u32[]{:S(2)}) collective-permute-start(bf16[128,2048]{1,0:T(8,128)(2,1)} %collective-permute-done.7.refs_3_), channel_id=1, source_target_pairs={{0,4},{4,0},{8,12},{12,8},{16,20},{20,16},{24,28},{28,24},{32,36},... | collective-permute-start | bytes 1572872 | tf_op jit(solution)/shard_map/ppermute | solution.py:537
  114.9 10.9 %copy-start.9 = (bf16[1,512,2048]{2,1,0:T(8,128)(2,1)S(1)}, bf16[1,512,2048]{2,1,0:T(8,128)(2,1)}, u32[]{:S(2)}) copy-start(bf16[1,512,2048]{2,1,0:T(8,128)(2,1)} %param.19) | copy-start | bytes 6291460
  114.9 37.9 %all-to-all-start.2 = ((bf16[64,8,1024]{2,1,0:T(8,128)(2,1)}), bf16[64,8,1024]{2,1,0:T(8,128)(2,1)}, u32[]{:S(2)}, u32[]{:S(2)}) async-start(bf16[64,8,1024]{2,1,0:T(8,128)(2,1)} %bitcast.41), calls=%async_computation.2 | async-start | bytes 2097152 | tf_op jit(solution)/shard_map/all_to_all | solution.py:494
  126.9 38.3 %collective-permute-start.12 = (bf16[512,1024]{1,0:T(8,128)(2,1)}, bf16[512,1024]{1,0:T(8,128)(2,1)}, u32[]{:S(2)}, u32[]{:S(2)}) collective-permute-start(bf16[512,1024]{1,0:T(8,128)(2,1)} %dynamic-slice_bitcast_fusion.refs_0_), channel_id=1, source_target_pairs={{2,0},{3,1},{0,2},{1,3},{6,4},{7,5},{4,6},{5,7},{10,8},{11,9},{8,1... | collective-permute-start | bytes 3145736 | tf_op jit(solution)/shard_map/ppermute | solution.py:512
  128.7 35.4 %collective-permute-start.13 = (bf16[256,1024]{1,0:T(8,128)(2,1)}, bf16[256,1024]{1,0:T(8,128)(2,1)S(1)}, u32[]{:S(2)}, u32[]{:S(2)}) collective-permute-start(bf16[256,1024]{1,0:T(8,128)(2,1)} %get-tuple-element.21), channel_id=1, source_target_pairs={{1,0},{2,1},{3,2},{0,3},{5,4},{6,5},{7,6},{4,7},{9,8},{10,9},{11,1... | collective-permute-start | bytes 1572872 | tf_op jit(solution)/shard_map/ppermute | solution.py:512
  129.8 35.4 %collective-permute-start.14 = (bf16[256,1024]{1,0:T(8,128)(2,1)}, bf16[256,1024]{1,0:T(8,128)(2,1)}, u32[]{:S(2)}, u32[]{:S(2)}) collective-permute-start(bf16[256,1024]{1,0:T(8,128)(2,1)} %get-tuple-element.21), channel_id=1, source_target_pairs={{3,0},{0,1},{1,2},{2,3},{7,4},{4,5},{5,6},{6,7},{11,8},{8,9},{9,10... | collective-permute-start | bytes 1572872 | tf_op jit(solution)/shard_map/ppermute | solution.py:512
  160.5 26.0 %collective-permute-start.15 = (bf16[256,2048]{1,0:T(8,128)(2,1)}, bf16[256,2048]{1,0:T(8,128)(2,1)}, u32[]{:S(2)}, u32[]{:S(2)}) collective-permute-start(bf16[256,2048]{1,0:T(8,128)(2,1)} %up.1.hid_ref), channel_id=1, source_target_pairs={{0,1},{1,0},{2,3},{3,2},{4,5},{5,4},{6,7},{7,6},{8,9},{9,8},{10,11... | collective-permute-start | bytes 3145736 | tf_op jit(solution)/shard_map/ppermute | solution.py:547
  164.0 1.2 copy-start.7
  169.6 27.4 %all-to-all-start.3 = ((bf16[64,8,512]{2,1,0:T(8,128)(2,1)}), bf16[64,8,512]{2,1,0:T(8,128)(2,1)S(1)}, u32[]{:S(2)}, u32[]{:S(2)}) async-start(bf16[64,8,512]{2,1,0:T(8,128)(2,1)} %bitcast.39), calls=%async_computation.3 | async-start | bytes 1048576 | tf_op jit(solution)/shard_map/all_to_all | solution.py:494
  180.3 40.3 %copy-start.3 = (f32[512,64]{1,0:T(8,128)S(1)}, f32[512,64]{1,0:T(8,128)}, u32[]{:S(2)}) copy-start(f32[512,64]{1,0:T(8,128)} %get-tuple-element.17.gates_ref) | copy-start | bytes 393220
  180.3 40.3 %copy-start.4 = (s32[64,1,16]{0,2,1:T(8,128)S(1)}, s32[64,1,16]{0,2,1:T(8,128)}, u32[]{:S(2)}) copy-start(s32[64,1,16]{0,2,1:T(8,128)} %param.20) | copy-start | bytes 12292
  180.3 40.3 %copy-start.5 = (s32[64,1]{0,1:T(1,128)S(1)}, s32[64,1]{0,1:T(1,128)}, u32[]{:S(2)}) copy-start(s32[64,1]{0,1:T(1,128)} %param.21) | copy-start | bytes 772
  220.6 20.6 %copy-start.1 = (f32[16,12288]{1,0:T(8,128)S(1)}, f32[16,12288]{1,0:T(8,128)}, u32[]{:S(2)}) copy-start(f32[16,12288]{1,0:T(8,128)} %gate_ref.3) | copy-start | bytes 2359300
  220.6 20.6 %copy-start.2 = (f32[128,2048]{1,0:T(8,128)S(1)}, f32[128,2048]{1,0:T(8,128)}, u32[]{:S(2)}) copy-start(f32[128,2048]{1,0:T(8,128)} %get-tuple-element.16.share_ref) | copy-start | bytes 3145732
  (1 other events, 0.8 us)
Sparse Core Ops, SparseCore 0:
  9.2 116.6 all-gather.1
